TPU v7x, 128 devices: a whole 4x4x4 slice. The times are simulated.
128 devices in a mesh: wide: 32 (over z, y, x_lo), narrow: 4 (over x_hi, core).
Axes of the slice: x: 4 (x_hi: 2, x_lo: 2; x = x_hi * 2 + x_lo), y: 4, z: 4, core: 2. Of those that a mesh axis runs over, the one named last changes fastest.
Arguments:
- embedded: bfloat16 [16384, 4096], P('wide'), may hold values from -6 to 6
- cotangent: bfloat16 [16384, 4096], P('wide', 'narrow'), may hold values from -3 to 3
- cross_weight: bfloat16 [4096, 4096], P(None, 'narrow'), may hold values from -0.09375 to 0.09375
- cross_bias: float32 [4096], P('narrow'), may hold values from -6 to 6
- bag_size: int32 [16384, 32], P('wide'), may hold values from 1 to 2
- row_owner: int32 [4, 16384, 16, 1], P('narrow', 'wide'), may hold values from 0 to 31; in each aligned block of 8192 rows (0 to 8191, 8192 to 16383, ..., all dimensions but the last counted through in order) at most 512 rows name the same one
- row_id: int32 [4, 16384, 16], P('narrow', 'wide'), may hold values from 0 to 2047
- emb_table: float32 [65536, 128], P('wide'), may hold values from -6 to 6
- adagrad_state: float32 [65536], P('wide'), may hold values from 0.1 to 4
Outputs:
- weight_grad: float32 [4096, 4096], P('wide', 'narrow')
- bias_grad: float32 [4096], P('narrow')
- new_table: float32 [65536, 128], P('wide')
- new_state: float32 [65536], P('wide')
Inputs may be any that keep to these rules, and one draw needn't show every extreme that they name: `row_owner`: within the entries of one device (one index n of the first dimension and 512 aligned samples), no owner is named more than 512 times, a bound that some block reaches.
All inputs are finite; a program needn't handle non-finite values.
Results may differ from a plain program's by a relative error of at most 0.007.
Values may be sent and summed in bfloat16 or wider, within the bound.
No kernel may reach another device: no remote copies, remote signals or barrier semaphores. Data moves between devices by JAX's collectives and lax.ppermute only.
A program may use at most 128 MiB of HBM per device.

v0:
```python
import math

import jax
import jax.numpy as jnp
from jax import lax
from jax.experimental import pallas as pl
from jax.experimental.pallas import tpu as pltpu
from jax.sharding import PartitionSpec as P

LEARN_RATE = 0.3
E = 128
N_WIDE = 32
CAP = 512
TAIL = 32
BLOCK = CAP + TAIL
N_ROWS = 2048
HI = 4
LO = N_ROWS // HI
F32 = jnp.float32
BF16 = jnp.bfloat16
LIGHT = pl.CostEstimate(flops=1, bytes_accessed=1, transcendentals=0)
VMEM_BYTES = 56 << 20
NT = (((1,), (1,)), ((), ()))


def z_perm(d):
    return [(i, ((i // 8 + d) % 4) * 8 + i % 8) for i in range(N_WIDE)]


def y_perm(d):
    return [(i, (i // 8) * 8 + (((i // 2) % 4 + d) % 4) * 2 + i % 2) for i in range(N_WIDE)]


def y_flip(m):
    return [(i, i ^ (2 * m)) for i in range(N_WIDE)]


def z_flip(m):
    return [(i, i ^ (8 * m)) for i in range(N_WIDE)]


X_LO = [(i, i ^ 1) for i in range(N_WIDE)]
CORE = [(i, i ^ 1) for i in range(4)]
X_HI = [(i, i ^ 2) for i in range(4)]


def slots_kernel(panel_ref, owner_ref, row_ref, bag_ref, slots_ref, ids_ref, count_ref, onehots):
    depth, samples = owner_ref.shape
    feats = depth // 2
    bag = bag_ref[pl.ds(pl.multiple_of(panel_ref[0] * feats, feats), feats), :]
    bag = jnp.concatenate([bag[k // 2 : k // 2 + 1, :] for k in range(depth)], axis=0)
    live = (lax.broadcasted_iota(jnp.int32, (depth, samples), 0) & 1) < bag
    owner = jnp.where(live, owner_ref[...], N_WIDE)
    for t in range(N_WIDE):
        onehots[t * depth : (t + 1) * depth, :] = jnp.where(owner == t, 1.0, 0.0).astype(BF16)

    size = N_WIDE * depth
    first = lax.broadcasted_iota(jnp.int32, (samples, samples), 0)
    second = lax.broadcasted_iota(jnp.int32, (samples, samples), 1)
    before = jnp.where(first < second, 1.0, 0.0).astype(BF16)
    within = jnp.dot(onehots[...], before, preferred_element_type=F32)
    in_row = jnp.dot(onehots[...], jnp.ones((samples, E), BF16), preferred_element_type=F32)
    top = jnp.floor(in_row * (1.0 / 16.0))
    low = (in_row - 16.0 * top).astype(BF16)
    top = top.astype(BF16)
    r = lax.broadcasted_iota(jnp.int32, (size, size), 0)
    c = lax.broadcasted_iota(jnp.int32, (size, size), 1)
    shift = depth.bit_length() - 1
    earlier = jnp.where((r >> shift == c >> shift) & (c < r), 1.0, 0.0).astype(BF16)
    rows_before = 16.0 * jnp.dot(earlier, top, preferred_element_type=F32) + jnp.dot(
        earlier, low, preferred_element_type=F32
    )
    t_rows = lax.broadcasted_iota(jnp.int32, (N_WIDE, size), 0)
    t_cols = lax.broadcasted_iota(jnp.int32, (N_WIDE, size), 1)
    members = jnp.where(t_rows == t_cols >> shift, 1.0, 0.0).astype(BF16)
    count_ref[...] = 16.0 * jnp.dot(members, top, preferred_element_type=F32) + jnp.dot(
        members, low, preferred_element_type=F32
    )
    place = jnp.zeros((depth, samples), F32)
    for t in range(N_WIDE):
        at = slice(t * depth, (t + 1) * depth)
        ahead = jnp.concatenate([rows_before[at, :]] * (samples // E), axis=1)
        place = place + jnp.where(owner == t, within[at, :] + ahead, 0.0)
    place = place.astype(jnp.int32)
    slots = jnp.where(live, owner * CAP + place, N_WIDE * CAP)
    for k in range(samples // E):
        slots_ref[k * depth : (k + 1) * depth, :] = slots[:, k * E : (k + 1) * E]

    marked = row_ref[...] + 1
    top = (marked >> 6).astype(F32)
    low = (marked & 63).astype(F32)
    owners = lax.broadcasted_iota(jnp.int32, (N_WIDE, samples), 0)
    places = lax.broadcasted_iota(jnp.int32, (CAP, samples), 0)
    ids = jnp.zeros((2 * N_WIDE, CAP), F32)
    for k in range(depth):
        at = slice(k, k + 1)
        mine = owners == owner[at, :]
        marks = jnp.concatenate([jnp.where(mine, top[at, :], 0.0), jnp.where(mine, low[at, :], 0.0)], axis=0)
        there = jnp.where(places == place[at, :], 1.0, 0.0).astype(BF16)
        ids = ids + lax.dot_general(
            marks.astype(BF16), there, (((1,), (1,)), ((), ())), preferred_element_type=F32
        )
    ids_ref[...] = ids


def entry_slots(panel, owner, row, bag):
    vmem = pl.BlockSpec(memory_space=pltpu.VMEM)
    depth, samples = owner.shape
    return pl.pallas_call(
        slots_kernel,
        out_shape=(
            jax.ShapeDtypeStruct((depth * samples // E, E), jnp.int32),
            jax.ShapeDtypeStruct((2 * N_WIDE, CAP), F32),
            jax.ShapeDtypeStruct((N_WIDE, E), F32),
        ),
        in_specs=[pl.BlockSpec(memory_space=pltpu.SMEM), vmem, vmem, vmem],
        out_specs=(vmem, vmem, vmem),
        scratch_shapes=[pltpu.VMEM((N_WIDE * depth, samples), BF16)],
        compiler_params=pltpu.CompilerParams(vmem_limit_bytes=VMEM_BYTES),
        cost_estimate=LIGHT,
        name="entry_slots",
    )(panel.reshape(1), owner, row, bag)


def place_kernel(
    slots_ref, base_hbm, mate_hbm, far_hbm, ids_ref, count_ref, bias_ref, out_ref, base, mate, far, rows, blocks, sems, sems_in
):
    depth = 16
    dump = N_WIDE * CAP
    loads = [
        pltpu.make_async_copy(src, dst, sems_in.at[k])
        for k, (src, dst) in enumerate(((base_hbm, base), (mate_hbm, mate), (far_hbm, far)))
    ]
    for load in loads:
        load.start()

    def clear(i, _):
        rows[pl.ds(pl.multiple_of(i * 256, 256), 256), :] = jnp.zeros((256, E), F32)
        return 0

    lax.fori_loop(0, dump // 256, clear, 0)
    for load in loads:
        load.wait()

    def place(i, _):
        first = pl.multiple_of(i * 16, 16)
        at = (first // E) * (depth * E) + first % E
        for f in range(8):
            cols = slice(f * E, (f + 1) * E)
            tile = base[pl.ds(first, 16), cols] + (
                mate[pl.ds(first, 16), cols].astype(F32) + far[pl.ds(first, 16), cols].astype(F32)
            )
            for b in range(16):
                row = tile[b : b + 1, :]
                for j in range(2):
                    slot = slots_ref[at + (2 * f + j) * E + b]
                    rows[pl.ds(slot, 1), :] = row
        return 0

    lax.fori_loop(0, base.shape[0] // 16, place, 0)

    bias_top = bias_ref[...].astype(BF16)
    bias_low = (bias_ref[...] - bias_top.astype(F32)).astype(BF16)

    def copy_out(w):
        return pltpu.make_async_copy(blocks.at[w], out_ref.at[w], sems.at[w])

    def narrow_down(w, _):
        blocks[w, :CAP, :] = rows[pl.ds(pl.multiple_of(w * CAP, CAP), CAP), :].astype(BF16)
        top = ids_ref[pl.ds(w, 1), :]
        low = ids_ref[pl.ds(N_WIDE + w, 1), :]
        count = count_ref[pl.ds(w, 1), :]
        count_top = jnp.floor(count * (1.0 / 64.0))
        parts = [top[:, k * E : (k + 1) * E] for k in range(4)] + [low[:, k * E : (k + 1) * E] for k in range(4)]
        ends = [count_top] * 4 + [count - 64.0 * count_top] * 4
        blocks[w, CAP:, :] = jnp.concatenate(
            [
                jnp.concatenate(parts, axis=0).astype(BF16),
                bias_top,
                bias_low,
                jnp.concatenate(ends, axis=0).astype(BF16),
            ],
            axis=0,
        )
        copy_out(w).start()
        return 0

    lax.fori_loop(0, N_WIDE, narrow_down, 0)

    def finish(w, _):
        copy_out(w).wait()
        return 0

    lax.fori_loop(0, N_WIDE, finish, 0)


def place_entries(slots, base, mate, far, ids, counts, bias):
    vmem = pl.BlockSpec(memory_space=pltpu.VMEM)
    hbm = pl.BlockSpec(memory_space=pltpu.HBM)
    return pl.pallas_call(
        place_kernel,
        out_shape=jax.ShapeDtypeStruct((N_WIDE, BLOCK, E), BF16),
        in_specs=[pl.BlockSpec(memory_space=pltpu.SMEM), hbm, hbm, hbm, vmem, vmem, vmem],
        out_specs=hbm,
        scratch_shapes=[
            pltpu.VMEM(base.shape, F32),
            pltpu.VMEM(base.shape, BF16),
            pltpu.VMEM(base.shape, BF16),
            pltpu.VMEM((N_WIDE * CAP + 8, E), F32),
            pltpu.VMEM((N_WIDE, BLOCK, E), BF16),
            pltpu.SemaphoreType.DMA((N_WIDE,)),
            pltpu.SemaphoreType.DMA((3,)),
        ],
        compiler_params=pltpu.CompilerParams(vmem_limit_bytes=VMEM_BYTES),
        cost_estimate=LIGHT,
        name="place_entries",
    )(slots, base, mate, far, ids, counts, bias)


def sums_kernel(count_ref, recv_ref, out_ref, bias_ref, total, left, right, todo):
    lane_rows = lax.broadcasted_iota(jnp.int32, (LO, E), 0)

    def listing(w, n):
        todo[n] = 2 * w
        n = n + jnp.where(count_ref[w] > 0, 1, 0)
        todo[n] = 2 * w + 1
        return n + jnp.where(count_ref[w] > CAP // 2, 1, 0)

    n = lax.fori_loop(0, N_WIDE, listing, 0)
    for k in range(12):
        todo[n + k] = -1
    total[...] = jnp.zeros_like(total)
    bias_ref[...] = jnp.sum(
        recv_ref[:, CAP + 8 : CAP + 16, :].astype(F32) + recv_ref[:, CAP + 16 : CAP + 24, :].astype(F32),
        axis=0,
    )

    def build(i, buf):
        for p in range(4):
            item = todo[i * 4 + p]
            w = jnp.maximum(item, 0) // 2
            half = jnp.maximum(item, 0) % 2
            ids = recv_ref[w, CAP : CAP + 16, :].astype(F32)
            row = (ids[0:4, :] * 64.0 + ids[4:8, :]).astype(jnp.int32) - 1
            row = jnp.where(half == 0, row[0:2, :], row[2:4, :])
            row = jnp.where(item < 0, -1, row)
            hi = row >> (LO.bit_length() - 1)
            lo = jnp.where(row < 0, -1, row & (LO - 1))
            hi_col = jnp.transpose(jnp.concatenate([hi] * 4, axis=0).astype(F32), (1, 0))
            for j in range(2):
                at = (2 * p + j) * E
                left[buf, :, at : at + E] = jnp.where(lane_rows == lo[j : j + 1, :], 1.0, 0.0).astype(BF16)
                v = recv_ref[w, pl.ds(pl.multiple_of(half * (CAP // 2), CAP // 2) + j * E, E), :]
                own = jnp.broadcast_to(hi_col[:, j : j + 1], (E, E)).astype(BF16)
                for h in range(HI):
                    right[buf, at : at + E, h * E : (h + 1) * E] = jnp.where(own == BF16(h), v, BF16(0))

    build(0, 0)

    def step(i, _):
        for b in range(2):
            build(2 * i + b + 1, 1 - b)
            total[...] += jnp.dot(left[b], right[b], preferred_element_type=F32)
        return 0

    lax.fori_loop(0, (n + 7) // 8, step, 0)
    for h in range(HI):
        out_ref[h * LO : (h + 1) * LO, :] = total[:, h * E : (h + 1) * E].astype(BF16)


def owned_sums(counts, recv):
    vmem = pl.BlockSpec(memory_space=pltpu.VMEM)
    return pl.pallas_call(
        sums_kernel,
        out_shape=(jax.ShapeDtypeStruct((N_ROWS, E), BF16), jax.ShapeDtypeStruct((8, E), F32)),
        in_specs=[pl.BlockSpec(memory_space=pltpu.SMEM), vmem],
        out_specs=(vmem, vmem),
        scratch_shapes=[
            pltpu.VMEM((LO, HI * E), F32),
            pltpu.VMEM((2, LO, 2 * CAP), BF16),
            pltpu.VMEM((2, 2 * CAP, HI * E), BF16),
            pltpu.SMEM((2 * N_WIDE + 16,), jnp.int32),
        ],
        compiler_params=pltpu.CompilerParams(vmem_limit_bytes=VMEM_BYTES),
        cost_estimate=LIGHT,
        name="owned_sums",
    )(counts, recv)


def summed(own, others):
    total = own.astype(F32)
    for other in others:
        total = total + other.astype(F32)
    return total


def own_chunk(a):
    return pl.multiple_of(a * 1024, 1024)


def ring_term(route, turned, embedded, z, y, d):
    part = turned[route * 512 : (route + 1) * 512, :]
    if route == 0:
        rows = embedded[:, pl.ds(own_chunk((z + d) % 4), 1024)]
        return jnp.dot(part, rows, preferred_element_type=F32)
    start = ((y + d) % 4) * 256
    blocks = [embedded[:, pl.ds(pl.multiple_of(k * 1024 + start, 256), 256)] for k in range(4)]
    return jnp.concatenate([jnp.dot(part, rows, preferred_element_type=F32) for rows in blocks], axis=1)


def sent_kernel(n_ref, z_ref, y_ref, cot_hbm, embedded_hbm, weight_hbm, *refs):
    parts_hbm, first_hbm, second_hbm, (scaled_hbm, turned_hbm, bias_ref) = refs[:3], refs[3:7], refs[7:11], refs[11:14]
    cot, embedded, weight, scaled, turned, parts, first, second, sems, sems_out = refs[14:]
    n, z, y = n_ref[0], z_ref[0], y_ref[0]

    def columns(q):
        at = pl.ds(own_chunk(n ^ q), 1024)
        return pltpu.make_async_copy(embedded_hbm.at[:, at], embedded.at[:, at], sems.at[q])

    def rows(q):
        at = pl.ds(own_chunk(n ^ q), 1024)
        return pltpu.make_async_copy(weight_hbm.at[at, :], weight.at[q - 1], sems.at[3 + q])

    outs = [(parts.at[q], parts_hbm[q]) for q in range(3)]
    outs += [(first.at[q], first_hbm[q]) for q in range(4)] + [(second.at[q], second_hbm[q]) for q in range(4)]
    outs += [(scaled, scaled_hbm), (turned, turned_hbm)]
    outs = [pltpu.make_async_copy(src, dst, sems_out.at[k]) for k, (src, dst) in enumerate(outs)]

    get_cot = pltpu.make_async_copy(cot_hbm, cot, sems.at[7])
    get_cot.start()
    columns(0).start()
    rows(3).start()
    get_cot.wait()
    columns(0).wait()
    for q in (1, 2):
        rows(q).start()
    for q in (1, 2, 3):
        columns(q).start()
    grads = (cot[...].astype(F32) * embedded[:, pl.ds(own_chunk(n), 1024)].astype(F32)).astype(BF16)
    scaled[...] = grads
    turned[...] = jnp.transpose(grads, (1, 0))
    sums = jnp.sum(grads.astype(F32), axis=0, keepdims=True)
    bias_ref[...] = jnp.concatenate([sums[:, k * E : (k + 1) * E] for k in range(8)], axis=0)
    outs[11].start()
    outs[12].start()
    for k, q in enumerate((3, 1, 2)):
        rows(q).wait()
        part = lax.dot_general(scaled[...], weight[q - 1], NT, preferred_element_type=F32)
        parts[k] = part.astype(BF16)
        outs[k].start()
    for q in (1, 2, 3):
        columns(q).wait()
    for route in range(2):
        term = ring_term(route, turned, embedded, z, y, 2).astype(BF16)
        for way in range(2):
            first[2 * route + way, :256, :] = term[way * 256 : (way + 1) * 256, :]
        for way in range(2):
            q = 2 * route + way
            term = ring_term(route, turned, embedded, z, y, 3 if way else 1).astype(BF16)
            first[q, 256:, :] = term[(1 - way) * 256 : (2 - way) * 256, :]
            second[q] = term[way * 256 : (way + 1) * 256, :]
            outs[3 + q].start()
            outs[7 + q].start()
    for copy in outs:
        copy.wait()


def sent_terms(n, z, y, cotangent, embedded, weight):
    hbm = pl.BlockSpec(memory_space=pltpu.HBM)
    smem = pl.BlockSpec(memory_space=pltpu.SMEM)
    samples, width = cotangent.shape
    shape = jax.ShapeDtypeStruct
    full, half = shape((samples, width), BF16), shape((256, 1024), BF16)
    results = pl.pallas_call(
        sent_kernel,
        out_shape=[full] * 3 + [shape((512, 1024), BF16)] * 4 + [half] * 4
        + [full, shape((width, samples), BF16), shape((8, E), F32)],
        in_specs=[smem] * 3 + [hbm] * 3,
        out_specs=[hbm] * 13 + [pl.BlockSpec(memory_space=pltpu.VMEM)],
        scratch_shapes=[
            pltpu.VMEM(cotangent.shape, BF16),
            pltpu.VMEM(embedded.shape, BF16),
            pltpu.VMEM((3, 1024, 1024), BF16),
            pltpu.VMEM((samples, width), BF16),
            pltpu.VMEM((width, samples), BF16),
            pltpu.VMEM((3, samples, width), BF16),
            pltpu.VMEM((4, 512, 1024), BF16),
            pltpu.VMEM((4, 256, 1024), BF16),
            pltpu.SemaphoreType.DMA((8,)),
            pltpu.SemaphoreType.DMA((13,)),
        ],
        compiler_params=pltpu.CompilerParams(vmem_limit_bytes=VMEM_BYTES),
        cost_estimate=LIGHT,
        name="sent_terms",
    )(n, z, y, cotangent, embedded, weight)
    return results[:3], results[3:7], results[7:11], *results[11:]


def kept_kernel(n_ref, z_ref, y_ref, cot_hbm, embedded_hbm, weight_hbm, bias_ref, scaled_hbm, turned_hbm, *refs):
    base_hbm, own_hbm, (cot, embedded, weight, scaled, turned, cross, base, own, sems, sems_out) = refs[0], refs[1:3], refs[3:]
    n, z, y = n_ref[0], z_ref[0], y_ref[0]

    def columns(q):
        at = pl.ds(own_chunk(n ^ q), 1024)
        return pltpu.make_async_copy(embedded_hbm.at[:, at], embedded.at[:, at], sems.at[q])

    def rows(q):
        at = pl.ds(own_chunk(n ^ q), 1024)
        return pltpu.make_async_copy(weight_hbm.at[at, :], weight.at[q], sems.at[4 + q])

    others = [(scaled_hbm, scaled), (cot_hbm, cot), (turned_hbm, turned)]
    others = [pltpu.make_async_copy(src, dst, sems.at[8 + k]) for k, (src, dst) in enumerate(others)]
    outs = [(base, base_hbm), (own.at[0], own_hbm[0]), (own.at[1], own_hbm[1])]
    outs = [pltpu.make_async_copy(src, dst, sems_out.at[k]) for k, (src, dst) in enumerate(outs)]
    rows(0).start()
    columns(0).start()
    others[0].start()
    rows(0).wait()
    columns(0).wait()
    for q in (1, 2, 3):
        rows(q).start()
        columns(q).start()
    others[1].start()
    others[2].start()
    cross[...] = jnp.dot(embedded[:, pl.ds(own_chunk(n), 1024)], weight[0], preferred_element_type=F32)
    others[0].wait()
    base[...] = lax.dot_general(scaled[...], weight[0], NT, preferred_element_type=F32)
    for q in (1, 2):
        rows(q).wait()
        columns(q).wait()
        cross[...] += jnp.dot(embedded[:, pl.ds(own_chunk(n ^ q), 1024)], weight[q], preferred_element_type=F32)
    rows(3).wait()
    columns(3).wait()
    others[1].wait()
    grad = cot[...].astype(F32)
    last = jnp.dot(embedded[:, pl.ds(own_chunk(n ^ 3), 1024)], weight[3], preferred_element_type=F32)
    base[...] += grad + grad * (cross[...] + last + bias_ref[...])
    outs[0].start()
    others[2].wait()
    for route in range(2):
        own[route] = ring_term(route, turned, embedded, z, y, 0).astype(BF16)
        outs[1 + route].start()
    for copy in outs:
        copy.wait()


def kept_terms(n, z, y, cotangent, embedded, weight, bias, scaled, turned):
    hbm = pl.BlockSpec(memory_space=pltpu.HBM)
    smem = pl.BlockSpec(memory_space=pltpu.SMEM)
    samples, width = cotangent.shape
    return pl.pallas_call(
        kept_kernel,
        out_shape=[jax.ShapeDtypeStruct((samples, width), F32)] + [jax.ShapeDtypeStruct((512, 1024), BF16)] * 2,
        in_specs=[smem] * 3 + [hbm] * 3 + [pl.BlockSpec(memory_space=pltpu.VMEM)] + [hbm] * 2,
        out_specs=[hbm] * 3,
        scratch_shapes=[
            pltpu.VMEM(cotangent.shape, BF16),
            pltpu.VMEM(embedded.shape, BF16),
            pltpu.VMEM((4, 1024, 1024), BF16),
            pltpu.VMEM((samples, width), BF16),
            pltpu.VMEM((width, samples), BF16),
            pltpu.VMEM((samples, width), F32),
            pltpu.VMEM((samples, width), F32),
            pltpu.VMEM((2, 512, 1024), BF16),
            pltpu.SemaphoreType.DMA((11,)),
            pltpu.SemaphoreType.DMA((3,)),
        ],
        compiler_params=pltpu.CompilerParams(vmem_limit_bytes=VMEM_BYTES),
        cost_estimate=LIGHT,
        name="kept_terms",
    )(n, z, y, cotangent, embedded, weight, bias.reshape(1, -1), scaled, turned)


def halves_of(array, bit, axis):
    size = array.shape[axis] // 2
    return (
        lax.dynamic_slice_in_dim(array, bit * size, size, axis),
        lax.dynamic_slice_in_dim(array, (1 - bit) * size, size, axis),
    )


def over_narrow(part, core):
    rows = part.shape[0] // 2
    keep = lax.dynamic_slice_in_dim(part, core * rows, rows, 0)
    send = lax.dynamic_slice_in_dim(part, (1 - core) * rows, rows, 0)
    chip = summed(keep, [lax.ppermute(send, "narrow", CORE)]).astype(BF16)
    mine = summed(chip, [lax.ppermute(chip, "narrow", X_HI)])
    mate = lax.ppermute(mine, "narrow", CORE)
    low = jnp.where(core == 0, mine, mate)
    high = jnp.where(core == 0, mate, mine)
    return jnp.concatenate([low, high], axis=0)


def body(
    embedded,
    cotangent,
    cross_weight,
    cross_bias,
    bag_size,
    row_owner,
    row_id,
    emb_table,
    adagrad_state,
):
    panel = lax.axis_index("narrow")
    wide = lax.axis_index("wide")
    z, y, x_lo = wide // 8, (wide // 2) % 4, wide % 2
    core = panel % 2
    batch_rows = cotangent.shape[0]
    norm_factor = 1.0 / math.sqrt(batch_rows * N_WIDE)

    at = (panel.reshape(1), z.reshape(1), y.reshape(1))

    parts, first, second, scaled, turned, bias_part = sent_terms(*at, cotangent, embedded, cross_weight)
    from_mate_far = lax.ppermute(parts[0], "narrow", CORE)
    from_mate = lax.ppermute(parts[1], "narrow", CORE)
    ways = [z_perm(1), z_perm(3), y_perm(1), y_perm(3)]
    first = [lax.ppermute(first[q], "wide", ways[q]) for q in range(4)]
    chip_far = (parts[2].astype(F32) + from_mate_far.astype(F32)).astype(BF16)
    chip_far, scaled, from_mate = lax.optimization_barrier((chip_far, scaled, from_mate))
    far = lax.ppermute(chip_far, "narrow", X_HI)

    base, *own = kept_terms(*at, cotangent, embedded, cross_weight, cross_bias, scaled, turned)
    row_owner, row_id, bag_size, base = lax.optimization_barrier((row_owner, row_id, bag_size, base))
    slots, ids, counts = entry_slots(
        panel, row_owner.reshape(row_owner.shape[1:3]).T, row_id.reshape(row_id.shape[1:]).T, bag_size.T
    )
    slots, ids, counts, far, *first = lax.optimization_barrier((slots, ids, counts, far, *first))
    second = [(second[q].astype(F32) + first[q][:256].astype(F32)).astype(BF16) for q in range(4)]
    slots, *second = lax.optimization_barrier((slots, *second))
    second = [lax.ppermute(second[q], "wide", ways[q]) for q in range(4)]

    payload = place_entries(slots.reshape(-1), base, from_mate, far, ids, counts, bias_part)
    payload, *second = lax.optimization_barrier((payload, *second))
    recv = lax.all_to_all(payload, "wide", split_axis=0, concat_axis=0, tiled=True)

    kept = []
    for route, (place, flip) in enumerate(((y, y_flip), (z, z_flip))):
        up, down = 2 * route, 2 * route + 1
        total = own[route].astype(F32) + jnp.concatenate(
            [second[up].astype(F32) + first[down][256:].astype(F32), second[down].astype(F32) + first[up][256:].astype(F32)],
            axis=0,
        )
        keep, send = halves_of(total, place // 2, 1)
        kept.append(keep + lax.ppermute(send.astype(BF16), "wide", flip(2)).astype(F32))
    quarters = []
    for total, place in zip(kept, (y, z)):
        keep, send = halves_of(total, place % 2, 1)
        quarters.append((keep.astype(BF16), send.astype(BF16)))
    recv, *sends = lax.optimization_barrier((recv, quarters[0][1], quarters[1][1]))
    pair = jnp.concatenate(
        [
            summed(quarters[0][0], [lax.ppermute(sends[0], "wide", y_flip(1))]),
            summed(quarters[1][0], [lax.ppermute(sends[1], "wide", z_flip(1))]),
        ],
        axis=0,
    ).astype(BF16)
    keep, send = halves_of(pair, x_lo, 1)
    weight_grad = summed(keep, [lax.ppermute(send, "wide", X_LO)]).T * norm_factor

    recv_counts = (recv[:, CAP + 24, 0].astype(F32) * 64.0 + recv[:, CAP + 28, 0].astype(F32)).astype(jnp.int32)
    sums, bias_sums = owned_sums(recv_counts, recv)
    bias_grad = bias_sums.reshape(-1) * norm_factor
    row_grad = over_narrow(sums, core)
    new_state = adagrad_state + jnp.mean(row_grad * row_grad, axis=1)
    new_table = emb_table - LEARN_RATE * row_grad / jnp.sqrt(new_state)[:, None]
    return (weight_grad, bias_grad, new_table, new_state)


def solution(mesh):
    in_specs = (
        P("wide", None),
        P("wide", "narrow"),
        P(None, "narrow"),
        P("narrow"),
        P("wide", None),
        P("narrow", "wide", None, None),
        P("narrow", "wide", None),
        P("wide", None),
        P("wide"),
    )
    out_specs = (P("wide", "narrow"), P("narrow"), P("wide", None), P("wide"))
    return jax.shard_map(body, mesh=mesh, in_specs=in_specs, out_specs=out_specs, check_vma=False)
```

profile of v0, /device:TPU:24, one launch (start us, length us, event | category | flops | bytes accessed | tf_op | source)
XLA Modules:
  0.0 181.5 jit_solution(10338504215223903291)
XLA Ops:
  0.7 11.6 %sent_terms.1 = (bf16[512,1024]{1,0:T(8,128)(2,1)}, bf16[512,1024]{1,0:T(8,128)(2,1)}, bf16[512,1024]{1,0:T(8,128)(2,1)}, bf16[512,1024]{1,0:T(8,128)(2,1)}, bf1...) custom-call(s32[1]{0:T(128)} %bitcast.n_ref.panel_ref, ...), custom_call_target="tpu_custom_call" | custom-call | flops 1 | bytes 1 | tf_op jit(solution)/shard_map/sent_terms/pallas_call | solution.py:374
  12.4 0.5 collective-permute-start.1
  12.9 1.9 %collective-permute-start.3 = (bf16[512,1024]{1,0:T(8,128)(2,1)}, bf16[512,1024]{1,0:T(8,128)(2,1)S(1)}, u32[]{:S(2)}, u32[]{:S(2)}) collective-permute-start(bf16[512,1024]{1,0:T(8,128)(2,1)} %get-tuple-element.69), channel_id=1, source_target_pairs={{0,32},{4,36},{8,40},{12,44},{16,48},{20,52},{24,56},{28,60},{32,6... | collective-permute-start | bytes 3145736 | tf_op jit(solution)/shard_map/ppermute | solution.py:518
  14.8 2.1 %collective-permute-start.4 = (bf16[512,1024]{1,0:T(8,128)(2,1)}, bf16[512,1024]{1,0:T(8,128)(2,1)S(1)}, u32[]{:S(2)}, u32[]{:S(2)}) collective-permute-start(bf16[512,1024]{1,0:T(8,128)(2,1)} %get-tuple-element.70), channel_id=1, source_target_pairs={{0,96},{4,100},{8,104},{12,108},{16,112},{20,116},{24,120},{28,124... | collective-permute-start | bytes 3145736 | tf_op jit(solution)/shard_map/ppermute | solution.py:518
  17.2 1.8 collective-permute-start.6
  19.0 1.6 add_convert_fusion
  20.6 3.3 %collective-permute-start.2 = (bf16[512,1024]{1,0:T(8,128)(2,1)S(1)}, bf16[512,1024]{1,0:T(8,128)(2,1)S(1)}, u32[]{:S(2)}, u32[]{:S(2)}) collective-permute-start(bf16[512,1024]{1,0:T(8,128)(2,1)S(1)} %add_convert_fusion), channel_id=1, source_target_pairs={{0,2},{1,3},{2,0},{3,1},{4,6},{5,7},{6,4},{7,5},{8,10},{9,11},{10,... | collective-permute-start | bytes 3145736 | tf_op jit(solution)/shard_map/ppermute | solution.py:521
  23.9 11.1 %kept_terms.1 = (f32[512,1024]{1,0:T(8,128)}, bf16[512,1024]{1,0:T(8,128)(2,1)}, bf16[512,1024]{1,0:T(8,128)(2,1)}) custom-call(s32[1]{0:T(128)} %bitcast.n_ref.panel_ref, s32[1]{0:T(128)} %bitcast.1.z_ref, s32[1]{0:T(128)} %bitcast.2.y_ref, bf16[512,1024]{1,0:T(8,128)(2,1)} %cot_hbm.3, bf16[512,4096]{1,0:T(8,128)(2,1)} %embedded_hbm.3, ...), custom_call_target="tpu_custom_call" | custom-call | flops 1 | bytes 1 | tf_op jit(solution)/shard_map/kept_terms/pallas_call | solution.py:451
  35.0 0.6 copy.18
  35.6 5.4 %entry_slots.1 = (s32[64,128]{1,0:T(8,128)}, f32[64,512]{1,0:T(8,128)}, f32[32,128]{1,0:T(8,128)}) custom-call(s32[1]{0:T(128)} %bitcast.n_ref.panel_ref, s32[16,512]{1,0:T(8,128)} %bitcast.18, s32[16,512]{1,0:T(8,128)} %bitcast.21, s32[32,512]{1,0:T(8,128)} %bitcast.19), custom_call_target="tpu_custom_call" | custom-call | flops 1 | bytes 1 | tf_op jit(solution)/shard_map/entry_slots/pallas_call | solution.py:109
  41.1 0.9 collective-permute-done.5
  42.0 1.2 collective-permute-done.6
  43.2 3.5 %collective-permute-done.2.far_hbm = bf16[512,1024]{1,0:T(8,128)(2,1)S(1)} collective-permute-done((bf16[512,1024]{1,0:T(8,128)(2,1)S(1)}, bf16[512,1024]{1,0:T(8,128)(2,1)S(1)}, u32[]{:S(2)}, u32[]{:S(2)}) %collective-permute-start.2) | collective-permute-done | bytes 1048608 | tf_op jit(solution)/shard_map/ppermute | solution.py:521
  46.7 2.0 %add_convert_fusion.1 = (bf16[256,1024]{1,0:T(8,128)(2,1)S(1)}, bf16[256,1024]{1,0:T(8,128)(2,1)S(1)}) fusion(bf16[256,1024]{1,0:T(8,128)(2,1)} %get-tuple-element.80, bf16[512,1024]{1,0:T(8,128)(2,1)S(1)} %collective-permute-done.6, bf16[512,1024]{1,0:T(8,128)(2,1)S(1)} %collective-permute-done.5, bf16[256,1024]{1,0:T(8,128)(2,1)} %get-tuple-element.78), kind=kLoop, calls=%fused_computation.14 | loop fusion | flops 2097152 | bytes 3145728 | tf_op jit(solution)/shard_map/convert_element_type | solution.py:529
  48.7 1.2 add_convert_fusion.3
  49.9 0.8 collective-permute-start.10
  50.7 3.2 %collective-permute-start.8 = (bf16[256,1024]{1,0:T(8,128)(2,1)S(1)}, bf16[256,1024]{1,0:T(8,128)(2,1)}, u32[]{:S(2)}, u32[]{:S(2)}) collective-permute-start(bf16[256,1024]{1,0:T(8,128)(2,1)S(1)} %get-tuple-element.90), channel_id=1, source_target_pairs={{0,96},{4,100},{8,104},{12,108},{16,112},{20,116},{24,120},{28,124... | collective-permute-start | bytes 1572872 | tf_op jit(solution)/shard_map/ppermute | solution.py:531
  53.9 2.5 %collective-permute-start.9 = (bf16[256,1024]{1,0:T(8,128)(2,1)S(1)}, bf16[256,1024]{1,0:T(8,128)(2,1)}, u32[]{:S(2)}, u32[]{:S(2)}) collective-permute-start(bf16[256,1024]{1,0:T(8,128)(2,1)S(1)} %get-tuple-element.91), channel_id=1, source_target_pairs={{0,8},{4,12},{8,16},{12,20},{16,24},{20,28},{24,0},{28,4},{32,40},... | collective-permute-start | bytes 1572872 | tf_op jit(solution)/shard_map/ppermute | solution.py:531
  56.4 12.7 %place_entries.1 = bf16[32,544,128]{2,1,0:T(8,128)(2,1)} custom-call(s32[8192]{0:T(1024)} %bitcast.20, f32[512,1024]{1,0:T(8,128)} %get-tuple-element.83.base_hbm, bf16[512,1024]{1,0:T(8,128)(2,1)} %copy-done.7, bf16[512,1024]{1,0:T(8,128)(2,1)} %copy-done.8, f32[64,512]{1,0:T(8,128)} %get-tuple-element.86.ids_ref, f32[32,128]{1,0:T(8,128)} %get-tuple-element.87.count_ref, ...), custom_call_target="tpu_custom_call" | custom-call | flops 1 | bytes 1 | tf_op jit(solution)/shard_map/place_entries/pallas_call | solution.py:200
  69.1 5.7 %all-to-all-start = ((bf16[32,544,128]{2,1,0:T(8,128)(2,1)}), bf16[32,544,128]{2,1,0:T(8,128)(2,1)}, u32[]{:S(2)}, u32[]{:S(2)}) async-start(bf16[32,544,128]{2,1,0:T(8,128)(2,1)} %place_entries.1), calls=%async_computation | async-start | bytes 8912896 | tf_op jit(solution)/shard_map/all_to_all | solution.py:535
  74.8 1.3 convert_add_fusion.2
  76.1 1.2 convert_add_fusion.1
  77.7 0.9 dynamic-slice_convert_fusion
  78.6 3.0 %collective-permute-start.12 = (bf16[512,512]{1,0:T(8,128)(2,1)}, bf16[512,512]{1,0:T(8,128)(2,1)}, u32[]{:S(2)}, u32[]{:S(2)}) collective-permute-start(bf16[512,512]{1,0:T(8,128)(2,1)} %dynamic-slice_convert_fusion), channel_id=1, source_target_pairs={{0,64},{4,68},{8,72},{12,76},{16,80},{20,84},{24,88},{28,92},{32,9... | collective-permute-start | bytes 1572872 | tf_op jit(solution)/shard_map/ppermute | solution.py:545
  81.6 1.2 convert_add_fusion.5
  82.8 1.2 convert_add_fusion.4
  84.5 1.3 copy-done
  85.8 0.9 dynamic-slice_convert_fusion.1
  86.7 1.4 collective-permute-start.11
  88.1 46.9 %collective-permute-done.12 = bf16[512,512]{1,0:T(8,128)(2,1)} collective-permute-done((bf16[512,512]{1,0:T(8,128)(2,1)}, bf16[512,512]{1,0:T(8,128)(2,1)}, u32[]{:S(2)}, u32[]{:S(2)}) %collective-permute-start.12) | collective-permute-done | bytes 524320 | tf_op jit(solution)/shard_map/ppermute | solution.py:545
  135.1 1.2 convert_add_fusion
  136.5 2.1 %convert_reduce_fusion.count_ref = s32[32]{0:T(128)} fusion(bf16[32,544,128]{2,1,0:T(8,128)(2,1)} %all-to-all-done.recv_ref), kind=kLoop, calls=%fused_computation.36 | loop fusion | flops 160 | bytes 256 | tf_op jit(solution)/shard_map/convert_element_type | solution.py:561
  138.6 10.7 %owned_sums.1 = (bf16[2048,128]{1,0:T(8,128)(2,1)}, f32[8,128]{1,0:T(8,128)}) custom-call(s32[32]{0:T(128)} %convert_reduce_fusion.count_ref, bf16[32,544,128]{2,1,0:T(8,128)(2,1)} %all-to-all-done.recv_ref), custom_call_target="tpu_custom_call" | custom-call | flops 1 | bytes 1 | tf_op jit(solution)/shard_map/owned_sums/pallas_call | solution.py:273
  149.3 1.0 constant_dynamic-slice_fusion
  150.4 2.6 %collective-permute-start.14 = (bf16[512,256]{1,0:T(8,128)(2,1)S(1)}, bf16[512,256]{1,0:T(8,128)(2,1)S(1)}, u32[]{:S(2)}, u32[]{:S(2)}) collective-permute-start(bf16[512,256]{1,0:T(8,128)(2,1)S(1)} %dynamic-slice_convert_fusion.3), channel_id=1, source_target_pairs={{0,32},{4,36},{8,40},{12,44},{16,48},{20,52},{24,56},{28,60},{32,0... | collective-permute-start | bytes 786440 | tf_op jit(solution)/shard_map/ppermute | solution.py:554
  153.0 0.6 collective-permute-start.13
  153.6 1.0 add_convert_fusion.5
  154.7 2.8 %collective-permute-start.17 = (bf16[1024,128]{1,0:T(8,128)(2,1)S(1)}, bf16[1024,128]{1,0:T(8,128)(2,1)S(1)}, u32[]{:S(2)}, u32[]{:S(2)}) collective-permute-start(bf16[1024,128]{1,0:T(8,128)(2,1)S(1)} %add_convert_fusion.5), channel_id=1, source_target_pairs={{0,2},{1,3},{2,0},{3,1},{4,6},{5,7},{6,4},{7,5},{8,10},{9,11},{10,... | collective-permute-start | bytes 786440 | tf_op jit(solution)/shard_map/ppermute | solution.py:487
  157.5 2.4 %collective-permute-done.14 = bf16[512,256]{1,0:T(8,128)(2,1)S(1)} collective-permute-done((bf16[512,256]{1,0:T(8,128)(2,1)S(1)}, bf16[512,256]{1,0:T(8,128)(2,1)S(1)}, u32[]{:S(2)}, u32[]{:S(2)}) %collective-permute-start.14) | collective-permute-done | bytes 262176 | tf_op jit(solution)/shard_map/ppermute | solution.py:554
  160.0 1.4 collective-permute-done.13
  161.5 2.9 %collective-permute-done.17 = bf16[1024,128]{1,0:T(8,128)(2,1)S(1)} collective-permute-done((bf16[1024,128]{1,0:T(8,128)(2,1)S(1)}, bf16[1024,128]{1,0:T(8,128)(2,1)S(1)}, u32[]{:S(2)}, u32[]{:S(2)}) %collective-permute-start.17) | collective-permute-done | bytes 262176 | tf_op jit(solution)/shard_map/ppermute | solution.py:487
  164.3 0.8 convert_add_fusion.6
  165.2 5.9 %collective-permute-start.15 = (bf16[1024,128]{1,0:T(8,128)(2,1)S(1)}, bf16[1024,128]{1,0:T(8,128)(2,1)S(1)}, u32[]{:S(2)}, u32[]{:S(2)}) collective-permute-start(bf16[1024,128]{1,0:T(8,128)(2,1)S(1)} %fusion), channel_id=1, source_target_pairs={{0,4},{4,0},{8,12},{12,8},{16,20},{20,16},{24,28},{28,24},{32,36},... | collective-permute-start | bytes 786440 | tf_op jit(solution)/shard_map/ppermute | solution.py:559
  171.1 0.6 multiply_bitcast_fusion.1
  171.7 6.4 %collective-permute-done.15 = bf16[1024,128]{1,0:T(8,128)(2,1)S(1)} collective-permute-done((bf16[1024,128]{1,0:T(8,128)(2,1)S(1)}, bf16[1024,128]{1,0:T(8,128)(2,1)S(1)}, u32[]{:S(2)}, u32[]{:S(2)}) %collective-permute-start.15) | collective-permute-done | bytes 262176 | tf_op jit(solution)/shard_map/ppermute | solution.py:559
  178.1 1.0 copy.15
  179.6 0.6 fusion.2
  180.2 1.3 divide_subtract_fusion
  (55 shorter events, 2.1 us)
Async XLA Ops:
  12.3 4.9 %collective-permute-start = (bf16[512,1024]{1,0:T(8,128)(2,1)}, bf16[512,1024]{1,0:T(8,128)(2,1)S(1)}, u32[]{:S(2)}, u32[]{:S(2)}) collective-permute-start(bf16[512,1024]{1,0:T(8,128)(2,1)} %get-tuple-element.55), channel_id=1, source_target_pairs={{0,1},{1,0},{2,3},{3,2},{4,5},{5,4},{6,7},{7,6},{8,9},{9,8},{10,11... | collective-permute-start | bytes 3145736 | tf_op jit(solution)/shard_map/ppermute | solution.py:515
  12.4 8.2 %collective-permute-start.1 = (bf16[512,1024]{1,0:T(8,128)(2,1)}, bf16[512,1024]{1,0:T(8,128)(2,1)S(1)}, u32[]{:S(2)}, u32[]{:S(2)}) collective-permute-start(bf16[512,1024]{1,0:T(8,128)(2,1)} %get-tuple-element.57), channel_id=1, source_target_pairs={{0,1},{1,0},{2,3},{3,2},{4,5},{5,4},{6,7},{7,6},{8,9},{9,8},{10,11... | collective-permute-start | bytes 3145736 | tf_op jit(solution)/shard_map/ppermute | solution.py:516
  12.9 28.2 %collective-permute-start.3 = (bf16[512,1024]{1,0:T(8,128)(2,1)}, bf16[512,1024]{1,0:T(8,128)(2,1)S(1)}, u32[]{:S(2)}, u32[]{:S(2)}) collective-permute-start(bf16[512,1024]{1,0:T(8,128)(2,1)} %get-tuple-element.69), channel_id=1, source_target_pairs={{0,32},{4,36},{8,40},{12,44},{16,48},{20,52},{24,56},{28,60},{32,6... | collective-permute-start | bytes 3145736 | tf_op jit(solution)/shard_map/ppermute | solution.py:518
  14.8 26.3 %collective-permute-start.4 = (bf16[512,1024]{1,0:T(8,128)(2,1)}, bf16[512,1024]{1,0:T(8,128)(2,1)S(1)}, u32[]{:S(2)}, u32[]{:S(2)}) collective-permute-start(bf16[512,1024]{1,0:T(8,128)(2,1)} %get-tuple-element.70), channel_id=1, source_target_pairs={{0,96},{4,100},{8,104},{12,108},{16,112},{20,116},{24,120},{28,124... | collective-permute-start | bytes 3145736 | tf_op jit(solution)/shard_map/ppermute | solution.py:518
  16.9 25.1 %collective-permute-start.5 = (bf16[512,1024]{1,0:T(8,128)(2,1)}, bf16[512,1024]{1,0:T(8,128)(2,1)S(1)}, u32[]{:S(2)}, u32[]{:S(2)}) collective-permute-start(bf16[512,1024]{1,0:T(8,128)(2,1)} %get-tuple-element.71), channel_id=1, source_target_pairs={{0,8},{4,12},{8,16},{12,20},{16,24},{20,28},{24,0},{28,4},{32,40},... | collective-permute-start | bytes 3145736 | tf_op jit(solution)/shard_map/ppermute | solution.py:518
  17.2 26.1 %collective-permute-start.6 = (bf16[512,1024]{1,0:T(8,128)(2,1)}, bf16[512,1024]{1,0:T(8,128)(2,1)S(1)}, u32[]{:S(2)}, u32[]{:S(2)}) collective-permute-start(bf16[512,1024]{1,0:T(8,128)(2,1)} %get-tuple-element.72), channel_id=1, source_target_pairs={{0,24},{4,28},{8,0},{12,4},{16,8},{20,12},{24,16},{28,20},{32,56},... | collective-permute-start | bytes 3145736 | tf_op jit(solution)/shard_map/ppermute | solution.py:518
  20.6 14.4 %copy-start.7 = (bf16[512,1024]{1,0:T(8,128)(2,1)}, bf16[512,1024]{1,0:T(8,128)(2,1)S(1)}, u32[]{:S(2)}) copy-start(bf16[512,1024]{1,0:T(8,128)(2,1)S(1)} %collective-permute-done.1.mate_hbm) | copy-start | bytes 3145732
  20.6 26.1 %collective-permute-start.2 = (bf16[512,1024]{1,0:T(8,128)(2,1)S(1)}, bf16[512,1024]{1,0:T(8,128)(2,1)S(1)}, u32[]{:S(2)}, u32[]{:S(2)}) collective-permute-start(bf16[512,1024]{1,0:T(8,128)(2,1)S(1)} %add_convert_fusion), channel_id=1, source_target_pairs={{0,2},{1,3},{2,0},{3,1},{4,6},{5,7},{6,4},{7,5},{8,10},{9,11},{10,... | collective-permute-start | bytes 3145736 | tf_op jit(solution)/shard_map/ppermute | solution.py:521
  23.9 11.1 %copy-start.11 = (s32[1,512,16,1]{1,3,2,0:T(1,128)S(1)}, s32[1,512,16,1]{1,3,2,0:T(1,128)}, u32[]{:S(2)}) copy-start(s32[1,512,16,1]{1,3,2,0:T(1,128)} %param.14) | copy-start | bytes 98308
  35.0 13.7 %copy-start.9 = (bf16[256,1024]{1,0:T(8,128)(2,1)S(1)}, bf16[256,1024]{1,0:T(8,128)(2,1)}, u32[]{:S(2)}) copy-start(bf16[256,1024]{1,0:T(8,128)(2,1)} %get-tuple-element.74) | copy-start | bytes 1572868
  35.0 13.7 %copy-start.10 = (bf16[256,1024]{1,0:T(8,128)(2,1)S(1)}, bf16[256,1024]{1,0:T(8,128)(2,1)}, u32[]{:S(2)}) copy-start(bf16[256,1024]{1,0:T(8,128)(2,1)} %get-tuple-element.76) | copy-start | bytes 1572868
  41.1 8.8 %copy-start.5 = (bf16[512,1024]{1,0:T(8,128)(2,1)}, bf16[512,1024]{1,0:T(8,128)(2,1)S(1)}, u32[]{:S(2)}) copy-start(bf16[512,1024]{1,0:T(8,128)(2,1)S(1)} %collective-permute-done.4) | copy-start | bytes 3145732
  46.7 3.2 %copy-start.8 = (bf16[512,1024]{1,0:T(8,128)(2,1)}, bf16[512,1024]{1,0:T(8,128)(2,1)S(1)}, u32[]{:S(2)}) copy-start(bf16[512,1024]{1,0:T(8,128)(2,1)S(1)} %collective-permute-done.2.far_hbm) | copy-start | bytes 3145732
  49.9 19.2 %collective-permute-start.10 = (bf16[256,1024]{1,0:T(8,128)(2,1)S(1)}, bf16[256,1024]{1,0:T(8,128)(2,1)}, u32[]{:S(2)}, u32[]{:S(2)}) collective-permute-start(bf16[256,1024]{1,0:T(8,128)(2,1)S(1)} %get-tuple-element.92), channel_id=1, source_target_pairs={{0,24},{4,28},{8,0},{12,4},{16,8},{20,12},{24,16},{28,20},{32,56},... | collective-permute-start | bytes 1572872 | tf_op jit(solution)/shard_map/ppermute | solution.py:531
  50.6 18.4 %collective-permute-start.7 = (bf16[256,1024]{1,0:T(8,128)(2,1)}, bf16[256,1024]{1,0:T(8,128)(2,1)}, u32[]{:S(2)}, u32[]{:S(2)}) collective-permute-start(bf16[256,1024]{1,0:T(8,128)(2,1)} %get-tuple-element.89), channel_id=1, source_target_pairs={{0,32},{4,36},{8,40},{12,44},{16,48},{20,52},{24,56},{28,60},{32,6... | collective-permute-start | bytes 1572872 | tf_op jit(solution)/shard_map/ppermute | solution.py:531
  50.7 18.4 %collective-permute-start.8 = (bf16[256,1024]{1,0:T(8,128)(2,1)S(1)}, bf16[256,1024]{1,0:T(8,128)(2,1)}, u32[]{:S(2)}, u32[]{:S(2)}) collective-permute-start(bf16[256,1024]{1,0:T(8,128)(2,1)S(1)} %get-tuple-element.90), channel_id=1, source_target_pairs={{0,96},{4,100},{8,104},{12,108},{16,112},{20,116},{24,120},{28,124... | collective-permute-start | bytes 1572872 | tf_op jit(solution)/shard_map/ppermute | solution.py:531
  53.9 15.2 %collective-permute-start.9 = (bf16[256,1024]{1,0:T(8,128)(2,1)S(1)}, bf16[256,1024]{1,0:T(8,128)(2,1)}, u32[]{:S(2)}, u32[]{:S(2)}) collective-permute-start(bf16[256,1024]{1,0:T(8,128)(2,1)S(1)} %get-tuple-element.91), channel_id=1, source_target_pairs={{0,8},{4,12},{8,16},{12,20},{16,24},{20,28},{24,0},{28,4},{32,40},... | collective-permute-start | bytes 1572872 | tf_op jit(solution)/shard_map/ppermute | solution.py:531
  69.1 67.4 %all-to-all-start = ((bf16[32,544,128]{2,1,0:T(8,128)(2,1)}), bf16[32,544,128]{2,1,0:T(8,128)(2,1)}, u32[]{:S(2)}, u32[]{:S(2)}) async-start(bf16[32,544,128]{2,1,0:T(8,128)(2,1)} %place_entries.1), calls=%async_computation | async-start | bytes 8912896 | tf_op jit(solution)/shard_map/all_to_all | solution.py:535
  74.8 2.5 %copy-start.4 = (bf16[512,1024]{1,0:T(8,128)(2,1)S(1)}, bf16[512,1024]{1,0:T(8,128)(2,1)}, u32[]{:S(2)}) copy-start(bf16[512,1024]{1,0:T(8,128)(2,1)} %get-tuple-element.96) | copy-start | bytes 3145732
  77.4 4.2 %copy-start.6 = (bf16[512,1024]{1,0:T(8,128)(2,1)S(1)}, bf16[512,1024]{1,0:T(8,128)(2,1)}, u32[]{:S(2)}) copy-start(bf16[512,1024]{1,0:T(8,128)(2,1)} %copy-done.5) | copy-start | bytes 3145732
  78.6 5.4 %copy-start.3 = (bf16[512,1024]{1,0:T(8,128)(2,1)S(1)}, bf16[512,1024]{1,0:T(8,128)(2,1)}, u32[]{:S(2)}) copy-start(bf16[512,1024]{1,0:T(8,128)(2,1)} %get-tuple-element.60) | copy-start | bytes 3145732
  78.6 56.5 %collective-permute-start.12 = (bf16[512,512]{1,0:T(8,128)(2,1)}, bf16[512,512]{1,0:T(8,128)(2,1)}, u32[]{:S(2)}, u32[]{:S(2)}) collective-permute-start(bf16[512,512]{1,0:T(8,128)(2,1)} %dynamic-slice_convert_fusion), channel_id=1, source_target_pairs={{0,64},{4,68},{8,72},{12,76},{16,80},{20,84},{24,88},{28,92},{32,9... | collective-permute-start | bytes 1572872 | tf_op jit(solution)/shard_map/ppermute | solution.py:545
  84.5 1.3 copy-start
  86.7 49.6 %collective-permute-start.11 = (bf16[512,512]{1,0:T(8,128)(2,1)}, bf16[512,512]{1,0:T(8,128)(2,1)S(1)}, u32[]{:S(2)}, u32[]{:S(2)}) collective-permute-start(bf16[512,512]{1,0:T(8,128)(2,1)} %dynamic-slice_convert_fusion.1), channel_id=1, source_target_pairs={{0,16},{4,20},{8,24},{12,28},{16,0},{20,4},{24,8},{28,12},{32,48},... | collective-permute-start | bytes 1572872 | tf_op jit(solution)/shard_map/ppermute | solution.py:545
  88.1 48.2 %copy-start.1 = (f32[512,1024]{1,0:T(8,128)S(1)}, f32[512,1024]{1,0:T(8,128)}, u32[]{:S(2)}) copy-start(f32[512,1024]{1,0:T(8,128)} %copy-done) | copy-start | bytes 6291460
  150.3 3.3 %collective-permute-start.16 = (bf16[1024,128]{1,0:T(8,128)(2,1)S(1)}, bf16[1024,128]{1,0:T(8,128)(2,1)S(1)}, u32[]{:S(2)}, u32[]{:S(2)}) collective-permute-start(bf16[1024,128]{1,0:T(8,128)(2,1)S(1)} %constant_dynamic-slice_fusion), channel_id=1, source_target_pairs={{0,1},{1,0},{2,3},{3,2},{4,5},{5,4},{6,7},{7,6},{8,9},{9,8},{10,11... | collective-permute-start | bytes 786440 | tf_op jit(solution)/shard_map/ppermute | solution.py:486
  150.4 9.5 %collective-permute-start.14 = (bf16[512,256]{1,0:T(8,128)(2,1)S(1)}, bf16[512,256]{1,0:T(8,128)(2,1)S(1)}, u32[]{:S(2)}, u32[]{:S(2)}) collective-permute-start(bf16[512,256]{1,0:T(8,128)(2,1)S(1)} %dynamic-slice_convert_fusion.3), channel_id=1, source_target_pairs={{0,32},{4,36},{8,40},{12,44},{16,48},{20,52},{24,56},{28,60},{32,0... | collective-permute-start | bytes 786440 | tf_op jit(solution)/shard_map/ppermute | solution.py:554
  153.0 18.0 %copy-start.13 = (f32[8,128]{1,0:T(8,128)S(1)}, f32[8,128]{1,0:T(8,128)}, u32[]{:S(2)}) copy-start(f32[8,128]{1,0:T(8,128)} %get-tuple-element.102) | copy-start | bytes 12292
  153.0 8.4 %collective-permute-start.13 = (bf16[512,256]{1,0:T(8,128)(2,1)S(1)}, bf16[512,256]{1,0:T(8,128)(2,1)S(1)}, u32[]{:S(2)}, u32[]{:S(2)}) collective-permute-start(bf16[512,256]{1,0:T(8,128)(2,1)S(1)} %dynamic-slice_convert_fusion.4), channel_id=1, source_target_pairs={{0,8},{4,12},{8,0},{12,4},{16,24},{20,28},{24,16},{28,20},{32,40},... | collective-permute-start | bytes 786440 | tf_op jit(solution)/shard_map/ppermute | solution.py:553
  154.7 9.7 %collective-permute-start.17 = (bf16[1024,128]{1,0:T(8,128)(2,1)S(1)}, bf16[1024,128]{1,0:T(8,128)(2,1)S(1)}, u32[]{:S(2)}, u32[]{:S(2)}) collective-permute-start(bf16[1024,128]{1,0:T(8,128)(2,1)S(1)} %add_convert_fusion.5), channel_id=1, source_target_pairs={{0,2},{1,3},{2,0},{3,1},{4,6},{5,7},{6,4},{7,5},{8,10},{9,11},{10,... | collective-permute-start | bytes 786440 | tf_op jit(solution)/shard_map/ppermute | solution.py:487
  165.2 14.0 %collective-permute-start.18 = (f32[1024,128]{1,0:T(8,128)}, f32[1024,128]{1,0:T(8,128)S(1)}, u32[]{:S(2)}, u32[]{:S(2)}) collective-permute-start(f32[1024,128]{1,0:T(8,128)} %convert_add_fusion.6), channel_id=1, source_target_pairs={{0,1},{1,0},{2,3},{3,2},{4,5},{5,4},{6,7},{7,6},{8,9},{9,8},{10,11... | collective-permute-start | bytes 1572872 | tf_op jit(solution)/shard_map/ppermute | solution.py:488
  165.2 12.8 %collective-permute-start.15 = (bf16[1024,128]{1,0:T(8,128)(2,1)S(1)}, bf16[1024,128]{1,0:T(8,128)(2,1)S(1)}, u32[]{:S(2)}, u32[]{:S(2)}) collective-permute-start(bf16[1024,128]{1,0:T(8,128)(2,1)S(1)} %fusion), channel_id=1, source_target_pairs={{0,4},{4,0},{8,12},{12,8},{16,20},{20,16},{24,28},{28,24},{32,36},... | collective-permute-start | bytes 786440 | tf_op jit(solution)/shard_map/ppermute | solution.py:559
  178.1 1.5 copy-start.12
  178.1 2.1 %copy-start.2 = (f32[2048,128]{1,0:T(8,128)S(1)}, f32[2048,128]{1,0:T(8,128)}, u32[]{:S(2)}) copy-start(f32[2048,128]{1,0:T(8,128)} %param.16) | copy-start | bytes 3145732
where the time goes:
time: 185 us; the launch traced here: 182 us
  waiting for transfers between devices  65.7 us (36%)
  Pallas kernels  51.5 us (28%)
  starting transfers between devices  38.5 us (21%)
  other arithmetic  19 us (10%)
  local copies, waits for them, and re-layouts  5.76 us (3%)
    ppermute x2, waiting for transfers between devices, body(): lax.ppermute(send.astype(BF16), 'wide', flip(2)).astype(F32)  47 us
    pallas_call x1, Pallas kernels, place_entries(): pl.pallas_call(place_kernel, out_shape=jax.ShapeDtypeStruct((N_WIDE, BLOC...  12.7 us
    pallas_call x1, Pallas kernels, sent_terms(): pl.pallas_call(sent_kernel, out_shape=[full] * 3 + [shape((512, 1024), BF...  11.6 us
    pallas_call x1, Pallas kernels, kept_terms(): pl.pallas_call(kept_kernel, out_shape=[jax.ShapeDtypeStruct((samples, wid...  11.1 us
    pallas_call x1, Pallas kernels, owned_sums(): pl.pallas_call(sums_kernel, out_shape=(jax.ShapeDtypeStruct((N_ROWS, E),...  10.7 us
    ppermute x4, starting transfers between devices, body(): second = [lax.ppermute(second[q], 'wide', ways[q]) for q in range(4)]  6.47 us
    ppermute x1, waiting for transfers between devices, body(): lax.ppermute(send, 'wide', X_LO)  6.38 us
    ppermute x4, starting transfers between devices, body(): first = [lax.ppermute(first[q], 'wide', ways[q]) for q in range(4)]  6.06 us
  transfers between devices with their start and end apart: 20, of which 8 were waited for; matrix products, arithmetic and copies ran while one was open for 8% of the time, Pallas kernels for 16%

commit v1 on v0

--- a/solution.py
+++ b/solution.py
@@ -200,7 +200,7 @@
     return pl.pallas_call(
         place_kernel,
         out_shape=jax.ShapeDtypeStruct((N_WIDE, BLOCK, E), BF16),
-        in_specs=[pl.BlockSpec(memory_space=pltpu.SMEM), hbm, hbm, hbm, vmem, vmem, vmem],
+        in_specs=[pl.BlockSpec(memory_space=pltpu.SMEM)] + [pl.BlockSpec(memory_space=pl.ANY)] * 3 + [vmem] * 3,
         out_specs=hbm,
         scratch_shapes=[
             pltpu.VMEM(base.shape, F32),
@@ -217,16 +217,17 @@
     )(slots, base, mate, far, ids, counts, bias)
 
 
-def sums_kernel(count_ref, recv_ref, out_ref, bias_ref, total, left, right, todo):
+def sums_kernel(core_ref, recv_ref, keep_ref, send_ref, bias_ref, total, left, right, todo):
     lane_rows = lax.broadcasted_iota(jnp.int32, (LO, E), 0)
 
-    def listing(w, n):
+    n = 0
+    for w in range(N_WIDE):
+        ends = recv_ref[w, CAP + 16 :, :].astype(F32)
+        count = jnp.max(ends[8:12, :] * 64.0 + ends[12:16, :])
         todo[n] = 2 * w
-        n = n + jnp.where(count_ref[w] > 0, 1, 0)
+        n = n + jnp.where(count > 0.0, 1, 0)
         todo[n] = 2 * w + 1
-        return n + jnp.where(count_ref[w] > CAP // 2, 1, 0)
-
-    n = lax.fori_loop(0, N_WIDE, listing, 0)
+        n = n + jnp.where(count > float(CAP // 2), 1, 0)
     for k in range(12):
         todo[n + k] = -1
     total[...] = jnp.zeros_like(total)
@@ -264,17 +265,19 @@
         return 0
 
     lax.fori_loop(0, (n + 7) // 8, step, 0)
-    for h in range(HI):
-        out_ref[h * LO : (h + 1) * LO, :] = total[:, h * E : (h + 1) * E].astype(BF16)
-
-
-def owned_sums(counts, recv):
+    for k in range(HI // 2):
+        for out_ref, half in ((keep_ref, core_ref[0]), (send_ref, 1 - core_ref[0])):
+            at = pl.multiple_of((half * (HI // 2) + k) * E, E)
+            out_ref[k * LO : (k + 1) * LO, :] = total[:, pl.ds(at, E)].astype(BF16)
+
+
+def owned_sums(core, recv):
     vmem = pl.BlockSpec(memory_space=pltpu.VMEM)
     return pl.pallas_call(
         sums_kernel,
-        out_shape=(jax.ShapeDtypeStruct((N_ROWS, E), BF16), jax.ShapeDtypeStruct((8, E), F32)),
+        out_shape=[jax.ShapeDtypeStruct((N_ROWS // 2, E), BF16)] * 2 + [jax.ShapeDtypeStruct((8, E), F32)],
         in_specs=[pl.BlockSpec(memory_space=pltpu.SMEM), vmem],
-        out_specs=(vmem, vmem),
+        out_specs=[vmem] * 3,
         scratch_shapes=[
             pltpu.VMEM((LO, HI * E), F32),
             pltpu.VMEM((2, LO, 2 * CAP), BF16),
@@ -284,7 +287,7 @@
         compiler_params=pltpu.CompilerParams(vmem_limit_bytes=VMEM_BYTES),
         cost_estimate=LIGHT,
         name="owned_sums",
-    )(counts, recv)
+    )(core, recv)
 
 
 def summed(own, others):
@@ -396,9 +399,47 @@
     return results[:3], results[3:7], results[7:11], *results[11:]
 
 
-def kept_kernel(n_ref, z_ref, y_ref, cot_hbm, embedded_hbm, weight_hbm, bias_ref, scaled_hbm, turned_hbm, *refs):
-    base_hbm, own_hbm, (cot, embedded, weight, scaled, turned, cross, base, own, sems, sems_out) = refs[0], refs[1:3], refs[3:]
-    n, z, y = n_ref[0], z_ref[0], y_ref[0]
+def pass_kernel(*refs):
+    passed_hbm, mine_hbm, sent_hbm, (passed, mine, sent, sems, sems_out) = refs[:4], refs[4:8], refs[8:12], refs[12:]
+    loads, outs = [], []
+    for q in range(4):
+        loads.append(pltpu.make_async_copy(passed_hbm[q].at[pl.ds(0, 256), :], passed.at[q], sems.at[2 * q]))
+        loads.append(pltpu.make_async_copy(mine_hbm[q], mine.at[q], sems.at[2 * q + 1]))
+        outs.append(pltpu.make_async_copy(sent.at[q], sent_hbm[q], sems_out.at[q]))
+    for load in loads:
+        load.start()
+    for q in range(4):
+        loads[2 * q].wait()
+        loads[2 * q + 1].wait()
+        sent[q] = (passed[q].astype(F32) + mine[q].astype(F32)).astype(BF16)
+        outs[q].start()
+    for copy in outs:
+        copy.wait()
+
+
+def passed_on(first, second):
+    hbm = pl.BlockSpec(memory_space=pltpu.HBM)
+    return pl.pallas_call(
+        pass_kernel,
+        out_shape=[jax.ShapeDtypeStruct((256, 1024), BF16)] * 4,
+        in_specs=[pl.BlockSpec(memory_space=pl.ANY)] * 8,
+        out_specs=[hbm] * 4,
+        scratch_shapes=[
+            pltpu.VMEM((4, 256, 1024), BF16),
+            pltpu.VMEM((4, 256, 1024), BF16),
+            pltpu.VMEM((4, 256, 1024), BF16),
+            pltpu.SemaphoreType.DMA((8,)),
+            pltpu.SemaphoreType.DMA((4,)),
+        ],
+        compiler_params=pltpu.CompilerParams(vmem_limit_bytes=VMEM_BYTES),
+        cost_estimate=LIGHT,
+        name="passed_on",
+    )(*first, *second)
+
+
+def kept_kernel(n_ref, cot_hbm, embedded_hbm, weight_hbm, bias_ref, scaled_hbm, base_ref, *scratch):
+    cot, embedded, weight, scaled, cross, sems = scratch
+    n = n_ref[0]
 
     def columns(q):
         at = pl.ds(own_chunk(n ^ q), 1024)
@@ -408,67 +449,99 @@
         at = pl.ds(own_chunk(n ^ q), 1024)
         return pltpu.make_async_copy(weight_hbm.at[at, :], weight.at[q], sems.at[4 + q])
 
-    others = [(scaled_hbm, scaled), (cot_hbm, cot), (turned_hbm, turned)]
-    others = [pltpu.make_async_copy(src, dst, sems.at[8 + k]) for k, (src, dst) in enumerate(others)]
-    outs = [(base, base_hbm), (own.at[0], own_hbm[0]), (own.at[1], own_hbm[1])]
-    outs = [pltpu.make_async_copy(src, dst, sems_out.at[k]) for k, (src, dst) in enumerate(outs)]
+    get_scaled = pltpu.make_async_copy(scaled_hbm, scaled, sems.at[8])
+    get_cot = pltpu.make_async_copy(cot_hbm, cot, sems.at[9])
     rows(0).start()
     columns(0).start()
-    others[0].start()
+    get_scaled.start()
     rows(0).wait()
     columns(0).wait()
     for q in (1, 2, 3):
         rows(q).start()
         columns(q).start()
-    others[1].start()
-    others[2].start()
+    get_cot.start()
     cross[...] = jnp.dot(embedded[:, pl.ds(own_chunk(n), 1024)], weight[0], preferred_element_type=F32)
-    others[0].wait()
-    base[...] = lax.dot_general(scaled[...], weight[0], NT, preferred_element_type=F32)
+    get_scaled.wait()
+    base_ref[...] = lax.dot_general(scaled[...], weight[0], NT, preferred_element_type=F32)
     for q in (1, 2):
         rows(q).wait()
         columns(q).wait()
         cross[...] += jnp.dot(embedded[:, pl.ds(own_chunk(n ^ q), 1024)], weight[q], preferred_element_type=F32)
     rows(3).wait()
     columns(3).wait()
-    others[1].wait()
+    get_cot.wait()
     grad = cot[...].astype(F32)
     last = jnp.dot(embedded[:, pl.ds(own_chunk(n ^ 3), 1024)], weight[3], preferred_element_type=F32)
-    base[...] += grad + grad * (cross[...] + last + bias_ref[...])
-    outs[0].start()
-    others[2].wait()
-    for route in range(2):
-        own[route] = ring_term(route, turned, embedded, z, y, 0).astype(BF16)
-        outs[1 + route].start()
-    for copy in outs:
-        copy.wait()
-
-
-def kept_terms(n, z, y, cotangent, embedded, weight, bias, scaled, turned):
+    base_ref[...] += grad + grad * (cross[...] + last + bias_ref[...])
+
+
+def kept_terms(n, cotangent, embedded, weight, bias, scaled):
     hbm = pl.BlockSpec(memory_space=pltpu.HBM)
-    smem = pl.BlockSpec(memory_space=pltpu.SMEM)
+    vmem = pl.BlockSpec(memory_space=pltpu.VMEM)
     samples, width = cotangent.shape
     return pl.pallas_call(
         kept_kernel,
-        out_shape=[jax.ShapeDtypeStruct((samples, width), F32)] + [jax.ShapeDtypeStruct((512, 1024), BF16)] * 2,
-        in_specs=[smem] * 3 + [hbm] * 3 + [pl.BlockSpec(memory_space=pltpu.VMEM)] + [hbm] * 2,
-        out_specs=[hbm] * 3,
+        out_shape=jax.ShapeDtypeStruct((samples, width), F32),
+        in_specs=[pl.BlockSpec(memory_space=pltpu.SMEM)] + [hbm] * 3 + [vmem, hbm],
+        out_specs=vmem,
         scratch_shapes=[
             pltpu.VMEM(cotangent.shape, BF16),
             pltpu.VMEM(embedded.shape, BF16),
             pltpu.VMEM((4, 1024, 1024), BF16),
             pltpu.VMEM((samples, width), BF16),
-            pltpu.VMEM((width, samples), BF16),
             pltpu.VMEM((samples, width), F32),
-            pltpu.VMEM((samples, width), F32),
-            pltpu.VMEM((2, 512, 1024), BF16),
-            pltpu.SemaphoreType.DMA((11,)),
-            pltpu.SemaphoreType.DMA((3,)),
+            pltpu.SemaphoreType.DMA((10,)),
         ],
         compiler_params=pltpu.CompilerParams(vmem_limit_bytes=VMEM_BYTES),
         cost_estimate=LIGHT,
         name="kept_terms",
-    )(n, z, y, cotangent, embedded, weight, bias.reshape(1, -1), scaled, turned)
+    )(n, cotangent, embedded, weight, bias.reshape(1, -1), scaled)
+
+
+def own_kernel(z_ref, y_ref, embedded_hbm, turned_hbm, *refs):
+    got_hbm, results, (embedded, turned, got, sems) = refs[:8], refs[8:12], refs[12:]
+    z, y = z_ref[0], y_ref[0]
+    loads = [(embedded_hbm, embedded), (turned_hbm, turned)]
+    loads += [(got_hbm[k].at[pl.ds(256, 256), :], got.at[k]) for k in range(4)]
+    loads += [(got_hbm[k], got.at[k]) for k in range(4, 8)]
+    loads = [pltpu.make_async_copy(src, dst, sems.at[k]) for k, (src, dst) in enumerate(loads)]
+    for load in loads:
+        load.start()
+    for load in loads:
+        load.wait()
+    for route, place in ((0, y), (1, z)):
+        term = ring_term(route, turned, embedded, z, y, 0)
+        up, down = 2 * route, 2 * route + 1
+        total = jnp.concatenate(
+            [
+                term[:256, :] + got[4 + up].astype(F32) + got[down].astype(F32),
+                term[256:, :] + got[4 + down].astype(F32) + got[up].astype(F32),
+            ],
+            axis=0,
+        ).astype(BF16)
+        high = place >= 2
+        results[2 * route][...] = jnp.where(high, total[:, 512:], total[:, :512])
+        results[2 * route + 1][...] = jnp.where(high, total[:, :512], total[:, 512:])
+
+
+def own_terms(z, y, embedded, turned, first, second):
+    hbm = pl.BlockSpec(memory_space=pltpu.HBM)
+    vmem = pl.BlockSpec(memory_space=pltpu.VMEM)
+    return pl.pallas_call(
+        own_kernel,
+        out_shape=[jax.ShapeDtypeStruct((512, 512), BF16)] * 4,
+        in_specs=[pl.BlockSpec(memory_space=pltpu.SMEM)] * 2 + [hbm] + [pl.BlockSpec(memory_space=pl.ANY)] * 9,
+        out_specs=[vmem] * 4,
+        scratch_shapes=[
+            pltpu.VMEM(embedded.shape, BF16),
+            pltpu.VMEM(turned.shape, BF16),
+            pltpu.VMEM((8, 256, 1024), BF16),
+            pltpu.SemaphoreType.DMA((10,)),
+        ],
+        compiler_params=pltpu.CompilerParams(vmem_limit_bytes=VMEM_BYTES),
+        cost_estimate=LIGHT,
+        name="own_terms",
+    )(z, y, embedded, turned, *first, *second)
 
 
 def halves_of(array, bit, axis):
@@ -477,18 +550,6 @@
         lax.dynamic_slice_in_dim(array, bit * size, size, axis),
         lax.dynamic_slice_in_dim(array, (1 - bit) * size, size, axis),
     )
-
-
-def over_narrow(part, core):
-    rows = part.shape[0] // 2
-    keep = lax.dynamic_slice_in_dim(part, core * rows, rows, 0)
-    send = lax.dynamic_slice_in_dim(part, (1 - core) * rows, rows, 0)
-    chip = summed(keep, [lax.ppermute(send, "narrow", CORE)]).astype(BF16)
-    mine = summed(chip, [lax.ppermute(chip, "narrow", X_HI)])
-    mate = lax.ppermute(mine, "narrow", CORE)
-    low = jnp.where(core == 0, mine, mate)
-    high = jnp.where(core == 0, mate, mine)
-    return jnp.concatenate([low, high], axis=0)
 
 
 def body(
@@ -520,48 +581,43 @@
     chip_far, scaled, from_mate = lax.optimization_barrier((chip_far, scaled, from_mate))
     far = lax.ppermute(chip_far, "narrow", X_HI)
 
-    base, *own = kept_terms(*at, cotangent, embedded, cross_weight, cross_bias, scaled, turned)
+    base = kept_terms(at[0], cotangent, embedded, cross_weight, cross_bias, scaled)
     row_owner, row_id, bag_size, base = lax.optimization_barrier((row_owner, row_id, bag_size, base))
     slots, ids, counts = entry_slots(
         panel, row_owner.reshape(row_owner.shape[1:3]).T, row_id.reshape(row_id.shape[1:]).T, bag_size.T
     )
-    slots, ids, counts, far, *first = lax.optimization_barrier((slots, ids, counts, far, *first))
-    second = [(second[q].astype(F32) + first[q][:256].astype(F32)).astype(BF16) for q in range(4)]
-    slots, *second = lax.optimization_barrier((slots, *second))
+    slots, ids, counts, *first = lax.optimization_barrier((slots, ids, counts, *first))
+    second = passed_on(first, second)
+    slots, far, *second = lax.optimization_barrier((slots, far, *second))
     second = [lax.ppermute(second[q], "wide", ways[q]) for q in range(4)]
 
     payload = place_entries(slots.reshape(-1), base, from_mate, far, ids, counts, bias_part)
     payload, *second = lax.optimization_barrier((payload, *second))
     recv = lax.all_to_all(payload, "wide", split_axis=0, concat_axis=0, tiled=True)
 
-    kept = []
-    for route, (place, flip) in enumerate(((y, y_flip), (z, z_flip))):
-        up, down = 2 * route, 2 * route + 1
-        total = own[route].astype(F32) + jnp.concatenate(
-            [second[up].astype(F32) + first[down][256:].astype(F32), second[down].astype(F32) + first[up][256:].astype(F32)],
-            axis=0,
-        )
-        keep, send = halves_of(total, place // 2, 1)
-        kept.append(keep + lax.ppermute(send.astype(BF16), "wide", flip(2)).astype(F32))
+    keep_y, send_y, keep_z, send_z = own_terms(at[1], at[2], embedded, turned, first, second)
+    kept = [
+        summed(keep_y, [lax.ppermute(send_y, "wide", y_flip(2))]),
+        summed(keep_z, [lax.ppermute(send_z, "wide", z_flip(2))]),
+    ]
     quarters = []
     for total, place in zip(kept, (y, z)):
         keep, send = halves_of(total, place % 2, 1)
         quarters.append((keep.astype(BF16), send.astype(BF16)))
     recv, *sends = lax.optimization_barrier((recv, quarters[0][1], quarters[1][1]))
-    pair = jnp.concatenate(
-        [
-            summed(quarters[0][0], [lax.ppermute(sends[0], "wide", y_flip(1))]),
-            summed(quarters[1][0], [lax.ppermute(sends[1], "wide", z_flip(1))]),
-        ],
-        axis=0,
-    ).astype(BF16)
-    keep, send = halves_of(pair, x_lo, 1)
-    weight_grad = summed(keep, [lax.ppermute(send, "wide", X_LO)]).T * norm_factor
-
-    recv_counts = (recv[:, CAP + 24, 0].astype(F32) * 64.0 + recv[:, CAP + 28, 0].astype(F32)).astype(jnp.int32)
-    sums, bias_sums = owned_sums(recv_counts, recv)
+    got = [lax.ppermute(sends[0], "wide", y_flip(1)), lax.ppermute(sends[1], "wide", z_flip(1))]
+    keep, send, bias_sums = owned_sums(core.reshape(1), recv)
+    keep, send, *got = lax.optimization_barrier((keep, send, *got))
+    chip = summed(keep, [lax.ppermute(send, "narrow", CORE)]).astype(BF16)
+    pair = jnp.concatenate([summed(quarters[0][0], got[:1]), summed(quarters[1][0], got[1:])], axis=0).astype(BF16)
+    x_keep, x_send = halves_of(pair, x_lo, 1)
+    other_chip, x_send = lax.optimization_barrier((lax.ppermute(chip, "narrow", X_HI), x_send))
+    weight_grad = summed(x_keep, [lax.ppermute(x_send, "wide", X_LO)]).T * norm_factor
+
     bias_grad = bias_sums.reshape(-1) * norm_factor
-    row_grad = over_narrow(sums, core)
+    mine = summed(chip, [other_chip])
+    mate = lax.ppermute(mine, "narrow", CORE)
+    row_grad = jnp.concatenate([jnp.where(core == 0, mine, mate), jnp.where(core == 0, mate, mine)], axis=0)
     new_state = adagrad_state + jnp.mean(row_grad * row_grad, axis=1)
     new_table = emb_table - LEARN_RATE * row_grad / jnp.sqrt(new_state)[:, None]
     return (weight_grad, bias_grad, new_table, new_state)

time: 185 us -> 185 us (level); the launches traced: 182 us -> 185 us
  Pallas kernels: 51.5 us -> 66.4 us
  other arithmetic: 19 us -> 9.97 us
  starting transfers between devices: 38.5 us -> 34.6 us
  waiting for transfers between devices: 65.7 us -> 68.6 us
    pallas_call x2 -> x4, Pallas kernels: 21.8 us -> 36.6 us  [the longest x1 17 us: owned_sums(): pl.pallas_call(sums_kernel, out_shape=[jax.ShapeDtypeStruct((N_ROWS // 2,...]
    ppermute x6, waiting for transfers between devices: 56.2 us -> 65.5 us  [the longest x1 49.8 us: body(): lax.ppermute(send_z, 'wide', z_flip(2))]
    add x8 -> x0, other arithmetic: 7.04 us -> none  [the longest x2 2.51 us: body(): second[up].astype(F32) + first[down][256:].astype(F32)]
    convert_element_type x4 -> x1, other arithmetic: 6.29 us -> 1.02 us  [body(): chip = summed(keep, [lax.ppermute(send, 'narrow', CORE)]).astype(BF16)]
    ppermute x6, starting transfers between devices: 13.2 us -> 9.12 us  [the longest x1 3.26 us: body(): lax.ppermute(x_send, 'wide', X_LO)]
    ppermute x1, waiting for transfers between devices: 3.45 us -> 0.01 us  [body(): far = lax.ppermute(chip_far, 'narrow', X_HI)]
    ppermute x1, waiting for transfers between devices: 2.42 us -> 0.01 us  [body(): lax.ppermute(sends[1], 'wide', z_flip(1))]
    add x1 -> x3, other arithmetic: 0.85 us -> 3.2 us  [summed(): total = total + other.astype(F32)]
  transfers between devices with their start and end apart: 20 -> 20, of which waited for: 8 -> 7; matrix products, arithmetic and copies ran while one was open for 8% -> 4% of each run, Pallas kernels for 16% -> 30%
where the time goes in v1:
time: 185 us
  waiting for transfers between devices  68.6 us (37%)
  Pallas kernels  66.4 us (36%)
  starting transfers between devices  34.6 us (19%)
  other arithmetic  9.97 us (5%)
  local copies, waits for them, and re-layouts  3.99 us (2%)
    ppermute x1, waiting for transfers between devices, body(): lax.ppermute(send_z, 'wide', z_flip(2))  49.8 us
    pallas_call x1, Pallas kernels, owned_sums(): pl.pallas_call(sums_kernel, out_shape=[jax.ShapeDtypeStruct((N_ROWS // 2,...  17 us
    pallas_call x1, Pallas kernels, place_entries(): pl.pallas_call(place_kernel, out_shape=jax.ShapeDtypeStruct((N_WIDE, BLOC...  12.7 us
    pallas_call x1, Pallas kernels, sent_terms(): pl.pallas_call(sent_kernel, out_shape=[full] * 3 + [shape((512, 1024), BF...  11.6 us
    pallas_call x1, Pallas kernels, kept_terms(): pl.pallas_call(kept_kernel, out_shape=jax.ShapeDtypeStruct((samples, widt...  10.1 us
    ppermute x1, waiting for transfers between devices, body(): lax.ppermute(chip, 'narrow', X_HI)  7.55 us
    ppermute x4, starting transfers between devices, body(): second = [lax.ppermute(second[q], 'wide', ways[q]) for q in range(4)]  6.54 us
    all_to_all x1, starting transfers between devices, body(): lax.all_to_all(payload, 'wide', split_axis=0, concat_axis=0, tiled=True)  6.51 us
  transfers between devices with their start and end apart: 20, of which 7 were waited for; matrix products, arithmetic and copies ran while one was open for 4% of the time, Pallas kernels for 30%

profile of v1, /device:TPU:24, one launch (start us, length us, event | category | flops | bytes accessed | tf_op | source)
XLA Modules:
  0.0 184.5 jit_solution(2425977362779565247)
XLA Ops:
  0.7 11.6 %sent_terms.1 = (bf16[512,1024]{1,0:T(8,128)(2,1)}, bf16[512,1024]{1,0:T(8,128)(2,1)}, bf16[512,1024]{1,0:T(8,128)(2,1)}, bf16[512,1024]{1,0:T(8,128)(2,1)}, bf1...) custom-call(s32[1]{0:T(128)} %bitcast.2.n_ref.panel_ref, ...), custom_call_target="tpu_custom_call" | custom-call | flops 1 | bytes 1 | tf_op jit(solution)/shard_map/sent_terms/pallas_call | solution.py:377
  12.4 0.5 collective-permute-start.1
  12.9 1.9 %collective-permute-start.2 = (bf16[512,1024]{1,0:T(8,128)(2,1)}, bf16[512,1024]{1,0:T(8,128)(2,1)S(1)}, u32[]{:S(2)}, u32[]{:S(2)}) collective-permute-start(bf16[512,1024]{1,0:T(8,128)(2,1)} %get-tuple-element.78), channel_id=1, source_target_pairs={{0,32},{4,36},{8,40},{12,44},{16,48},{20,52},{24,56},{28,60},{32,6... | collective-permute-start | bytes 3145736 | tf_op jit(solution)/shard_map/ppermute | solution.py:579
  14.8 2.1 %collective-permute-start.3 = (bf16[512,1024]{1,0:T(8,128)(2,1)}, bf16[512,1024]{1,0:T(8,128)(2,1)S(1)}, u32[]{:S(2)}, u32[]{:S(2)}) collective-permute-start(bf16[512,1024]{1,0:T(8,128)(2,1)} %get-tuple-element.79), channel_id=1, source_target_pairs={{0,96},{4,100},{8,104},{12,108},{16,112},{20,116},{24,120},{28,124... | collective-permute-start | bytes 3145736 | tf_op jit(solution)/shard_map/ppermute | solution.py:579
  16.9 0.3 collective-permute-start.4
  17.3 1.7 collective-permute-start.5
  19.0 1.6 add_convert_fusion
  20.6 3.3 %collective-permute-start.6 = (bf16[512,1024]{1,0:T(8,128)(2,1)S(1)}, bf16[512,1024]{1,0:T(8,128)(2,1)S(1)}, u32[]{:S(2)}, u32[]{:S(2)}) collective-permute-start(bf16[512,1024]{1,0:T(8,128)(2,1)S(1)} %add_convert_fusion), channel_id=1, source_target_pairs={{0,2},{1,3},{2,0},{3,1},{4,6},{5,7},{6,4},{7,5},{8,10},{9,11},{10,... | collective-permute-start | bytes 3145736 | tf_op jit(solution)/shard_map/ppermute | solution.py:582
  23.9 10.1 %kept_terms.1.base_hbm = f32[512,1024]{1,0:T(8,128)} custom-call(s32[1]{0:T(128)} %bitcast.2.n_ref.panel_ref, bf16[512,1024]{1,0:T(8,128)(2,1)} %cot_hbm.3, bf16[512,4096]{1,0:T(8,128)(2,1)} %embedded_hbm.5, bf16[4096,1024]{1,0:T(8,128)(2,1)} %weight_hbm.3, f32[1,1024]{1,0:T(1,128)} %bitcast.23, bf16[512,1024]{1,0:T(8,128)(2,1)} %get-tuple-element.71.scaled_hbm), custom_call_target="tpu_custom_call" | custom-call | flops 1 | bytes 1 | tf_op jit(solution)/shard_map/kept_terms/pallas_call | solution.py:482
  34.1 0.6 copy.16
  34.7 5.4 %entry_slots.1 = (s32[64,128]{1,0:T(8,128)}, f32[64,512]{1,0:T(8,128)}, f32[32,128]{1,0:T(8,128)}) custom-call(s32[1]{0:T(128)} %bitcast.2.n_ref.panel_ref, s32[16,512]{1,0:T(8,128)} %bitcast.19, s32[16,512]{1,0:T(8,128)} %bitcast.22, s32[32,512]{1,0:T(8,128)} %bitcast.20), custom_call_target="tpu_custom_call" | custom-call | flops 1 | bytes 1 | tf_op jit(solution)/shard_map/entry_slots/pallas_call | solution.py:109
  40.2 0.4 collective-permute-done.2.refs_0_
  40.6 1.5 collective-permute-done.4.refs_2_
  42.0 1.2 collective-permute-done.5.refs_3_
  43.3 1.0 copy-done.3
  44.3 3.2 %passed_on.1 = (bf16[256,1024]{1,0:T(8,128)(2,1)}, bf16[256,1024]{1,0:T(8,128)(2,1)}, bf16[256,1024]{1,0:T(8,128)(2,1)}, bf16[256,1024]{1,0:T(8,128)(2,1)}) custom-call(bf16[512,1024]{1,0:T(8,128)(2,1)} %copy-done, bf16[512,1024]{1,0:T(8,128)(2,1)} %copy-done.1, bf16[512,1024]{1,0:T(8,128)(2,1)} %copy-done.2, bf16[512,1024]{1,0:T(8,128)(2,1)} %copy-done.3, ...), custom_call_target="tpu_custom_call" | custom-call | flops 1 | bytes 1 | tf_op jit(solution)/shard_map/passed_on/pallas_call | solution.py:422
  47.5 0.6 collective-permute-start.10
  48.1 0.1 collective-permute-start.7
  48.2 3.1 %collective-permute-start.8 = (bf16[256,1024]{1,0:T(8,128)(2,1)}, bf16[256,1024]{1,0:T(8,128)(2,1)S(1)}, u32[]{:S(2)}, u32[]{:S(2)}) collective-permute-start(bf16[256,1024]{1,0:T(8,128)(2,1)} %get-tuple-element.104), channel_id=1, source_target_pairs={{0,96},{4,100},{8,104},{12,108},{16,112},{20,116},{24,120},{28,124... | collective-permute-start | bytes 1572872 | tf_op jit(solution)/shard_map/ppermute | solution.py:592
  51.3 2.7 %collective-permute-start.9 = (bf16[256,1024]{1,0:T(8,128)(2,1)}, bf16[256,1024]{1,0:T(8,128)(2,1)S(1)}, u32[]{:S(2)}, u32[]{:S(2)}) collective-permute-start(bf16[256,1024]{1,0:T(8,128)(2,1)} %get-tuple-element.105), channel_id=1, source_target_pairs={{0,8},{4,12},{8,16},{12,20},{16,24},{20,28},{24,0},{28,4},{32,40},... | collective-permute-start | bytes 1572872 | tf_op jit(solution)/shard_map/ppermute | solution.py:592
  54.1 12.7 %place_entries.1 = bf16[32,544,128]{2,1,0:T(8,128)(2,1)} custom-call(s32[8192]{0:T(1024)} %bitcast.21, f32[512,1024]{1,0:T(8,128)} %kept_terms.1.base_hbm, bf16[512,1024]{1,0:T(8,128)(2,1)} %copy-done.5, bf16[512,1024]{1,0:T(8,128)(2,1)} %copy-done.6, f32[64,512]{1,0:T(8,128)} %get-tuple-element.100.ids_ref, f32[32,128]{1,0:T(8,128)} %get-tuple-element.101.count_ref, ...), custom_call_target="tpu_custom_call" | custom-call | flops 1 | bytes 1 | tf_op jit(solution)/shard_map/place_entries/pallas_call | solution.py:200
  66.8 0.7 copy-done.7
  67.6 0.2 copy-done.8
  67.7 0.2 copy-done.9
  67.9 0.2 copy-done.10
  68.1 6.5 %all-to-all-start = ((bf16[32,544,128]{2,1,0:T(8,128)(2,1)}), bf16[32,544,128]{2,1,0:T(8,128)(2,1)}, u32[]{:S(2)}, u32[]{:S(2)}) async-start(bf16[32,544,128]{2,1,0:T(8,128)(2,1)} %place_entries.1), calls=%async_computation | async-start | bytes 8912896 | tf_op jit(solution)/shard_map/all_to_all | solution.py:596
  74.6 6.3 %own_terms.1 = (bf16[512,512]{1,0:T(8,128)(2,1)}, bf16[512,512]{1,0:T(8,128)(2,1)}, bf16[512,512]{1,0:T(8,128)(2,1)}, bf16[512,512]{1,0:T(8,128)(2,1)}) custom-call(s32[1]{0:T(128)} %bitcast.z_ref, s32[1]{0:T(128)} %bitcast.1.y_ref, bf16[512,4096]{1,0:T(8,128)(2,1)} %embedded_hbm.5, bf16[1024,512]{1,0:T(8,128)(2,1)} %get-tuple-element.66.turned_hbm, ...), custom_call_target="tpu_custom_call" | custom-call | flops 1 | bytes 1 | tf_op jit(solution)/shard_map/own_terms/pallas_call | solution.py:530
  80.9 3.1 %collective-permute-start.12 = (bf16[512,512]{1,0:T(8,128)(2,1)}, bf16[512,512]{1,0:T(8,128)(2,1)S(1)}, u32[]{:S(2)}, u32[]{:S(2)}) collective-permute-start(bf16[512,512]{1,0:T(8,128)(2,1)} %get-tuple-element.115), channel_id=1, source_target_pairs={{0,64},{4,68},{8,72},{12,76},{16,80},{20,84},{24,88},{28,92},{32,9... | collective-permute-start | bytes 1572872 | tf_op jit(solution)/shard_map/ppermute | solution.py:601
  84.0 1.4 collective-permute-start.11
  85.4 49.8 %collective-permute-done.12 = bf16[512,512]{1,0:T(8,128)(2,1)S(1)} collective-permute-done((bf16[512,512]{1,0:T(8,128)(2,1)}, bf16[512,512]{1,0:T(8,128)(2,1)S(1)}, u32[]{:S(2)}, u32[]{:S(2)}) %collective-permute-start.12) | collective-permute-done | bytes 524320 | tf_op jit(solution)/shard_map/ppermute | solution.py:601
  135.2 1.2 convert_add_fusion
  136.5 1.2 convert_add_fusion.1
  137.7 1.5 collective-permute-start.13
  139.2 1.0 collective-permute-start.14
  140.2 17.0 %owned_sums.1 = (bf16[1024,128]{1,0:T(8,128)(2,1)}, bf16[1024,128]{1,0:T(8,128)(2,1)}, f32[8,128]{1,0:T(8,128)}) custom-call(s32[1]{0:T(128)} %bitcast.9.core_ref, bf16[32,544,128]{2,1,0:T(8,128)(2,1)} %all-to-all-done.recv_ref), custom_call_target="tpu_custom_call" | custom-call | flops 1 | bytes 1 | tf_op jit(solution)/shard_map/owned_sums/pallas_call | solution.py:276
  157.3 1.7 collective-permute-done.15
  159.0 1.0 add_convert_fusion.1
  160.1 1.3 collective-permute-start.16
  161.3 1.1 add_convert_fusion.2
  162.4 7.5 %collective-permute-done.16 = bf16[1024,128]{1,0:T(8,128)(2,1)S(1)} collective-permute-done((bf16[1024,128]{1,0:T(8,128)(2,1)S(1)}, bf16[1024,128]{1,0:T(8,128)(2,1)S(1)}, u32[]{:S(2)}, u32[]{:S(2)}) %collective-permute-start.16) | collective-permute-done | bytes 262176 | tf_op jit(solution)/shard_map/ppermute | solution.py:614
  170.0 0.8 convert_add_fusion.2
  170.8 3.3 %collective-permute-start.17 = (bf16[1024,128]{1,0:T(8,128)(2,1)S(1)}, bf16[1024,128]{1,0:T(8,128)(2,1)S(1)}, u32[]{:S(2)}, u32[]{:S(2)}) collective-permute-start(bf16[1024,128]{1,0:T(8,128)(2,1)S(1)} %fusion), channel_id=1, source_target_pairs={{0,4},{4,0},{8,12},{12,8},{16,20},{20,16},{24,28},{28,24},{32,36},... | collective-permute-start | bytes 786440 | tf_op jit(solution)/shard_map/ppermute | solution.py:615
  174.1 0.6 multiply_bitcast_fusion.1
  174.7 6.4 %collective-permute-done.17 = bf16[1024,128]{1,0:T(8,128)(2,1)S(1)} collective-permute-done((bf16[1024,128]{1,0:T(8,128)(2,1)S(1)}, bf16[1024,128]{1,0:T(8,128)(2,1)S(1)}, u32[]{:S(2)}, u32[]{:S(2)}) %collective-permute-start.17) | collective-permute-done | bytes 262176 | tf_op jit(solution)/shard_map/ppermute | solution.py:615
  181.1 1.0 copy.13
  182.2 0.3 multiply_reduce_fusion
  182.6 0.6 fusion.2
  183.2 1.3 divide_subtract_fusion
  (46 shorter events, 0.5 us)
Async XLA Ops:
  12.3 4.9 %collective-permute-start = (bf16[512,1024]{1,0:T(8,128)(2,1)}, bf16[512,1024]{1,0:T(8,128)(2,1)S(1)}, u32[]{:S(2)}, u32[]{:S(2)}) collective-permute-start(bf16[512,1024]{1,0:T(8,128)(2,1)} %get-tuple-element.68), channel_id=1, source_target_pairs={{0,1},{1,0},{2,3},{3,2},{4,5},{5,4},{6,7},{7,6},{8,9},{9,8},{10,11... | collective-permute-start | bytes 3145736 | tf_op jit(solution)/shard_map/ppermute | solution.py:576
  12.4 8.2 %collective-permute-start.1 = (bf16[512,1024]{1,0:T(8,128)(2,1)}, bf16[512,1024]{1,0:T(8,128)(2,1)S(1)}, u32[]{:S(2)}, u32[]{:S(2)}) collective-permute-start(bf16[512,1024]{1,0:T(8,128)(2,1)} %get-tuple-element.70), channel_id=1, source_target_pairs={{0,1},{1,0},{2,3},{3,2},{4,5},{5,4},{6,7},{7,6},{8,9},{9,8},{10,11... | collective-permute-start | bytes 3145736 | tf_op jit(solution)/shard_map/ppermute | solution.py:577
  12.9 27.7 %collective-permute-start.2 = (bf16[512,1024]{1,0:T(8,128)(2,1)}, bf16[512,1024]{1,0:T(8,128)(2,1)S(1)}, u32[]{:S(2)}, u32[]{:S(2)}) collective-permute-start(bf16[512,1024]{1,0:T(8,128)(2,1)} %get-tuple-element.78), channel_id=1, source_target_pairs={{0,32},{4,36},{8,40},{12,44},{16,48},{20,52},{24,56},{28,60},{32,6... | collective-permute-start | bytes 3145736 | tf_op jit(solution)/shard_map/ppermute | solution.py:579
  14.8 25.7 %collective-permute-start.3 = (bf16[512,1024]{1,0:T(8,128)(2,1)}, bf16[512,1024]{1,0:T(8,128)(2,1)S(1)}, u32[]{:S(2)}, u32[]{:S(2)}) collective-permute-start(bf16[512,1024]{1,0:T(8,128)(2,1)} %get-tuple-element.79), channel_id=1, source_target_pairs={{0,96},{4,100},{8,104},{12,108},{16,112},{20,116},{24,120},{28,124... | collective-permute-start | bytes 3145736 | tf_op jit(solution)/shard_map/ppermute | solution.py:579
  16.9 25.1 %collective-permute-start.4 = (bf16[512,1024]{1,0:T(8,128)(2,1)}, bf16[512,1024]{1,0:T(8,128)(2,1)S(1)}, u32[]{:S(2)}, u32[]{:S(2)}) collective-permute-start(bf16[512,1024]{1,0:T(8,128)(2,1)} %get-tuple-element.80), channel_id=1, source_target_pairs={{0,8},{4,12},{8,16},{12,20},{16,24},{20,28},{24,0},{28,4},{32,40},... | collective-permute-start | bytes 3145736 | tf_op jit(solution)/shard_map/ppermute | solution.py:579
  17.3 26.0 %collective-permute-start.5 = (bf16[512,1024]{1,0:T(8,128)(2,1)}, bf16[512,1024]{1,0:T(8,128)(2,1)S(1)}, u32[]{:S(2)}, u32[]{:S(2)}) collective-permute-start(bf16[512,1024]{1,0:T(8,128)(2,1)} %get-tuple-element.81), channel_id=1, source_target_pairs={{0,24},{4,28},{8,0},{12,4},{16,8},{20,12},{24,16},{28,20},{32,56},... | collective-permute-start | bytes 3145736 | tf_op jit(solution)/shard_map/ppermute | solution.py:579
  20.6 13.5 %copy-start.5 = (bf16[512,1024]{1,0:T(8,128)(2,1)}, bf16[512,1024]{1,0:T(8,128)(2,1)S(1)}, u32[]{:S(2)}) copy-start(bf16[512,1024]{1,0:T(8,128)(2,1)S(1)} %collective-permute-done.1.mate_hbm) | copy-start | bytes 3145732
  20.6 26.9 %collective-permute-start.6 = (bf16[512,1024]{1,0:T(8,128)(2,1)S(1)}, bf16[512,1024]{1,0:T(8,128)(2,1)S(1)}, u32[]{:S(2)}, u32[]{:S(2)}) collective-permute-start(bf16[512,1024]{1,0:T(8,128)(2,1)S(1)} %add_convert_fusion), channel_id=1, source_target_pairs={{0,2},{1,3},{2,0},{3,1},{4,6},{5,7},{6,4},{7,5},{8,10},{9,11},{10,... | collective-permute-start | bytes 3145736 | tf_op jit(solution)/shard_map/ppermute | solution.py:582
  23.9 10.2 %copy-start.12 = (s32[1,512,16,1]{1,3,2,0:T(1,128)S(1)}, s32[1,512,16,1]{1,3,2,0:T(1,128)}, u32[]{:S(2)}) copy-start(s32[1,512,16,1]{1,3,2,0:T(1,128)} %param.14) | copy-start | bytes 98308
  40.6 2.7 %copy-start = (bf16[512,1024]{1,0:T(8,128)(2,1)}, bf16[512,1024]{1,0:T(8,128)(2,1)S(1)}, u32[]{:S(2)}) copy-start(bf16[512,1024]{1,0:T(8,128)(2,1)S(1)} %collective-permute-done.2.refs_0_) | copy-start | bytes 3145732
  40.6 2.7 %copy-start.1 = (bf16[512,1024]{1,0:T(8,128)(2,1)}, bf16[512,1024]{1,0:T(8,128)(2,1)S(1)}, u32[]{:S(2)}) copy-start(bf16[512,1024]{1,0:T(8,128)(2,1)S(1)} %collective-permute-done.3.refs_1_) | copy-start | bytes 3145732
  42.0 1.3 copy-start.2
  43.3 1.0 copy-start.3
  47.5 6.6 %copy-start.6 = (bf16[512,1024]{1,0:T(8,128)(2,1)}, bf16[512,1024]{1,0:T(8,128)(2,1)S(1)}, u32[]{:S(2)}) copy-start(bf16[512,1024]{1,0:T(8,128)(2,1)S(1)} %collective-permute-done.6.far_hbm) | copy-start | bytes 3145732
  47.5 19.2 %collective-permute-start.10 = (bf16[256,1024]{1,0:T(8,128)(2,1)}, bf16[256,1024]{1,0:T(8,128)(2,1)S(1)}, u32[]{:S(2)}, u32[]{:S(2)}) collective-permute-start(bf16[256,1024]{1,0:T(8,128)(2,1)} %get-tuple-element.106), channel_id=1, source_target_pairs={{0,24},{4,28},{8,0},{12,4},{16,8},{20,12},{24,16},{28,20},{32,56},... | collective-permute-start | bytes 1572872 | tf_op jit(solution)/shard_map/ppermute | solution.py:592
  48.1 18.7 %collective-permute-start.7 = (bf16[256,1024]{1,0:T(8,128)(2,1)}, bf16[256,1024]{1,0:T(8,128)(2,1)S(1)}, u32[]{:S(2)}, u32[]{:S(2)}) collective-permute-start(bf16[256,1024]{1,0:T(8,128)(2,1)} %get-tuple-element.103), channel_id=1, source_target_pairs={{0,32},{4,36},{8,40},{12,44},{16,48},{20,52},{24,56},{28,60},{32,6... | collective-permute-start | bytes 1572872 | tf_op jit(solution)/shard_map/ppermute | solution.py:592
  48.2 18.6 %collective-permute-start.8 = (bf16[256,1024]{1,0:T(8,128)(2,1)}, bf16[256,1024]{1,0:T(8,128)(2,1)S(1)}, u32[]{:S(2)}, u32[]{:S(2)}) collective-permute-start(bf16[256,1024]{1,0:T(8,128)(2,1)} %get-tuple-element.104), channel_id=1, source_target_pairs={{0,96},{4,100},{8,104},{12,108},{16,112},{20,116},{24,120},{28,124... | collective-permute-start | bytes 1572872 | tf_op jit(solution)/shard_map/ppermute | solution.py:592
  51.3 15.5 %collective-permute-start.9 = (bf16[256,1024]{1,0:T(8,128)(2,1)}, bf16[256,1024]{1,0:T(8,128)(2,1)S(1)}, u32[]{:S(2)}, u32[]{:S(2)}) collective-permute-start(bf16[256,1024]{1,0:T(8,128)(2,1)} %get-tuple-element.105), channel_id=1, source_target_pairs={{0,8},{4,12},{8,16},{12,20},{16,24},{20,28},{24,0},{28,4},{32,40},... | collective-permute-start | bytes 1572872 | tf_op jit(solution)/shard_map/ppermute | solution.py:592
  66.8 0.8 copy-start.7
  66.8 0.9 copy-start.8
  66.8 1.1 copy-start.9
  66.8 1.3 copy-start.10
  68.1 69.6 %all-to-all-start = ((bf16[32,544,128]{2,1,0:T(8,128)(2,1)}), bf16[32,544,128]{2,1,0:T(8,128)(2,1)}, u32[]{:S(2)}, u32[]{:S(2)}) async-start(bf16[32,544,128]{2,1,0:T(8,128)(2,1)} %place_entries.1), calls=%async_computation | async-start | bytes 8912896 | tf_op jit(solution)/shard_map/all_to_all | solution.py:596
  80.9 54.3 %collective-permute-start.12 = (bf16[512,512]{1,0:T(8,128)(2,1)}, bf16[512,512]{1,0:T(8,128)(2,1)S(1)}, u32[]{:S(2)}, u32[]{:S(2)}) collective-permute-start(bf16[512,512]{1,0:T(8,128)(2,1)} %get-tuple-element.115), channel_id=1, source_target_pairs={{0,64},{4,68},{8,72},{12,76},{16,80},{20,84},{24,88},{28,92},{32,9... | collective-permute-start | bytes 1572872 | tf_op jit(solution)/shard_map/ppermute | solution.py:601
  84.0 52.5 %collective-permute-start.11 = (bf16[512,512]{1,0:T(8,128)(2,1)}, bf16[512,512]{1,0:T(8,128)(2,1)S(1)}, u32[]{:S(2)}, u32[]{:S(2)}) collective-permute-start(bf16[512,512]{1,0:T(8,128)(2,1)} %get-tuple-element.112), channel_id=1, source_target_pairs={{0,16},{4,20},{8,24},{12,28},{16,0},{20,4},{24,8},{28,12},{32,48},... | collective-permute-start | bytes 1572872 | tf_op jit(solution)/shard_map/ppermute | solution.py:600
  137.7 19.5 %collective-permute-start.13 = (bf16[512,256]{1,0:T(8,128)(2,1)S(1)}, bf16[512,256]{1,0:T(8,128)(2,1)S(1)}, u32[]{:S(2)}, u32[]{:S(2)}) collective-permute-start(bf16[512,256]{1,0:T(8,128)(2,1)S(1)} %dynamic-slice_convert_fusion.2), channel_id=1, source_target_pairs={{0,8},{4,12},{8,0},{12,4},{16,24},{20,28},{24,16},{28,20},{32,40},... | collective-permute-start | bytes 786440 | tf_op jit(solution)/shard_map/ppermute | solution.py:608
  139.2 18.0 %collective-permute-start.14 = (bf16[512,256]{1,0:T(8,128)(2,1)S(1)}, bf16[512,256]{1,0:T(8,128)(2,1)S(1)}, u32[]{:S(2)}, u32[]{:S(2)}) collective-permute-start(bf16[512,256]{1,0:T(8,128)(2,1)S(1)} %dynamic-slice_convert_fusion.1), channel_id=1, source_target_pairs={{0,32},{4,36},{8,40},{12,44},{16,48},{20,52},{24,56},{28,60},{32,0... | collective-permute-start | bytes 786440 | tf_op jit(solution)/shard_map/ppermute | solution.py:608
  157.2 16.9 %copy-start.14 = (f32[8,128]{1,0:T(8,128)S(1)}, f32[8,128]{1,0:T(8,128)}, u32[]{:S(2)}) copy-start(f32[8,128]{1,0:T(8,128)} %get-tuple-element.126) | copy-start | bytes 12292
  157.2 1.8 copy-start.11
  157.2 1.8 collective-permute-start.15
  160.0 22.6 %copy-start.13 = (f32[2048]{0:T(1024)S(1)}, f32[2048]{0:T(1024)}, u32[]{:S(2)}) copy-start(f32[2048]{0:T(1024)} %param.17) | copy-start | bytes 24580
  160.0 23.2 %copy-start.4 = (f32[2048,128]{1,0:T(8,128)S(1)}, f32[2048,128]{1,0:T(8,128)}, u32[]{:S(2)}) copy-start(f32[2048,128]{1,0:T(8,128)} %param.16) | copy-start | bytes 3145732
  160.1 9.9 %collective-permute-start.16 = (bf16[1024,128]{1,0:T(8,128)(2,1)S(1)}, bf16[1024,128]{1,0:T(8,128)(2,1)S(1)}, u32[]{:S(2)}, u32[]{:S(2)}) collective-permute-start(bf16[1024,128]{1,0:T(8,128)(2,1)S(1)} %add_convert_fusion.1), channel_id=1, source_target_pairs={{0,2},{1,3},{2,0},{3,1},{4,6},{5,7},{6,4},{7,5},{8,10},{9,11},{10,... | collective-permute-start | bytes 786440 | tf_op jit(solution)/shard_map/ppermute | solution.py:614
  170.8 11.3 %collective-permute-start.18 = (f32[1024,128]{1,0:T(8,128)}, f32[1024,128]{1,0:T(8,128)S(1)}, u32[]{:S(2)}, u32[]{:S(2)}) collective-permute-start(f32[1024,128]{1,0:T(8,128)} %convert_add_fusion.2), channel_id=1, source_target_pairs={{0,1},{1,0},{2,3},{3,2},{4,5},{5,4},{6,7},{7,6},{8,9},{9,8},{10,11... | collective-permute-start | bytes 1572872 | tf_op jit(solution)/shard_map/ppermute | solution.py:619
  170.8 10.2 %collective-permute-start.17 = (bf16[1024,128]{1,0:T(8,128)(2,1)S(1)}, bf16[1024,128]{1,0:T(8,128)(2,1)S(1)}, u32[]{:S(2)}, u32[]{:S(2)}) collective-permute-start(bf16[1024,128]{1,0:T(8,128)(2,1)S(1)} %fusion), channel_id=1, source_target_pairs={{0,4},{4,0},{8,12},{12,8},{16,20},{20,16},{24,28},{28,24},{32,36},... | collective-permute-start | bytes 786440 | tf_op jit(solution)/shard_map/ppermute | solution.py:615

commit v2 on v1

--- a/solution.py
+++ b/solution.py
@@ -11,7 +11,7 @@
 E = 128
 N_WIDE = 32
 CAP = 512
-TAIL = 32
+TAIL = 16
 BLOCK = CAP + TAIL
 N_ROWS = 2048
 HI = 4
@@ -44,10 +44,10 @@
 X_HI = [(i, i ^ 2) for i in range(4)]
 
 
-def slots_kernel(panel_ref, owner_ref, row_ref, bag_ref, slots_ref, ids_ref, count_ref, onehots):
+def find_slots(panel, owner_ref, row_ref, bag_ref, slots_ref, ids_ref, onehots):
     depth, samples = owner_ref.shape
     feats = depth // 2
-    bag = bag_ref[pl.ds(pl.multiple_of(panel_ref[0] * feats, feats), feats), :]
+    bag = bag_ref[pl.ds(pl.multiple_of(panel * feats, feats), feats), :]
     bag = jnp.concatenate([bag[k // 2 : k // 2 + 1, :] for k in range(depth)], axis=0)
     live = (lax.broadcasted_iota(jnp.int32, (depth, samples), 0) & 1) < bag
     owner = jnp.where(live, owner_ref[...], N_WIDE)
@@ -70,12 +70,6 @@
     rows_before = 16.0 * jnp.dot(earlier, top, preferred_element_type=F32) + jnp.dot(
         earlier, low, preferred_element_type=F32
     )
-    t_rows = lax.broadcasted_iota(jnp.int32, (N_WIDE, size), 0)
-    t_cols = lax.broadcasted_iota(jnp.int32, (N_WIDE, size), 1)
-    members = jnp.where(t_rows == t_cols >> shift, 1.0, 0.0).astype(BF16)
-    count_ref[...] = 16.0 * jnp.dot(members, top, preferred_element_type=F32) + jnp.dot(
-        members, low, preferred_element_type=F32
-    )
     place = jnp.zeros((depth, samples), F32)
     for t in range(N_WIDE):
         at = slice(t * depth, (t + 1) * depth)
@@ -103,27 +97,8 @@
     ids_ref[...] = ids
 
 
-def entry_slots(panel, owner, row, bag):
-    vmem = pl.BlockSpec(memory_space=pltpu.VMEM)
-    depth, samples = owner.shape
-    return pl.pallas_call(
-        slots_kernel,
-        out_shape=(
-            jax.ShapeDtypeStruct((depth * samples // E, E), jnp.int32),
-            jax.ShapeDtypeStruct((2 * N_WIDE, CAP), F32),
-            jax.ShapeDtypeStruct((N_WIDE, E), F32),
-        ),
-        in_specs=[pl.BlockSpec(memory_space=pltpu.SMEM), vmem, vmem, vmem],
-        out_specs=(vmem, vmem, vmem),
-        scratch_shapes=[pltpu.VMEM((N_WIDE * depth, samples), BF16)],
-        compiler_params=pltpu.CompilerParams(vmem_limit_bytes=VMEM_BYTES),
-        cost_estimate=LIGHT,
-        name="entry_slots",
-    )(panel.reshape(1), owner, row, bag)
-
-
 def place_kernel(
-    slots_ref, base_hbm, mate_hbm, far_hbm, ids_ref, count_ref, bias_ref, out_ref, base, mate, far, rows, blocks, sems, sems_in
+    slots_ref, base_hbm, mate_hbm, far_hbm, ids_ref, bias_ref, out_ref, base, mate, far, rows, blocks, sems, sems_in
 ):
     depth = 16
     dump = N_WIDE * CAP
@@ -159,8 +134,7 @@
 
     lax.fori_loop(0, base.shape[0] // 16, place, 0)
 
-    bias_top = bias_ref[...].astype(BF16)
-    bias_low = (bias_ref[...] - bias_top.astype(F32)).astype(BF16)
+    bias = bias_ref[...]
 
     def copy_out(w):
         return pltpu.make_async_copy(blocks.at[w], out_ref.at[w], sems.at[w])
@@ -169,19 +143,8 @@
         blocks[w, :CAP, :] = rows[pl.ds(pl.multiple_of(w * CAP, CAP), CAP), :].astype(BF16)
         top = ids_ref[pl.ds(w, 1), :]
         low = ids_ref[pl.ds(N_WIDE + w, 1), :]
-        count = count_ref[pl.ds(w, 1), :]
-        count_top = jnp.floor(count * (1.0 / 64.0))
         parts = [top[:, k * E : (k + 1) * E] for k in range(4)] + [low[:, k * E : (k + 1) * E] for k in range(4)]
-        ends = [count_top] * 4 + [count - 64.0 * count_top] * 4
-        blocks[w, CAP:, :] = jnp.concatenate(
-            [
-                jnp.concatenate(parts, axis=0).astype(BF16),
-                bias_top,
-                bias_low,
-                jnp.concatenate(ends, axis=0).astype(BF16),
-            ],
-            axis=0,
-        )
+        blocks[w, CAP:, :] = jnp.concatenate(parts + [bias], axis=0).astype(BF16)
         copy_out(w).start()
         return 0
 
@@ -194,13 +157,13 @@
     lax.fori_loop(0, N_WIDE, finish, 0)
 
 
-def place_entries(slots, base, mate, far, ids, counts, bias):
+def place_entries(slots, base, mate, far, ids, bias):
     vmem = pl.BlockSpec(memory_space=pltpu.VMEM)
     hbm = pl.BlockSpec(memory_space=pltpu.HBM)
     return pl.pallas_call(
         place_kernel,
         out_shape=jax.ShapeDtypeStruct((N_WIDE, BLOCK, E), BF16),
-        in_specs=[pl.BlockSpec(memory_space=pltpu.SMEM)] + [pl.BlockSpec(memory_space=pl.ANY)] * 3 + [vmem] * 3,
+        in_specs=[pl.BlockSpec(memory_space=pltpu.SMEM)] + [pl.BlockSpec(memory_space=pl.ANY)] * 3 + [vmem] * 2,
         out_specs=hbm,
         scratch_shapes=[
             pltpu.VMEM(base.shape, F32),
@@ -214,7 +177,7 @@
         compiler_params=pltpu.CompilerParams(vmem_limit_bytes=VMEM_BYTES),
         cost_estimate=LIGHT,
         name="place_entries",
-    )(slots, base, mate, far, ids, counts, bias)
+    )(slots, base, mate, far, ids, bias)
 
 
 def sums_kernel(core_ref, recv_ref, keep_ref, send_ref, bias_ref, total, left, right, todo):
@@ -222,19 +185,17 @@
 
     n = 0
     for w in range(N_WIDE):
-        ends = recv_ref[w, CAP + 16 :, :].astype(F32)
-        count = jnp.max(ends[8:12, :] * 64.0 + ends[12:16, :])
+        ids = recv_ref[w, CAP:, :].astype(F32)
+        ids = ids[0:4, :] + ids[4:8, :]
+        halves = jnp.max(jnp.where(ids[2:3, :] > 0.0, 2.0, jnp.where(ids[0:1, :] > 0.0, 1.0, 0.0)))
         todo[n] = 2 * w
-        n = n + jnp.where(count > 0.0, 1, 0)
+        n = n + jnp.where(halves > 0.5, 1, 0)
         todo[n] = 2 * w + 1
-        n = n + jnp.where(count > float(CAP // 2), 1, 0)
+        n = n + jnp.where(halves > 1.5, 1, 0)
     for k in range(12):
         todo[n + k] = -1
     total[...] = jnp.zeros_like(total)
-    bias_ref[...] = jnp.sum(
-        recv_ref[:, CAP + 8 : CAP + 16, :].astype(F32) + recv_ref[:, CAP + 16 : CAP + 24, :].astype(F32),
-        axis=0,
-    )
+    bias_ref[...] = jnp.sum(recv_ref[:, CAP + 8 : CAP + 16, :].astype(F32), axis=0)
 
     def build(i, buf):
         for p in range(4):
@@ -437,8 +398,10 @@
     )(*first, *second)
 
 
-def kept_kernel(n_ref, cot_hbm, embedded_hbm, weight_hbm, bias_ref, scaled_hbm, base_ref, *scratch):
-    cot, embedded, weight, scaled, cross, sems = scratch
+def kept_kernel(
+    n_ref, cot_hbm, embedded_hbm, weight_hbm, bias_ref, scaled_hbm, owner_ref, row_ref, bag_ref, base_ref, slots_ref, ids_ref, *scratch
+):
+    cot, embedded, weight, scaled, cross, onehots, sems = scratch
     n = n_ref[0]
 
     def columns(q):
@@ -454,12 +417,13 @@
     rows(0).start()
     columns(0).start()
     get_scaled.start()
-    rows(0).wait()
-    columns(0).wait()
     for q in (1, 2, 3):
         rows(q).start()
         columns(q).start()
     get_cot.start()
+    find_slots(n, owner_ref, row_ref, bag_ref, slots_ref, ids_ref, onehots)
+    rows(0).wait()
+    columns(0).wait()
     cross[...] = jnp.dot(embedded[:, pl.ds(own_chunk(n), 1024)], weight[0], preferred_element_type=F32)
     get_scaled.wait()
     base_ref[...] = lax.dot_general(scaled[...], weight[0], NT, preferred_element_type=F32)
@@ -475,27 +439,33 @@
     base_ref[...] += grad + grad * (cross[...] + last + bias_ref[...])
 
 
-def kept_terms(n, cotangent, embedded, weight, bias, scaled):
+def kept_terms(n, cotangent, embedded, weight, bias, scaled, owner, row, bag):
     hbm = pl.BlockSpec(memory_space=pltpu.HBM)
     vmem = pl.BlockSpec(memory_space=pltpu.VMEM)
     samples, width = cotangent.shape
+    depth = owner.shape[0]
     return pl.pallas_call(
         kept_kernel,
-        out_shape=jax.ShapeDtypeStruct((samples, width), F32),
-        in_specs=[pl.BlockSpec(memory_space=pltpu.SMEM)] + [hbm] * 3 + [vmem, hbm],
-        out_specs=vmem,
+        out_shape=[
+            jax.ShapeDtypeStruct((samples, width), F32),
+            jax.ShapeDtypeStruct((depth * samples // E, E), jnp.int32),
+            jax.ShapeDtypeStruct((2 * N_WIDE, CAP), F32),
+        ],
+        in_specs=[pl.BlockSpec(memory_space=pltpu.SMEM)] + [hbm] * 3 + [vmem, hbm] + [vmem] * 3,
+        out_specs=[vmem] * 3,
         scratch_shapes=[
             pltpu.VMEM(cotangent.shape, BF16),
             pltpu.VMEM(embedded.shape, BF16),
             pltpu.VMEM((4, 1024, 1024), BF16),
             pltpu.VMEM((samples, width), BF16),
             pltpu.VMEM((samples, width), F32),
+            pltpu.VMEM((N_WIDE * depth, samples), BF16),
             pltpu.SemaphoreType.DMA((10,)),
         ],
         compiler_params=pltpu.CompilerParams(vmem_limit_bytes=VMEM_BYTES),
         cost_estimate=LIGHT,
         name="kept_terms",
-    )(n, cotangent, embedded, weight, bias.reshape(1, -1), scaled)
+    )(n, cotangent, embedded, weight, bias.reshape(1, -1), scaled, owner, row, bag)
 
 
 def own_kernel(z_ref, y_ref, embedded_hbm, turned_hbm, *refs):
@@ -581,42 +551,38 @@
     chip_far, scaled, from_mate = lax.optimization_barrier((chip_far, scaled, from_mate))
     far = lax.ppermute(chip_far, "narrow", X_HI)
 
-    base = kept_terms(at[0], cotangent, embedded, cross_weight, cross_bias, scaled)
-    row_owner, row_id, bag_size, base = lax.optimization_barrier((row_owner, row_id, bag_size, base))
-    slots, ids, counts = entry_slots(
-        panel, row_owner.reshape(row_owner.shape[1:3]).T, row_id.reshape(row_id.shape[1:]).T, bag_size.T
-    )
-    slots, ids, counts, *first = lax.optimization_barrier((slots, ids, counts, *first))
+    entries = (row_owner.reshape(row_owner.shape[1:3]).T, row_id.reshape(row_id.shape[1:]).T, bag_size.T)
+    base, slots, ids = kept_terms(at[0], cotangent, embedded, cross_weight, cross_bias, scaled, *entries)
+    slots, ids, *first = lax.optimization_barrier((slots, ids, *first))
     second = passed_on(first, second)
     slots, far, *second = lax.optimization_barrier((slots, far, *second))
     second = [lax.ppermute(second[q], "wide", ways[q]) for q in range(4)]
 
-    payload = place_entries(slots.reshape(-1), base, from_mate, far, ids, counts, bias_part)
+    payload = place_entries(slots.reshape(-1), base, from_mate, far, ids, bias_part)
     payload, *second = lax.optimization_barrier((payload, *second))
     recv = lax.all_to_all(payload, "wide", split_axis=0, concat_axis=0, tiled=True)
 
     keep_y, send_y, keep_z, send_z = own_terms(at[1], at[2], embedded, turned, first, second)
-    kept = [
-        summed(keep_y, [lax.ppermute(send_y, "wide", y_flip(2))]),
-        summed(keep_z, [lax.ppermute(send_z, "wide", z_flip(2))]),
-    ]
+    recv, send_y, send_z = lax.optimization_barrier((recv, send_y, send_z))
+    got = [lax.ppermute(send_y, "wide", y_flip(2)), lax.ppermute(send_z, "wide", z_flip(2))]
+    keep, send, bias_sums = owned_sums(core.reshape(1), recv)
+    from_core = lax.ppermute(send, "narrow", CORE)
+    keep, *got = lax.optimization_barrier((keep, *got))
     quarters = []
-    for total, place in zip(kept, (y, z)):
-        keep, send = halves_of(total, place % 2, 1)
-        quarters.append((keep.astype(BF16), send.astype(BF16)))
-    recv, *sends = lax.optimization_barrier((recv, quarters[0][1], quarters[1][1]))
-    got = [lax.ppermute(sends[0], "wide", y_flip(1)), lax.ppermute(sends[1], "wide", z_flip(1))]
-    keep, send, bias_sums = owned_sums(core.reshape(1), recv)
-    keep, send, *got = lax.optimization_barrier((keep, send, *got))
-    chip = summed(keep, [lax.ppermute(send, "narrow", CORE)]).astype(BF16)
+    for half, other, place in ((keep_y, got[0], y), (keep_z, got[1], z)):
+        quarters.append([part.astype(BF16) for part in halves_of(summed(half, [other]), place % 2, 1)])
+    got = [lax.ppermute(quarters[0][1], "wide", y_flip(1)), lax.ppermute(quarters[1][1], "wide", z_flip(1))]
+    keep, from_core, *_ = lax.optimization_barrier((keep, from_core, quarters[0][1], quarters[1][1]))
+    chip = summed(keep, [from_core]).astype(BF16)
     pair = jnp.concatenate([summed(quarters[0][0], got[:1]), summed(quarters[1][0], got[1:])], axis=0).astype(BF16)
     x_keep, x_send = halves_of(pair, x_lo, 1)
     other_chip, x_send = lax.optimization_barrier((lax.ppermute(chip, "narrow", X_HI), x_send))
-    weight_grad = summed(x_keep, [lax.ppermute(x_send, "wide", X_LO)]).T * norm_factor
+    x_got = lax.ppermute(x_send, "wide", X_LO)
 
     bias_grad = bias_sums.reshape(-1) * norm_factor
     mine = summed(chip, [other_chip])
-    mate = lax.ppermute(mine, "narrow", CORE)
+    mate, x_got = lax.optimization_barrier((lax.ppermute(mine, "narrow", CORE), x_got))
+    weight_grad = summed(x_keep, [x_got]).T * norm_factor
     row_grad = jnp.concatenate([jnp.where(core == 0, mine, mate), jnp.where(core == 0, mate, mine)], axis=0)
     new_state = adagrad_state + jnp.mean(row_grad * row_grad, axis=1)
     new_table = emb_table - LEARN_RATE * row_grad / jnp.sqrt(new_state)[:, None]

time: 185 us -> 174 us (0.941); the launches traced: 185 us -> 172 us
  Pallas kernels: 66.4 us -> 58.2 us
  other arithmetic: 9.97 us -> 5.9 us
    ppermute x1, waiting for transfers between devices: 49.8 us -> 0.01 us  [body(): lax.ppermute(send_z, 'wide', z_flip(2))]
    all_to_all x1, waiting for transfers between devices: 0.01 us -> 44.6 us  [body(): lax.all_to_all(payload, 'wide', split_axis=0, concat_axis=0, tiled=True)]
    ppermute x5, waiting for transfers between devices: 8.09 us -> 15.2 us  [the longest x1 8.22 us: body(): x_got = lax.ppermute(x_send, 'wide', X_LO)]
    ppermute x1, waiting for transfers between devices: 7.55 us -> 0.87 us  [body(): lax.ppermute(chip, 'narrow', X_HI)]
    pallas_call x1, Pallas kernels: 17 us -> 12.2 us  [owned_sums(): pl.pallas_call(sums_kernel, out_shape=[jax.ShapeDtypeStruct((N_ROWS // 2,...]
    pallas_call x2 -> x1, Pallas kernels: 15.6 us -> 12.4 us  [kept_terms(): pl.pallas_call(kept_kernel, out_shape=[jax.ShapeDtypeStruct((samples, wid...]
    ppermute x4, waiting for transfers between devices: 3.12 us -> 6.29 us  [body(): first = [lax.ppermute(first[q], 'wide', ways[q]) for q in range(4)]]
    add x3, other arithmetic: 3.2 us -> 0.32 us  [summed(): total = total + other.astype(F32)]
  transfers between devices with their start and end apart: 20 -> 20, of which waited for: 7 -> 8; matrix products, arithmetic and copies ran while one was open for 4% -> 2% of each run, Pallas kernels for 30% -> 27%
where the time goes in v2:
time: 174 us; the launch traced here: 172 us
  waiting for transfers between devices  67.1 us (39%)
  Pallas kernels  58.2 us (33%)
  starting transfers between devices  35.4 us (20%)
  other arithmetic  5.9 us (3%)
  local copies, waits for them, and re-layouts  3.98 us (2%)
    all_to_all x1, waiting for transfers between devices, body(): lax.all_to_all(payload, 'wide', split_axis=0, concat_axis=0, tiled=True)  44.6 us
    pallas_call x1, Pallas kernels, place_entries(): pl.pallas_call(place_kernel, out_shape=jax.ShapeDtypeStruct((N_WIDE, BLOC...  12.5 us
    pallas_call x1, Pallas kernels, kept_terms(): pl.pallas_call(kept_kernel, out_shape=[jax.ShapeDtypeStruct((samples, wid...  12.4 us
    pallas_call x1, Pallas kernels, owned_sums(): pl.pallas_call(sums_kernel, out_shape=[jax.ShapeDtypeStruct((N_ROWS // 2,...  12.2 us
    pallas_call x1, Pallas kernels, sent_terms(): pl.pallas_call(sent_kernel, out_shape=[full] * 3 + [shape((512, 1024), BF...  11.6 us
    ppermute x1, waiting for transfers between devices, body(): x_got = lax.ppermute(x_send, 'wide', X_LO)  8.22 us
    all_to_all x1, starting transfers between devices, body(): lax.all_to_all(payload, 'wide', split_axis=0, concat_axis=0, tiled=True)  6.55 us
    ppermute x4, starting transfers between devices, body(): second = [lax.ppermute(second[q], 'wide', ways[q]) for q in range(4)]  6.54 us
  transfers between devices with their start and end apart: 20, of which 8 were waited for; matrix products, arithmetic and copies ran while one was open for 2% of the time, Pallas kernels for 27%

profile of v2, /device:TPU:24, one launch (start us, length us, event | category | flops | bytes accessed | tf_op | source)
XLA Modules:
  0.0 171.5 jit_solution(5752984178633711414)
XLA Ops:
  0.7 11.6 %sent_terms.1 = (bf16[512,1024]{1,0:T(8,128)(2,1)}, bf16[512,1024]{1,0:T(8,128)(2,1)}, bf16[512,1024]{1,0:T(8,128)(2,1)}, bf16[512,1024]{1,0:T(8,128)(2,1)}, bf1...) custom-call(s32[1]{0:T(128)} %bitcast.2.n_ref, ...), custom_call_target="tpu_custom_call" | custom-call | flops 1 | bytes 1 | tf_op jit(solution)/shard_map/sent_terms/pallas_call | solution.py:338
  12.3 0.1 collective-permute-start
  12.4 0.5 collective-permute-start.1
  12.9 1.9 %collective-permute-start.2 = (bf16[512,1024]{1,0:T(8,128)(2,1)}, bf16[512,1024]{1,0:T(8,128)(2,1)S(1)}, u32[]{:S(2)}, u32[]{:S(2)}) collective-permute-start(bf16[512,1024]{1,0:T(8,128)(2,1)} %get-tuple-element.72), channel_id=1, source_target_pairs={{0,32},{4,36},{8,40},{12,44},{16,48},{20,52},{24,56},{28,60},{32,6... | collective-permute-start | bytes 3145736 | tf_op jit(solution)/shard_map/ppermute | solution.py:549
  14.8 2.1 %collective-permute-start.3 = (bf16[512,1024]{1,0:T(8,128)(2,1)}, bf16[512,1024]{1,0:T(8,128)(2,1)S(1)}, u32[]{:S(2)}, u32[]{:S(2)}) collective-permute-start(bf16[512,1024]{1,0:T(8,128)(2,1)} %get-tuple-element.73), channel_id=1, source_target_pairs={{0,96},{4,100},{8,104},{12,108},{16,112},{20,116},{24,120},{28,124... | collective-permute-start | bytes 3145736 | tf_op jit(solution)/shard_map/ppermute | solution.py:549
  17.0 0.2 collective-permute-start.4
  17.2 1.8 %collective-permute-start.5 = (bf16[512,1024]{1,0:T(8,128)(2,1)}, bf16[512,1024]{1,0:T(8,128)(2,1)S(1)}, u32[]{:S(2)}, u32[]{:S(2)}) collective-permute-start(bf16[512,1024]{1,0:T(8,128)(2,1)} %get-tuple-element.75), channel_id=1, source_target_pairs={{0,24},{4,28},{8,0},{12,4},{16,8},{20,12},{24,16},{28,20},{32,56},... | collective-permute-start | bytes 3145736 | tf_op jit(solution)/shard_map/ppermute | solution.py:549
  19.0 1.6 add_convert_fusion
  20.6 3.3 %collective-permute-start.6 = (bf16[512,1024]{1,0:T(8,128)(2,1)S(1)}, bf16[512,1024]{1,0:T(8,128)(2,1)S(1)}, u32[]{:S(2)}, u32[]{:S(2)}) collective-permute-start(bf16[512,1024]{1,0:T(8,128)(2,1)S(1)} %add_convert_fusion), channel_id=1, source_target_pairs={{0,2},{1,3},{2,0},{3,1},{4,6},{5,7},{6,4},{7,5},{8,10},{9,11},{10,... | collective-permute-start | bytes 3145736 | tf_op jit(solution)/shard_map/ppermute | solution.py:552
  23.9 0.6 copy.16
  24.5 12.4 %kept_terms.1 = (f32[512,1024]{1,0:T(8,128)}, s32[64,128]{1,0:T(8,128)}, f32[64,512]{1,0:T(8,128)}) custom-call(s32[1]{0:T(128)} %bitcast.2.n_ref, bf16[512,1024]{1,0:T(8,128)(2,1)} %cot_hbm.3, bf16[512,4096]{1,0:T(8,128)(2,1)} %embedded_hbm.5, bf16[4096,1024]{1,0:T(8,128)(2,1)} %weight_hbm.3, f32[1,1024]{1,0:T(1,128)} %bitcast.23, ...), custom_call_target="tpu_custom_call" | custom-call | flops 1 | bytes 1 | tf_op jit(solution)/shard_map/kept_terms/pallas_call | solution.py:447
  37.0 3.6 %collective-permute-done.2.refs_0_ = bf16[512,1024]{1,0:T(8,128)(2,1)S(1)} collective-permute-done((bf16[512,1024]{1,0:T(8,128)(2,1)}, bf16[512,1024]{1,0:T(8,128)(2,1)S(1)}, u32[]{:S(2)}, u32[]{:S(2)}) %collective-permute-start.2) | collective-permute-done | bytes 1048608 | tf_op jit(solution)/shard_map/ppermute | solution.py:549
  40.6 1.5 collective-permute-done.4.refs_2_
  42.0 1.2 collective-permute-done.5.refs_3_
  43.3 1.0 copy-done.3
  44.3 3.2 %passed_on.1 = (bf16[256,1024]{1,0:T(8,128)(2,1)}, bf16[256,1024]{1,0:T(8,128)(2,1)}, bf16[256,1024]{1,0:T(8,128)(2,1)}, bf16[256,1024]{1,0:T(8,128)(2,1)}) custom-call(bf16[512,1024]{1,0:T(8,128)(2,1)} %copy-done, bf16[512,1024]{1,0:T(8,128)(2,1)} %copy-done.1, bf16[512,1024]{1,0:T(8,128)(2,1)} %copy-done.2, bf16[512,1024]{1,0:T(8,128)(2,1)} %copy-done.3, ...), custom_call_target="tpu_custom_call" | custom-call | flops 1 | bytes 1 | tf_op jit(solution)/shard_map/passed_on/pallas_call | solution.py:383
  47.5 0.6 collective-permute-start.10
  48.1 0.1 collective-permute-start.7
  48.2 3.1 %collective-permute-start.8 = (bf16[256,1024]{1,0:T(8,128)(2,1)}, bf16[256,1024]{1,0:T(8,128)(2,1)S(1)}, u32[]{:S(2)}, u32[]{:S(2)}) collective-permute-start(bf16[256,1024]{1,0:T(8,128)(2,1)} %get-tuple-element.97), channel_id=1, source_target_pairs={{0,96},{4,100},{8,104},{12,108},{16,112},{20,116},{24,120},{28,124... | collective-permute-start | bytes 1572872 | tf_op jit(solution)/shard_map/ppermute | solution.py:559
  51.3 2.7 %collective-permute-start.9 = (bf16[256,1024]{1,0:T(8,128)(2,1)}, bf16[256,1024]{1,0:T(8,128)(2,1)S(1)}, u32[]{:S(2)}, u32[]{:S(2)}) collective-permute-start(bf16[256,1024]{1,0:T(8,128)(2,1)} %get-tuple-element.98), channel_id=1, source_target_pairs={{0,8},{4,12},{8,16},{12,20},{16,24},{20,28},{24,0},{28,4},{32,40},... | collective-permute-start | bytes 1572872 | tf_op jit(solution)/shard_map/ppermute | solution.py:559
  54.0 12.5 %place_entries.1 = bf16[32,528,128]{2,1,0:T(8,128)(2,1)} custom-call(s32[8192]{0:T(1024)} %bitcast.22, f32[512,1024]{1,0:T(8,128)} %get-tuple-element.91.base_hbm, bf16[512,1024]{1,0:T(8,128)(2,1)} %copy-done.5, bf16[512,1024]{1,0:T(8,128)(2,1)} %copy-done.6, f32[64,512]{1,0:T(8,128)} %get-tuple-element.94.ids_ref, f32[8,128]{1,0:T(8,128)} %get-tuple-element.95.bias_ref), custom_call_target="tpu_custom_call" | custom-call | flops 1 | bytes 1 | tf_op jit(solution)/shard_map/place_entries/pallas_call | solution.py:163
  66.6 0.7 copy-done.9
  67.3 0.2 copy-done.10
  67.5 0.2 copy-done.11
  67.7 0.2 copy-done.12
  67.8 6.5 %all-to-all-start = ((bf16[32,528,128]{2,1,0:T(8,128)(2,1)}), bf16[32,528,128]{2,1,0:T(8,128)(2,1)}, u32[]{:S(2)}, u32[]{:S(2)}) async-start(bf16[32,528,128]{2,1,0:T(8,128)(2,1)} %place_entries.1), calls=%async_computation | async-start | bytes 8650752 | tf_op jit(solution)/shard_map/all_to_all | solution.py:563
  74.4 6.3 %own_terms.1 = (bf16[512,512]{1,0:T(8,128)(2,1)}, bf16[512,512]{1,0:T(8,128)(2,1)}, bf16[512,512]{1,0:T(8,128)(2,1)}, bf16[512,512]{1,0:T(8,128)(2,1)}) custom-call(s32[1]{0:T(128)} %bitcast.z_ref, s32[1]{0:T(128)} %bitcast.1.y_ref, bf16[512,4096]{1,0:T(8,128)(2,1)} %embedded_hbm.5, bf16[1024,512]{1,0:T(8,128)(2,1)} %get-tuple-element.64.turned_hbm, ...), custom_call_target="tpu_custom_call" | custom-call | flops 1 | bytes 1 | tf_op jit(solution)/shard_map/own_terms/pallas_call | solution.py:500
  80.8 44.6 %all-to-all-done.recv_ref = bf16[32,528,128]{2,1,0:T(8,128)(2,1)} async-done(((bf16[32,528,128]{2,1,0:T(8,128)(2,1)}), bf16[32,528,128]{2,1,0:T(8,128)(2,1)}, u32[]{:S(2)}, u32[]{:S(2)}) %all-to-all-start) | async-done | bytes 4325408 | tf_op jit(solution)/shard_map/all_to_all | solution.py:563
  125.4 3.9 %collective-permute-start.11 = (bf16[512,512]{1,0:T(8,128)(2,1)}, bf16[512,512]{1,0:T(8,128)(2,1)S(1)}, u32[]{:S(2)}, u32[]{:S(2)}) collective-permute-start(bf16[512,512]{1,0:T(8,128)(2,1)} %get-tuple-element.110), channel_id=1, source_target_pairs={{0,16},{4,20},{8,24},{12,28},{16,0},{20,4},{24,8},{28,12},{32,48},... | collective-permute-start | bytes 1572872 | tf_op jit(solution)/shard_map/ppermute | solution.py:567
  129.3 1.2 collective-permute-start.12
  130.6 12.2 %owned_sums.1 = (bf16[1024,128]{1,0:T(8,128)(2,1)}, bf16[1024,128]{1,0:T(8,128)(2,1)}, f32[8,128]{1,0:T(8,128)}) custom-call(s32[1]{0:T(128)} %bitcast.9.core_ref, bf16[32,528,128]{2,1,0:T(8,128)(2,1)} %all-to-all-done.recv_ref), custom_call_target="tpu_custom_call" | custom-call | flops 1 | bytes 1 | tf_op jit(solution)/shard_map/owned_sums/pallas_call | solution.py:237
  142.8 0.1 convert_add_fusion.1
  142.9 0.1 convert_add_fusion
  143.1 5.8 %collective-permute-start.14 = (bf16[512,256]{1,0:T(8,128)(2,1)S(1)}, bf16[512,256]{1,0:T(8,128)(2,1)S(1)}, u32[]{:S(2)}, u32[]{:S(2)}) collective-permute-start(bf16[512,256]{1,0:T(8,128)(2,1)S(1)} %get-tuple-element.132), channel_id=1, source_target_pairs={{0,32},{4,36},{8,40},{12,44},{16,48},{20,52},{24,56},{28,60},{32,0... | collective-permute-start | bytes 786440 | tf_op jit(solution)/shard_map/ppermute | solution.py:574
  149.0 1.2 collective-permute-start.16
  150.2 5.6 %collective-permute-done.14 = bf16[512,256]{1,0:T(8,128)(2,1)S(1)} collective-permute-done((bf16[512,256]{1,0:T(8,128)(2,1)S(1)}, bf16[512,256]{1,0:T(8,128)(2,1)S(1)}, u32[]{:S(2)}, u32[]{:S(2)}) %collective-permute-start.14) | collective-permute-done | bytes 262176 | tf_op jit(solution)/shard_map/ppermute | solution.py:574
  156.0 1.4 collective-permute-done.13
  157.4 0.7 fusion
  158.1 0.9 collective-permute-done.16
  159.1 0.1 collective-permute-start.17
  159.1 0.1 collective-permute-start.18
  159.3 0.6 multiply_bitcast_fusion.1
  159.9 8.2 %collective-permute-done.18 = bf16[1024,128]{1,0:T(8,128)(2,1)S(1)} collective-permute-done((bf16[1024,128]{1,0:T(8,128)(2,1)}, bf16[1024,128]{1,0:T(8,128)(2,1)S(1)}, u32[]{:S(2)}, u32[]{:S(2)}) %collective-permute-start.18) | collective-permute-done | bytes 262176 | tf_op jit(solution)/shard_map/ppermute | solution.py:580
  168.2 1.0 copy.13
  169.2 0.1 broadcast_select_fusion.1
  169.2 0.3 multiply_reduce_fusion
  169.6 0.6 fusion.2
  170.2 1.3 divide_subtract_fusion
  (49 shorter events, 0.5 us)
Async XLA Ops:
  0.7 23.3 %copy-start.14 = (s32[1,512,16,1]{1,3,2,0:T(1,128)S(1)}, s32[1,512,16,1]{1,3,2,0:T(1,128)}, u32[]{:S(2)}) copy-start(s32[1,512,16,1]{1,3,2,0:T(1,128)} %param.14) | copy-start | bytes 98308
  12.3 4.9 %collective-permute-start = (bf16[512,1024]{1,0:T(8,128)(2,1)}, bf16[512,1024]{1,0:T(8,128)(2,1)S(1)}, u32[]{:S(2)}, u32[]{:S(2)}) collective-permute-start(bf16[512,1024]{1,0:T(8,128)(2,1)} %get-tuple-element.66), channel_id=1, source_target_pairs={{0,1},{1,0},{2,3},{3,2},{4,5},{5,4},{6,7},{7,6},{8,9},{9,8},{10,11... | collective-permute-start | bytes 3145736 | tf_op jit(solution)/shard_map/ppermute | solution.py:546
  12.4 8.2 %collective-permute-start.1 = (bf16[512,1024]{1,0:T(8,128)(2,1)}, bf16[512,1024]{1,0:T(8,128)(2,1)S(1)}, u32[]{:S(2)}, u32[]{:S(2)}) collective-permute-start(bf16[512,1024]{1,0:T(8,128)(2,1)} %get-tuple-element.68), channel_id=1, source_target_pairs={{0,1},{1,0},{2,3},{3,2},{4,5},{5,4},{6,7},{7,6},{8,9},{9,8},{10,11... | collective-permute-start | bytes 3145736 | tf_op jit(solution)/shard_map/ppermute | solution.py:547
  12.9 27.7 %collective-permute-start.2 = (bf16[512,1024]{1,0:T(8,128)(2,1)}, bf16[512,1024]{1,0:T(8,128)(2,1)S(1)}, u32[]{:S(2)}, u32[]{:S(2)}) collective-permute-start(bf16[512,1024]{1,0:T(8,128)(2,1)} %get-tuple-element.72), channel_id=1, source_target_pairs={{0,32},{4,36},{8,40},{12,44},{16,48},{20,52},{24,56},{28,60},{32,6... | collective-permute-start | bytes 3145736 | tf_op jit(solution)/shard_map/ppermute | solution.py:549
  14.8 25.7 %collective-permute-start.3 = (bf16[512,1024]{1,0:T(8,128)(2,1)}, bf16[512,1024]{1,0:T(8,128)(2,1)S(1)}, u32[]{:S(2)}, u32[]{:S(2)}) collective-permute-start(bf16[512,1024]{1,0:T(8,128)(2,1)} %get-tuple-element.73), channel_id=1, source_target_pairs={{0,96},{4,100},{8,104},{12,108},{16,112},{20,116},{24,120},{28,124... | collective-permute-start | bytes 3145736 | tf_op jit(solution)/shard_map/ppermute | solution.py:549
  17.0 25.1 %collective-permute-start.4 = (bf16[512,1024]{1,0:T(8,128)(2,1)}, bf16[512,1024]{1,0:T(8,128)(2,1)S(1)}, u32[]{:S(2)}, u32[]{:S(2)}) collective-permute-start(bf16[512,1024]{1,0:T(8,128)(2,1)} %get-tuple-element.74), channel_id=1, source_target_pairs={{0,8},{4,12},{8,16},{12,20},{16,24},{20,28},{24,0},{28,4},{32,40},... | collective-permute-start | bytes 3145736 | tf_op jit(solution)/shard_map/ppermute | solution.py:549
  17.2 26.1 %collective-permute-start.5 = (bf16[512,1024]{1,0:T(8,128)(2,1)}, bf16[512,1024]{1,0:T(8,128)(2,1)S(1)}, u32[]{:S(2)}, u32[]{:S(2)}) collective-permute-start(bf16[512,1024]{1,0:T(8,128)(2,1)} %get-tuple-element.75), channel_id=1, source_target_pairs={{0,24},{4,28},{8,0},{12,4},{16,8},{20,12},{24,16},{28,20},{32,56},... | collective-permute-start | bytes 3145736 | tf_op jit(solution)/shard_map/ppermute | solution.py:549
  20.6 16.3 %copy-start.5 = (bf16[512,1024]{1,0:T(8,128)(2,1)}, bf16[512,1024]{1,0:T(8,128)(2,1)S(1)}, u32[]{:S(2)}) copy-start(bf16[512,1024]{1,0:T(8,128)(2,1)S(1)} %collective-permute-done.1.mate_hbm) | copy-start | bytes 3145732
  20.6 26.8 %collective-permute-start.6 = (bf16[512,1024]{1,0:T(8,128)(2,1)S(1)}, bf16[512,1024]{1,0:T(8,128)(2,1)S(1)}, u32[]{:S(2)}, u32[]{:S(2)}) collective-permute-start(bf16[512,1024]{1,0:T(8,128)(2,1)S(1)} %add_convert_fusion), channel_id=1, source_target_pairs={{0,2},{1,3},{2,0},{3,1},{4,6},{5,7},{6,4},{7,5},{8,10},{9,11},{10,... | collective-permute-start | bytes 3145736 | tf_op jit(solution)/shard_map/ppermute | solution.py:552
  40.6 2.7 %copy-start = (bf16[512,1024]{1,0:T(8,128)(2,1)}, bf16[512,1024]{1,0:T(8,128)(2,1)S(1)}, u32[]{:S(2)}) copy-start(bf16[512,1024]{1,0:T(8,128)(2,1)S(1)} %collective-permute-done.2.refs_0_) | copy-start | bytes 3145732
  40.6 2.7 %copy-start.1 = (bf16[512,1024]{1,0:T(8,128)(2,1)}, bf16[512,1024]{1,0:T(8,128)(2,1)S(1)}, u32[]{:S(2)}) copy-start(bf16[512,1024]{1,0:T(8,128)(2,1)S(1)} %collective-permute-done.3.refs_1_) | copy-start | bytes 3145732
  42.0 1.2 copy-start.2
  43.3 1.0 copy-start.3
  47.5 6.6 %copy-start.6 = (bf16[512,1024]{1,0:T(8,128)(2,1)}, bf16[512,1024]{1,0:T(8,128)(2,1)S(1)}, u32[]{:S(2)}) copy-start(bf16[512,1024]{1,0:T(8,128)(2,1)S(1)} %collective-permute-done.6.far_hbm) | copy-start | bytes 3145732
  47.5 19.0 %collective-permute-start.10 = (bf16[256,1024]{1,0:T(8,128)(2,1)}, bf16[256,1024]{1,0:T(8,128)(2,1)S(1)}, u32[]{:S(2)}, u32[]{:S(2)}) collective-permute-start(bf16[256,1024]{1,0:T(8,128)(2,1)} %get-tuple-element.99), channel_id=1, source_target_pairs={{0,24},{4,28},{8,0},{12,4},{16,8},{20,12},{24,16},{28,20},{32,56},... | collective-permute-start | bytes 1572872 | tf_op jit(solution)/shard_map/ppermute | solution.py:559
  48.1 18.5 %collective-permute-start.7 = (bf16[256,1024]{1,0:T(8,128)(2,1)}, bf16[256,1024]{1,0:T(8,128)(2,1)S(1)}, u32[]{:S(2)}, u32[]{:S(2)}) collective-permute-start(bf16[256,1024]{1,0:T(8,128)(2,1)} %get-tuple-element.96), channel_id=1, source_target_pairs={{0,32},{4,36},{8,40},{12,44},{16,48},{20,52},{24,56},{28,60},{32,6... | collective-permute-start | bytes 1572872 | tf_op jit(solution)/shard_map/ppermute | solution.py:559
  48.2 18.4 %collective-permute-start.8 = (bf16[256,1024]{1,0:T(8,128)(2,1)}, bf16[256,1024]{1,0:T(8,128)(2,1)S(1)}, u32[]{:S(2)}, u32[]{:S(2)}) collective-permute-start(bf16[256,1024]{1,0:T(8,128)(2,1)} %get-tuple-element.97), channel_id=1, source_target_pairs={{0,96},{4,100},{8,104},{12,108},{16,112},{20,116},{24,120},{28,124... | collective-permute-start | bytes 1572872 | tf_op jit(solution)/shard_map/ppermute | solution.py:559
  51.3 15.3 %collective-permute-start.9 = (bf16[256,1024]{1,0:T(8,128)(2,1)}, bf16[256,1024]{1,0:T(8,128)(2,1)S(1)}, u32[]{:S(2)}, u32[]{:S(2)}) collective-permute-start(bf16[256,1024]{1,0:T(8,128)(2,1)} %get-tuple-element.98), channel_id=1, source_target_pairs={{0,8},{4,12},{8,16},{12,20},{16,24},{20,28},{24,0},{28,4},{32,40},... | collective-permute-start | bytes 1572872 | tf_op jit(solution)/shard_map/ppermute | solution.py:559
  66.5 0.8 copy-start.9
  66.6 0.9 copy-start.10
  66.6 1.1 copy-start.11
  66.6 1.2 copy-start.12
  67.8 57.6 %all-to-all-start = ((bf16[32,528,128]{2,1,0:T(8,128)(2,1)}), bf16[32,528,128]{2,1,0:T(8,128)(2,1)}, u32[]{:S(2)}, u32[]{:S(2)}) async-start(bf16[32,528,128]{2,1,0:T(8,128)(2,1)} %place_entries.1), calls=%async_computation | async-start | bytes 8650752 | tf_op jit(solution)/shard_map/all_to_all | solution.py:563
  80.7 62.0 %copy-start.8 = (bf16[512,512]{1,0:T(8,128)(2,1)S(1)}, bf16[512,512]{1,0:T(8,128)(2,1)}, u32[]{:S(2)}) copy-start(bf16[512,512]{1,0:T(8,128)(2,1)} %get-tuple-element.104) | copy-start | bytes 1572868
  80.7 62.2 %copy-start.7 = (bf16[512,512]{1,0:T(8,128)(2,1)S(1)}, bf16[512,512]{1,0:T(8,128)(2,1)}, u32[]{:S(2)}) copy-start(bf16[512,512]{1,0:T(8,128)(2,1)} %get-tuple-element.113) | copy-start | bytes 1572868
  125.4 17.3 %collective-permute-start.11 = (bf16[512,512]{1,0:T(8,128)(2,1)}, bf16[512,512]{1,0:T(8,128)(2,1)S(1)}, u32[]{:S(2)}, u32[]{:S(2)}) collective-permute-start(bf16[512,512]{1,0:T(8,128)(2,1)} %get-tuple-element.110), channel_id=1, source_target_pairs={{0,16},{4,20},{8,24},{12,28},{16,0},{20,4},{24,8},{28,12},{32,48},... | collective-permute-start | bytes 1572872 | tf_op jit(solution)/shard_map/ppermute | solution.py:567
  129.3 13.4 %collective-permute-start.12 = (bf16[512,512]{1,0:T(8,128)(2,1)}, bf16[512,512]{1,0:T(8,128)(2,1)S(1)}, u32[]{:S(2)}, u32[]{:S(2)}) collective-permute-start(bf16[512,512]{1,0:T(8,128)(2,1)} %get-tuple-element.111), channel_id=1, source_target_pairs={{0,64},{4,68},{8,72},{12,76},{16,80},{20,84},{24,88},{28,92},{32,9... | collective-permute-start | bytes 1572872 | tf_op jit(solution)/shard_map/ppermute | solution.py:567
  142.7 6.2 %copy-start.13 = (bf16[1024,128]{1,0:T(8,128)(2,1)S(1)}, bf16[1024,128]{1,0:T(8,128)(2,1)}, u32[]{:S(2)}) copy-start(bf16[1024,128]{1,0:T(8,128)(2,1)} %get-tuple-element.117) | copy-start | bytes 786436
  142.7 6.2 %collective-permute-start.15 = (bf16[1024,128]{1,0:T(8,128)(2,1)}, bf16[1024,128]{1,0:T(8,128)(2,1)S(1)}, u32[]{:S(2)}, u32[]{:S(2)}) collective-permute-start(bf16[1024,128]{1,0:T(8,128)(2,1)} %get-tuple-element.116), channel_id=1, source_target_pairs={{0,1},{1,0},{2,3},{3,2},{4,5},{5,4},{6,7},{7,6},{8,9},{9,8},{10,11... | collective-permute-start | bytes 786440 | tf_op jit(solution)/shard_map/ppermute | solution.py:569
  142.7 16.5 %copy-start.16 = (f32[8,128]{1,0:T(8,128)S(1)}, f32[8,128]{1,0:T(8,128)}, u32[]{:S(2)}) copy-start(f32[8,128]{1,0:T(8,128)} %get-tuple-element.122) | copy-start | bytes 12292
  143.1 12.8 %collective-permute-start.14 = (bf16[512,256]{1,0:T(8,128)(2,1)S(1)}, bf16[512,256]{1,0:T(8,128)(2,1)S(1)}, u32[]{:S(2)}, u32[]{:S(2)}) collective-permute-start(bf16[512,256]{1,0:T(8,128)(2,1)S(1)} %get-tuple-element.132), channel_id=1, source_target_pairs={{0,32},{4,36},{8,40},{12,44},{16,48},{20,52},{24,56},{28,60},{32,0... | collective-permute-start | bytes 786440 | tf_op jit(solution)/shard_map/ppermute | solution.py:574
  148.9 8.4 %collective-permute-start.13 = (bf16[512,256]{1,0:T(8,128)(2,1)S(1)}, bf16[512,256]{1,0:T(8,128)(2,1)S(1)}, u32[]{:S(2)}, u32[]{:S(2)}) collective-permute-start(bf16[512,256]{1,0:T(8,128)(2,1)S(1)} %get-tuple-element.133), channel_id=1, source_target_pairs={{0,8},{4,12},{8,0},{12,4},{16,24},{20,28},{24,16},{28,20},{32,40},... | collective-permute-start | bytes 786440 | tf_op jit(solution)/shard_map/ppermute | solution.py:574
  149.0 10.0 %collective-permute-start.16 = (bf16[1024,128]{1,0:T(8,128)(2,1)S(1)}, bf16[1024,128]{1,0:T(8,128)(2,1)S(1)}, u32[]{:S(2)}, u32[]{:S(2)}) collective-permute-start(bf16[1024,128]{1,0:T(8,128)(2,1)S(1)} %add_convert_fusion.1), channel_id=1, source_target_pairs={{0,2},{1,3},{2,0},{3,1},{4,6},{5,7},{6,4},{7,5},{8,10},{9,11},{10,... | collective-permute-start | bytes 786440 | tf_op jit(solution)/shard_map/ppermute | solution.py:579
  155.9 13.7 %copy-start.15 = (f32[2048]{0:T(1024)S(1)}, f32[2048]{0:T(1024)}, u32[]{:S(2)}) copy-start(f32[2048]{0:T(1024)} %param.17) | copy-start | bytes 24580
  155.9 14.3 %copy-start.4 = (f32[2048,128]{1,0:T(8,128)S(1)}, f32[2048,128]{1,0:T(8,128)}, u32[]{:S(2)}) copy-start(f32[2048,128]{1,0:T(8,128)} %param.16) | copy-start | bytes 3145732
  159.1 9.0 %collective-permute-start.17 = (f32[1024,128]{1,0:T(8,128)S(1)}, f32[1024,128]{1,0:T(8,128)S(1)}, u32[]{:S(2)}, u32[]{:S(2)}) collective-permute-start(f32[1024,128]{1,0:T(8,128)S(1)} %convert_add_fusion.2), channel_id=1, source_target_pairs={{0,1},{1,0},{2,3},{3,2},{4,5},{5,4},{6,7},{7,6},{8,9},{9,8},{10,11... | collective-permute-start | bytes 1572872 | tf_op jit(solution)/shard_map/ppermute | solution.py:584
  159.1 8.9 %collective-permute-start.18 = (bf16[1024,128]{1,0:T(8,128)(2,1)}, bf16[1024,128]{1,0:T(8,128)(2,1)S(1)}, u32[]{:S(2)}, u32[]{:S(2)}) collective-permute-start(bf16[1024,128]{1,0:T(8,128)(2,1)} %fusion), channel_id=1, source_target_pairs={{0,4},{4,0},{8,12},{12,8},{16,20},{20,16},{24,28},{28,24},{32,36},... | collective-permute-start | bytes 786440 | tf_op jit(solution)/shard_map/ppermute | solution.py:580

commit v3 on v2

--- a/solution.py
+++ b/solution.py
@@ -180,52 +180,46 @@
     )(slots, base, mate, far, ids, bias)
 
 
-def sums_kernel(core_ref, recv_ref, keep_ref, send_ref, bias_ref, total, left, right, todo):
+def sums_kernel(core_ref, recv_hbm, keep_ref, send_ref, bias_ref, recv_ref, total, left, right, sems):
     lane_rows = lax.broadcasted_iota(jnp.int32, (LO, E), 0)
-
-    n = 0
-    for w in range(N_WIDE):
-        ids = recv_ref[w, CAP:, :].astype(F32)
-        ids = ids[0:4, :] + ids[4:8, :]
-        halves = jnp.max(jnp.where(ids[2:3, :] > 0.0, 2.0, jnp.where(ids[0:1, :] > 0.0, 1.0, 0.0)))
-        todo[n] = 2 * w
-        n = n + jnp.where(halves > 0.5, 1, 0)
-        todo[n] = 2 * w + 1
-        n = n + jnp.where(halves > 1.5, 1, 0)
-    for k in range(12):
-        todo[n + k] = -1
-    total[...] = jnp.zeros_like(total)
-    bias_ref[...] = jnp.sum(recv_ref[:, CAP + 8 : CAP + 16, :].astype(F32), axis=0)
+    steps = N_WIDE // 2
+
+    def load(i):
+        at = pl.ds(2 * i, 2)
+        return pltpu.make_async_copy(recv_hbm.at[at], recv_ref.at[at], sems.at[i])
 
     def build(i, buf):
-        for p in range(4):
-            item = todo[i * 4 + p]
-            w = jnp.maximum(item, 0) // 2
-            half = jnp.maximum(item, 0) % 2
+        for p in range(2):
+            w = 2 * i + p
             ids = recv_ref[w, CAP : CAP + 16, :].astype(F32)
             row = (ids[0:4, :] * 64.0 + ids[4:8, :]).astype(jnp.int32) - 1
-            row = jnp.where(half == 0, row[0:2, :], row[2:4, :])
-            row = jnp.where(item < 0, -1, row)
             hi = row >> (LO.bit_length() - 1)
             lo = jnp.where(row < 0, -1, row & (LO - 1))
-            hi_col = jnp.transpose(jnp.concatenate([hi] * 4, axis=0).astype(F32), (1, 0))
-            for j in range(2):
-                at = (2 * p + j) * E
+            hi_col = jnp.transpose(jnp.concatenate([hi, hi], axis=0).astype(F32), (1, 0))
+            for j in range(CAP // E):
+                at = p * CAP + j * E
                 left[buf, :, at : at + E] = jnp.where(lane_rows == lo[j : j + 1, :], 1.0, 0.0).astype(BF16)
-                v = recv_ref[w, pl.ds(pl.multiple_of(half * (CAP // 2), CAP // 2) + j * E, E), :]
+                v = recv_ref[w, j * E : (j + 1) * E, :]
                 own = jnp.broadcast_to(hi_col[:, j : j + 1], (E, E)).astype(BF16)
                 for h in range(HI):
                     right[buf, at : at + E, h * E : (h + 1) * E] = jnp.where(own == BF16(h), v, BF16(0))
 
+    for i in range(steps):
+        load(i).start()
+    total[...] = jnp.zeros_like(total)
+    load(0).wait()
     build(0, 0)
+    for i in range(1, steps):
+        load(i).wait()
 
     def step(i, _):
         for b in range(2):
-            build(2 * i + b + 1, 1 - b)
+            build(jnp.minimum(2 * i + b + 1, steps - 1), 1 - b)
             total[...] += jnp.dot(left[b], right[b], preferred_element_type=F32)
         return 0
 
-    lax.fori_loop(0, (n + 7) // 8, step, 0)
+    lax.fori_loop(0, steps // 2, step, 0)
+    bias_ref[...] = jnp.sum(recv_ref[:, CAP + 8 : CAP + 16, :].astype(F32), axis=0)
     for k in range(HI // 2):
         for out_ref, half in ((keep_ref, core_ref[0]), (send_ref, 1 - core_ref[0])):
             at = pl.multiple_of((half * (HI // 2) + k) * E, E)
@@ -237,13 +231,14 @@
     return pl.pallas_call(
         sums_kernel,
         out_shape=[jax.ShapeDtypeStruct((N_ROWS // 2, E), BF16)] * 2 + [jax.ShapeDtypeStruct((8, E), F32)],
-        in_specs=[pl.BlockSpec(memory_space=pltpu.SMEM), vmem],
+        in_specs=[pl.BlockSpec(memory_space=pltpu.SMEM), pl.BlockSpec(memory_space=pltpu.HBM)],
         out_specs=[vmem] * 3,
         scratch_shapes=[
+            pltpu.VMEM((N_WIDE, BLOCK, E), BF16),
             pltpu.VMEM((LO, HI * E), F32),
             pltpu.VMEM((2, LO, 2 * CAP), BF16),
             pltpu.VMEM((2, 2 * CAP, HI * E), BF16),
-            pltpu.SMEM((2 * N_WIDE + 16,), jnp.int32),
+            pltpu.SemaphoreType.DMA((N_WIDE // 2,)),
         ],
         compiler_params=pltpu.CompilerParams(vmem_limit_bytes=VMEM_BYTES),
         cost_estimate=LIGHT,
@@ -294,20 +289,23 @@
     get_cot.start()
     columns(0).start()
     rows(3).start()
+    rows(1).start()
     get_cot.wait()
     columns(0).wait()
-    for q in (1, 2):
-        rows(q).start()
+    rows(2).start()
     for q in (1, 2, 3):
         columns(q).start()
     grads = (cot[...].astype(F32) * embedded[:, pl.ds(own_chunk(n), 1024)].astype(F32)).astype(BF16)
     scaled[...] = grads
+    outs[11].start()
+    rows(3).wait()
+    parts[0] = lax.dot_general(scaled[...], weight[2], NT, preferred_element_type=F32).astype(BF16)
     turned[...] = jnp.transpose(grads, (1, 0))
     sums = jnp.sum(grads.astype(F32), axis=0, keepdims=True)
     bias_ref[...] = jnp.concatenate([sums[:, k * E : (k + 1) * E] for k in range(8)], axis=0)
-    outs[11].start()
+    outs[0].start()
     outs[12].start()
-    for k, q in enumerate((3, 1, 2)):
+    for k, q in ((1, 1), (2, 2)):
         rows(q).wait()
         part = lax.dot_general(scaled[...], weight[q - 1], NT, preferred_element_type=F32)
         parts[k] = part.astype(BF16)
@@ -321,8 +319,10 @@
         for way in range(2):
             q = 2 * route + way
             term = ring_term(route, turned, embedded, z, y, 3 if way else 1).astype(BF16)
-            first[q, 256:, :] = term[(1 - way) * 256 : (2 - way) * 256, :]
-            second[q] = term[way * 256 : (way + 1) * 256, :]
+            other = term[(1 - way) * 256 : (2 - way) * 256, :]
+            first[q, 256:, :] = other[:128, :]
+            second[q, :256, :] = term[way * 256 : (way + 1) * 256, :]
+            second[q, 256:, :] = other[128:, :]
             outs[3 + q].start()
             outs[7 + q].start()
     for copy in outs:
@@ -334,10 +334,10 @@
     smem = pl.BlockSpec(memory_space=pltpu.SMEM)
     samples, width = cotangent.shape
     shape = jax.ShapeDtypeStruct
-    full, half = shape((samples, width), BF16), shape((256, 1024), BF16)
+    full, ring = shape((samples, width), BF16), shape((384, 1024), BF16)
     results = pl.pallas_call(
         sent_kernel,
-        out_shape=[full] * 3 + [shape((512, 1024), BF16)] * 4 + [half] * 4
+        out_shape=[full] * 3 + [ring] * 8
         + [full, shape((width, samples), BF16), shape((8, E), F32)],
         in_specs=[smem] * 3 + [hbm] * 3,
         out_specs=[hbm] * 13 + [pl.BlockSpec(memory_space=pltpu.VMEM)],
@@ -348,8 +348,8 @@
             pltpu.VMEM((samples, width), BF16),
             pltpu.VMEM((width, samples), BF16),
             pltpu.VMEM((3, samples, width), BF16),
-            pltpu.VMEM((4, 512, 1024), BF16),
-            pltpu.VMEM((4, 256, 1024), BF16),
+            pltpu.VMEM((4, 384, 1024), BF16),
+            pltpu.VMEM((4, 384, 1024), BF16),
             pltpu.SemaphoreType.DMA((8,)),
             pltpu.SemaphoreType.DMA((13,)),
         ],
@@ -361,18 +361,18 @@
 
 
 def pass_kernel(*refs):
-    passed_hbm, mine_hbm, sent_hbm, (passed, mine, sent, sems, sems_out) = refs[:4], refs[4:8], refs[8:12], refs[12:]
+    passed_hbm, mine_hbm, sent_hbm, (passed, mine, sems, sems_out) = refs[:4], refs[4:8], refs[8:12], refs[12:]
     loads, outs = [], []
     for q in range(4):
         loads.append(pltpu.make_async_copy(passed_hbm[q].at[pl.ds(0, 256), :], passed.at[q], sems.at[2 * q]))
         loads.append(pltpu.make_async_copy(mine_hbm[q], mine.at[q], sems.at[2 * q + 1]))
-        outs.append(pltpu.make_async_copy(sent.at[q], sent_hbm[q], sems_out.at[q]))
+        outs.append(pltpu.make_async_copy(mine.at[q], sent_hbm[q], sems_out.at[q]))
     for load in loads:
         load.start()
     for q in range(4):
         loads[2 * q].wait()
         loads[2 * q + 1].wait()
-        sent[q] = (passed[q].astype(F32) + mine[q].astype(F32)).astype(BF16)
+        mine[q, :256, :] = (passed[q].astype(F32) + mine[q, :256, :].astype(F32)).astype(BF16)
         outs[q].start()
     for copy in outs:
         copy.wait()
@@ -382,13 +382,12 @@
     hbm = pl.BlockSpec(memory_space=pltpu.HBM)
     return pl.pallas_call(
         pass_kernel,
-        out_shape=[jax.ShapeDtypeStruct((256, 1024), BF16)] * 4,
+        out_shape=[jax.ShapeDtypeStruct((384, 1024), BF16)] * 4,
         in_specs=[pl.BlockSpec(memory_space=pl.ANY)] * 8,
         out_specs=[hbm] * 4,
         scratch_shapes=[
             pltpu.VMEM((4, 256, 1024), BF16),
-            pltpu.VMEM((4, 256, 1024), BF16),
-            pltpu.VMEM((4, 256, 1024), BF16),
+            pltpu.VMEM((4, 384, 1024), BF16),
             pltpu.SemaphoreType.DMA((8,)),
             pltpu.SemaphoreType.DMA((4,)),
         ],
@@ -469,11 +468,11 @@
 
 
 def own_kernel(z_ref, y_ref, embedded_hbm, turned_hbm, *refs):
-    got_hbm, results, (embedded, turned, got, sems) = refs[:8], refs[8:12], refs[12:]
+    got_hbm, results, (embedded, turned, first, second, sems) = refs[:8], refs[8:12], refs[12:]
     z, y = z_ref[0], y_ref[0]
     loads = [(embedded_hbm, embedded), (turned_hbm, turned)]
-    loads += [(got_hbm[k].at[pl.ds(256, 256), :], got.at[k]) for k in range(4)]
-    loads += [(got_hbm[k], got.at[k]) for k in range(4, 8)]
+    loads += [(got_hbm[k].at[pl.ds(256, 128), :], first.at[k]) for k in range(4)]
+    loads += [(got_hbm[4 + k], second.at[k]) for k in range(4)]
     loads = [pltpu.make_async_copy(src, dst, sems.at[k]) for k, (src, dst) in enumerate(loads)]
     for load in loads:
         load.start()
@@ -482,13 +481,12 @@
     for route, place in ((0, y), (1, z)):
         term = ring_term(route, turned, embedded, z, y, 0)
         up, down = 2 * route, 2 * route + 1
-        total = jnp.concatenate(
-            [
-                term[:256, :] + got[4 + up].astype(F32) + got[down].astype(F32),
-                term[256:, :] + got[4 + down].astype(F32) + got[up].astype(F32),
-            ],
-            axis=0,
-        ).astype(BF16)
+        total = []
+        for at, mine, other in ((0, up, down), (256, down, up)):
+            top = second[mine, :128, :].astype(F32) + first[other].astype(F32)
+            low = second[mine, 128:256, :].astype(F32) + second[other, 256:, :].astype(F32)
+            total += [term[at : at + 128, :] + top, term[at + 128 : at + 256, :] + low]
+        total = jnp.concatenate(total, axis=0).astype(BF16)
         high = place >= 2
         results[2 * route][...] = jnp.where(high, total[:, 512:], total[:, :512])
         results[2 * route + 1][...] = jnp.where(high, total[:, :512], total[:, 512:])
@@ -505,7 +503,8 @@
         scratch_shapes=[
             pltpu.VMEM(embedded.shape, BF16),
             pltpu.VMEM(turned.shape, BF16),
-            pltpu.VMEM((8, 256, 1024), BF16),
+            pltpu.VMEM((4, 128, 1024), BF16),
+            pltpu.VMEM((4, 384, 1024), BF16),
             pltpu.SemaphoreType.DMA((10,)),
         ],
         compiler_params=pltpu.CompilerParams(vmem_limit_bytes=VMEM_BYTES),
@@ -559,9 +558,9 @@
     second = [lax.ppermute(second[q], "wide", ways[q]) for q in range(4)]
 
     payload = place_entries(slots.reshape(-1), base, from_mate, far, ids, bias_part)
-    payload, *second = lax.optimization_barrier((payload, *second))
     recv = lax.all_to_all(payload, "wide", split_axis=0, concat_axis=0, tiled=True)
 
+    turned, payload = lax.optimization_barrier((turned, payload))
     keep_y, send_y, keep_z, send_z = own_terms(at[1], at[2], embedded, turned, first, second)
     recv, send_y, send_z = lax.optimization_barrier((recv, send_y, send_z))
     got = [lax.ppermute(send_y, "wide", y_flip(2)), lax.ppermute(send_z, "wide", z_flip(2))]

time: 174 us -> 191 us (1.098)
  waiting for transfers between devices: 67.1 us -> 80 us
  Pallas kernels: 58.2 us -> 62 us
  starting transfers between devices: 35.4 us -> 33 us
    ppermute x4, waiting for transfers between devices: 0.01 us -> 58.7 us  [body(): second = [lax.ppermute(second[q], 'wide', ways[q]) for q in range(4)]]
    all_to_all x1, waiting for transfers between devices: 44.6 us -> 0.01 us  [body(): lax.all_to_all(payload, 'wide', split_axis=0, concat_axis=0, tiled=True)]
    ppermute x1, starting transfers between devices: 5.79 us -> 0.52 us  [body(): lax.ppermute(quarters[1][1], 'wide', z_flip(1))]
    pallas_call x1, Pallas kernels: 12.2 us -> 15.4 us  [owned_sums(): pl.pallas_call(sums_kernel, out_shape=[jax.ShapeDtypeStruct((N_ROWS // 2,...]
    ppermute x1, starting transfers between devices: 3.91 us -> 0.71 us  [body(): lax.ppermute(send_y, 'wide', y_flip(2))]
    ppermute x1, starting transfers between devices: 0.08 us -> 2.56 us  [body(): x_got = lax.ppermute(x_send, 'wide', X_LO)]
    ppermute x1, waiting for transfers between devices: 0.01 us -> 2.36 us  [body(): from_mate_far = lax.ppermute(parts[0], 'narrow', CORE)]
    ppermute x1, starting transfers between devices: 0.01 us -> 2.13 us  [body(): lax.ppermute(quarters[0][1], 'wide', y_flip(1))]
  transfers between devices with their start and end apart: 20 -> 20, of which waited for: 8 -> 9; matrix products, arithmetic and copies ran while one was open for 2% -> 2% of each run, Pallas kernels for 27% -> 20%
where the time goes in v3:
time: 191 us; the launch traced here: 188 us
  waiting for transfers between devices  80 us (42%)
  Pallas kernels  62 us (32%)
  starting transfers between devices  33 us (17%)
  other arithmetic  5.9 us (3%)
  local copies, waits for them, and re-layouts  5.89 us (3%)
    ppermute x4, waiting for transfers between devices, body(): second = [lax.ppermute(second[q], 'wide', ways[q]) for q in range(4)]  58.7 us
    pallas_call x1, Pallas kernels, owned_sums(): pl.pallas_call(sums_kernel, out_shape=[jax.ShapeDtypeStruct((N_ROWS // 2,...  15.4 us
    pallas_call x1, Pallas kernels, place_entries(): pl.pallas_call(place_kernel, out_shape=jax.ShapeDtypeStruct((N_WIDE, BLOC...  12.5 us
    pallas_call x1, Pallas kernels, kept_terms(): pl.pallas_call(kept_kernel, out_shape=[jax.ShapeDtypeStruct((samples, wid...  12.4 us
    pallas_call x1, Pallas kernels, sent_terms(): pl.pallas_call(sent_kernel, out_shape=[full] * 3 + [ring] * 8 + [full, sh...  11.6 us
    ppermute x4, starting transfers between devices, body(): second = [lax.ppermute(second[q], 'wide', ways[q]) for q in range(4)]  6.54 us
    ppermute x1, waiting for transfers between devices, body(): x_got = lax.ppermute(x_send, 'wide', X_LO)  6.5 us
    all_to_all x1, starting transfers between devices, body(): lax.all_to_all(payload, 'wide', split_axis=0, concat_axis=0, tiled=True)  6.21 us
  transfers between devices with their start and end apart: 20, of which 9 were waited for; matrix products, arithmetic and copies ran while one was open for 2% of the time, Pallas kernels for 20%

profile of v3, /device:TPU:24, one launch (start us, length us, event | category | flops | bytes accessed | tf_op | source)
XLA Modules:
  0.0 187.8 jit_solution(6235724509246449836)
XLA Ops:
  0.7 11.6 %sent_terms.1 = (bf16[512,1024]{1,0:T(8,128)(2,1)}, bf16[512,1024]{1,0:T(8,128)(2,1)}, bf16[512,1024]{1,0:T(8,128)(2,1)}, bf16[384,1024]{1,0:T(8,128)(2,1)}, bf1...) custom-call(s32[1]{0:T(128)} %bitcast.2.n_ref, ...), custom_call_target="tpu_custom_call" | custom-call | flops 1 | bytes 1 | tf_op jit(solution)/shard_map/sent_terms/pallas_call | solution.py:338
  12.3 0.5 collective-permute-start.1
  12.8 2.4 %collective-permute-done = bf16[512,1024]{1,0:T(8,128)(2,1)S(1)} collective-permute-done((bf16[512,1024]{1,0:T(8,128)(2,1)}, bf16[512,1024]{1,0:T(8,128)(2,1)S(1)}, u32[]{:S(2)}, u32[]{:S(2)}) %collective-permute-start) | collective-permute-done | bytes 1048608 | tf_op jit(solution)/shard_map/ppermute | solution.py:545
  15.2 1.6 add_convert_fusion
  16.8 3.1 %collective-permute-start.6 = (bf16[512,1024]{1,0:T(8,128)(2,1)S(1)}, bf16[512,1024]{1,0:T(8,128)(2,1)S(1)}, u32[]{:S(2)}, u32[]{:S(2)}) collective-permute-start(bf16[512,1024]{1,0:T(8,128)(2,1)S(1)} %add_convert_fusion), channel_id=1, source_target_pairs={{0,2},{1,3},{2,0},{3,1},{4,6},{5,7},{6,4},{7,5},{8,10},{9,11},{10,... | collective-permute-start | bytes 3145736 | tf_op jit(solution)/shard_map/ppermute | solution.py:551
  19.9 1.9 %collective-permute-start.2 = (bf16[384,1024]{1,0:T(8,128)(2,1)}, bf16[384,1024]{1,0:T(8,128)(2,1)S(1)}, u32[]{:S(2)}, u32[]{:S(2)}) collective-permute-start(bf16[384,1024]{1,0:T(8,128)(2,1)} %get-tuple-element.68), channel_id=1, source_target_pairs={{0,32},{4,36},{8,40},{12,44},{16,48},{20,52},{24,56},{28,60},{32,6... | collective-permute-start | bytes 2359304 | tf_op jit(solution)/shard_map/ppermute | solution.py:548
  21.9 2.1 %collective-permute-start.3 = (bf16[384,1024]{1,0:T(8,128)(2,1)}, bf16[384,1024]{1,0:T(8,128)(2,1)S(1)}, u32[]{:S(2)}, u32[]{:S(2)}) collective-permute-start(bf16[384,1024]{1,0:T(8,128)(2,1)} %get-tuple-element.69), channel_id=1, source_target_pairs={{0,96},{4,100},{8,104},{12,108},{16,112},{20,116},{24,120},{28,124... | collective-permute-start | bytes 2359304 | tf_op jit(solution)/shard_map/ppermute | solution.py:548
  24.0 0.2 collective-permute-start.4
  24.2 1.8 collective-permute-start.5
  26.0 0.6 copy.16
  26.6 12.4 %kept_terms.1 = (f32[512,1024]{1,0:T(8,128)}, s32[64,128]{1,0:T(8,128)}, f32[64,512]{1,0:T(8,128)}) custom-call(s32[1]{0:T(128)} %bitcast.2.n_ref, bf16[512,1024]{1,0:T(8,128)(2,1)} %cot_hbm.3, bf16[512,4096]{1,0:T(8,128)(2,1)} %embedded_hbm.5, bf16[4096,1024]{1,0:T(8,128)(2,1)} %weight_hbm.3, f32[1,1024]{1,0:T(1,128)} %bitcast.23, ...), custom_call_target="tpu_custom_call" | custom-call | flops 1 | bytes 1 | tf_op jit(solution)/shard_map/kept_terms/pallas_call | solution.py:446
  39.0 2.7 %collective-permute-done.2.refs_0_ = bf16[384,1024]{1,0:T(8,128)(2,1)S(1)} collective-permute-done((bf16[384,1024]{1,0:T(8,128)(2,1)}, bf16[384,1024]{1,0:T(8,128)(2,1)S(1)}, u32[]{:S(2)}, u32[]{:S(2)}) %collective-permute-start.2) | collective-permute-done | bytes 786464 | tf_op jit(solution)/shard_map/ppermute | solution.py:548
  41.8 1.5 collective-permute-done.4.refs_2_
  43.2 1.2 collective-permute-done.5.refs_3_
  44.4 0.9 copy-done.3
  45.4 4.0 %passed_on.1 = (bf16[384,1024]{1,0:T(8,128)(2,1)}, bf16[384,1024]{1,0:T(8,128)(2,1)}, bf16[384,1024]{1,0:T(8,128)(2,1)}, bf16[384,1024]{1,0:T(8,128)(2,1)}) custom-call(bf16[384,1024]{1,0:T(8,128)(2,1)} %copy-done, bf16[384,1024]{1,0:T(8,128)(2,1)} %copy-done.1, bf16[384,1024]{1,0:T(8,128)(2,1)} %copy-done.2, bf16[384,1024]{1,0:T(8,128)(2,1)} %copy-done.3, ...), custom_call_target="tpu_custom_call" | custom-call | flops 1 | bytes 1 | tf_op jit(solution)/shard_map/passed_on/pallas_call | solution.py:383
  49.4 1.0 copy-done.6
  50.3 12.5 %place_entries.1 = bf16[32,528,128]{2,1,0:T(8,128)(2,1)} custom-call(s32[8192]{0:T(1024)} %bitcast.22, f32[512,1024]{1,0:T(8,128)} %get-tuple-element.87.base_hbm, bf16[512,1024]{1,0:T(8,128)(2,1)} %copy-done.5, bf16[512,1024]{1,0:T(8,128)(2,1)} %copy-done.6, f32[64,512]{1,0:T(8,128)} %get-tuple-element.90.ids_ref, f32[8,128]{1,0:T(8,128)} %get-tuple-element.91.bias_ref), custom_call_target="tpu_custom_call" | custom-call | flops 1 | bytes 1 | tf_op jit(solution)/shard_map/place_entries/pallas_call | solution.py:163
  62.9 6.2 %all-to-all-start = ((bf16[32,528,128]{2,1,0:T(8,128)(2,1)}), bf16[32,528,128]{2,1,0:T(8,128)(2,1)}, u32[]{:S(2)}, u32[]{:S(2)}) async-start(bf16[32,528,128]{2,1,0:T(8,128)(2,1)} %place_entries.1), calls=%async_computation | async-start | bytes 8650752 | tf_op jit(solution)/shard_map/all_to_all | solution.py:561
  69.1 0.9 collective-permute-start.10
  70.1 1.5 collective-permute-start.7
  71.5 1.8 collective-permute-start.8
  73.3 2.4 %collective-permute-start.9 = (bf16[384,1024]{1,0:T(8,128)(2,1)S(1)}, bf16[384,1024]{1,0:T(8,128)(2,1)S(1)}, u32[]{:S(2)}, u32[]{:S(2)}) collective-permute-start(bf16[384,1024]{1,0:T(8,128)(2,1)S(1)} %copy-done.17), channel_id=1, source_target_pairs={{0,8},{4,12},{8,16},{12,20},{16,24},{20,28},{24,0},{28,4},{32,40},... | collective-permute-start | bytes 2359304 | tf_op jit(solution)/shard_map/ppermute | solution.py:558
  75.7 58.7 %collective-permute-done.10.refs_7_ = bf16[384,1024]{1,0:T(8,128)(2,1)S(1)} collective-permute-done((bf16[384,1024]{1,0:T(8,128)(2,1)S(1)}, bf16[384,1024]{1,0:T(8,128)(2,1)S(1)}, u32[]{:S(2)}, u32[]{:S(2)}) %collective-permute-start.10) | collective-permute-done | bytes 786464 | tf_op jit(solution)/shard_map/ppermute | solution.py:558
  134.4 0.9 copy-done.7
  135.2 0.2 copy-done.8
  135.5 0.3 copy-done.9
  135.8 0.9 copy-done.10
  136.6 6.2 %own_terms.1 = (bf16[512,512]{1,0:T(8,128)(2,1)}, bf16[512,512]{1,0:T(8,128)(2,1)}, bf16[512,512]{1,0:T(8,128)(2,1)}, bf16[512,512]{1,0:T(8,128)(2,1)}) custom-call(s32[1]{0:T(128)} %bitcast.z_ref, s32[1]{0:T(128)} %bitcast.1.y_ref, bf16[512,4096]{1,0:T(8,128)(2,1)} %embedded_hbm.5, bf16[1024,512]{1,0:T(8,128)(2,1)} %get-tuple-element.92.turned_hbm, ...), custom_call_target="tpu_custom_call" | custom-call | flops 1 | bytes 1 | tf_op jit(solution)/shard_map/own_terms/pallas_call | solution.py:498
  142.8 0.7 collective-permute-start.11
  143.6 2.3 %collective-permute-start.12 = (bf16[512,512]{1,0:T(8,128)(2,1)}, bf16[512,512]{1,0:T(8,128)(2,1)S(1)}, u32[]{:S(2)}, u32[]{:S(2)}) collective-permute-start(bf16[512,512]{1,0:T(8,128)(2,1)} %get-tuple-element.103), channel_id=1, source_target_pairs={{0,64},{4,68},{8,72},{12,76},{16,80},{20,84},{24,88},{28,92},{32,9... | collective-permute-start | bytes 1572872 | tf_op jit(solution)/shard_map/ppermute | solution.py:566
  145.9 15.4 %owned_sums.1 = (bf16[1024,128]{1,0:T(8,128)(2,1)}, bf16[1024,128]{1,0:T(8,128)(2,1)}, f32[8,128]{1,0:T(8,128)}) custom-call(s32[1]{0:T(128)} %bitcast.9.core_ref, bf16[32,528,128]{2,1,0:T(8,128)(2,1)} %all-to-all-done.recv_hbm), custom_call_target="tpu_custom_call" | custom-call | flops 1 | bytes 1 | tf_op jit(solution)/shard_map/owned_sums/pallas_call | solution.py:231
  161.4 0.1 convert_add_fusion.1
  161.6 0.1 convert_add_fusion
  161.8 0.5 collective-permute-start.14
  162.3 2.1 %collective-permute-start.13 = (bf16[512,256]{1,0:T(8,128)(2,1)S(1)}, bf16[512,256]{1,0:T(8,128)(2,1)S(1)}, u32[]{:S(2)}, u32[]{:S(2)}) collective-permute-start(bf16[512,256]{1,0:T(8,128)(2,1)S(1)} %get-tuple-element.125), channel_id=1, source_target_pairs={{0,8},{4,12},{8,0},{12,4},{16,24},{20,28},{24,16},{28,20},{32,40},... | collective-permute-start | bytes 786440 | tf_op jit(solution)/shard_map/ppermute | solution.py:573
  164.5 2.1 %collective-permute-start.16 = (bf16[1024,128]{1,0:T(8,128)(2,1)S(1)}, bf16[1024,128]{1,0:T(8,128)(2,1)S(1)}, u32[]{:S(2)}, u32[]{:S(2)}) collective-permute-start(bf16[1024,128]{1,0:T(8,128)(2,1)S(1)} %add_convert_fusion.1), channel_id=1, source_target_pairs={{0,2},{1,3},{2,0},{3,1},{4,6},{5,7},{6,4},{7,5},{8,10},{9,11},{10,... | collective-permute-start | bytes 786440 | tf_op jit(solution)/shard_map/ppermute | solution.py:578
  166.6 3.9 %collective-permute-done.14 = bf16[512,256]{1,0:T(8,128)(2,1)S(1)} collective-permute-done((bf16[512,256]{1,0:T(8,128)(2,1)S(1)}, bf16[512,256]{1,0:T(8,128)(2,1)S(1)}, u32[]{:S(2)}, u32[]{:S(2)}) %collective-permute-start.14) | collective-permute-done | bytes 262176 | tf_op jit(solution)/shard_map/ppermute | solution.py:573
  170.6 0.7 collective-permute-done.13
  171.5 0.7 fusion
  172.2 2.3 %collective-permute-done.16 = bf16[1024,128]{1,0:T(8,128)(2,1)S(1)} collective-permute-done((bf16[1024,128]{1,0:T(8,128)(2,1)S(1)}, bf16[1024,128]{1,0:T(8,128)(2,1)S(1)}, u32[]{:S(2)}, u32[]{:S(2)}) %collective-permute-start.16) | collective-permute-done | bytes 262176 | tf_op jit(solution)/shard_map/ppermute | solution.py:578
  174.7 2.6 %collective-permute-start.18 = (bf16[1024,128]{1,0:T(8,128)(2,1)}, bf16[1024,128]{1,0:T(8,128)(2,1)S(1)}, u32[]{:S(2)}, u32[]{:S(2)}) collective-permute-start(bf16[1024,128]{1,0:T(8,128)(2,1)} %fusion), channel_id=1, source_target_pairs={{0,4},{4,0},{8,12},{12,8},{16,20},{20,16},{24,28},{28,24},{32,36},... | collective-permute-start | bytes 786440 | tf_op jit(solution)/shard_map/ppermute | solution.py:579
  177.2 0.6 multiply_bitcast_fusion.1
  177.8 6.5 %collective-permute-done.18 = bf16[1024,128]{1,0:T(8,128)(2,1)S(1)} collective-permute-done((bf16[1024,128]{1,0:T(8,128)(2,1)}, bf16[1024,128]{1,0:T(8,128)(2,1)S(1)}, u32[]{:S(2)}, u32[]{:S(2)}) %collective-permute-start.18) | collective-permute-done | bytes 262176 | tf_op jit(solution)/shard_map/ppermute | solution.py:579
  184.4 1.0 copy.13
  185.5 0.3 multiply_reduce_fusion
  185.8 0.6 fusion.2
  186.4 1.3 divide_subtract_fusion
  (57 shorter events, 0.8 us)
Async XLA Ops:
  0.7 25.3 %copy-start.14 = (s32[1,512,16,1]{1,3,2,0:T(1,128)S(1)}, s32[1,512,16,1]{1,3,2,0:T(1,128)}, u32[]{:S(2)}) copy-start(s32[1,512,16,1]{1,3,2,0:T(1,128)} %param.14) | copy-start | bytes 98308
  12.2 3.0 %collective-permute-start = (bf16[512,1024]{1,0:T(8,128)(2,1)}, bf16[512,1024]{1,0:T(8,128)(2,1)S(1)}, u32[]{:S(2)}, u32[]{:S(2)}) collective-permute-start(bf16[512,1024]{1,0:T(8,128)(2,1)} %get-tuple-element.62), channel_id=1, source_target_pairs={{0,1},{1,0},{2,3},{3,2},{4,5},{5,4},{6,7},{7,6},{8,9},{9,8},{10,11... | collective-permute-start | bytes 3145736 | tf_op jit(solution)/shard_map/ppermute | solution.py:545
  12.3 4.5 %collective-permute-start.1 = (bf16[512,1024]{1,0:T(8,128)(2,1)}, bf16[512,1024]{1,0:T(8,128)(2,1)S(1)}, u32[]{:S(2)}, u32[]{:S(2)}) collective-permute-start(bf16[512,1024]{1,0:T(8,128)(2,1)} %get-tuple-element.64), channel_id=1, source_target_pairs={{0,1},{1,0},{2,3},{3,2},{4,5},{5,4},{6,7},{7,6},{8,9},{9,8},{10,11... | collective-permute-start | bytes 3145736 | tf_op jit(solution)/shard_map/ppermute | solution.py:546
  16.8 22.2 %copy-start.5 = (bf16[512,1024]{1,0:T(8,128)(2,1)}, bf16[512,1024]{1,0:T(8,128)(2,1)S(1)}, u32[]{:S(2)}) copy-start(bf16[512,1024]{1,0:T(8,128)(2,1)S(1)} %collective-permute-done.1.mate_hbm) | copy-start | bytes 3145732
  16.8 32.5 %collective-permute-start.6 = (bf16[512,1024]{1,0:T(8,128)(2,1)S(1)}, bf16[512,1024]{1,0:T(8,128)(2,1)S(1)}, u32[]{:S(2)}, u32[]{:S(2)}) collective-permute-start(bf16[512,1024]{1,0:T(8,128)(2,1)S(1)} %add_convert_fusion), channel_id=1, source_target_pairs={{0,2},{1,3},{2,0},{3,1},{4,6},{5,7},{6,4},{7,5},{8,10},{9,11},{10,... | collective-permute-start | bytes 3145736 | tf_op jit(solution)/shard_map/ppermute | solution.py:551
  19.9 21.8 %collective-permute-start.2 = (bf16[384,1024]{1,0:T(8,128)(2,1)}, bf16[384,1024]{1,0:T(8,128)(2,1)S(1)}, u32[]{:S(2)}, u32[]{:S(2)}) collective-permute-start(bf16[384,1024]{1,0:T(8,128)(2,1)} %get-tuple-element.68), channel_id=1, source_target_pairs={{0,32},{4,36},{8,40},{12,44},{16,48},{20,52},{24,56},{28,60},{32,6... | collective-permute-start | bytes 2359304 | tf_op jit(solution)/shard_map/ppermute | solution.py:548
  21.9 19.9 %collective-permute-start.3 = (bf16[384,1024]{1,0:T(8,128)(2,1)}, bf16[384,1024]{1,0:T(8,128)(2,1)S(1)}, u32[]{:S(2)}, u32[]{:S(2)}) collective-permute-start(bf16[384,1024]{1,0:T(8,128)(2,1)} %get-tuple-element.69), channel_id=1, source_target_pairs={{0,96},{4,100},{8,104},{12,108},{16,112},{20,116},{24,120},{28,124... | collective-permute-start | bytes 2359304 | tf_op jit(solution)/shard_map/ppermute | solution.py:548
  24.0 19.2 %collective-permute-start.4 = (bf16[384,1024]{1,0:T(8,128)(2,1)}, bf16[384,1024]{1,0:T(8,128)(2,1)S(1)}, u32[]{:S(2)}, u32[]{:S(2)}) collective-permute-start(bf16[384,1024]{1,0:T(8,128)(2,1)} %get-tuple-element.70), channel_id=1, source_target_pairs={{0,8},{4,12},{8,16},{12,20},{16,24},{20,28},{24,0},{28,4},{32,40},... | collective-permute-start | bytes 2359304 | tf_op jit(solution)/shard_map/ppermute | solution.py:548
  24.2 20.2 %collective-permute-start.5 = (bf16[384,1024]{1,0:T(8,128)(2,1)}, bf16[384,1024]{1,0:T(8,128)(2,1)S(1)}, u32[]{:S(2)}, u32[]{:S(2)}) collective-permute-start(bf16[384,1024]{1,0:T(8,128)(2,1)} %get-tuple-element.71), channel_id=1, source_target_pairs={{0,24},{4,28},{8,0},{12,4},{16,8},{20,12},{24,16},{28,20},{32,56},... | collective-permute-start | bytes 2359304 | tf_op jit(solution)/shard_map/ppermute | solution.py:548
  41.7 2.7 %copy-start = (bf16[384,1024]{1,0:T(8,128)(2,1)}, bf16[384,1024]{1,0:T(8,128)(2,1)S(1)}, u32[]{:S(2)}) copy-start(bf16[384,1024]{1,0:T(8,128)(2,1)S(1)} %collective-permute-done.2.refs_0_) | copy-start | bytes 2359300
  41.7 2.7 %copy-start.1 = (bf16[384,1024]{1,0:T(8,128)(2,1)}, bf16[384,1024]{1,0:T(8,128)(2,1)S(1)}, u32[]{:S(2)}) copy-start(bf16[384,1024]{1,0:T(8,128)(2,1)S(1)} %collective-permute-done.3.refs_1_) | copy-start | bytes 2359300
  43.2 1.2 copy-start.2
  44.4 1.0 copy-start.3
  49.4 1.0 copy-start.6
  62.9 6.3 %copy-start.20 = (bf16[384,1024]{1,0:T(8,128)(2,1)S(1)}, bf16[384,1024]{1,0:T(8,128)(2,1)}, u32[]{:S(2)}) copy-start(bf16[384,1024]{1,0:T(8,128)(2,1)} %get-tuple-element.96) | copy-start | bytes 2359300
  62.9 7.2 %copy-start.19 = (bf16[384,1024]{1,0:T(8,128)(2,1)S(1)}, bf16[384,1024]{1,0:T(8,128)(2,1)}, u32[]{:S(2)}) copy-start(bf16[384,1024]{1,0:T(8,128)(2,1)} %get-tuple-element.93) | copy-start | bytes 2359300
  62.9 8.6 %copy-start.18 = (bf16[384,1024]{1,0:T(8,128)(2,1)S(1)}, bf16[384,1024]{1,0:T(8,128)(2,1)}, u32[]{:S(2)}) copy-start(bf16[384,1024]{1,0:T(8,128)(2,1)} %get-tuple-element.94) | copy-start | bytes 2359300
  62.9 10.4 %copy-start.17 = (bf16[384,1024]{1,0:T(8,128)(2,1)S(1)}, bf16[384,1024]{1,0:T(8,128)(2,1)}, u32[]{:S(2)}) copy-start(bf16[384,1024]{1,0:T(8,128)(2,1)} %get-tuple-element.95) | copy-start | bytes 2359300
  62.9 79.9 %all-to-all-start = ((bf16[32,528,128]{2,1,0:T(8,128)(2,1)}), bf16[32,528,128]{2,1,0:T(8,128)(2,1)}, u32[]{:S(2)}, u32[]{:S(2)}) async-start(bf16[32,528,128]{2,1,0:T(8,128)(2,1)} %place_entries.1), calls=%async_computation | async-start | bytes 8650752 | tf_op jit(solution)/shard_map/all_to_all | solution.py:561
  69.1 65.2 %collective-permute-start.10 = (bf16[384,1024]{1,0:T(8,128)(2,1)S(1)}, bf16[384,1024]{1,0:T(8,128)(2,1)S(1)}, u32[]{:S(2)}, u32[]{:S(2)}) collective-permute-start(bf16[384,1024]{1,0:T(8,128)(2,1)S(1)} %copy-done.20), channel_id=1, source_target_pairs={{0,24},{4,28},{8,0},{12,4},{16,8},{20,12},{24,16},{28,20},{32,56},... | collective-permute-start | bytes 2359304 | tf_op jit(solution)/shard_map/ppermute | solution.py:558
  70.1 64.3 %collective-permute-start.7 = (bf16[384,1024]{1,0:T(8,128)(2,1)S(1)}, bf16[384,1024]{1,0:T(8,128)(2,1)S(1)}, u32[]{:S(2)}, u32[]{:S(2)}) collective-permute-start(bf16[384,1024]{1,0:T(8,128)(2,1)S(1)} %copy-done.19), channel_id=1, source_target_pairs={{0,32},{4,36},{8,40},{12,44},{16,48},{20,52},{24,56},{28,60},{32,6... | collective-permute-start | bytes 2359304 | tf_op jit(solution)/shard_map/ppermute | solution.py:558
  71.5 62.8 %collective-permute-start.8 = (bf16[384,1024]{1,0:T(8,128)(2,1)S(1)}, bf16[384,1024]{1,0:T(8,128)(2,1)S(1)}, u32[]{:S(2)}, u32[]{:S(2)}) collective-permute-start(bf16[384,1024]{1,0:T(8,128)(2,1)S(1)} %copy-done.18), channel_id=1, source_target_pairs={{0,96},{4,100},{8,104},{12,108},{16,112},{20,116},{24,120},{28,124... | collective-permute-start | bytes 2359304 | tf_op jit(solution)/shard_map/ppermute | solution.py:558
  73.3 61.1 %collective-permute-start.9 = (bf16[384,1024]{1,0:T(8,128)(2,1)S(1)}, bf16[384,1024]{1,0:T(8,128)(2,1)S(1)}, u32[]{:S(2)}, u32[]{:S(2)}) collective-permute-start(bf16[384,1024]{1,0:T(8,128)(2,1)S(1)} %copy-done.17), channel_id=1, source_target_pairs={{0,8},{4,12},{8,16},{12,20},{16,24},{20,28},{24,0},{28,4},{32,40},... | collective-permute-start | bytes 2359304 | tf_op jit(solution)/shard_map/ppermute | solution.py:558
  134.3 0.9 copy-start.7
  134.4 1.1 copy-start.8
  134.4 1.4 copy-start.9
  135.7 0.9 copy-start.10
  142.8 18.6 %copy-start.12 = (bf16[512,512]{1,0:T(8,128)(2,1)S(1)}, bf16[512,512]{1,0:T(8,128)(2,1)}, u32[]{:S(2)}) copy-start(bf16[512,512]{1,0:T(8,128)(2,1)} %get-tuple-element.97) | copy-start | bytes 1572868
  142.8 18.8 %copy-start.11 = (bf16[512,512]{1,0:T(8,128)(2,1)S(1)}, bf16[512,512]{1,0:T(8,128)(2,1)}, u32[]{:S(2)}) copy-start(bf16[512,512]{1,0:T(8,128)(2,1)} %get-tuple-element.105) | copy-start | bytes 1572868
  142.8 18.5 %collective-permute-start.11 = (bf16[512,512]{1,0:T(8,128)(2,1)}, bf16[512,512]{1,0:T(8,128)(2,1)S(1)}, u32[]{:S(2)}, u32[]{:S(2)}) collective-permute-start(bf16[512,512]{1,0:T(8,128)(2,1)} %get-tuple-element.102), channel_id=1, source_target_pairs={{0,16},{4,20},{8,24},{12,28},{16,0},{20,4},{24,8},{28,12},{32,48},... | collective-permute-start | bytes 1572872 | tf_op jit(solution)/shard_map/ppermute | solution.py:566
  143.6 17.8 %collective-permute-start.12 = (bf16[512,512]{1,0:T(8,128)(2,1)}, bf16[512,512]{1,0:T(8,128)(2,1)S(1)}, u32[]{:S(2)}, u32[]{:S(2)}) collective-permute-start(bf16[512,512]{1,0:T(8,128)(2,1)} %get-tuple-element.103), channel_id=1, source_target_pairs={{0,64},{4,68},{8,72},{12,76},{16,80},{20,84},{24,88},{28,92},{32,9... | collective-permute-start | bytes 1572872 | tf_op jit(solution)/shard_map/ppermute | solution.py:566
  161.3 3.2 %copy-start.13 = (bf16[1024,128]{1,0:T(8,128)(2,1)S(1)}, bf16[1024,128]{1,0:T(8,128)(2,1)}, u32[]{:S(2)}) copy-start(bf16[1024,128]{1,0:T(8,128)(2,1)} %get-tuple-element.109) | copy-start | bytes 786436
  161.3 3.1 %collective-permute-start.15 = (bf16[1024,128]{1,0:T(8,128)(2,1)}, bf16[1024,128]{1,0:T(8,128)(2,1)S(1)}, u32[]{:S(2)}, u32[]{:S(2)}) collective-permute-start(bf16[1024,128]{1,0:T(8,128)(2,1)} %get-tuple-element.108), channel_id=1, source_target_pairs={{0,1},{1,0},{2,3},{3,2},{4,5},{5,4},{6,7},{7,6},{8,9},{9,8},{10,11... | collective-permute-start | bytes 786440 | tf_op jit(solution)/shard_map/ppermute | solution.py:568
  161.4 15.8 %copy-start.16 = (f32[8,128]{1,0:T(8,128)S(1)}, f32[8,128]{1,0:T(8,128)}, u32[]{:S(2)}) copy-start(f32[8,128]{1,0:T(8,128)} %get-tuple-element.114) | copy-start | bytes 12292
  161.8 8.8 %collective-permute-start.14 = (bf16[512,256]{1,0:T(8,128)(2,1)S(1)}, bf16[512,256]{1,0:T(8,128)(2,1)S(1)}, u32[]{:S(2)}, u32[]{:S(2)}) collective-permute-start(bf16[512,256]{1,0:T(8,128)(2,1)S(1)} %get-tuple-element.124), channel_id=1, source_target_pairs={{0,32},{4,36},{8,40},{12,44},{16,48},{20,52},{24,56},{28,60},{32,0... | collective-permute-start | bytes 786440 | tf_op jit(solution)/shard_map/ppermute | solution.py:573
  162.3 9.1 %collective-permute-start.13 = (bf16[512,256]{1,0:T(8,128)(2,1)S(1)}, bf16[512,256]{1,0:T(8,128)(2,1)S(1)}, u32[]{:S(2)}, u32[]{:S(2)}) collective-permute-start(bf16[512,256]{1,0:T(8,128)(2,1)S(1)} %get-tuple-element.125), channel_id=1, source_target_pairs={{0,8},{4,12},{8,0},{12,4},{16,24},{20,28},{24,16},{28,20},{32,40},... | collective-permute-start | bytes 786440 | tf_op jit(solution)/shard_map/ppermute | solution.py:573
  164.5 10.0 %collective-permute-start.16 = (bf16[1024,128]{1,0:T(8,128)(2,1)S(1)}, bf16[1024,128]{1,0:T(8,128)(2,1)S(1)}, u32[]{:S(2)}, u32[]{:S(2)}) collective-permute-start(bf16[1024,128]{1,0:T(8,128)(2,1)S(1)} %add_convert_fusion.1), channel_id=1, source_target_pairs={{0,2},{1,3},{2,0},{3,1},{4,6},{5,7},{6,4},{7,5},{8,10},{9,11},{10,... | collective-permute-start | bytes 786440 | tf_op jit(solution)/shard_map/ppermute | solution.py:578
  170.6 15.2 %copy-start.15 = (f32[2048]{0:T(1024)S(1)}, f32[2048]{0:T(1024)}, u32[]{:S(2)}) copy-start(f32[2048]{0:T(1024)} %param.17) | copy-start | bytes 24580
  170.6 15.8 %copy-start.4 = (f32[2048,128]{1,0:T(8,128)S(1)}, f32[2048,128]{1,0:T(8,128)}, u32[]{:S(2)}) copy-start(f32[2048,128]{1,0:T(8,128)} %param.16) | copy-start | bytes 3145732
  174.6 9.8 %collective-permute-start.17 = (f32[1024,128]{1,0:T(8,128)S(1)}, f32[1024,128]{1,0:T(8,128)S(1)}, u32[]{:S(2)}, u32[]{:S(2)}) collective-permute-start(f32[1024,128]{1,0:T(8,128)S(1)} %convert_add_fusion.2), channel_id=1, source_target_pairs={{0,1},{1,0},{2,3},{3,2},{4,5},{5,4},{6,7},{7,6},{8,9},{9,8},{10,11... | collective-permute-start | bytes 1572872 | tf_op jit(solution)/shard_map/ppermute | solution.py:583
  174.7 9.7 %collective-permute-start.18 = (bf16[1024,128]{1,0:T(8,128)(2,1)}, bf16[1024,128]{1,0:T(8,128)(2,1)S(1)}, u32[]{:S(2)}, u32[]{:S(2)}) collective-permute-start(bf16[1024,128]{1,0:T(8,128)(2,1)} %fusion), channel_id=1, source_target_pairs={{0,4},{4,0},{8,12},{12,8},{16,20},{20,16},{24,28},{28,24},{32,36},... | collective-permute-start | bytes 786440 | tf_op jit(solution)/shard_map/ppermute | solution.py:579

commit v4 on v2

--- a/solution.py
+++ b/solution.py
@@ -1,3 +1,4 @@
+import functools
 import math
 
 import jax
@@ -180,7 +181,7 @@
     )(slots, base, mate, far, ids, bias)
 
 
-def sums_kernel(core_ref, recv_ref, keep_ref, send_ref, bias_ref, total, left, right, todo):
+def sums_kernel(norm_factor, core_ref, recv_ref, keep_ref, send_ref, bias_ref, total, left, right, todo):
     lane_rows = lax.broadcasted_iota(jnp.int32, (LO, E), 0)
 
     n = 0
@@ -195,7 +196,7 @@
     for k in range(12):
         todo[n + k] = -1
     total[...] = jnp.zeros_like(total)
-    bias_ref[...] = jnp.sum(recv_ref[:, CAP + 8 : CAP + 16, :].astype(F32), axis=0)
+    bias_ref[...] = jnp.sum(recv_ref[:, CAP + 8 : CAP + 16, :].astype(F32), axis=0) * norm_factor
 
     def build(i, buf):
         for p in range(4):
@@ -232,10 +233,10 @@
             out_ref[k * LO : (k + 1) * LO, :] = total[:, pl.ds(at, E)].astype(BF16)
 
 
-def owned_sums(core, recv):
+def owned_sums(norm_factor, core, recv):
     vmem = pl.BlockSpec(memory_space=pltpu.VMEM)
     return pl.pallas_call(
-        sums_kernel,
+        functools.partial(sums_kernel, norm_factor),
         out_shape=[jax.ShapeDtypeStruct((N_ROWS // 2, E), BF16)] * 2 + [jax.ShapeDtypeStruct((8, E), F32)],
         in_specs=[pl.BlockSpec(memory_space=pltpu.SMEM), vmem],
         out_specs=[vmem] * 3,
@@ -262,14 +263,16 @@
     return pl.multiple_of(a * 1024, 1024)
 
 
-def ring_term(route, turned, embedded, z, y, d):
+def ring_terms(route, turned, embedded, z, y, d):
     part = turned[route * 512 : (route + 1) * 512, :]
     if route == 0:
         rows = embedded[:, pl.ds(own_chunk((z + d) % 4), 1024)]
-        return jnp.dot(part, rows, preferred_element_type=F32)
+        yield slice(0, 1024), jnp.dot(part, rows, preferred_element_type=F32)
+        return
     start = ((y + d) % 4) * 256
-    blocks = [embedded[:, pl.ds(pl.multiple_of(k * 1024 + start, 256), 256)] for k in range(4)]
-    return jnp.concatenate([jnp.dot(part, rows, preferred_element_type=F32) for rows in blocks], axis=1)
+    for k in range(4):
+        rows = embedded[:, pl.ds(pl.multiple_of(k * 1024 + start, 256), 256)]
+        yield slice(k * 256, (k + 1) * 256), jnp.dot(part, rows, preferred_element_type=F32)
 
 
 def sent_kernel(n_ref, z_ref, y_ref, cot_hbm, embedded_hbm, weight_hbm, *refs):
@@ -302,12 +305,15 @@
         columns(q).start()
     grads = (cot[...].astype(F32) * embedded[:, pl.ds(own_chunk(n), 1024)].astype(F32)).astype(BF16)
     scaled[...] = grads
+    outs[11].start()
+    rows(3).wait()
+    parts[0] = lax.dot_general(scaled[...], weight[2], NT, preferred_element_type=F32).astype(BF16)
     turned[...] = jnp.transpose(grads, (1, 0))
     sums = jnp.sum(grads.astype(F32), axis=0, keepdims=True)
     bias_ref[...] = jnp.concatenate([sums[:, k * E : (k + 1) * E] for k in range(8)], axis=0)
-    outs[11].start()
+    outs[0].start()
     outs[12].start()
-    for k, q in enumerate((3, 1, 2)):
+    for k, q in ((1, 1), (2, 2)):
         rows(q).wait()
         part = lax.dot_general(scaled[...], weight[q - 1], NT, preferred_element_type=F32)
         parts[k] = part.astype(BF16)
@@ -315,14 +321,16 @@
     for q in (1, 2, 3):
         columns(q).wait()
     for route in range(2):
-        term = ring_term(route, turned, embedded, z, y, 2).astype(BF16)
-        for way in range(2):
-            first[2 * route + way, :256, :] = term[way * 256 : (way + 1) * 256, :]
+        for at, term in ring_terms(route, turned, embedded, z, y, 2):
+            term = term.astype(BF16)
+            for way in range(2):
+                first[2 * route + way, :256, at] = term[way * 256 : (way + 1) * 256, :]
         for way in range(2):
             q = 2 * route + way
-            term = ring_term(route, turned, embedded, z, y, 3 if way else 1).astype(BF16)
-            first[q, 256:, :] = term[(1 - way) * 256 : (2 - way) * 256, :]
-            second[q] = term[way * 256 : (way + 1) * 256, :]
+            for at, term in ring_terms(route, turned, embedded, z, y, 3 if way else 1):
+                term = term.astype(BF16)
+                first[q, 256:, at] = term[(1 - way) * 256 : (2 - way) * 256, :]
+                second[q, :, at] = term[way * 256 : (way + 1) * 256, :]
             outs[3 + q].start()
             outs[7 + q].start()
     for copy in outs:
@@ -480,7 +488,7 @@
     for load in loads:
         load.wait()
     for route, place in ((0, y), (1, z)):
-        term = ring_term(route, turned, embedded, z, y, 0)
+        term = jnp.concatenate([term for _, term in ring_terms(route, turned, embedded, z, y, 0)], axis=1)
         up, down = 2 * route, 2 * route + 1
         total = jnp.concatenate(
             [
@@ -565,7 +573,7 @@
     keep_y, send_y, keep_z, send_z = own_terms(at[1], at[2], embedded, turned, first, second)
     recv, send_y, send_z = lax.optimization_barrier((recv, send_y, send_z))
     got = [lax.ppermute(send_y, "wide", y_flip(2)), lax.ppermute(send_z, "wide", z_flip(2))]
-    keep, send, bias_sums = owned_sums(core.reshape(1), recv)
+    keep, send, bias_sums = owned_sums(norm_factor, core.reshape(1), recv)
     from_core = lax.ppermute(send, "narrow", CORE)
     keep, *got = lax.optimization_barrier((keep, *got))
     quarters = []
@@ -576,14 +584,14 @@
     chip = summed(keep, [from_core]).astype(BF16)
     pair = jnp.concatenate([summed(quarters[0][0], got[:1]), summed(quarters[1][0], got[1:])], axis=0).astype(BF16)
     x_keep, x_send = halves_of(pair, x_lo, 1)
-    other_chip, x_send = lax.optimization_barrier((lax.ppermute(chip, "narrow", X_HI), x_send))
-    x_got = lax.ppermute(x_send, "wide", X_LO)
-
-    bias_grad = bias_sums.reshape(-1) * norm_factor
-    mine = summed(chip, [other_chip])
+    other_chip, _ = lax.optimization_barrier((lax.ppermute(chip, "narrow", X_HI), x_send))
+    x_got = lax.ppermute(jnp.pad(x_send, ((0, 16), (0, 0))), "wide", X_LO)[:1024]
+
+    bias_grad = bias_sums.reshape(-1)
+    mine = summed(chip, [other_chip]).astype(BF16)
     mate, x_got = lax.optimization_barrier((lax.ppermute(mine, "narrow", CORE), x_got))
     weight_grad = summed(x_keep, [x_got]).T * norm_factor
-    row_grad = jnp.concatenate([jnp.where(core == 0, mine, mate), jnp.where(core == 0, mate, mine)], axis=0)
+    row_grad = jnp.concatenate([jnp.where(core == 0, mine, mate), jnp.where(core == 0, mate, mine)], axis=0).astype(F32)
     new_state = adagrad_state + jnp.mean(row_grad * row_grad, axis=1)
     new_table = emb_table - LEARN_RATE * row_grad / jnp.sqrt(new_state)[:, None]
     return (weight_grad, bias_grad, new_table, new_state)

time: 174 us -> 170 us (0.977)
  waiting for transfers between devices: 67.1 us -> 60.4 us
  starting transfers between devices: 35.4 us -> 40.9 us
    ppermute x1, waiting for transfers between devices: 5.64 us -> 0.01 us  [body(): lax.ppermute(quarters[1][1], 'wide', z_flip(1))]
    ppermute x1, starting transfers between devices: 0.01 us -> 4.63 us  [body(): lax.ppermute(quarters[0][1], 'wide', y_flip(1))]
    ppermute x1, starting transfers between devices: 5.79 us -> 2.61 us  [body(): lax.ppermute(quarters[1][1], 'wide', z_flip(1))]
    ppermute x1, waiting for transfers between devices: 8.22 us -> 5.3 us  [body(): lax.ppermute(jnp.pad(x_send, ((0, 16), (0, 0))), 'wide', X_LO)[:1024]]
    ppermute x1, starting transfers between devices: 0.08 us -> 2.55 us  [body(): lax.ppermute(jnp.pad(x_send, ((0, 16), (0, 0))), 'wide', X_LO)[:1024]]
    ppermute x1, waiting for transfers between devices: 1.36 us -> 3.68 us  [body(): lax.ppermute(quarters[0][1], 'wide', y_flip(1))]
    unnamed x36 -> x34, local copies, waits for them, and re-layouts: 3.94 us -> 3.94 us
  transfers between devices with their start and end apart: 20 -> 20, of which waited for: 8 -> 7; matrix products, arithmetic and copies ran while one was open for 2% -> 2% of each run, Pallas kernels for 27% -> 27%
where the time goes in v4:
time: 170 us; the launch traced here: 168 us
  waiting for transfers between devices  60.4 us (36%)
  Pallas kernels  56.6 us (33%)
  starting transfers between devices  40.9 us (24%)
  other arithmetic  4.58 us (3%)
  local copies, waits for them, and re-layouts  4.02 us (2%)
    all_to_all x1, waiting for transfers between devices, body(): lax.all_to_all(payload, 'wide', split_axis=0, concat_axis=0, tiled=True)  44.6 us
    pallas_call x1, Pallas kernels, place_entries(): pl.pallas_call(place_kernel, out_shape=jax.ShapeDtypeStruct((N_WIDE, BLOC...  12.5 us
    pallas_call x1, Pallas kernels, kept_terms(): pl.pallas_call(kept_kernel, out_shape=[jax.ShapeDtypeStruct((samples, wid...  12.4 us
    pallas_call x1, Pallas kernels, sent_terms(): pl.pallas_call(sent_kernel, out_shape=[full] * 3 + [shape((512, 1024), BF...  11.7 us
    pallas_call x1, Pallas kernels, owned_sums(): pl.pallas_call(functools.partial(sums_kernel, norm_factor), out_shape=[ja...  10.6 us
    ppermute x4, starting transfers between devices, body(): second = [lax.ppermute(second[q], 'wide', ways[q]) for q in range(4)]  6.54 us
    all_to_all x1, starting transfers between devices, body(): lax.all_to_all(payload, 'wide', split_axis=0, concat_axis=0, tiled=True)  6.54 us
    pallas_call x1, Pallas kernels, own_terms(): pl.pallas_call(own_kernel, out_shape=[jax.ShapeDtypeStruct((512, 512), BF...  6.32 us
  transfers between devices with their start and end apart: 20, of which 7 were waited for; matrix products, arithmetic and copies ran while one was open for 2% of the time, Pallas kernels for 27%

profile of v4, /device:TPU:24, one launch (start us, length us, event | category | flops | bytes accessed | tf_op | source)
XLA Modules:
  0.0 167.6 jit_solution(6704247154909453107)
XLA Ops:
  0.7 11.7 %sent_terms.1 = (bf16[512,1024]{1,0:T(8,128)(2,1)}, bf16[512,1024]{1,0:T(8,128)(2,1)}, bf16[512,1024]{1,0:T(8,128)(2,1)}, bf16[512,1024]{1,0:T(8,128)(2,1)}, bf1...) custom-call(s32[1]{0:T(128)} %bitcast.2.n_ref, ...), custom_call_target="tpu_custom_call" | custom-call | flops 1 | bytes 1 | tf_op jit(solution)/shard_map/sent_terms/pallas_call | solution.py:346
  12.3 0.1 collective-permute-start
  12.4 0.5 collective-permute-start.1
  12.9 1.9 %collective-permute-start.2 = (bf16[512,1024]{1,0:T(8,128)(2,1)}, bf16[512,1024]{1,0:T(8,128)(2,1)S(1)}, u32[]{:S(2)}, u32[]{:S(2)}) collective-permute-start(bf16[512,1024]{1,0:T(8,128)(2,1)} %get-tuple-element.71), channel_id=1, source_target_pairs={{0,32},{4,36},{8,40},{12,44},{16,48},{20,52},{24,56},{28,60},{32,6... | collective-permute-start | bytes 3145736 | tf_op jit(solution)/shard_map/ppermute | solution.py:557
  14.9 2.1 %collective-permute-start.3 = (bf16[512,1024]{1,0:T(8,128)(2,1)}, bf16[512,1024]{1,0:T(8,128)(2,1)S(1)}, u32[]{:S(2)}, u32[]{:S(2)}) collective-permute-start(bf16[512,1024]{1,0:T(8,128)(2,1)} %get-tuple-element.72), channel_id=1, source_target_pairs={{0,96},{4,100},{8,104},{12,108},{16,112},{20,116},{24,120},{28,124... | collective-permute-start | bytes 3145736 | tf_op jit(solution)/shard_map/ppermute | solution.py:557
  17.0 0.2 collective-permute-start.4
  17.2 1.8 %collective-permute-start.5 = (bf16[512,1024]{1,0:T(8,128)(2,1)}, bf16[512,1024]{1,0:T(8,128)(2,1)S(1)}, u32[]{:S(2)}, u32[]{:S(2)}) collective-permute-start(bf16[512,1024]{1,0:T(8,128)(2,1)} %get-tuple-element.74), channel_id=1, source_target_pairs={{0,24},{4,28},{8,0},{12,4},{16,8},{20,12},{24,16},{28,20},{32,56},... | collective-permute-start | bytes 3145736 | tf_op jit(solution)/shard_map/ppermute | solution.py:557
  19.0 1.6 add_convert_fusion
  20.7 3.3 %collective-permute-start.6 = (bf16[512,1024]{1,0:T(8,128)(2,1)S(1)}, bf16[512,1024]{1,0:T(8,128)(2,1)S(1)}, u32[]{:S(2)}, u32[]{:S(2)}) collective-permute-start(bf16[512,1024]{1,0:T(8,128)(2,1)S(1)} %add_convert_fusion), channel_id=1, source_target_pairs={{0,2},{1,3},{2,0},{3,1},{4,6},{5,7},{6,4},{7,5},{8,10},{9,11},{10,... | collective-permute-start | bytes 3145736 | tf_op jit(solution)/shard_map/ppermute | solution.py:560
  23.9 0.6 copy.16
  24.6 12.4 %kept_terms.1 = (f32[512,1024]{1,0:T(8,128)}, s32[64,128]{1,0:T(8,128)}, f32[64,512]{1,0:T(8,128)}) custom-call(s32[1]{0:T(128)} %bitcast.2.n_ref, bf16[512,1024]{1,0:T(8,128)(2,1)} %cot_hbm.3, bf16[512,4096]{1,0:T(8,128)(2,1)} %embedded_hbm.5, bf16[4096,1024]{1,0:T(8,128)(2,1)} %weight_hbm.3, f32[1,1024]{1,0:T(1,128)} %bitcast.22, ...), custom_call_target="tpu_custom_call" | custom-call | flops 1 | bytes 1 | tf_op jit(solution)/shard_map/kept_terms/pallas_call | solution.py:455
  37.0 3.6 %collective-permute-done.2.refs_0_ = bf16[512,1024]{1,0:T(8,128)(2,1)S(1)} collective-permute-done((bf16[512,1024]{1,0:T(8,128)(2,1)}, bf16[512,1024]{1,0:T(8,128)(2,1)S(1)}, u32[]{:S(2)}, u32[]{:S(2)}) %collective-permute-start.2) | collective-permute-done | bytes 1048608 | tf_op jit(solution)/shard_map/ppermute | solution.py:557
  40.6 1.5 collective-permute-done.4.refs_2_
  42.1 1.2 collective-permute-done.5.refs_3_
  43.3 1.0 copy-done.3
  44.3 3.2 %passed_on.1 = (bf16[256,1024]{1,0:T(8,128)(2,1)}, bf16[256,1024]{1,0:T(8,128)(2,1)}, bf16[256,1024]{1,0:T(8,128)(2,1)}, bf16[256,1024]{1,0:T(8,128)(2,1)}) custom-call(bf16[512,1024]{1,0:T(8,128)(2,1)} %copy-done, bf16[512,1024]{1,0:T(8,128)(2,1)} %copy-done.1, bf16[512,1024]{1,0:T(8,128)(2,1)} %copy-done.2, bf16[512,1024]{1,0:T(8,128)(2,1)} %copy-done.3, ...), custom_call_target="tpu_custom_call" | custom-call | flops 1 | bytes 1 | tf_op jit(solution)/shard_map/passed_on/pallas_call | solution.py:391
  47.5 0.6 collective-permute-start.10
  48.1 0.1 collective-permute-start.7
  48.2 3.1 %collective-permute-start.8 = (bf16[256,1024]{1,0:T(8,128)(2,1)}, bf16[256,1024]{1,0:T(8,128)(2,1)S(1)}, u32[]{:S(2)}, u32[]{:S(2)}) collective-permute-start(bf16[256,1024]{1,0:T(8,128)(2,1)} %get-tuple-element.96), channel_id=1, source_target_pairs={{0,96},{4,100},{8,104},{12,108},{16,112},{20,116},{24,120},{28,124... | collective-permute-start | bytes 1572872 | tf_op jit(solution)/shard_map/ppermute | solution.py:567
  51.4 2.7 %collective-permute-start.9 = (bf16[256,1024]{1,0:T(8,128)(2,1)}, bf16[256,1024]{1,0:T(8,128)(2,1)S(1)}, u32[]{:S(2)}, u32[]{:S(2)}) collective-permute-start(bf16[256,1024]{1,0:T(8,128)(2,1)} %get-tuple-element.97), channel_id=1, source_target_pairs={{0,8},{4,12},{8,16},{12,20},{16,24},{20,28},{24,0},{28,4},{32,40},... | collective-permute-start | bytes 1572872 | tf_op jit(solution)/shard_map/ppermute | solution.py:567
  54.1 12.5 %place_entries.1 = bf16[32,528,128]{2,1,0:T(8,128)(2,1)} custom-call(s32[8192]{0:T(1024)} %bitcast.21, f32[512,1024]{1,0:T(8,128)} %get-tuple-element.90.base_hbm, bf16[512,1024]{1,0:T(8,128)(2,1)} %copy-done.5, bf16[512,1024]{1,0:T(8,128)(2,1)} %copy-done.6, f32[64,512]{1,0:T(8,128)} %get-tuple-element.93.ids_ref, f32[8,128]{1,0:T(8,128)} %get-tuple-element.94.bias_ref), custom_call_target="tpu_custom_call" | custom-call | flops 1 | bytes 1 | tf_op jit(solution)/shard_map/place_entries/pallas_call | solution.py:164
  66.6 0.7 copy-done.9
  67.4 0.2 copy-done.10
  67.5 0.2 copy-done.11
  67.7 0.2 copy-done.12
  67.9 6.5 %all-to-all-start = ((bf16[32,528,128]{2,1,0:T(8,128)(2,1)}), bf16[32,528,128]{2,1,0:T(8,128)(2,1)}, u32[]{:S(2)}, u32[]{:S(2)}) async-start(bf16[32,528,128]{2,1,0:T(8,128)(2,1)} %place_entries.1), calls=%async_computation | async-start | bytes 8650752 | tf_op jit(solution)/shard_map/all_to_all | solution.py:571
  74.4 6.3 %own_terms.1 = (bf16[512,512]{1,0:T(8,128)(2,1)}, bf16[512,512]{1,0:T(8,128)(2,1)}, bf16[512,512]{1,0:T(8,128)(2,1)}, bf16[512,512]{1,0:T(8,128)(2,1)}) custom-call(s32[1]{0:T(128)} %bitcast.z_ref, s32[1]{0:T(128)} %bitcast.1.y_ref, bf16[512,4096]{1,0:T(8,128)(2,1)} %embedded_hbm.5, bf16[1024,512]{1,0:T(8,128)(2,1)} %get-tuple-element.63.turned_hbm, ...), custom_call_target="tpu_custom_call" | custom-call | flops 1 | bytes 1 | tf_op jit(solution)/shard_map/own_terms/pallas_call | solution.py:508
  80.8 44.6 %all-to-all-done.recv_ref = bf16[32,528,128]{2,1,0:T(8,128)(2,1)} async-done(((bf16[32,528,128]{2,1,0:T(8,128)(2,1)}), bf16[32,528,128]{2,1,0:T(8,128)(2,1)}, u32[]{:S(2)}, u32[]{:S(2)}) %all-to-all-start) | async-done | bytes 4325408 | tf_op jit(solution)/shard_map/all_to_all | solution.py:571
  125.4 3.9 %collective-permute-start.11 = (bf16[512,512]{1,0:T(8,128)(2,1)}, bf16[512,512]{1,0:T(8,128)(2,1)S(1)}, u32[]{:S(2)}, u32[]{:S(2)}) collective-permute-start(bf16[512,512]{1,0:T(8,128)(2,1)} %get-tuple-element.109), channel_id=1, source_target_pairs={{0,16},{4,20},{8,24},{12,28},{16,0},{20,4},{24,8},{28,12},{32,48},... | collective-permute-start | bytes 1572872 | tf_op jit(solution)/shard_map/ppermute | solution.py:575
  129.4 1.2 collective-permute-start.12
  130.6 10.6 %owned_sums.1 = (bf16[1024,128]{1,0:T(8,128)(2,1)}, bf16[1024,128]{1,0:T(8,128)(2,1)}, f32[8,128]{1,0:T(8,128)}) custom-call(s32[1]{0:T(128)} %bitcast.9.core_ref, bf16[32,528,128]{2,1,0:T(8,128)(2,1)} %all-to-all-done.recv_ref), custom_call_target="tpu_custom_call" | custom-call | flops 1 | bytes 1 | tf_op jit(solution)/shard_map/owned_sums/pallas_call | solution.py:238
  141.2 0.1 convert_add_fusion.1
  141.4 0.1 convert_add_fusion
  141.6 2.6 %collective-permute-start.14 = (bf16[512,256]{1,0:T(8,128)(2,1)S(1)}, bf16[512,256]{1,0:T(8,128)(2,1)S(1)}, u32[]{:S(2)}, u32[]{:S(2)}) collective-permute-start(bf16[512,256]{1,0:T(8,128)(2,1)S(1)} %get-tuple-element.130), channel_id=1, source_target_pairs={{0,32},{4,36},{8,40},{12,44},{16,48},{20,52},{24,56},{28,60},{32,0... | collective-permute-start | bytes 786440 | tf_op jit(solution)/shard_map/ppermute | solution.py:582
  144.2 4.6 %collective-permute-start.13 = (bf16[512,256]{1,0:T(8,128)(2,1)S(1)}, bf16[512,256]{1,0:T(8,128)(2,1)S(1)}, u32[]{:S(2)}, u32[]{:S(2)}) collective-permute-start(bf16[512,256]{1,0:T(8,128)(2,1)S(1)} %get-tuple-element.131), channel_id=1, source_target_pairs={{0,8},{4,12},{8,0},{12,4},{16,24},{20,28},{24,16},{28,20},{32,40},... | collective-permute-start | bytes 786440 | tf_op jit(solution)/shard_map/ppermute | solution.py:582
  148.8 0.1 add_convert_fusion.2
  148.9 2.8 %collective-permute-start.16 = (bf16[1024,128]{1,0:T(8,128)(2,1)S(1)}, bf16[1024,128]{1,0:T(8,128)(2,1)S(1)}, u32[]{:S(2)}, u32[]{:S(2)}) collective-permute-start(bf16[1024,128]{1,0:T(8,128)(2,1)S(1)} %add_convert_fusion.2), channel_id=1, source_target_pairs={{0,2},{1,3},{2,0},{3,1},{4,6},{5,7},{6,4},{7,5},{8,10},{9,11},{10,... | collective-permute-start | bytes 786440 | tf_op jit(solution)/shard_map/ppermute | solution.py:587
  151.8 3.7 %collective-permute-done.13 = bf16[512,256]{1,0:T(8,128)(2,1)S(1)} collective-permute-done((bf16[512,256]{1,0:T(8,128)(2,1)S(1)}, bf16[512,256]{1,0:T(8,128)(2,1)S(1)}, u32[]{:S(2)}, u32[]{:S(2)}) %collective-permute-start.13) | collective-permute-done | bytes 262176 | tf_op jit(solution)/shard_map/ppermute | solution.py:582
  155.6 2.5 %collective-permute-start.18 = (bf16[1040,128]{1,0:T(8,128)(2,1)S(1)}, bf16[1040,128]{1,0:T(8,128)(2,1)S(1)}, u32[]{:S(2)}, u32[]{:S(2)}) collective-permute-start(bf16[1040,128]{1,0:T(8,128)(2,1)S(1)} %pad.4), channel_id=1, source_target_pairs={{0,4},{4,0},{8,12},{12,8},{16,20},{20,16},{24,28},{28,24},{32,36},... | collective-permute-start | bytes 798728 | tf_op jit(solution)/shard_map/ppermute | solution.py:588
  158.2 0.5 collective-permute-done.16
  158.6 0.1 add_convert_fusion.1
  158.7 0.1 collective-permute-start.17
  158.8 5.3 %collective-permute-done.18 = bf16[1040,128]{1,0:T(8,128)(2,1)S(1)} collective-permute-done((bf16[1040,128]{1,0:T(8,128)(2,1)S(1)}, bf16[1040,128]{1,0:T(8,128)(2,1)S(1)}, u32[]{:S(2)}, u32[]{:S(2)}) %collective-permute-start.18) | collective-permute-done | bytes 266272 | tf_op jit(solution)/shard_map/ppermute | solution.py:588
  164.2 0.1 multiply_bitcast_fusion
  164.2 1.0 copy.13
  165.3 0.3 fusion.2
  165.6 0.6 fusion.5
  166.2 1.3 fusion.1
  (48 shorter events, 0.4 us)
Async XLA Ops:
  0.7 23.3 %copy-start.14 = (s32[1,512,16,1]{1,3,2,0:T(1,128)S(1)}, s32[1,512,16,1]{1,3,2,0:T(1,128)}, u32[]{:S(2)}) copy-start(s32[1,512,16,1]{1,3,2,0:T(1,128)} %param.14) | copy-start | bytes 98308
  12.3 4.9 %collective-permute-start = (bf16[512,1024]{1,0:T(8,128)(2,1)}, bf16[512,1024]{1,0:T(8,128)(2,1)S(1)}, u32[]{:S(2)}, u32[]{:S(2)}) collective-permute-start(bf16[512,1024]{1,0:T(8,128)(2,1)} %get-tuple-element.65), channel_id=1, source_target_pairs={{0,1},{1,0},{2,3},{3,2},{4,5},{5,4},{6,7},{7,6},{8,9},{9,8},{10,11... | collective-permute-start | bytes 3145736 | tf_op jit(solution)/shard_map/ppermute | solution.py:554
  12.4 8.2 %collective-permute-start.1 = (bf16[512,1024]{1,0:T(8,128)(2,1)}, bf16[512,1024]{1,0:T(8,128)(2,1)S(1)}, u32[]{:S(2)}, u32[]{:S(2)}) collective-permute-start(bf16[512,1024]{1,0:T(8,128)(2,1)} %get-tuple-element.67), channel_id=1, source_target_pairs={{0,1},{1,0},{2,3},{3,2},{4,5},{5,4},{6,7},{7,6},{8,9},{9,8},{10,11... | collective-permute-start | bytes 3145736 | tf_op jit(solution)/shard_map/ppermute | solution.py:555
  12.9 27.7 %collective-permute-start.2 = (bf16[512,1024]{1,0:T(8,128)(2,1)}, bf16[512,1024]{1,0:T(8,128)(2,1)S(1)}, u32[]{:S(2)}, u32[]{:S(2)}) collective-permute-start(bf16[512,1024]{1,0:T(8,128)(2,1)} %get-tuple-element.71), channel_id=1, source_target_pairs={{0,32},{4,36},{8,40},{12,44},{16,48},{20,52},{24,56},{28,60},{32,6... | collective-permute-start | bytes 3145736 | tf_op jit(solution)/shard_map/ppermute | solution.py:557
  14.9 25.7 %collective-permute-start.3 = (bf16[512,1024]{1,0:T(8,128)(2,1)}, bf16[512,1024]{1,0:T(8,128)(2,1)S(1)}, u32[]{:S(2)}, u32[]{:S(2)}) collective-permute-start(bf16[512,1024]{1,0:T(8,128)(2,1)} %get-tuple-element.72), channel_id=1, source_target_pairs={{0,96},{4,100},{8,104},{12,108},{16,112},{20,116},{24,120},{28,124... | collective-permute-start | bytes 3145736 | tf_op jit(solution)/shard_map/ppermute | solution.py:557
  17.0 25.1 %collective-permute-start.4 = (bf16[512,1024]{1,0:T(8,128)(2,1)}, bf16[512,1024]{1,0:T(8,128)(2,1)S(1)}, u32[]{:S(2)}, u32[]{:S(2)}) collective-permute-start(bf16[512,1024]{1,0:T(8,128)(2,1)} %get-tuple-element.73), channel_id=1, source_target_pairs={{0,8},{4,12},{8,16},{12,20},{16,24},{20,28},{24,0},{28,4},{32,40},... | collective-permute-start | bytes 3145736 | tf_op jit(solution)/shard_map/ppermute | solution.py:557
  17.2 26.1 %collective-permute-start.5 = (bf16[512,1024]{1,0:T(8,128)(2,1)}, bf16[512,1024]{1,0:T(8,128)(2,1)S(1)}, u32[]{:S(2)}, u32[]{:S(2)}) collective-permute-start(bf16[512,1024]{1,0:T(8,128)(2,1)} %get-tuple-element.74), channel_id=1, source_target_pairs={{0,24},{4,28},{8,0},{12,4},{16,8},{20,12},{24,16},{28,20},{32,56},... | collective-permute-start | bytes 3145736 | tf_op jit(solution)/shard_map/ppermute | solution.py:557
  20.7 16.3 %copy-start.5 = (bf16[512,1024]{1,0:T(8,128)(2,1)}, bf16[512,1024]{1,0:T(8,128)(2,1)S(1)}, u32[]{:S(2)}) copy-start(bf16[512,1024]{1,0:T(8,128)(2,1)S(1)} %collective-permute-done.1.mate_hbm) | copy-start | bytes 3145732
  20.7 26.8 %collective-permute-start.6 = (bf16[512,1024]{1,0:T(8,128)(2,1)S(1)}, bf16[512,1024]{1,0:T(8,128)(2,1)S(1)}, u32[]{:S(2)}, u32[]{:S(2)}) collective-permute-start(bf16[512,1024]{1,0:T(8,128)(2,1)S(1)} %add_convert_fusion), channel_id=1, source_target_pairs={{0,2},{1,3},{2,0},{3,1},{4,6},{5,7},{6,4},{7,5},{8,10},{9,11},{10,... | collective-permute-start | bytes 3145736 | tf_op jit(solution)/shard_map/ppermute | solution.py:560
  40.6 2.7 %copy-start = (bf16[512,1024]{1,0:T(8,128)(2,1)}, bf16[512,1024]{1,0:T(8,128)(2,1)S(1)}, u32[]{:S(2)}) copy-start(bf16[512,1024]{1,0:T(8,128)(2,1)S(1)} %collective-permute-done.2.refs_0_) | copy-start | bytes 3145732
  40.6 2.7 %copy-start.1 = (bf16[512,1024]{1,0:T(8,128)(2,1)}, bf16[512,1024]{1,0:T(8,128)(2,1)S(1)}, u32[]{:S(2)}) copy-start(bf16[512,1024]{1,0:T(8,128)(2,1)S(1)} %collective-permute-done.3.refs_1_) | copy-start | bytes 3145732
  42.1 1.2 copy-start.2
  43.3 1.0 copy-start.3
  47.5 6.6 %copy-start.6 = (bf16[512,1024]{1,0:T(8,128)(2,1)}, bf16[512,1024]{1,0:T(8,128)(2,1)S(1)}, u32[]{:S(2)}) copy-start(bf16[512,1024]{1,0:T(8,128)(2,1)S(1)} %collective-permute-done.6.far_hbm) | copy-start | bytes 3145732
  47.5 19.0 %collective-permute-start.10 = (bf16[256,1024]{1,0:T(8,128)(2,1)}, bf16[256,1024]{1,0:T(8,128)(2,1)S(1)}, u32[]{:S(2)}, u32[]{:S(2)}) collective-permute-start(bf16[256,1024]{1,0:T(8,128)(2,1)} %get-tuple-element.98), channel_id=1, source_target_pairs={{0,24},{4,28},{8,0},{12,4},{16,8},{20,12},{24,16},{28,20},{32,56},... | collective-permute-start | bytes 1572872 | tf_op jit(solution)/shard_map/ppermute | solution.py:567
  48.1 18.5 %collective-permute-start.7 = (bf16[256,1024]{1,0:T(8,128)(2,1)}, bf16[256,1024]{1,0:T(8,128)(2,1)S(1)}, u32[]{:S(2)}, u32[]{:S(2)}) collective-permute-start(bf16[256,1024]{1,0:T(8,128)(2,1)} %get-tuple-element.95), channel_id=1, source_target_pairs={{0,32},{4,36},{8,40},{12,44},{16,48},{20,52},{24,56},{28,60},{32,6... | collective-permute-start | bytes 1572872 | tf_op jit(solution)/shard_map/ppermute | solution.py:567
  48.2 18.4 %collective-permute-start.8 = (bf16[256,1024]{1,0:T(8,128)(2,1)}, bf16[256,1024]{1,0:T(8,128)(2,1)S(1)}, u32[]{:S(2)}, u32[]{:S(2)}) collective-permute-start(bf16[256,1024]{1,0:T(8,128)(2,1)} %get-tuple-element.96), channel_id=1, source_target_pairs={{0,96},{4,100},{8,104},{12,108},{16,112},{20,116},{24,120},{28,124... | collective-permute-start | bytes 1572872 | tf_op jit(solution)/shard_map/ppermute | solution.py:567
  51.4 15.3 %collective-permute-start.9 = (bf16[256,1024]{1,0:T(8,128)(2,1)}, bf16[256,1024]{1,0:T(8,128)(2,1)S(1)}, u32[]{:S(2)}, u32[]{:S(2)}) collective-permute-start(bf16[256,1024]{1,0:T(8,128)(2,1)} %get-tuple-element.97), channel_id=1, source_target_pairs={{0,8},{4,12},{8,16},{12,20},{16,24},{20,28},{24,0},{28,4},{32,40},... | collective-permute-start | bytes 1572872 | tf_op jit(solution)/shard_map/ppermute | solution.py:567
  66.6 0.8 copy-start.9
  66.6 0.9 copy-start.10
  66.6 1.1 copy-start.11
  66.6 1.3 copy-start.12
  67.9 57.5 %all-to-all-start = ((bf16[32,528,128]{2,1,0:T(8,128)(2,1)}), bf16[32,528,128]{2,1,0:T(8,128)(2,1)}, u32[]{:S(2)}, u32[]{:S(2)}) async-start(bf16[32,528,128]{2,1,0:T(8,128)(2,1)} %place_entries.1), calls=%async_computation | async-start | bytes 8650752 | tf_op jit(solution)/shard_map/all_to_all | solution.py:571
  80.8 60.4 %copy-start.8 = (bf16[512,512]{1,0:T(8,128)(2,1)S(1)}, bf16[512,512]{1,0:T(8,128)(2,1)}, u32[]{:S(2)}) copy-start(bf16[512,512]{1,0:T(8,128)(2,1)} %get-tuple-element.103) | copy-start | bytes 1572868
  80.8 60.6 %copy-start.7 = (bf16[512,512]{1,0:T(8,128)(2,1)S(1)}, bf16[512,512]{1,0:T(8,128)(2,1)}, u32[]{:S(2)}) copy-start(bf16[512,512]{1,0:T(8,128)(2,1)} %get-tuple-element.112) | copy-start | bytes 1572868
  125.4 15.8 %collective-permute-start.11 = (bf16[512,512]{1,0:T(8,128)(2,1)}, bf16[512,512]{1,0:T(8,128)(2,1)S(1)}, u32[]{:S(2)}, u32[]{:S(2)}) collective-permute-start(bf16[512,512]{1,0:T(8,128)(2,1)} %get-tuple-element.109), channel_id=1, source_target_pairs={{0,16},{4,20},{8,24},{12,28},{16,0},{20,4},{24,8},{28,12},{32,48},... | collective-permute-start | bytes 1572872 | tf_op jit(solution)/shard_map/ppermute | solution.py:575
  129.4 11.9 %collective-permute-start.12 = (bf16[512,512]{1,0:T(8,128)(2,1)}, bf16[512,512]{1,0:T(8,128)(2,1)S(1)}, u32[]{:S(2)}, u32[]{:S(2)}) collective-permute-start(bf16[512,512]{1,0:T(8,128)(2,1)} %get-tuple-element.110), channel_id=1, source_target_pairs={{0,64},{4,68},{8,72},{12,76},{16,80},{20,84},{24,88},{28,92},{32,9... | collective-permute-start | bytes 1572872 | tf_op jit(solution)/shard_map/ppermute | solution.py:575
  141.2 7.6 %copy-start.13 = (bf16[1024,128]{1,0:T(8,128)(2,1)S(1)}, bf16[1024,128]{1,0:T(8,128)(2,1)}, u32[]{:S(2)}) copy-start(bf16[1024,128]{1,0:T(8,128)(2,1)} %get-tuple-element.116) | copy-start | bytes 786436
  141.2 7.6 %collective-permute-start.15 = (bf16[1024,128]{1,0:T(8,128)(2,1)}, bf16[1024,128]{1,0:T(8,128)(2,1)S(1)}, u32[]{:S(2)}, u32[]{:S(2)}) collective-permute-start(bf16[1024,128]{1,0:T(8,128)(2,1)} %get-tuple-element.115), channel_id=1, source_target_pairs={{0,1},{1,0},{2,3},{3,2},{4,5},{5,4},{6,7},{7,6},{8,9},{9,8},{10,11... | collective-permute-start | bytes 786440 | tf_op jit(solution)/shard_map/ppermute | solution.py:577
  141.6 10.2 %collective-permute-start.14 = (bf16[512,256]{1,0:T(8,128)(2,1)S(1)}, bf16[512,256]{1,0:T(8,128)(2,1)S(1)}, u32[]{:S(2)}, u32[]{:S(2)}) collective-permute-start(bf16[512,256]{1,0:T(8,128)(2,1)S(1)} %get-tuple-element.130), channel_id=1, source_target_pairs={{0,32},{4,36},{8,40},{12,44},{16,48},{20,52},{24,56},{28,60},{32,0... | collective-permute-start | bytes 786440 | tf_op jit(solution)/shard_map/ppermute | solution.py:582
  144.2 11.3 %collective-permute-start.13 = (bf16[512,256]{1,0:T(8,128)(2,1)S(1)}, bf16[512,256]{1,0:T(8,128)(2,1)S(1)}, u32[]{:S(2)}, u32[]{:S(2)}) collective-permute-start(bf16[512,256]{1,0:T(8,128)(2,1)S(1)} %get-tuple-element.131), channel_id=1, source_target_pairs={{0,8},{4,12},{8,0},{12,4},{16,24},{20,28},{24,16},{28,20},{32,40},... | collective-permute-start | bytes 786440 | tf_op jit(solution)/shard_map/ppermute | solution.py:582
  148.9 16.7 %copy-start.15 = (f32[2048]{0:T(1024)S(1)}, f32[2048]{0:T(1024)}, u32[]{:S(2)}) copy-start(f32[2048]{0:T(1024)} %param.17) | copy-start | bytes 24580
  148.9 17.3 %copy-start.4 = (f32[2048,128]{1,0:T(8,128)S(1)}, f32[2048,128]{1,0:T(8,128)}, u32[]{:S(2)}) copy-start(f32[2048,128]{1,0:T(8,128)} %param.16) | copy-start | bytes 3145732
  148.9 9.7 %collective-permute-start.16 = (bf16[1024,128]{1,0:T(8,128)(2,1)S(1)}, bf16[1024,128]{1,0:T(8,128)(2,1)S(1)}, u32[]{:S(2)}, u32[]{:S(2)}) collective-permute-start(bf16[1024,128]{1,0:T(8,128)(2,1)S(1)} %add_convert_fusion.2), channel_id=1, source_target_pairs={{0,2},{1,3},{2,0},{3,1},{4,6},{5,7},{6,4},{7,5},{8,10},{9,11},{10,... | collective-permute-start | bytes 786440 | tf_op jit(solution)/shard_map/ppermute | solution.py:587
  155.6 8.5 %collective-permute-start.18 = (bf16[1040,128]{1,0:T(8,128)(2,1)S(1)}, bf16[1040,128]{1,0:T(8,128)(2,1)S(1)}, u32[]{:S(2)}, u32[]{:S(2)}) collective-permute-start(bf16[1040,128]{1,0:T(8,128)(2,1)S(1)} %pad.4), channel_id=1, source_target_pairs={{0,4},{4,0},{8,12},{12,8},{16,20},{20,16},{24,28},{28,24},{32,36},... | collective-permute-start | bytes 798728 | tf_op jit(solution)/shard_map/ppermute | solution.py:588
  158.7 5.4 %collective-permute-start.17 = (bf16[1024,128]{1,0:T(8,128)(2,1)S(1)}, bf16[1024,128]{1,0:T(8,128)(2,1)S(1)}, u32[]{:S(2)}, u32[]{:S(2)}) collective-permute-start(bf16[1024,128]{1,0:T(8,128)(2,1)S(1)} %add_convert_fusion.1), channel_id=1, source_target_pairs={{0,1},{1,0},{2,3},{3,2},{4,5},{5,4},{6,7},{7,6},{8,9},{9,8},{10,11... | collective-permute-start | bytes 786440 | tf_op jit(solution)/shard_map/ppermute | solution.py:592

commit v5 on v4

--- a/solution.py
+++ b/solution.py
@@ -181,12 +181,19 @@
     )(slots, base, mate, far, ids, bias)
 
 
-def sums_kernel(norm_factor, core_ref, recv_ref, keep_ref, send_ref, bias_ref, total, left, right, todo):
+def sums_kernel(
+    norm_factor, core_ref, recv_hbm, keep_ref, send_ref, bias_ref, recv_ref, tails, total, left, right, todo, sems
+):
+    get_tails = pltpu.make_async_copy(recv_hbm.at[:, pl.ds(CAP, TAIL), :], tails, sems.at[0])
+    get_values = pltpu.make_async_copy(recv_hbm.at[:, pl.ds(0, CAP), :], recv_ref, sems.at[1])
+    get_tails.start()
+    get_values.start()
+    get_tails.wait()
     lane_rows = lax.broadcasted_iota(jnp.int32, (LO, E), 0)
 
     n = 0
     for w in range(N_WIDE):
-        ids = recv_ref[w, CAP:, :].astype(F32)
+        ids = tails[w].astype(F32)
         ids = ids[0:4, :] + ids[4:8, :]
         halves = jnp.max(jnp.where(ids[2:3, :] > 0.0, 2.0, jnp.where(ids[0:1, :] > 0.0, 1.0, 0.0)))
         todo[n] = 2 * w
@@ -196,14 +203,15 @@
     for k in range(12):
         todo[n + k] = -1
     total[...] = jnp.zeros_like(total)
-    bias_ref[...] = jnp.sum(recv_ref[:, CAP + 8 : CAP + 16, :].astype(F32), axis=0) * norm_factor
+    bias_ref[...] = jnp.sum(tails[:, 8:, :].astype(F32), axis=0) * norm_factor
+    get_values.wait()
 
     def build(i, buf):
         for p in range(4):
             item = todo[i * 4 + p]
             w = jnp.maximum(item, 0) // 2
             half = jnp.maximum(item, 0) % 2
-            ids = recv_ref[w, CAP : CAP + 16, :].astype(F32)
+            ids = tails[w].astype(F32)
             row = (ids[0:4, :] * 64.0 + ids[4:8, :]).astype(jnp.int32) - 1
             row = jnp.where(half == 0, row[0:2, :], row[2:4, :])
             row = jnp.where(item < 0, -1, row)
@@ -238,13 +246,16 @@
     return pl.pallas_call(
         functools.partial(sums_kernel, norm_factor),
         out_shape=[jax.ShapeDtypeStruct((N_ROWS // 2, E), BF16)] * 2 + [jax.ShapeDtypeStruct((8, E), F32)],
-        in_specs=[pl.BlockSpec(memory_space=pltpu.SMEM), vmem],
+        in_specs=[pl.BlockSpec(memory_space=pltpu.SMEM), pl.BlockSpec(memory_space=pltpu.HBM)],
         out_specs=[vmem] * 3,
         scratch_shapes=[
+            pltpu.VMEM((N_WIDE, CAP, E), BF16),
+            pltpu.VMEM((N_WIDE, TAIL, E), BF16),
             pltpu.VMEM((LO, HI * E), F32),
             pltpu.VMEM((2, LO, 2 * CAP), BF16),
             pltpu.VMEM((2, 2 * CAP, HI * E), BF16),
             pltpu.SMEM((2 * N_WIDE + 16,), jnp.int32),
+            pltpu.SemaphoreType.DMA((2,)),
         ],
         compiler_params=pltpu.CompilerParams(vmem_limit_bytes=VMEM_BYTES),
         cost_estimate=LIGHT,
@@ -263,8 +274,7 @@
     return pl.multiple_of(a * 1024, 1024)
 
 
-def ring_terms(route, turned, embedded, z, y, d):
-    part = turned[route * 512 : (route + 1) * 512, :]
+def ring_terms(route, part, embedded, z, y, d):
     if route == 0:
         rows = embedded[:, pl.ds(own_chunk((z + d) % 4), 1024)]
         yield slice(0, 1024), jnp.dot(part, rows, preferred_element_type=F32)
@@ -276,8 +286,8 @@
 
 
 def sent_kernel(n_ref, z_ref, y_ref, cot_hbm, embedded_hbm, weight_hbm, *refs):
-    parts_hbm, first_hbm, second_hbm, (scaled_hbm, turned_hbm, bias_ref) = refs[:3], refs[3:7], refs[7:11], refs[11:14]
-    cot, embedded, weight, scaled, turned, parts, first, second, sems, sems_out = refs[14:]
+    parts_hbm, first_hbm, (scaled_hbm, turned_hbm) = refs[:2], refs[2:6], refs[6:8]
+    cot, embedded, weight, scaled, turned, parts, first, sems, sems_out = refs[8:]
     n, z, y = n_ref[0], z_ref[0], y_ref[0]
 
     def columns(q):
@@ -286,53 +296,47 @@
 
     def rows(q):
         at = pl.ds(own_chunk(n ^ q), 1024)
-        return pltpu.make_async_copy(weight_hbm.at[at, :], weight.at[q - 1], sems.at[3 + q])
-
-    outs = [(parts.at[q], parts_hbm[q]) for q in range(3)]
-    outs += [(first.at[q], first_hbm[q]) for q in range(4)] + [(second.at[q], second_hbm[q]) for q in range(4)]
+        return pltpu.make_async_copy(weight_hbm.at[at, :], weight.at[q - 2], sems.at[2 + q])
+
+    outs = [(parts.at[q], parts_hbm[q]) for q in range(2)]
+    outs += [(first.at[q], first_hbm[q]) for q in range(4)]
     outs += [(scaled, scaled_hbm), (turned, turned_hbm)]
     outs = [pltpu.make_async_copy(src, dst, sems_out.at[k]) for k, (src, dst) in enumerate(outs)]
 
-    get_cot = pltpu.make_async_copy(cot_hbm, cot, sems.at[7])
+    get_cot = pltpu.make_async_copy(cot_hbm, cot, sems.at[6])
     get_cot.start()
     columns(0).start()
     rows(3).start()
     get_cot.wait()
     columns(0).wait()
-    for q in (1, 2):
-        rows(q).start()
+    rows(2).start()
     for q in (1, 2, 3):
         columns(q).start()
     grads = (cot[...].astype(F32) * embedded[:, pl.ds(own_chunk(n), 1024)].astype(F32)).astype(BF16)
     scaled[...] = grads
-    outs[11].start()
+    outs[6].start()
     rows(3).wait()
-    parts[0] = lax.dot_general(scaled[...], weight[2], NT, preferred_element_type=F32).astype(BF16)
+    parts[0] = lax.dot_general(scaled[...], weight[1], NT, preferred_element_type=F32).astype(BF16)
     turned[...] = jnp.transpose(grads, (1, 0))
-    sums = jnp.sum(grads.astype(F32), axis=0, keepdims=True)
-    bias_ref[...] = jnp.concatenate([sums[:, k * E : (k + 1) * E] for k in range(8)], axis=0)
     outs[0].start()
-    outs[12].start()
-    for k, q in ((1, 1), (2, 2)):
-        rows(q).wait()
-        part = lax.dot_general(scaled[...], weight[q - 1], NT, preferred_element_type=F32)
-        parts[k] = part.astype(BF16)
-        outs[k].start()
+    outs[7].start()
+    rows(2).wait()
+    parts[1] = lax.dot_general(scaled[...], weight[0], NT, preferred_element_type=F32).astype(BF16)
+    outs[1].start()
     for q in (1, 2, 3):
         columns(q).wait()
     for route in range(2):
-        for at, term in ring_terms(route, turned, embedded, z, y, 2):
+        low = route * 512
+        for at, term in ring_terms(route, turned[low : low + 512, :], embedded, z, y, 2):
             term = term.astype(BF16)
             for way in range(2):
                 first[2 * route + way, :256, at] = term[way * 256 : (way + 1) * 256, :]
         for way in range(2):
             q = 2 * route + way
-            for at, term in ring_terms(route, turned, embedded, z, y, 3 if way else 1):
-                term = term.astype(BF16)
-                first[q, 256:, at] = term[(1 - way) * 256 : (2 - way) * 256, :]
-                second[q, :, at] = term[way * 256 : (way + 1) * 256, :]
-            outs[3 + q].start()
-            outs[7 + q].start()
+            other = turned[low + (1 - way) * 256 : low + (2 - way) * 256, :]
+            for at, term in ring_terms(route, other, embedded, z, y, 3 if way else 1):
+                first[q, 256:, at] = term.astype(BF16)
+            outs[2 + q].start()
     for copy in outs:
         copy.wait()
 
@@ -342,30 +346,28 @@
     smem = pl.BlockSpec(memory_space=pltpu.SMEM)
     samples, width = cotangent.shape
     shape = jax.ShapeDtypeStruct
-    full, half = shape((samples, width), BF16), shape((256, 1024), BF16)
+    full = shape((samples, width), BF16)
     results = pl.pallas_call(
         sent_kernel,
-        out_shape=[full] * 3 + [shape((512, 1024), BF16)] * 4 + [half] * 4
-        + [full, shape((width, samples), BF16), shape((8, E), F32)],
+        out_shape=[full] * 2 + [shape((512, 1024), BF16)] * 4 + [full, shape((width, samples), BF16)],
         in_specs=[smem] * 3 + [hbm] * 3,
-        out_specs=[hbm] * 13 + [pl.BlockSpec(memory_space=pltpu.VMEM)],
+        out_specs=[hbm] * 8,
         scratch_shapes=[
             pltpu.VMEM(cotangent.shape, BF16),
             pltpu.VMEM(embedded.shape, BF16),
-            pltpu.VMEM((3, 1024, 1024), BF16),
+            pltpu.VMEM((2, 1024, 1024), BF16),
             pltpu.VMEM((samples, width), BF16),
             pltpu.VMEM((width, samples), BF16),
-            pltpu.VMEM((3, samples, width), BF16),
+            pltpu.VMEM((2, samples, width), BF16),
             pltpu.VMEM((4, 512, 1024), BF16),
-            pltpu.VMEM((4, 256, 1024), BF16),
+            pltpu.SemaphoreType.DMA((7,)),
             pltpu.SemaphoreType.DMA((8,)),
-            pltpu.SemaphoreType.DMA((13,)),
         ],
         compiler_params=pltpu.CompilerParams(vmem_limit_bytes=VMEM_BYTES),
         cost_estimate=LIGHT,
         name="sent_terms",
     )(n, z, y, cotangent, embedded, weight)
-    return results[:3], results[3:7], results[7:11], *results[11:]
+    return results[:2], results[2:6], *results[6:]
 
 
 def pass_kernel(*refs):
@@ -407,10 +409,11 @@
 
 
 def kept_kernel(
-    n_ref, cot_hbm, embedded_hbm, weight_hbm, bias_ref, scaled_hbm, owner_ref, row_ref, bag_ref, base_ref, slots_ref, ids_ref, *scratch
+    n_ref, z_ref, y_ref, cot_hbm, embedded_hbm, weight_hbm, bias_ref, scaled_hbm, turned_hbm, owner_ref, row_ref, bag_ref, *refs
 ):
-    cot, embedded, weight, scaled, cross, onehots, sems = scratch
-    n = n_ref[0]
+    base_ref, slots_ref, ids_ref, bias_sum_ref, mate_hbm, second_hbm = *refs[:5], refs[5:9]
+    cot, embedded, weight, scaled, turned, cross, onehots, mate, second, sems, sems_out = refs[9:]
+    n, z, y = n_ref[0], z_ref[0], y_ref[0]
 
     def columns(q):
         at = pl.ds(own_chunk(n ^ q), 1024)
@@ -422,6 +425,9 @@
 
     get_scaled = pltpu.make_async_copy(scaled_hbm, scaled, sems.at[8])
     get_cot = pltpu.make_async_copy(cot_hbm, cot, sems.at[9])
+    get_turned = pltpu.make_async_copy(turned_hbm, turned, sems.at[10])
+    outs = [(mate, mate_hbm)] + [(second.at[q], second_hbm[q]) for q in range(4)]
+    outs = [pltpu.make_async_copy(src, dst, sems_out.at[k]) for k, (src, dst) in enumerate(outs)]
     rows(0).start()
     columns(0).start()
     get_scaled.start()
@@ -429,51 +435,76 @@
         rows(q).start()
         columns(q).start()
     get_cot.start()
+    get_turned.start()
     find_slots(n, owner_ref, row_ref, bag_ref, slots_ref, ids_ref, onehots)
+    get_scaled.wait()
+    rows(1).wait()
+    mate[...] = lax.dot_general(scaled[...], weight[1], NT, preferred_element_type=F32).astype(BF16)
+    outs[0].start()
+    for q in range(4):
+        columns(q).wait()
+    get_turned.wait()
+    for route in range(2):
+        for way in range(2):
+            q = 2 * route + way
+            low = route * 512 + way * 256
+            for at, term in ring_terms(route, turned[low : low + 256, :], embedded, z, y, 3 if way else 1):
+                second[q, :, at] = term.astype(BF16)
+            outs[1 + q].start()
+    sums = jnp.sum(scaled[...].astype(F32), axis=0, keepdims=True)
+    bias_sum_ref[...] = jnp.concatenate([sums[:, k * E : (k + 1) * E] for k in range(8)], axis=0)
     rows(0).wait()
-    columns(0).wait()
     cross[...] = jnp.dot(embedded[:, pl.ds(own_chunk(n), 1024)], weight[0], preferred_element_type=F32)
-    get_scaled.wait()
     base_ref[...] = lax.dot_general(scaled[...], weight[0], NT, preferred_element_type=F32)
     for q in (1, 2):
-        rows(q).wait()
-        columns(q).wait()
+        if q > 1:
+            rows(q).wait()
         cross[...] += jnp.dot(embedded[:, pl.ds(own_chunk(n ^ q), 1024)], weight[q], preferred_element_type=F32)
     rows(3).wait()
-    columns(3).wait()
     get_cot.wait()
     grad = cot[...].astype(F32)
     last = jnp.dot(embedded[:, pl.ds(own_chunk(n ^ 3), 1024)], weight[3], preferred_element_type=F32)
     base_ref[...] += grad + grad * (cross[...] + last + bias_ref[...])
-
-
-def kept_terms(n, cotangent, embedded, weight, bias, scaled, owner, row, bag):
+    for copy in outs:
+        copy.wait()
+
+
+def kept_terms(n, z, y, cotangent, embedded, weight, bias, scaled, turned, owner, row, bag):
     hbm = pl.BlockSpec(memory_space=pltpu.HBM)
     vmem = pl.BlockSpec(memory_space=pltpu.VMEM)
     samples, width = cotangent.shape
     depth = owner.shape[0]
-    return pl.pallas_call(
+    shape = jax.ShapeDtypeStruct
+    results = pl.pallas_call(
         kept_kernel,
         out_shape=[
-            jax.ShapeDtypeStruct((samples, width), F32),
-            jax.ShapeDtypeStruct((depth * samples // E, E), jnp.int32),
-            jax.ShapeDtypeStruct((2 * N_WIDE, CAP), F32),
-        ],
-        in_specs=[pl.BlockSpec(memory_space=pltpu.SMEM)] + [hbm] * 3 + [vmem, hbm] + [vmem] * 3,
-        out_specs=[vmem] * 3,
+            shape((samples, width), F32),
+            shape((depth * samples // E, E), jnp.int32),
+            shape((2 * N_WIDE, CAP), F32),
+            shape((8, E), F32),
+            shape((samples, width), BF16),
+        ]
+        + [shape((256, 1024), BF16)] * 4,
+        in_specs=[pl.BlockSpec(memory_space=pltpu.SMEM)] * 3 + [hbm] * 3 + [vmem, hbm, hbm] + [vmem] * 3,
+        out_specs=[vmem] * 4 + [hbm] * 5,
         scratch_shapes=[
             pltpu.VMEM(cotangent.shape, BF16),
             pltpu.VMEM(embedded.shape, BF16),
             pltpu.VMEM((4, 1024, 1024), BF16),
             pltpu.VMEM((samples, width), BF16),
+            pltpu.VMEM((width, samples), BF16),
             pltpu.VMEM((samples, width), F32),
             pltpu.VMEM((N_WIDE * depth, samples), BF16),
-            pltpu.SemaphoreType.DMA((10,)),
+            pltpu.VMEM((samples, width), BF16),
+            pltpu.VMEM((4, 256, 1024), BF16),
+            pltpu.SemaphoreType.DMA((11,)),
+            pltpu.SemaphoreType.DMA((5,)),
         ],
         compiler_params=pltpu.CompilerParams(vmem_limit_bytes=VMEM_BYTES),
         cost_estimate=LIGHT,
         name="kept_terms",
-    )(n, cotangent, embedded, weight, bias.reshape(1, -1), scaled, owner, row, bag)
+    )(n, z, y, cotangent, embedded, weight, bias.reshape(1, -1), scaled, turned, owner, row, bag)
+    return *results[:5], results[5:]
 
 
 def own_kernel(z_ref, y_ref, embedded_hbm, turned_hbm, *refs):
@@ -488,7 +519,7 @@
     for load in loads:
         load.wait()
     for route, place in ((0, y), (1, z)):
-        term = jnp.concatenate([term for _, term in ring_terms(route, turned, embedded, z, y, 0)], axis=1)
+        term = jnp.concatenate([term for _, term in ring_terms(route, turned[route * 512 : (route + 1) * 512, :], embedded, z, y, 0)], axis=1)
         up, down = 2 * route, 2 * route + 1
         total = jnp.concatenate(
             [
@@ -550,18 +581,20 @@
 
     at = (panel.reshape(1), z.reshape(1), y.reshape(1))
 
-    parts, first, second, scaled, turned, bias_part = sent_terms(*at, cotangent, embedded, cross_weight)
+    parts, first, scaled, turned = sent_terms(*at, cotangent, embedded, cross_weight)
     from_mate_far = lax.ppermute(parts[0], "narrow", CORE)
-    from_mate = lax.ppermute(parts[1], "narrow", CORE)
     ways = [z_perm(1), z_perm(3), y_perm(1), y_perm(3)]
     first = [lax.ppermute(first[q], "wide", ways[q]) for q in range(4)]
-    chip_far = (parts[2].astype(F32) + from_mate_far.astype(F32)).astype(BF16)
-    chip_far, scaled, from_mate = lax.optimization_barrier((chip_far, scaled, from_mate))
+    chip_far = (parts[1].astype(F32) + from_mate_far.astype(F32)).astype(BF16)
+    chip_far, scaled, turned = lax.optimization_barrier((chip_far, scaled, turned))
     far = lax.ppermute(chip_far, "narrow", X_HI)
 
     entries = (row_owner.reshape(row_owner.shape[1:3]).T, row_id.reshape(row_id.shape[1:]).T, bag_size.T)
-    base, slots, ids = kept_terms(at[0], cotangent, embedded, cross_weight, cross_bias, scaled, *entries)
-    slots, ids, *first = lax.optimization_barrier((slots, ids, *first))
+    base, slots, ids, bias_part, part, second = kept_terms(
+        *at, cotangent, embedded, cross_weight, cross_bias, scaled, turned, *entries
+    )
+    slots, ids, part, *first = lax.optimization_barrier((slots, ids, part, *first))
+    from_mate = lax.ppermute(part, "narrow", CORE)
     second = passed_on(first, second)
     slots, far, *second = lax.optimization_barrier((slots, far, *second))
     second = [lax.ppermute(second[q], "wide", ways[q]) for q in range(4)]

time: 170 us -> 167 us (0.982)
  starting transfers between devices: 40.9 us -> 38.7 us
    ppermute x1, starting transfers between devices: 4.63 us -> 0.01 us  [body(): lax.ppermute(quarters[0][1], 'wide', y_flip(1))]
    ppermute x1, waiting for transfers between devices: 0.01 us -> 4.01 us  [body(): lax.ppermute(quarters[1][1], 'wide', z_flip(1))]
    ppermute x1, starting transfers between devices: 2.61 us -> 5.17 us  [body(): lax.ppermute(quarters[1][1], 'wide', z_flip(1))]
    ppermute x4, waiting for transfers between devices: 6.31 us -> 3.83 us  [body(): first = [lax.ppermute(first[q], 'wide', ways[q]) for q in range(4)]]
    ppermute x1, waiting for transfers between devices: 3.68 us -> 1.39 us  [body(): lax.ppermute(quarters[0][1], 'wide', y_flip(1))]
  transfers between devices with their start and end apart: 20 -> 20, of which waited for: 7 -> 8; matrix products, arithmetic and copies ran while one was open for 2% -> 2% of each run, Pallas kernels for 27% -> 29%
where the time goes in v5:
time: 167 us; the launch traced here: 165 us
  waiting for transfers between devices  59.2 us (35%)
  Pallas kernels  56.1 us (34%)
  starting transfers between devices  38.7 us (23%)
  local copies, waits for them, and re-layouts  4.93 us (3%)
  other arithmetic  4.58 us (3%)
    all_to_all x1, waiting for transfers between devices, body(): lax.all_to_all(payload, 'wide', split_axis=0, concat_axis=0, tiled=True)  43.8 us
    pallas_call x1, Pallas kernels, kept_terms(): pl.pallas_call(kept_kernel, out_shape=[shape((samples, width), F32), shap...  15.2 us
    pallas_call x1, Pallas kernels, place_entries(): pl.pallas_call(place_kernel, out_shape=jax.ShapeDtypeStruct((N_WIDE, BLOC...  12.5 us
    pallas_call x1, Pallas kernels, owned_sums(): pl.pallas_call(functools.partial(sums_kernel, norm_factor), out_shape=[ja...  10.3 us
    pallas_call x1, Pallas kernels, sent_terms(): pl.pallas_call(sent_kernel, out_shape=[full] * 2 + [shape((512, 1024), BF...  8.51 us
    ppermute x4, starting transfers between devices, body(): second = [lax.ppermute(second[q], 'wide', ways[q]) for q in range(4)]  6.54 us
    pallas_call x1, Pallas kernels, own_terms(): pl.pallas_call(own_kernel, out_shape=[jax.ShapeDtypeStruct((512, 512), BF...  6.32 us
    ppermute x4, starting transfers between devices, body(): first = [lax.ppermute(first[q], 'wide', ways[q]) for q in range(4)]  6.21 us
  transfers between devices with their start and end apart: 20, of which 8 were waited for; matrix products, arithmetic and copies ran while one was open for 2% of the time, Pallas kernels for 29%

profile of v5, /device:TPU:24, one launch (start us, length us, event | category | flops | bytes accessed | tf_op | source)
XLA Modules:
  0.0 164.5 jit_solution(18137687599083054757)
XLA Ops:
  0.7 8.5 %sent_terms.1 = (bf16[512,1024]{1,0:T(8,128)(2,1)}, bf16[512,1024]{1,0:T(8,128)(2,1)}, bf16[512,1024]{1,0:T(8,128)(2,1)}, bf16[512,1024]{1,0:T(8,128)(2,1)}, bf1...) custom-call(s32[1]{0:T(128)} %bitcast.2.n_ref, ...), custom_call_target="tpu_custom_call" | custom-call | flops 1 | bytes 1 | tf_op jit(solution)/shard_map/sent_terms/pallas_call | solution.py:350
  9.2 0.1 collective-permute-start
  9.3 2.0 %collective-permute-start.1 = (bf16[512,1024]{1,0:T(8,128)(2,1)}, bf16[512,1024]{1,0:T(8,128)(2,1)S(1)}, u32[]{:S(2)}, u32[]{:S(2)}) collective-permute-start(bf16[512,1024]{1,0:T(8,128)(2,1)} %get-tuple-element.73), channel_id=1, source_target_pairs={{0,32},{4,36},{8,40},{12,44},{16,48},{20,52},{24,56},{28,60},{32,6... | collective-permute-start | bytes 3145736 | tf_op jit(solution)/shard_map/ppermute | solution.py:587
  11.3 2.2 %collective-permute-start.2 = (bf16[512,1024]{1,0:T(8,128)(2,1)}, bf16[512,1024]{1,0:T(8,128)(2,1)S(1)}, u32[]{:S(2)}, u32[]{:S(2)}) collective-permute-start(bf16[512,1024]{1,0:T(8,128)(2,1)} %get-tuple-element.74), channel_id=1, source_target_pairs={{0,96},{4,100},{8,104},{12,108},{16,112},{20,116},{24,120},{28,124... | collective-permute-start | bytes 3145736 | tf_op jit(solution)/shard_map/ppermute | solution.py:587
  13.5 0.2 collective-permute-start.3
  13.7 1.8 %collective-permute-start.4 = (bf16[512,1024]{1,0:T(8,128)(2,1)}, bf16[512,1024]{1,0:T(8,128)(2,1)S(1)}, u32[]{:S(2)}, u32[]{:S(2)}) collective-permute-start(bf16[512,1024]{1,0:T(8,128)(2,1)} %get-tuple-element.76), channel_id=1, source_target_pairs={{0,24},{4,28},{8,0},{12,4},{16,8},{20,12},{24,16},{28,20},{32,56},... | collective-permute-start | bytes 3145736 | tf_op jit(solution)/shard_map/ppermute | solution.py:587
  15.5 1.6 add_convert_fusion
  17.1 3.3 %collective-permute-start.5 = (bf16[512,1024]{1,0:T(8,128)(2,1)S(1)}, bf16[512,1024]{1,0:T(8,128)(2,1)S(1)}, u32[]{:S(2)}, u32[]{:S(2)}) collective-permute-start(bf16[512,1024]{1,0:T(8,128)(2,1)S(1)} %add_convert_fusion), channel_id=1, source_target_pairs={{0,2},{1,3},{2,0},{3,1},{4,6},{5,7},{6,4},{7,5},{8,10},{9,11},{10,... | collective-permute-start | bytes 3145736 | tf_op jit(solution)/shard_map/ppermute | solution.py:590
  20.4 0.6 copy.16
  21.0 15.2 %kept_terms.1 = (f32[512,1024]{1,0:T(8,128)}, s32[64,128]{1,0:T(8,128)}, f32[64,512]{1,0:T(8,128)}, f32[8,128]{1,0:T(8,128)}, bf16[512,1024]{1,0:T(8,128)(2,1)},...) custom-call(s32[1]{0:T(128)} %bitcast.2.n_ref, ...), custom_call_target="tpu_custom_call" | custom-call | flops 1 | bytes 1 | tf_op jit(solution)/shard_map/kept_terms/pallas_call | solution.py:478
  36.2 1.2 collective-permute-done.1.refs_0_
  37.4 1.5 collective-permute-done.3.refs_2_
  38.8 1.2 collective-permute-done.4.refs_3_
  40.1 0.9 copy-done.3
  41.0 3.2 %passed_on.1 = (bf16[256,1024]{1,0:T(8,128)(2,1)}, bf16[256,1024]{1,0:T(8,128)(2,1)}, bf16[256,1024]{1,0:T(8,128)(2,1)}, bf16[256,1024]{1,0:T(8,128)(2,1)}) custom-call(bf16[512,1024]{1,0:T(8,128)(2,1)} %copy-done, bf16[512,1024]{1,0:T(8,128)(2,1)} %copy-done.1, bf16[512,1024]{1,0:T(8,128)(2,1)} %copy-done.2, bf16[512,1024]{1,0:T(8,128)(2,1)} %copy-done.3, ...), custom_call_target="tpu_custom_call" | custom-call | flops 1 | bytes 1 | tf_op jit(solution)/shard_map/passed_on/pallas_call | solution.py:393
  44.3 0.6 collective-permute-start.10
  44.9 3.2 %collective-permute-start.8 = (bf16[256,1024]{1,0:T(8,128)(2,1)}, bf16[256,1024]{1,0:T(8,128)(2,1)S(1)}, u32[]{:S(2)}, u32[]{:S(2)}) collective-permute-start(bf16[256,1024]{1,0:T(8,128)(2,1)} %get-tuple-element.98), channel_id=1, source_target_pairs={{0,96},{4,100},{8,104},{12,108},{16,112},{20,116},{24,120},{28,124... | collective-permute-start | bytes 1572872 | tf_op jit(solution)/shard_map/ppermute | solution.py:600
  48.1 2.7 %collective-permute-start.9 = (bf16[256,1024]{1,0:T(8,128)(2,1)}, bf16[256,1024]{1,0:T(8,128)(2,1)S(1)}, u32[]{:S(2)}, u32[]{:S(2)}) collective-permute-start(bf16[256,1024]{1,0:T(8,128)(2,1)} %get-tuple-element.99), channel_id=1, source_target_pairs={{0,8},{4,12},{8,16},{12,20},{16,24},{20,28},{24,0},{28,4},{32,40},... | collective-permute-start | bytes 1572872 | tf_op jit(solution)/shard_map/ppermute | solution.py:600
  50.8 1.0 copy-done.6
  51.8 12.5 %place_entries.1 = bf16[32,528,128]{2,1,0:T(8,128)(2,1)} custom-call(s32[8192]{0:T(1024)} %bitcast.21, f32[512,1024]{1,0:T(8,128)} %get-tuple-element.92.base_hbm, bf16[512,1024]{1,0:T(8,128)(2,1)} %copy-done.6, bf16[512,1024]{1,0:T(8,128)(2,1)} %copy-done.5, f32[64,512]{1,0:T(8,128)} %get-tuple-element.95.ids_ref, f32[8,128]{1,0:T(8,128)} %get-tuple-element.96.bias_ref), custom_call_target="tpu_custom_call" | custom-call | flops 1 | bytes 1 | tf_op jit(solution)/shard_map/place_entries/pallas_call | solution.py:164
  64.4 0.7 copy-done.9
  65.2 0.2 copy-done.10
  65.3 0.2 copy-done.11
  65.5 0.1 copy-done.12
  65.7 5.7 %all-to-all-start = ((bf16[32,528,128]{2,1,0:T(8,128)(2,1)}), bf16[32,528,128]{2,1,0:T(8,128)(2,1)}, u32[]{:S(2)}, u32[]{:S(2)}) async-start(bf16[32,528,128]{2,1,0:T(8,128)(2,1)} %place_entries.1), calls=%async_computation | async-start | bytes 8650752 | tf_op jit(solution)/shard_map/all_to_all | solution.py:604
  71.4 6.3 %own_terms.1 = (bf16[512,512]{1,0:T(8,128)(2,1)}, bf16[512,512]{1,0:T(8,128)(2,1)}, bf16[512,512]{1,0:T(8,128)(2,1)}, bf16[512,512]{1,0:T(8,128)(2,1)}) custom-call(s32[1]{0:T(128)} %bitcast.z_ref, s32[1]{0:T(128)} %bitcast.1.y_ref, bf16[512,4096]{1,0:T(8,128)(2,1)} %embedded_hbm.5, bf16[1024,512]{1,0:T(8,128)(2,1)} %get-tuple-element.68.turned_hbm, ...), custom_call_target="tpu_custom_call" | custom-call | flops 1 | bytes 1 | tf_op jit(solution)/shard_map/own_terms/pallas_call | solution.py:539
  77.7 43.8 %all-to-all-done.recv_hbm = bf16[32,528,128]{2,1,0:T(8,128)(2,1)} async-done(((bf16[32,528,128]{2,1,0:T(8,128)(2,1)}), bf16[32,528,128]{2,1,0:T(8,128)(2,1)}, u32[]{:S(2)}, u32[]{:S(2)}) %all-to-all-start) | async-done | bytes 4325408 | tf_op jit(solution)/shard_map/all_to_all | solution.py:604
  121.5 5.4 %collective-permute-start.11 = (bf16[512,512]{1,0:T(8,128)(2,1)}, bf16[512,512]{1,0:T(8,128)(2,1)S(1)}, u32[]{:S(2)}, u32[]{:S(2)}) collective-permute-start(bf16[512,512]{1,0:T(8,128)(2,1)} %get-tuple-element.111), channel_id=1, source_target_pairs={{0,16},{4,20},{8,24},{12,28},{16,0},{20,4},{24,8},{28,12},{32,48},... | collective-permute-start | bytes 1572872 | tf_op jit(solution)/shard_map/ppermute | solution.py:608
  126.9 1.0 collective-permute-start.12
  127.9 10.3 %owned_sums.1 = (bf16[1024,128]{1,0:T(8,128)(2,1)}, bf16[1024,128]{1,0:T(8,128)(2,1)}, f32[8,128]{1,0:T(8,128)}) custom-call(s32[1]{0:T(128)} %bitcast.9.core_ref, bf16[32,528,128]{2,1,0:T(8,128)(2,1)} %all-to-all-done.recv_hbm), custom_call_target="tpu_custom_call" | custom-call | flops 1 | bytes 1 | tf_op jit(solution)/shard_map/owned_sums/pallas_call | solution.py:246
  138.2 0.1 collective-permute-start.15
  138.4 0.1 convert_add_fusion.1
  138.5 0.1 convert_add_fusion
  138.7 5.2 %collective-permute-start.14 = (bf16[512,256]{1,0:T(8,128)(2,1)S(1)}, bf16[512,256]{1,0:T(8,128)(2,1)S(1)}, u32[]{:S(2)}, u32[]{:S(2)}) collective-permute-start(bf16[512,256]{1,0:T(8,128)(2,1)S(1)} %get-tuple-element.132), channel_id=1, source_target_pairs={{0,32},{4,36},{8,40},{12,44},{16,48},{20,52},{24,56},{28,60},{32,0... | collective-permute-start | bytes 786440 | tf_op jit(solution)/shard_map/ppermute | solution.py:615
  143.9 0.1 add_convert_fusion.2
  144.0 2.8 %collective-permute-start.16 = (bf16[1024,128]{1,0:T(8,128)(2,1)S(1)}, bf16[1024,128]{1,0:T(8,128)(2,1)S(1)}, u32[]{:S(2)}, u32[]{:S(2)}) collective-permute-start(bf16[1024,128]{1,0:T(8,128)(2,1)S(1)} %add_convert_fusion.2), channel_id=1, source_target_pairs={{0,2},{1,3},{2,0},{3,1},{4,6},{5,7},{6,4},{7,5},{8,10},{9,11},{10,... | collective-permute-start | bytes 786440 | tf_op jit(solution)/shard_map/ppermute | solution.py:620
  146.8 4.0 %collective-permute-done.14 = bf16[512,256]{1,0:T(8,128)(2,1)S(1)} collective-permute-done((bf16[512,256]{1,0:T(8,128)(2,1)S(1)}, bf16[512,256]{1,0:T(8,128)(2,1)S(1)}, u32[]{:S(2)}, u32[]{:S(2)}) %collective-permute-start.14) | collective-permute-done | bytes 262176 | tf_op jit(solution)/shard_map/ppermute | solution.py:615
  150.9 1.4 collective-permute-done.13
  152.3 0.1 add_convert_fusion.4
  152.4 2.4 %collective-permute-start.18 = (bf16[1040,128]{1,0:T(8,128)(2,1)S(1)}, bf16[1040,128]{1,0:T(8,128)(2,1)S(1)}, u32[]{:S(2)}, u32[]{:S(2)}) collective-permute-start(bf16[1040,128]{1,0:T(8,128)(2,1)S(1)} %pad.4), channel_id=1, source_target_pairs={{0,4},{4,0},{8,12},{12,8},{16,20},{20,16},{24,28},{28,24},{32,36},... | collective-permute-start | bytes 798728 | tf_op jit(solution)/shard_map/ppermute | solution.py:621
  154.8 0.1 add_convert_fusion.1
  154.9 0.1 collective-permute-start.17
  155.0 6.1 %collective-permute-done.18 = bf16[1040,128]{1,0:T(8,128)(2,1)S(1)} collective-permute-done((bf16[1040,128]{1,0:T(8,128)(2,1)S(1)}, bf16[1040,128]{1,0:T(8,128)(2,1)S(1)}, u32[]{:S(2)}, u32[]{:S(2)}) %collective-permute-start.18) | collective-permute-done | bytes 266272 | tf_op jit(solution)/shard_map/ppermute | solution.py:621
  161.1 0.1 multiply_bitcast_fusion
  161.2 1.0 copy.13
  162.2 0.3 fusion.2
  162.6 0.6 fusion.5
  163.2 1.3 fusion.1
  (48 shorter events, 0.4 us)
Async XLA Ops:
  0.7 19.8 %copy-start.14 = (s32[1,512,16,1]{1,3,2,0:T(1,128)S(1)}, s32[1,512,16,1]{1,3,2,0:T(1,128)}, u32[]{:S(2)}) copy-start(s32[1,512,16,1]{1,3,2,0:T(1,128)} %param.14) | copy-start | bytes 98308
  9.2 6.3 %collective-permute-start = (bf16[512,1024]{1,0:T(8,128)(2,1)}, bf16[512,1024]{1,0:T(8,128)(2,1)S(1)}, u32[]{:S(2)}, u32[]{:S(2)}) collective-permute-start(bf16[512,1024]{1,0:T(8,128)(2,1)} %get-tuple-element.65), channel_id=1, source_target_pairs={{0,1},{1,0},{2,3},{3,2},{4,5},{5,4},{6,7},{7,6},{8,9},{9,8},{10,11... | collective-permute-start | bytes 3145736 | tf_op jit(solution)/shard_map/ppermute | solution.py:585
  9.3 28.1 %collective-permute-start.1 = (bf16[512,1024]{1,0:T(8,128)(2,1)}, bf16[512,1024]{1,0:T(8,128)(2,1)S(1)}, u32[]{:S(2)}, u32[]{:S(2)}) collective-permute-start(bf16[512,1024]{1,0:T(8,128)(2,1)} %get-tuple-element.73), channel_id=1, source_target_pairs={{0,32},{4,36},{8,40},{12,44},{16,48},{20,52},{24,56},{28,60},{32,6... | collective-permute-start | bytes 3145736 | tf_op jit(solution)/shard_map/ppermute | solution.py:587
  11.3 26.1 %collective-permute-start.2 = (bf16[512,1024]{1,0:T(8,128)(2,1)}, bf16[512,1024]{1,0:T(8,128)(2,1)S(1)}, u32[]{:S(2)}, u32[]{:S(2)}) collective-permute-start(bf16[512,1024]{1,0:T(8,128)(2,1)} %get-tuple-element.74), channel_id=1, source_target_pairs={{0,96},{4,100},{8,104},{12,108},{16,112},{20,116},{24,120},{28,124... | collective-permute-start | bytes 3145736 | tf_op jit(solution)/shard_map/ppermute | solution.py:587
  13.5 25.3 %collective-permute-start.3 = (bf16[512,1024]{1,0:T(8,128)(2,1)}, bf16[512,1024]{1,0:T(8,128)(2,1)S(1)}, u32[]{:S(2)}, u32[]{:S(2)}) collective-permute-start(bf16[512,1024]{1,0:T(8,128)(2,1)} %get-tuple-element.75), channel_id=1, source_target_pairs={{0,8},{4,12},{8,16},{12,20},{16,24},{20,28},{24,0},{28,4},{32,40},... | collective-permute-start | bytes 3145736 | tf_op jit(solution)/shard_map/ppermute | solution.py:587
  13.7 26.3 %collective-permute-start.4 = (bf16[512,1024]{1,0:T(8,128)(2,1)}, bf16[512,1024]{1,0:T(8,128)(2,1)S(1)}, u32[]{:S(2)}, u32[]{:S(2)}) collective-permute-start(bf16[512,1024]{1,0:T(8,128)(2,1)} %get-tuple-element.76), channel_id=1, source_target_pairs={{0,24},{4,28},{8,0},{12,4},{16,8},{20,12},{24,16},{28,20},{32,56},... | collective-permute-start | bytes 3145736 | tf_op jit(solution)/shard_map/ppermute | solution.py:587
  17.1 27.1 %collective-permute-start.5 = (bf16[512,1024]{1,0:T(8,128)(2,1)S(1)}, bf16[512,1024]{1,0:T(8,128)(2,1)S(1)}, u32[]{:S(2)}, u32[]{:S(2)}) collective-permute-start(bf16[512,1024]{1,0:T(8,128)(2,1)S(1)} %add_convert_fusion), channel_id=1, source_target_pairs={{0,2},{1,3},{2,0},{3,1},{4,6},{5,7},{6,4},{7,5},{8,10},{9,11},{10,... | collective-permute-start | bytes 3145736 | tf_op jit(solution)/shard_map/ppermute | solution.py:590
  37.4 2.7 %copy-start = (bf16[512,1024]{1,0:T(8,128)(2,1)}, bf16[512,1024]{1,0:T(8,128)(2,1)S(1)}, u32[]{:S(2)}) copy-start(bf16[512,1024]{1,0:T(8,128)(2,1)S(1)} %collective-permute-done.1.refs_0_) | copy-start | bytes 3145732
  37.4 2.7 %copy-start.1 = (bf16[512,1024]{1,0:T(8,128)(2,1)}, bf16[512,1024]{1,0:T(8,128)(2,1)S(1)}, u32[]{:S(2)}) copy-start(bf16[512,1024]{1,0:T(8,128)(2,1)S(1)} %collective-permute-done.2.refs_1_) | copy-start | bytes 3145732
  38.8 1.2 copy-start.2
  40.0 1.0 copy-start.3
  40.0 10.8 %collective-permute-start.6 = (bf16[512,1024]{1,0:T(8,128)(2,1)}, bf16[512,1024]{1,0:T(8,128)(2,1)S(1)}, u32[]{:S(2)}, u32[]{:S(2)}) collective-permute-start(bf16[512,1024]{1,0:T(8,128)(2,1)} %get-tuple-element.93), channel_id=1, source_target_pairs={{0,1},{1,0},{2,3},{3,2},{4,5},{5,4},{6,7},{7,6},{8,9},{9,8},{10,11... | collective-permute-start | bytes 3145736 | tf_op jit(solution)/shard_map/ppermute | solution.py:597
  44.3 6.6 %copy-start.5 = (bf16[512,1024]{1,0:T(8,128)(2,1)}, bf16[512,1024]{1,0:T(8,128)(2,1)S(1)}, u32[]{:S(2)}) copy-start(bf16[512,1024]{1,0:T(8,128)(2,1)S(1)} %collective-permute-done.5.far_hbm) | copy-start | bytes 3145732
  44.3 20.1 %collective-permute-start.10 = (bf16[256,1024]{1,0:T(8,128)(2,1)}, bf16[256,1024]{1,0:T(8,128)(2,1)S(1)}, u32[]{:S(2)}, u32[]{:S(2)}) collective-permute-start(bf16[256,1024]{1,0:T(8,128)(2,1)} %get-tuple-element.100), channel_id=1, source_target_pairs={{0,24},{4,28},{8,0},{12,4},{16,8},{20,12},{24,16},{28,20},{32,56},... | collective-permute-start | bytes 1572872 | tf_op jit(solution)/shard_map/ppermute | solution.py:600
  44.9 19.5 %collective-permute-start.7 = (bf16[256,1024]{1,0:T(8,128)(2,1)}, bf16[256,1024]{1,0:T(8,128)(2,1)S(1)}, u32[]{:S(2)}, u32[]{:S(2)}) collective-permute-start(bf16[256,1024]{1,0:T(8,128)(2,1)} %get-tuple-element.97), channel_id=1, source_target_pairs={{0,32},{4,36},{8,40},{12,44},{16,48},{20,52},{24,56},{28,60},{32,6... | collective-permute-start | bytes 1572872 | tf_op jit(solution)/shard_map/ppermute | solution.py:600
  44.9 19.5 %collective-permute-start.8 = (bf16[256,1024]{1,0:T(8,128)(2,1)}, bf16[256,1024]{1,0:T(8,128)(2,1)S(1)}, u32[]{:S(2)}, u32[]{:S(2)}) collective-permute-start(bf16[256,1024]{1,0:T(8,128)(2,1)} %get-tuple-element.98), channel_id=1, source_target_pairs={{0,96},{4,100},{8,104},{12,108},{16,112},{20,116},{24,120},{28,124... | collective-permute-start | bytes 1572872 | tf_op jit(solution)/shard_map/ppermute | solution.py:600
  48.1 16.3 %collective-permute-start.9 = (bf16[256,1024]{1,0:T(8,128)(2,1)}, bf16[256,1024]{1,0:T(8,128)(2,1)S(1)}, u32[]{:S(2)}, u32[]{:S(2)}) collective-permute-start(bf16[256,1024]{1,0:T(8,128)(2,1)} %get-tuple-element.99), channel_id=1, source_target_pairs={{0,8},{4,12},{8,16},{12,20},{16,24},{20,28},{24,0},{28,4},{32,40},... | collective-permute-start | bytes 1572872 | tf_op jit(solution)/shard_map/ppermute | solution.py:600
  50.8 1.0 copy-start.6
  64.4 0.8 copy-start.9
  64.4 0.9 copy-start.10
  64.4 1.1 copy-start.11
  64.4 1.3 copy-start.12
  65.7 55.8 %all-to-all-start = ((bf16[32,528,128]{2,1,0:T(8,128)(2,1)}), bf16[32,528,128]{2,1,0:T(8,128)(2,1)}, u32[]{:S(2)}, u32[]{:S(2)}) async-start(bf16[32,528,128]{2,1,0:T(8,128)(2,1)} %place_entries.1), calls=%async_computation | async-start | bytes 8650752 | tf_op jit(solution)/shard_map/all_to_all | solution.py:604
  77.7 60.7 %copy-start.8 = (bf16[512,512]{1,0:T(8,128)(2,1)S(1)}, bf16[512,512]{1,0:T(8,128)(2,1)}, u32[]{:S(2)}) copy-start(bf16[512,512]{1,0:T(8,128)(2,1)} %get-tuple-element.105) | copy-start | bytes 1572868
  77.7 60.8 %copy-start.7 = (bf16[512,512]{1,0:T(8,128)(2,1)S(1)}, bf16[512,512]{1,0:T(8,128)(2,1)}, u32[]{:S(2)}) copy-start(bf16[512,512]{1,0:T(8,128)(2,1)} %get-tuple-element.114) | copy-start | bytes 1572868
  121.5 16.8 %collective-permute-start.11 = (bf16[512,512]{1,0:T(8,128)(2,1)}, bf16[512,512]{1,0:T(8,128)(2,1)S(1)}, u32[]{:S(2)}, u32[]{:S(2)}) collective-permute-start(bf16[512,512]{1,0:T(8,128)(2,1)} %get-tuple-element.111), channel_id=1, source_target_pairs={{0,16},{4,20},{8,24},{12,28},{16,0},{20,4},{24,8},{28,12},{32,48},... | collective-permute-start | bytes 1572872 | tf_op jit(solution)/shard_map/ppermute | solution.py:608
  126.9 11.5 %collective-permute-start.12 = (bf16[512,512]{1,0:T(8,128)(2,1)}, bf16[512,512]{1,0:T(8,128)(2,1)S(1)}, u32[]{:S(2)}, u32[]{:S(2)}) collective-permute-start(bf16[512,512]{1,0:T(8,128)(2,1)} %get-tuple-element.112), channel_id=1, source_target_pairs={{0,64},{4,68},{8,72},{12,76},{16,80},{20,84},{24,88},{28,92},{32,9... | collective-permute-start | bytes 1572872 | tf_op jit(solution)/shard_map/ppermute | solution.py:608
  138.2 5.7 %copy-start.13 = (bf16[1024,128]{1,0:T(8,128)(2,1)S(1)}, bf16[1024,128]{1,0:T(8,128)(2,1)}, u32[]{:S(2)}) copy-start(bf16[1024,128]{1,0:T(8,128)(2,1)} %get-tuple-element.118) | copy-start | bytes 786436
  138.2 5.7 %collective-permute-start.15 = (bf16[1024,128]{1,0:T(8,128)(2,1)}, bf16[1024,128]{1,0:T(8,128)(2,1)S(1)}, u32[]{:S(2)}, u32[]{:S(2)}) collective-permute-start(bf16[1024,128]{1,0:T(8,128)(2,1)} %get-tuple-element.117), channel_id=1, source_target_pairs={{0,1},{1,0},{2,3},{3,2},{4,5},{5,4},{6,7},{7,6},{8,9},{9,8},{10,11... | collective-permute-start | bytes 786440 | tf_op jit(solution)/shard_map/ppermute | solution.py:610
  138.7 12.1 %collective-permute-start.14 = (bf16[512,256]{1,0:T(8,128)(2,1)S(1)}, bf16[512,256]{1,0:T(8,128)(2,1)S(1)}, u32[]{:S(2)}, u32[]{:S(2)}) collective-permute-start(bf16[512,256]{1,0:T(8,128)(2,1)S(1)} %get-tuple-element.132), channel_id=1, source_target_pairs={{0,32},{4,36},{8,40},{12,44},{16,48},{20,52},{24,56},{28,60},{32,0... | collective-permute-start | bytes 786440 | tf_op jit(solution)/shard_map/ppermute | solution.py:615
  143.9 8.4 %collective-permute-start.13 = (bf16[512,256]{1,0:T(8,128)(2,1)S(1)}, bf16[512,256]{1,0:T(8,128)(2,1)S(1)}, u32[]{:S(2)}, u32[]{:S(2)}) collective-permute-start(bf16[512,256]{1,0:T(8,128)(2,1)S(1)} %get-tuple-element.133), channel_id=1, source_target_pairs={{0,8},{4,12},{8,0},{12,4},{16,24},{20,28},{24,16},{28,20},{32,40},... | collective-permute-start | bytes 786440 | tf_op jit(solution)/shard_map/ppermute | solution.py:615
  144.0 18.6 %copy-start.15 = (f32[2048]{0:T(1024)S(1)}, f32[2048]{0:T(1024)}, u32[]{:S(2)}) copy-start(f32[2048]{0:T(1024)} %param.17) | copy-start | bytes 24580
  144.0 19.2 %copy-start.4 = (f32[2048,128]{1,0:T(8,128)S(1)}, f32[2048,128]{1,0:T(8,128)}, u32[]{:S(2)}) copy-start(f32[2048,128]{1,0:T(8,128)} %param.16) | copy-start | bytes 3145732
  144.0 10.8 %collective-permute-start.16 = (bf16[1024,128]{1,0:T(8,128)(2,1)S(1)}, bf16[1024,128]{1,0:T(8,128)(2,1)S(1)}, u32[]{:S(2)}, u32[]{:S(2)}) collective-permute-start(bf16[1024,128]{1,0:T(8,128)(2,1)S(1)} %add_convert_fusion.2), channel_id=1, source_target_pairs={{0,2},{1,3},{2,0},{3,1},{4,6},{5,7},{6,4},{7,5},{8,10},{9,11},{10,... | collective-permute-start | bytes 786440 | tf_op jit(solution)/shard_map/ppermute | solution.py:620
  152.4 8.6 %collective-permute-start.18 = (bf16[1040,128]{1,0:T(8,128)(2,1)S(1)}, bf16[1040,128]{1,0:T(8,128)(2,1)S(1)}, u32[]{:S(2)}, u32[]{:S(2)}) collective-permute-start(bf16[1040,128]{1,0:T(8,128)(2,1)S(1)} %pad.4), channel_id=1, source_target_pairs={{0,4},{4,0},{8,12},{12,8},{16,20},{20,16},{24,28},{28,24},{32,36},... | collective-permute-start | bytes 798728 | tf_op jit(solution)/shard_map/ppermute | solution.py:621
  154.9 6.2 %collective-permute-start.17 = (bf16[1024,128]{1,0:T(8,128)(2,1)S(1)}, bf16[1024,128]{1,0:T(8,128)(2,1)S(1)}, u32[]{:S(2)}, u32[]{:S(2)}) collective-permute-start(bf16[1024,128]{1,0:T(8,128)(2,1)S(1)} %add_convert_fusion.1), channel_id=1, source_target_pairs={{0,1},{1,0},{2,3},{3,2},{4,5},{5,4},{6,7},{7,6},{8,9},{9,8},{10,11... | collective-permute-start | bytes 786440 | tf_op jit(solution)/shard_map/ppermute | solution.py:625

commit v6 on v5

--- a/solution.py
+++ b/solution.py
@@ -20,7 +20,6 @@
 F32 = jnp.float32
 BF16 = jnp.bfloat16
 LIGHT = pl.CostEstimate(flops=1, bytes_accessed=1, transcendentals=0)
-VMEM_BYTES = 56 << 20
 NT = (((1,), (1,)), ((), ()))
 
 
@@ -175,7 +174,7 @@
             pltpu.SemaphoreType.DMA((N_WIDE,)),
             pltpu.SemaphoreType.DMA((3,)),
         ],
-        compiler_params=pltpu.CompilerParams(vmem_limit_bytes=VMEM_BYTES),
+        compiler_params=pltpu.CompilerParams(vmem_limit_bytes=28 << 20),
         cost_estimate=LIGHT,
         name="place_entries",
     )(slots, base, mate, far, ids, bias)
@@ -257,7 +256,7 @@
             pltpu.SMEM((2 * N_WIDE + 16,), jnp.int32),
             pltpu.SemaphoreType.DMA((2,)),
         ],
-        compiler_params=pltpu.CompilerParams(vmem_limit_bytes=VMEM_BYTES),
+        compiler_params=pltpu.CompilerParams(vmem_limit_bytes=24 << 20),
         cost_estimate=LIGHT,
         name="owned_sums",
     )(core, recv)
@@ -363,7 +362,7 @@
             pltpu.SemaphoreType.DMA((7,)),
             pltpu.SemaphoreType.DMA((8,)),
         ],
-        compiler_params=pltpu.CompilerParams(vmem_limit_bytes=VMEM_BYTES),
+        compiler_params=pltpu.CompilerParams(vmem_limit_bytes=60 << 20),
         cost_estimate=LIGHT,
         name="sent_terms",
     )(n, z, y, cotangent, embedded, weight)
@@ -402,7 +401,7 @@
             pltpu.SemaphoreType.DMA((8,)),
             pltpu.SemaphoreType.DMA((4,)),
         ],
-        compiler_params=pltpu.CompilerParams(vmem_limit_bytes=VMEM_BYTES),
+        compiler_params=pltpu.CompilerParams(vmem_limit_bytes=14 << 20),
         cost_estimate=LIGHT,
         name="passed_on",
     )(*first, *second)
@@ -500,7 +499,7 @@
             pltpu.SemaphoreType.DMA((11,)),
             pltpu.SemaphoreType.DMA((5,)),
         ],
-        compiler_params=pltpu.CompilerParams(vmem_limit_bytes=VMEM_BYTES),
+        compiler_params=pltpu.CompilerParams(vmem_limit_bytes=58 << 20),
         cost_estimate=LIGHT,
         name="kept_terms",
     )(n, z, y, cotangent, embedded, weight, bias.reshape(1, -1), scaled, turned, owner, row, bag)
@@ -547,7 +546,7 @@
             pltpu.VMEM((8, 256, 1024), BF16),
             pltpu.SemaphoreType.DMA((10,)),
         ],
-        compiler_params=pltpu.CompilerParams(vmem_limit_bytes=VMEM_BYTES),
+        compiler_params=pltpu.CompilerParams(vmem_limit_bytes=30 << 20),
         cost_estimate=LIGHT,
         name="own_terms",
     )(z, y, embedded, turned, *first, *second)

time: 167 us -> 176 us (1.054)
  local copies, waits for them, and re-layouts: 4.93 us -> 23.5 us
  starting transfers between devices: 38.7 us -> 31.8 us
  waiting for transfers between devices: 59.2 us -> 53.6 us
  other arithmetic: 4.58 us -> 6.5 us
    unnamed x34 -> x62, local copies, waits for them, and re-layouts: 4.84 us -> 23.4 us
    all_to_all x1, waiting for transfers between devices: 43.8 us -> 36.8 us  [body(): lax.all_to_all(payload, 'wide', split_axis=0, concat_axis=0, tiled=True)]
    ppermute x1, starting transfers between devices: 5.17 us -> 0.09 us  [body(): lax.ppermute(quarters[1][1], 'wide', z_flip(1))]
    pallas_call x1, Pallas kernels: 10.3 us -> 14.6 us  [owned_sums(): pl.pallas_call(functools.partial(sums_kernel, norm_factor), out_shape=[ja...]
    pallas_call x1, Pallas kernels: 6.32 us -> 2.28 us  [own_terms(): pl.pallas_call(own_kernel, out_shape=[jax.ShapeDtypeStruct((512, 512), BF...]
    pallas_call x1, Pallas kernels: 12.5 us -> 15.7 us  [place_entries(): pl.pallas_call(place_kernel, out_shape=jax.ShapeDtypeStruct((N_WIDE, BLOC...]
    ppermute x1, starting transfers between devices: 2.4 us -> 0.09 us  [body(): lax.ppermute(jnp.pad(x_send, ((0, 16), (0, 0))), 'wide', X_LO)[:1024]]
    pallas_call x1, Pallas kernels: 3.23 us -> 1.05 us  [passed_on(): pl.pallas_call(pass_kernel, out_shape=[jax.ShapeDtypeStruct((256, 1024),...]
  transfers between devices with their start and end apart: 20 -> 20, of which waited for: 8 -> 8; matrix products, arithmetic and copies ran while one was open for 2% -> 3% of each run, Pallas kernels for 29% -> 28%
where the time goes in v6:
time: 176 us; the launch traced here: 174 us
  Pallas kernels  57.3 us (33%)
  waiting for transfers between devices  53.6 us (30%)
  starting transfers between devices  31.8 us (18%)
  local copies, waits for them, and re-layouts  23.5 us (13%)
  other arithmetic  6.5 us (4%)
    all_to_all x1, waiting for transfers between devices, body(): lax.all_to_all(payload, 'wide', split_axis=0, concat_axis=0, tiled=True)  36.8 us
    unnamed x62, local copies, waits for them, and re-layouts  23.4 us
    pallas_call x1, Pallas kernels, place_entries(): pl.pallas_call(place_kernel, out_shape=jax.ShapeDtypeStruct((N_WIDE, BLOC...  15.7 us
    pallas_call x1, Pallas kernels, kept_terms(): pl.pallas_call(kept_kernel, out_shape=[shape((samples, width), F32), shap...  15.2 us
    pallas_call x1, Pallas kernels, owned_sums(): pl.pallas_call(functools.partial(sums_kernel, norm_factor), out_shape=[ja...  14.6 us
    pallas_call x1, Pallas kernels, sent_terms(): pl.pallas_call(sent_kernel, out_shape=[full] * 2 + [shape((512, 1024), BF...  8.54 us
    ppermute x1, waiting for transfers between devices, body(): lax.ppermute(jnp.pad(x_send, ((0, 16), (0, 0))), 'wide', X_LO)[:1024]  6.76 us
    ppermute x4, starting transfers between devices, body(): second = [lax.ppermute(second[q], 'wide', ways[q]) for q in range(4)]  6.54 us
  transfers between devices with their start and end apart: 20, of which 8 were waited for; matrix products, arithmetic and copies ran while one was open for 3% of the time, Pallas kernels for 28%

profile of v6, /device:TPU:24, one launch (start us, length us, event | category | flops | bytes accessed | tf_op | source)
XLA Modules:
  0.0 173.8 jit_solution(18388233733418100431)
XLA Ops:
  0.7 8.5 %sent_terms.1 = (bf16[512,1024]{1,0:T(8,128)(2,1)}, bf16[512,1024]{1,0:T(8,128)(2,1)}, bf16[512,1024]{1,0:T(8,128)(2,1)}, bf16[512,1024]{1,0:T(8,128)(2,1)}, bf1...) custom-call(s32[1]{0:T(128)} %bitcast.2.n_ref, ...), custom_call_target="tpu_custom_call" | custom-call | flops 1 | bytes 1 | tf_op jit(solution)/shard_map/sent_terms/pallas_call | solution.py:349
  9.3 2.0 %collective-permute-start.1 = (bf16[512,1024]{1,0:T(8,128)(2,1)}, bf16[512,1024]{1,0:T(8,128)(2,1)S(1)}, u32[]{:S(2)}, u32[]{:S(2)}) collective-permute-start(bf16[512,1024]{1,0:T(8,128)(2,1)} %get-tuple-element.73), channel_id=1, source_target_pairs={{0,32},{4,36},{8,40},{12,44},{16,48},{20,52},{24,56},{28,60},{32,6... | collective-permute-start | bytes 3145736 | tf_op jit(solution)/shard_map/ppermute | solution.py:586
  11.3 2.2 %collective-permute-start.2 = (bf16[512,1024]{1,0:T(8,128)(2,1)}, bf16[512,1024]{1,0:T(8,128)(2,1)S(1)}, u32[]{:S(2)}, u32[]{:S(2)}) collective-permute-start(bf16[512,1024]{1,0:T(8,128)(2,1)} %get-tuple-element.74), channel_id=1, source_target_pairs={{0,96},{4,100},{8,104},{12,108},{16,112},{20,116},{24,120},{28,124... | collective-permute-start | bytes 3145736 | tf_op jit(solution)/shard_map/ppermute | solution.py:586
  13.7 1.8 %collective-permute-start.4 = (bf16[512,1024]{1,0:T(8,128)(2,1)}, bf16[512,1024]{1,0:T(8,128)(2,1)S(1)}, u32[]{:S(2)}, u32[]{:S(2)}) collective-permute-start(bf16[512,1024]{1,0:T(8,128)(2,1)} %get-tuple-element.76), channel_id=1, source_target_pairs={{0,24},{4,28},{8,0},{12,4},{16,8},{20,12},{24,16},{28,20},{32,56},... | collective-permute-start | bytes 3145736 | tf_op jit(solution)/shard_map/ppermute | solution.py:586
  15.5 2.6 %add_convert_fusion = bf16[512,1024]{1,0:T(8,128)(2,1)} fusion(bf16[512,1024]{1,0:T(8,128)(2,1)S(1)} %collective-permute-done, bf16[512,1024]{1,0:T(8,128)(2,1)} %get-tuple-element.64), kind=kLoop, calls=%fused_computation | loop fusion | flops 2097152 | bytes 3145728 | tf_op jit(solution)/shard_map/convert_element_type | solution.py:587
  18.1 3.0 %collective-permute-start.5 = (bf16[512,1024]{1,0:T(8,128)(2,1)}, bf16[512,1024]{1,0:T(8,128)(2,1)S(1)}, u32[]{:S(2)}, u32[]{:S(2)}) collective-permute-start(bf16[512,1024]{1,0:T(8,128)(2,1)} %add_convert_fusion), channel_id=1, source_target_pairs={{0,2},{1,3},{2,0},{3,1},{4,6},{5,7},{6,4},{7,5},{8,10},{9,11},{10,... | collective-permute-start | bytes 3145736 | tf_op jit(solution)/shard_map/ppermute | solution.py:589
  21.2 0.6 copy.16
  21.8 15.2 %kept_terms.1 = (f32[512,1024]{1,0:T(8,128)}, s32[64,128]{1,0:T(8,128)}, f32[64,512]{1,0:T(8,128)}, f32[8,128]{1,0:T(8,128)}, bf16[512,1024]{1,0:T(8,128)(2,1)},...) custom-call(s32[1]{0:T(128)} %bitcast.2.n_ref, ...), custom_call_target="tpu_custom_call" | custom-call | flops 1 | bytes 1 | tf_op jit(solution)/shard_map/kept_terms/pallas_call | solution.py:477
  37.4 1.5 collective-permute-done.3.refs_2_
  38.9 1.2 collective-permute-done.4.refs_3_
  40.1 1.4 copy-done.18
  41.5 1.0 copy-done.19
  42.5 1.0 copy-done.20
  43.6 1.0 copy-done.21
  44.6 1.0 passed_on.1
  46.3 3.2 %collective-permute-start.8 = (bf16[256,1024]{1,0:T(8,128)(2,1)S(1)}, bf16[256,1024]{1,0:T(8,128)(2,1)S(1)}, u32[]{:S(2)}, u32[]{:S(2)}) collective-permute-start(bf16[256,1024]{1,0:T(8,128)(2,1)S(1)} %get-tuple-element.98), channel_id=1, source_target_pairs={{0,96},{4,100},{8,104},{12,108},{16,112},{20,116},{24,120},{28,124... | collective-permute-start | bytes 1572872 | tf_op jit(solution)/shard_map/ppermute | solution.py:599
  49.5 2.7 %collective-permute-start.9 = (bf16[256,1024]{1,0:T(8,128)(2,1)S(1)}, bf16[256,1024]{1,0:T(8,128)(2,1)S(1)}, u32[]{:S(2)}, u32[]{:S(2)}) collective-permute-start(bf16[256,1024]{1,0:T(8,128)(2,1)S(1)} %get-tuple-element.99), channel_id=1, source_target_pairs={{0,8},{4,12},{8,16},{12,20},{16,24},{20,28},{24,0},{28,4},{32,40},... | collective-permute-start | bytes 1572872 | tf_op jit(solution)/shard_map/ppermute | solution.py:599
  52.2 15.7 %place_entries.1 = bf16[32,528,128]{2,1,0:T(8,128)(2,1)S(1)} custom-call(s32[8192]{0:T(1024)S(1)} %bitcast.18, f32[512,1024]{1,0:T(8,128)S(1)} %copy-done.5, bf16[512,1024]{1,0:T(8,128)(2,1)S(1)} %collective-permute-done.6.mate_hbm, bf16[512,1024]{1,0:T(8,128)(2,1)S(1)} %collective-permute-done.5.far_hbm, f32[64,512]{1,0:T(8,128)S(1)} %copy-done.22, ...), custom_call_target="tpu_custom_call" | custom-call | flops 1 | bytes 1 | tf_op jit(solution)/shard_map/place_entries/pallas_call | solution.py:163
  67.9 2.0 %copy-done.1 = bf16[32,528,128]{2,1,0:T(8,128)(2,1)} copy-done((bf16[32,528,128]{2,1,0:T(8,128)(2,1)}, bf16[32,528,128]{2,1,0:T(8,128)(2,1)S(1)}, u32[]{:S(2)}) %copy-start.1) | copy-done | bytes 4325400
  70.0 0.8 copy-done.10
  70.8 0.8 copy-done.12
  71.6 0.8 copy-done.14
  72.4 0.8 copy-done.16
  73.2 5.6 %all-to-all-start = ((bf16[32,528,128]{2,1,0:T(8,128)(2,1)}), bf16[32,528,128]{2,1,0:T(8,128)(2,1)}, u32[]{:S(2)}, u32[]{:S(2)}) async-start(bf16[32,528,128]{2,1,0:T(8,128)(2,1)} %copy-done.1), calls=%async_computation | async-start | bytes 8650752 | tf_op jit(solution)/shard_map/all_to_all | solution.py:603
  78.9 2.2 %copy-done = bf16[512,4096]{1,0:T(8,128)(2,1)S(1)} copy-done((bf16[512,4096]{1,0:T(8,128)(2,1)S(1)}, bf16[512,4096]{1,0:T(8,128)(2,1)}, u32[]{:S(2)}) %copy-start) | copy-done | bytes 4194328
  81.0 1.2 copy-done.3
  82.3 1.2 copy-done.4
  83.5 1.0 copy-done.11
  84.5 1.0 copy-done.13
  85.6 1.0 copy-done.15
  86.6 1.0 copy-done.17
  87.7 2.3 %own_terms.1 = (bf16[512,512]{1,0:T(8,128)(2,1)S(1)}, bf16[512,512]{1,0:T(8,128)(2,1)S(1)}, bf16[512,512]{1,0:T(8,128)(2,1)S(1)}, bf16[512,512]{1,0:T(8,128)(2,1)S(1)}) custom-call(s32[1]{0:T(128)} %bitcast.z_ref, s32[1]{0:T(128)} %bitcast.1.y_ref, bf16[512,4096]{1,0:T(8,128)(2,1)S(1)} %copy-done, bf16[1024,512]{1,0:T(8,128)(2,1)S(1)} %copy-done.4, ...), custom_call_target="tpu_custom_call" | custom-call | flops 1 | bytes 1 | tf_op jit(solution)/shard_map/own_terms/pallas_call | solution.py:538
  90.0 0.8 copy-done.6
  90.7 0.8 copy-done.8
  91.6 0.8 copy-done.25
  92.3 0.8 copy-done.26
  93.2 36.8 %all-to-all-done.recv_hbm = bf16[32,528,128]{2,1,0:T(8,128)(2,1)} async-done(((bf16[32,528,128]{2,1,0:T(8,128)(2,1)}), bf16[32,528,128]{2,1,0:T(8,128)(2,1)}, u32[]{:S(2)}, u32[]{:S(2)}) %all-to-all-start) | async-done | bytes 4325408 | tf_op jit(solution)/shard_map/all_to_all | solution.py:603
  130.0 6.0 %collective-permute-start.11 = (bf16[512,512]{1,0:T(8,128)(2,1)}, bf16[512,512]{1,0:T(8,128)(2,1)S(1)}, u32[]{:S(2)}, u32[]{:S(2)}) collective-permute-start(bf16[512,512]{1,0:T(8,128)(2,1)} %copy-done.26), channel_id=1, source_target_pairs={{0,16},{4,20},{8,24},{12,28},{16,0},{20,4},{24,8},{28,12},{32,48},... | collective-permute-start | bytes 1572872 | tf_op jit(solution)/shard_map/ppermute | solution.py:607
  136.0 1.1 collective-permute-start.12
  137.2 14.6 %owned_sums.1 = (bf16[1024,128]{1,0:T(8,128)(2,1)S(1)}, bf16[1024,128]{1,0:T(8,128)(2,1)S(1)}, f32[8,128]{1,0:T(8,128)}) custom-call(s32[1]{0:T(128)} %bitcast.9.core_ref, bf16[32,528,128]{2,1,0:T(8,128)(2,1)} %all-to-all-done.recv_hbm), custom_call_target="tpu_custom_call" | custom-call | flops 1 | bytes 1 | tf_op jit(solution)/shard_map/owned_sums/pallas_call | solution.py:245
  152.5 0.9 collective-permute-done.15
  153.5 2.7 %collective-permute-start.16 = (bf16[1024,128]{1,0:T(8,128)(2,1)S(1)}, bf16[1024,128]{1,0:T(8,128)(2,1)S(1)}, u32[]{:S(2)}, u32[]{:S(2)}) collective-permute-start(bf16[1024,128]{1,0:T(8,128)(2,1)S(1)} %add_convert_fusion.2), channel_id=1, source_target_pairs={{0,2},{1,3},{2,0},{3,1},{4,6},{5,7},{6,4},{7,5},{8,10},{9,11},{10,... | collective-permute-start | bytes 786440 | tf_op jit(solution)/shard_map/ppermute | solution.py:619
  156.2 4.9 %collective-permute-done.14 = bf16[512,256]{1,0:T(8,128)(2,1)} collective-permute-done((bf16[512,256]{1,0:T(8,128)(2,1)S(1)}, bf16[512,256]{1,0:T(8,128)(2,1)}, u32[]{:S(2)}, u32[]{:S(2)}) %collective-permute-start.14) | collective-permute-done | bytes 262176 | tf_op jit(solution)/shard_map/ppermute | solution.py:614
  161.1 1.0 add_convert_fusion.3
  162.4 1.0 collective-permute-done.16
  163.6 6.8 %collective-permute-done.18 = bf16[1040,128]{1,0:T(8,128)(2,1)S(1)} collective-permute-done((bf16[1040,128]{1,0:T(8,128)(2,1)S(1)}, bf16[1040,128]{1,0:T(8,128)(2,1)S(1)}, u32[]{:S(2)}, u32[]{:S(2)}) %collective-permute-start.18) | collective-permute-done | bytes 266272 | tf_op jit(solution)/shard_map/ppermute | solution.py:620
  170.5 1.0 copy.13
  172.5 1.3 fusion.1
  (76 shorter events, 3.5 us)
Async XLA Ops:
  0.7 20.5 %copy-start.28 = (s32[1,512,16,1]{1,3,2,0:T(1,128)S(1)}, s32[1,512,16,1]{1,3,2,0:T(1,128)}, u32[]{:S(2)}) copy-start(s32[1,512,16,1]{1,3,2,0:T(1,128)} %param.14) | copy-start | bytes 98308
  9.2 6.3 %collective-permute-start = (bf16[512,1024]{1,0:T(8,128)(2,1)}, bf16[512,1024]{1,0:T(8,128)(2,1)S(1)}, u32[]{:S(2)}, u32[]{:S(2)}) collective-permute-start(bf16[512,1024]{1,0:T(8,128)(2,1)} %get-tuple-element.65), channel_id=1, source_target_pairs={{0,1},{1,0},{2,3},{3,2},{4,5},{5,4},{6,7},{7,6},{8,9},{9,8},{10,11... | collective-permute-start | bytes 3145736 | tf_op jit(solution)/shard_map/ppermute | solution.py:584
  9.3 28.1 %collective-permute-start.1 = (bf16[512,1024]{1,0:T(8,128)(2,1)}, bf16[512,1024]{1,0:T(8,128)(2,1)S(1)}, u32[]{:S(2)}, u32[]{:S(2)}) collective-permute-start(bf16[512,1024]{1,0:T(8,128)(2,1)} %get-tuple-element.73), channel_id=1, source_target_pairs={{0,32},{4,36},{8,40},{12,44},{16,48},{20,52},{24,56},{28,60},{32,6... | collective-permute-start | bytes 3145736 | tf_op jit(solution)/shard_map/ppermute | solution.py:586
  11.3 26.1 %collective-permute-start.2 = (bf16[512,1024]{1,0:T(8,128)(2,1)}, bf16[512,1024]{1,0:T(8,128)(2,1)S(1)}, u32[]{:S(2)}, u32[]{:S(2)}) collective-permute-start(bf16[512,1024]{1,0:T(8,128)(2,1)} %get-tuple-element.74), channel_id=1, source_target_pairs={{0,96},{4,100},{8,104},{12,108},{16,112},{20,116},{24,120},{28,124... | collective-permute-start | bytes 3145736 | tf_op jit(solution)/shard_map/ppermute | solution.py:586
  13.5 25.3 %collective-permute-start.3 = (bf16[512,1024]{1,0:T(8,128)(2,1)}, bf16[512,1024]{1,0:T(8,128)(2,1)S(1)}, u32[]{:S(2)}, u32[]{:S(2)}) collective-permute-start(bf16[512,1024]{1,0:T(8,128)(2,1)} %get-tuple-element.75), channel_id=1, source_target_pairs={{0,8},{4,12},{8,16},{12,20},{16,24},{20,28},{24,0},{28,4},{32,40},... | collective-permute-start | bytes 3145736 | tf_op jit(solution)/shard_map/ppermute | solution.py:586
  13.7 26.3 %collective-permute-start.4 = (bf16[512,1024]{1,0:T(8,128)(2,1)}, bf16[512,1024]{1,0:T(8,128)(2,1)S(1)}, u32[]{:S(2)}, u32[]{:S(2)}) collective-permute-start(bf16[512,1024]{1,0:T(8,128)(2,1)} %get-tuple-element.76), channel_id=1, source_target_pairs={{0,24},{4,28},{8,0},{12,4},{16,8},{20,12},{24,16},{28,20},{32,56},... | collective-permute-start | bytes 3145736 | tf_op jit(solution)/shard_map/ppermute | solution.py:586
  18.1 27.5 %collective-permute-start.5 = (bf16[512,1024]{1,0:T(8,128)(2,1)}, bf16[512,1024]{1,0:T(8,128)(2,1)S(1)}, u32[]{:S(2)}, u32[]{:S(2)}) collective-permute-start(bf16[512,1024]{1,0:T(8,128)(2,1)} %add_convert_fusion), channel_id=1, source_target_pairs={{0,2},{1,3},{2,0},{3,1},{4,6},{5,7},{6,4},{7,5},{8,10},{9,11},{10,... | collective-permute-start | bytes 3145736 | tf_op jit(solution)/shard_map/ppermute | solution.py:589
  37.0 15.2 %copy-start.5 = (f32[512,1024]{1,0:T(8,128)S(1)}, f32[512,1024]{1,0:T(8,128)}, u32[]{:S(2)}) copy-start(f32[512,1024]{1,0:T(8,128)} %get-tuple-element.92.base_hbm) | copy-start | bytes 6291460
  40.1 27.8 %copy-start.2 = (bf16[512,1024]{1,0:T(8,128)(2,1)}, bf16[512,1024]{1,0:T(8,128)(2,1)S(1)}, u32[]{:S(2)}) copy-start(bf16[512,1024]{1,0:T(8,128)(2,1)S(1)} %collective-permute-done.4.refs_3_) | copy-start | bytes 3145732
  40.1 12.1 %collective-permute-start.6 = (bf16[512,1024]{1,0:T(8,128)(2,1)}, bf16[512,1024]{1,0:T(8,128)(2,1)S(1)}, u32[]{:S(2)}, u32[]{:S(2)}) collective-permute-start(bf16[512,1024]{1,0:T(8,128)(2,1)} %get-tuple-element.93), channel_id=1, source_target_pairs={{0,1},{1,0},{2,3},{3,2},{4,5},{5,4},{6,7},{7,6},{8,9},{9,8},{10,11... | collective-permute-start | bytes 3145736 | tf_op jit(solution)/shard_map/ppermute | solution.py:596
  40.1 1.4 copy-start.18
  41.5 1.0 copy-start.19
  42.5 1.0 copy-start.20
  43.6 1.0 copy-start.21
  44.6 7.6 %copy-start.22 = (f32[64,512]{1,0:T(8,128)S(1)}, f32[64,512]{1,0:T(8,128)}, u32[]{:S(2)}) copy-start(f32[64,512]{1,0:T(8,128)} %get-tuple-element.95.ids_ref) | copy-start | bytes 393220
  44.6 7.6 %copy-start.23 = (s32[64,128]{1,0:T(8,128)S(1)}, s32[64,128]{1,0:T(8,128)}, u32[]{:S(2)}) copy-start(s32[64,128]{1,0:T(8,128)} %get-tuple-element.91) | copy-start | bytes 98308
  44.6 7.6 %copy-start.24 = (f32[8,128]{1,0:T(8,128)S(1)}, f32[8,128]{1,0:T(8,128)}, u32[]{:S(2)}) copy-start(f32[8,128]{1,0:T(8,128)} %get-tuple-element.96.bias_ref) | copy-start | bytes 12292
  45.7 24.3 %collective-permute-start.10 = (bf16[256,1024]{1,0:T(8,128)(2,1)S(1)}, bf16[256,1024]{1,0:T(8,128)(2,1)S(1)}, u32[]{:S(2)}, u32[]{:S(2)}) collective-permute-start(bf16[256,1024]{1,0:T(8,128)(2,1)S(1)} %get-tuple-element.100), channel_id=1, source_target_pairs={{0,24},{4,28},{8,0},{12,4},{16,8},{20,12},{24,16},{28,20},{32,56},... | collective-permute-start | bytes 1572872 | tf_op jit(solution)/shard_map/ppermute | solution.py:599
  46.3 24.5 %collective-permute-start.7 = (bf16[256,1024]{1,0:T(8,128)(2,1)S(1)}, bf16[256,1024]{1,0:T(8,128)(2,1)S(1)}, u32[]{:S(2)}, u32[]{:S(2)}) collective-permute-start(bf16[256,1024]{1,0:T(8,128)(2,1)S(1)} %get-tuple-element.97), channel_id=1, source_target_pairs={{0,32},{4,36},{8,40},{12,44},{16,48},{20,52},{24,56},{28,60},{32,6... | collective-permute-start | bytes 1572872 | tf_op jit(solution)/shard_map/ppermute | solution.py:599
  46.3 25.3 %collective-permute-start.8 = (bf16[256,1024]{1,0:T(8,128)(2,1)S(1)}, bf16[256,1024]{1,0:T(8,128)(2,1)S(1)}, u32[]{:S(2)}, u32[]{:S(2)}) collective-permute-start(bf16[256,1024]{1,0:T(8,128)(2,1)S(1)} %get-tuple-element.98), channel_id=1, source_target_pairs={{0,96},{4,100},{8,104},{12,108},{16,112},{20,116},{24,120},{28,124... | collective-permute-start | bytes 1572872 | tf_op jit(solution)/shard_map/ppermute | solution.py:599
  49.5 22.9 %collective-permute-start.9 = (bf16[256,1024]{1,0:T(8,128)(2,1)S(1)}, bf16[256,1024]{1,0:T(8,128)(2,1)S(1)}, u32[]{:S(2)}, u32[]{:S(2)}) collective-permute-start(bf16[256,1024]{1,0:T(8,128)(2,1)S(1)} %get-tuple-element.99), channel_id=1, source_target_pairs={{0,8},{4,12},{8,16},{12,20},{16,24},{20,28},{24,0},{28,4},{32,40},... | collective-permute-start | bytes 1572872 | tf_op jit(solution)/shard_map/ppermute | solution.py:599
  67.9 2.1 %copy-start.1 = (bf16[32,528,128]{2,1,0:T(8,128)(2,1)}, bf16[32,528,128]{2,1,0:T(8,128)(2,1)S(1)}, u32[]{:S(2)}) copy-start(bf16[32,528,128]{2,1,0:T(8,128)(2,1)S(1)} %place_entries.1) | copy-start | bytes 12976132
  70.8 0.8 copy-start.12
  71.6 0.8 copy-start.14
  72.4 0.8 copy-start.16
  73.2 56.8 %all-to-all-start = ((bf16[32,528,128]{2,1,0:T(8,128)(2,1)}), bf16[32,528,128]{2,1,0:T(8,128)(2,1)}, u32[]{:S(2)}, u32[]{:S(2)}) async-start(bf16[32,528,128]{2,1,0:T(8,128)(2,1)} %copy-done.1), calls=%async_computation | async-start | bytes 8650752 | tf_op jit(solution)/shard_map/all_to_all | solution.py:603
  78.8 2.2 %copy-start = (bf16[512,4096]{1,0:T(8,128)(2,1)S(1)}, bf16[512,4096]{1,0:T(8,128)(2,1)}, u32[]{:S(2)}) copy-start(bf16[512,4096]{1,0:T(8,128)(2,1)} %embedded_hbm.5) | copy-start | bytes 12582916
  81.0 1.2 copy-start.3
  82.3 1.2 copy-start.4
  83.5 1.0 copy-start.11
  84.5 1.0 copy-start.13
  85.6 1.0 copy-start.15
  86.6 1.0 copy-start.17
  90.0 0.8 copy-start.6
  90.7 0.8 copy-start.8
  92.3 0.8 copy-start.26
  130.0 21.9 %copy-start.9 = (bf16[512,512]{1,0:T(8,128)(2,1)S(1)}, bf16[512,512]{1,0:T(8,128)(2,1)}, u32[]{:S(2)}) copy-start(bf16[512,512]{1,0:T(8,128)(2,1)} %copy-done.8) | copy-start | bytes 1572868
  130.0 22.0 %copy-start.7 = (bf16[512,512]{1,0:T(8,128)(2,1)S(1)}, bf16[512,512]{1,0:T(8,128)(2,1)}, u32[]{:S(2)}) copy-start(bf16[512,512]{1,0:T(8,128)(2,1)} %copy-done.6) | copy-start | bytes 1572868
  130.0 21.9 %collective-permute-start.11 = (bf16[512,512]{1,0:T(8,128)(2,1)}, bf16[512,512]{1,0:T(8,128)(2,1)S(1)}, u32[]{:S(2)}, u32[]{:S(2)}) collective-permute-start(bf16[512,512]{1,0:T(8,128)(2,1)} %copy-done.26), channel_id=1, source_target_pairs={{0,16},{4,20},{8,24},{12,28},{16,0},{20,4},{24,8},{28,12},{32,48},... | collective-permute-start | bytes 1572872 | tf_op jit(solution)/shard_map/ppermute | solution.py:607
  136.0 15.9 %collective-permute-start.12 = (bf16[512,512]{1,0:T(8,128)(2,1)}, bf16[512,512]{1,0:T(8,128)(2,1)S(1)}, u32[]{:S(2)}, u32[]{:S(2)}) collective-permute-start(bf16[512,512]{1,0:T(8,128)(2,1)} %copy-done.25), channel_id=1, source_target_pairs={{0,64},{4,68},{8,72},{12,76},{16,80},{20,84},{24,88},{28,92},{32,9... | collective-permute-start | bytes 1572872 | tf_op jit(solution)/shard_map/ppermute | solution.py:607
  151.8 1.6 collective-permute-start.15
  152.3 8.9 %collective-permute-start.14 = (bf16[512,256]{1,0:T(8,128)(2,1)S(1)}, bf16[512,256]{1,0:T(8,128)(2,1)}, u32[]{:S(2)}, u32[]{:S(2)}) collective-permute-start(bf16[512,256]{1,0:T(8,128)(2,1)S(1)} %get-tuple-element.132), channel_id=1, source_target_pairs={{0,32},{4,36},{8,40},{12,44},{16,48},{20,52},{24,56},{28,60},{32,0... | collective-permute-start | bytes 786440 | tf_op jit(solution)/shard_map/ppermute | solution.py:614
  152.4 9.8 %collective-permute-start.13 = (bf16[512,256]{1,0:T(8,128)(2,1)S(1)}, bf16[512,256]{1,0:T(8,128)(2,1)S(1)}, u32[]{:S(2)}, u32[]{:S(2)}) collective-permute-start(bf16[512,256]{1,0:T(8,128)(2,1)S(1)} %get-tuple-element.133), channel_id=1, source_target_pairs={{0,8},{4,12},{8,0},{12,4},{16,24},{20,28},{24,16},{28,20},{32,40},... | collective-permute-start | bytes 786440 | tf_op jit(solution)/shard_map/ppermute | solution.py:614
  153.5 18.4 %copy-start.29 = (f32[2048]{0:T(1024)S(1)}, f32[2048]{0:T(1024)}, u32[]{:S(2)}) copy-start(f32[2048]{0:T(1024)} %param.17) | copy-start | bytes 24580
  153.5 19.0 %copy-start.27 = (f32[2048,128]{1,0:T(8,128)S(1)}, f32[2048,128]{1,0:T(8,128)}, u32[]{:S(2)}) copy-start(f32[2048,128]{1,0:T(8,128)} %param.16) | copy-start | bytes 3145732
  153.5 9.9 %collective-permute-start.16 = (bf16[1024,128]{1,0:T(8,128)(2,1)S(1)}, bf16[1024,128]{1,0:T(8,128)(2,1)S(1)}, u32[]{:S(2)}, u32[]{:S(2)}) collective-permute-start(bf16[1024,128]{1,0:T(8,128)(2,1)S(1)} %add_convert_fusion.2), channel_id=1, source_target_pairs={{0,2},{1,3},{2,0},{3,1},{4,6},{5,7},{6,4},{7,5},{8,10},{9,11},{10,... | collective-permute-start | bytes 786440 | tf_op jit(solution)/shard_map/ppermute | solution.py:619
  162.3 8.1 %collective-permute-start.18 = (bf16[1040,128]{1,0:T(8,128)(2,1)S(1)}, bf16[1040,128]{1,0:T(8,128)(2,1)S(1)}, u32[]{:S(2)}, u32[]{:S(2)}) collective-permute-start(bf16[1040,128]{1,0:T(8,128)(2,1)S(1)} %pad.4), channel_id=1, source_target_pairs={{0,4},{4,0},{8,12},{12,8},{16,20},{20,16},{24,28},{28,24},{32,36},... | collective-permute-start | bytes 798728 | tf_op jit(solution)/shard_map/ppermute | solution.py:620
  163.5 6.9 %collective-permute-start.17 = (bf16[1024,128]{1,0:T(8,128)(2,1)S(1)}, bf16[1024,128]{1,0:T(8,128)(2,1)S(1)}, u32[]{:S(2)}, u32[]{:S(2)}) collective-permute-start(bf16[1024,128]{1,0:T(8,128)(2,1)S(1)} %add_convert_fusion.1), channel_id=1, source_target_pairs={{0,1},{1,0},{2,3},{3,2},{4,5},{5,4},{6,7},{7,6},{8,9},{9,8},{10,11... | collective-permute-start | bytes 786440 | tf_op jit(solution)/shard_map/ppermute | solution.py:624
  (2 other events, 1.6 us)

commit v7 on v5

--- a/solution.py
+++ b/solution.py
@@ -21,6 +21,7 @@
 BF16 = jnp.bfloat16
 LIGHT = pl.CostEstimate(flops=1, bytes_accessed=1, transcendentals=0)
 VMEM_BYTES = 56 << 20
+VMEM_MOST = 63 << 20
 NT = (((1,), (1,)), ((), ()))
 
 
@@ -175,7 +176,7 @@
             pltpu.SemaphoreType.DMA((N_WIDE,)),
             pltpu.SemaphoreType.DMA((3,)),
         ],
-        compiler_params=pltpu.CompilerParams(vmem_limit_bytes=VMEM_BYTES),
+        compiler_params=pltpu.CompilerParams(vmem_limit_bytes=VMEM_MOST),
         cost_estimate=LIGHT,
         name="place_entries",
     )(slots, base, mate, far, ids, bias)
@@ -363,7 +364,7 @@
             pltpu.SemaphoreType.DMA((7,)),
             pltpu.SemaphoreType.DMA((8,)),
         ],
-        compiler_params=pltpu.CompilerParams(vmem_limit_bytes=VMEM_BYTES),
+        compiler_params=pltpu.CompilerParams(vmem_limit_bytes=VMEM_MOST),
         cost_estimate=LIGHT,
         name="sent_terms",
     )(n, z, y, cotangent, embedded, weight)
@@ -402,7 +403,7 @@
             pltpu.SemaphoreType.DMA((8,)),
             pltpu.SemaphoreType.DMA((4,)),
         ],
-        compiler_params=pltpu.CompilerParams(vmem_limit_bytes=VMEM_BYTES),
+        compiler_params=pltpu.CompilerParams(vmem_limit_bytes=VMEM_MOST),
         cost_estimate=LIGHT,
         name="passed_on",
     )(*first, *second)
@@ -500,7 +501,7 @@
             pltpu.SemaphoreType.DMA((11,)),
             pltpu.SemaphoreType.DMA((5,)),
         ],
-        compiler_params=pltpu.CompilerParams(vmem_limit_bytes=VMEM_BYTES),
+        compiler_params=pltpu.CompilerParams(vmem_limit_bytes=VMEM_MOST),
         cost_estimate=LIGHT,
         name="kept_terms",
     )(n, z, y, cotangent, embedded, weight, bias.reshape(1, -1), scaled, turned, owner, row, bag)

time: 167 us -> 166 us (level)
  starting transfers between devices: 38.7 us -> 42.5 us
  local copies, waits for them, and re-layouts: 4.93 us -> 2.47 us
  waiting for transfers between devices: 59.2 us -> 56.9 us
    ppermute x1, starting transfers between devices: 0.01 us -> 4.59 us  [body(): lax.ppermute(quarters[0][1], 'wide', y_flip(1))]
    ppermute x1, waiting for transfers between devices: 4.01 us -> 0.01 us  [body(): lax.ppermute(quarters[1][1], 'wide', z_flip(1))]
    unnamed x34 -> x16, local copies, waits for them, and re-layouts: 4.84 us -> 2.39 us
    ppermute x1, starting transfers between devices: 5.17 us -> 2.87 us  [body(): lax.ppermute(quarters[1][1], 'wide', z_flip(1))]
    ppermute x1, waiting for transfers between devices: 1.39 us -> 3.68 us  [body(): lax.ppermute(quarters[0][1], 'wide', y_flip(1))]
    ppermute x1, starting transfers between devices: 2.4 us -> 4.08 us  [body(): lax.ppermute(jnp.pad(x_send, ((0, 16), (0, 0))), 'wide', X_LO)[:1024]]
  transfers between devices with their start and end apart: 20 -> 20, of which waited for: 8 -> 7; matrix products, arithmetic and copies ran while one was open for 2% -> 2% of each run, Pallas kernels for 29% -> 29%
where the time goes in v7:
time: 166 us; the launch traced here: 164 us
  waiting for transfers between devices  56.9 us (34%)
  Pallas kernels  56 us (34%)
  starting transfers between devices  42.5 us (26%)
  other arithmetic  5.67 us (3%)
  local copies, waits for them, and re-layouts  2.47 us (1%)
    all_to_all x1, waiting for transfers between devices, body(): lax.all_to_all(payload, 'wide', split_axis=0, concat_axis=0, tiled=True)  43 us
    pallas_call x1, Pallas kernels, kept_terms(): pl.pallas_call(kept_kernel, out_shape=[shape((samples, width), F32), shap...  15.2 us
    pallas_call x1, Pallas kernels, place_entries(): pl.pallas_call(place_kernel, out_shape=jax.ShapeDtypeStruct((N_WIDE, BLOC...  12.5 us
    pallas_call x1, Pallas kernels, owned_sums(): pl.pallas_call(functools.partial(sums_kernel, norm_factor), out_shape=[ja...  10.3 us
    pallas_call x1, Pallas kernels, sent_terms(): pl.pallas_call(sent_kernel, out_shape=[full] * 2 + [shape((512, 1024), BF...  8.51 us
    ppermute x4, starting transfers between devices, body(): second = [lax.ppermute(second[q], 'wide', ways[q]) for q in range(4)]  6.47 us
    pallas_call x1, Pallas kernels, own_terms(): pl.pallas_call(own_kernel, out_shape=[jax.ShapeDtypeStruct((512, 512), BF...  6.28 us
    ppermute x4, starting transfers between devices, body(): first = [lax.ppermute(first[q], 'wide', ways[q]) for q in range(4)]  6.21 us
  transfers between devices with their start and end apart: 20, of which 7 were waited for; matrix products, arithmetic and copies ran while one was open for 2% of the time, Pallas kernels for 29%

profile of v7, /device:TPU:24, one launch (start us, length us, event | category | flops | bytes accessed | tf_op | source)
XLA Modules:
  0.0 164.4 jit_solution(17627487422242947185)
XLA Ops:
  0.7 8.5 %sent_terms.1 = (bf16[512,1024]{1,0:T(8,128)(2,1)}, bf16[512,1024]{1,0:T(8,128)(2,1)}, bf16[512,1024]{1,0:T(8,128)(2,1)}, bf16[512,1024]{1,0:T(8,128)(2,1)}, bf1...) custom-call(s32[1]{0:T(128)} %bitcast.2.n_ref, ...), custom_call_target="tpu_custom_call" | custom-call | flops 1 | bytes 1 | tf_op jit(solution)/shard_map/sent_terms/pallas_call | solution.py:351
  9.2 0.1 collective-permute-start
  9.3 2.0 %collective-permute-start.1 = (bf16[512,1024]{1,0:T(8,128)(2,1)}, bf16[512,1024]{1,0:T(8,128)(2,1)}, u32[]{:S(2)}, u32[]{:S(2)}) collective-permute-start(bf16[512,1024]{1,0:T(8,128)(2,1)} %get-tuple-element.73), channel_id=1, source_target_pairs={{0,32},{4,36},{8,40},{12,44},{16,48},{20,52},{24,56},{28,60},{32,6... | collective-permute-start | bytes 3145736 | tf_op jit(solution)/shard_map/ppermute | solution.py:588
  11.3 2.2 %collective-permute-start.2 = (bf16[512,1024]{1,0:T(8,128)(2,1)}, bf16[512,1024]{1,0:T(8,128)(2,1)}, u32[]{:S(2)}, u32[]{:S(2)}) collective-permute-start(bf16[512,1024]{1,0:T(8,128)(2,1)} %get-tuple-element.74), channel_id=1, source_target_pairs={{0,96},{4,100},{8,104},{12,108},{16,112},{20,116},{24,120},{28,124... | collective-permute-start | bytes 3145736 | tf_op jit(solution)/shard_map/ppermute | solution.py:588
  13.5 0.2 collective-permute-start.3
  13.7 1.8 %collective-permute-start.4 = (bf16[512,1024]{1,0:T(8,128)(2,1)}, bf16[512,1024]{1,0:T(8,128)(2,1)}, u32[]{:S(2)}, u32[]{:S(2)}) collective-permute-start(bf16[512,1024]{1,0:T(8,128)(2,1)} %get-tuple-element.76), channel_id=1, source_target_pairs={{0,24},{4,28},{8,0},{12,4},{16,8},{20,12},{24,16},{28,20},{32,56},... | collective-permute-start | bytes 3145736 | tf_op jit(solution)/shard_map/ppermute | solution.py:588
  15.5 2.7 %add_convert_fusion = bf16[512,1024]{1,0:T(8,128)(2,1)} fusion(bf16[512,1024]{1,0:T(8,128)(2,1)S(1)} %collective-permute-done, bf16[512,1024]{1,0:T(8,128)(2,1)} %get-tuple-element.64), kind=kLoop, calls=%fused_computation | loop fusion | flops 2097152 | bytes 3145728 | tf_op jit(solution)/shard_map/convert_element_type | solution.py:589
  18.2 3.0 %collective-permute-start.5 = (bf16[512,1024]{1,0:T(8,128)(2,1)}, bf16[512,1024]{1,0:T(8,128)(2,1)}, u32[]{:S(2)}, u32[]{:S(2)}) collective-permute-start(bf16[512,1024]{1,0:T(8,128)(2,1)} %add_convert_fusion), channel_id=1, source_target_pairs={{0,2},{1,3},{2,0},{3,1},{4,6},{5,7},{6,4},{7,5},{8,10},{9,11},{10,... | collective-permute-start | bytes 3145736 | tf_op jit(solution)/shard_map/ppermute | solution.py:591
  21.2 0.6 copy.16
  21.9 15.2 %kept_terms.1 = (f32[512,1024]{1,0:T(8,128)}, s32[64,128]{1,0:T(8,128)}, f32[64,512]{1,0:T(8,128)}, f32[8,128]{1,0:T(8,128)}, bf16[512,1024]{1,0:T(8,128)(2,1)},...) custom-call(s32[1]{0:T(128)} %bitcast.2.n_ref, ...), custom_call_target="tpu_custom_call" | custom-call | flops 1 | bytes 1 | tf_op jit(solution)/shard_map/kept_terms/pallas_call | solution.py:479
  37.1 0.4 collective-permute-done.1.refs_0_
  37.5 1.5 collective-permute-done.3.refs_2_
  38.9 1.2 collective-permute-done.4.refs_3_
  40.1 3.2 %passed_on.1 = (bf16[256,1024]{1,0:T(8,128)(2,1)}, bf16[256,1024]{1,0:T(8,128)(2,1)}, bf16[256,1024]{1,0:T(8,128)(2,1)}, bf16[256,1024]{1,0:T(8,128)(2,1)}) custom-call(bf16[512,1024]{1,0:T(8,128)(2,1)} %collective-permute-done.1.refs_0_, bf16[512,1024]{1,0:T(8,128)(2,1)} %collective-permute-done.2.refs_1_, ...), custom_call_target="tpu_custom_call" | custom-call | flops 1 | bytes 1 | tf_op jit(solution)/shard_map/passed_on/pallas_call | solution.py:394
  43.3 1.3 collective-permute-done.5.far_hbm
  44.6 0.8 collective-permute-start.10
  45.4 3.2 %collective-permute-start.8 = (bf16[256,1024]{1,0:T(8,128)(2,1)}, bf16[256,1024]{1,0:T(8,128)(2,1)}, u32[]{:S(2)}, u32[]{:S(2)}) collective-permute-start(bf16[256,1024]{1,0:T(8,128)(2,1)} %get-tuple-element.98), channel_id=1, source_target_pairs={{0,96},{4,100},{8,104},{12,108},{16,112},{20,116},{24,120},{28,124... | collective-permute-start | bytes 1572872 | tf_op jit(solution)/shard_map/ppermute | solution.py:601
  48.6 2.5 %collective-permute-start.9 = (bf16[256,1024]{1,0:T(8,128)(2,1)}, bf16[256,1024]{1,0:T(8,128)(2,1)}, u32[]{:S(2)}, u32[]{:S(2)}) collective-permute-start(bf16[256,1024]{1,0:T(8,128)(2,1)} %get-tuple-element.99), channel_id=1, source_target_pairs={{0,8},{4,12},{8,16},{12,20},{16,24},{20,28},{24,0},{28,4},{32,40},... | collective-permute-start | bytes 1572872 | tf_op jit(solution)/shard_map/ppermute | solution.py:601
  51.1 12.5 %place_entries.1 = bf16[32,528,128]{2,1,0:T(8,128)(2,1)} custom-call(s32[8192]{0:T(1024)} %bitcast.21, f32[512,1024]{1,0:T(8,128)} %get-tuple-element.92.base_hbm, bf16[512,1024]{1,0:T(8,128)(2,1)} %collective-permute-done.6.mate_hbm, bf16[512,1024]{1,0:T(8,128)(2,1)} %collective-permute-done.5.far_hbm, f32[64,512]{1,0:T(8,128)} %get-tuple-element.95.ids_ref, ...), custom_call_target="tpu_custom_call" | custom-call | flops 1 | bytes 1 | tf_op jit(solution)/shard_map/place_entries/pallas_call | solution.py:165
  63.6 0.0 copy-start.3
  63.6 0.8 copy-done.3
  64.4 5.7 %all-to-all-start = ((bf16[32,528,128]{2,1,0:T(8,128)(2,1)}), bf16[32,528,128]{2,1,0:T(8,128)(2,1)}, u32[]{:S(2)}, u32[]{:S(2)}) async-start(bf16[32,528,128]{2,1,0:T(8,128)(2,1)} %place_entries.1), calls=%async_computation | async-start | bytes 8650752 | tf_op jit(solution)/shard_map/all_to_all | solution.py:605
  70.1 6.3 %own_terms.1 = (bf16[512,512]{1,0:T(8,128)(2,1)}, bf16[512,512]{1,0:T(8,128)(2,1)}, bf16[512,512]{1,0:T(8,128)(2,1)}, bf16[512,512]{1,0:T(8,128)(2,1)}) custom-call(s32[1]{0:T(128)} %bitcast.z_ref, s32[1]{0:T(128)} %bitcast.1.y_ref, bf16[512,4096]{1,0:T(8,128)(2,1)} %embedded_hbm.5, bf16[1024,512]{1,0:T(8,128)(2,1)} %get-tuple-element.68.turned_hbm, ...), custom_call_target="tpu_custom_call" | custom-call | flops 1 | bytes 1 | tf_op jit(solution)/shard_map/own_terms/pallas_call | solution.py:540
  76.4 0.0 copy-start.2
  76.4 43.0 %all-to-all-done.recv_hbm = bf16[32,528,128]{2,1,0:T(8,128)(2,1)} async-done(((bf16[32,528,128]{2,1,0:T(8,128)(2,1)}), bf16[32,528,128]{2,1,0:T(8,128)(2,1)}, u32[]{:S(2)}, u32[]{:S(2)}) %all-to-all-start) | async-done | bytes 4325408 | tf_op jit(solution)/shard_map/all_to_all | solution.py:605
  119.4 5.5 %collective-permute-start.11 = (bf16[512,512]{1,0:T(8,128)(2,1)}, bf16[512,512]{1,0:T(8,128)(2,1)S(1)}, u32[]{:S(2)}, u32[]{:S(2)}) collective-permute-start(bf16[512,512]{1,0:T(8,128)(2,1)} %get-tuple-element.111), channel_id=1, source_target_pairs={{0,16},{4,20},{8,24},{12,28},{16,0},{20,4},{24,8},{28,12},{32,48},... | collective-permute-start | bytes 1572872 | tf_op jit(solution)/shard_map/ppermute | solution.py:609
  125.0 1.0 collective-permute-start.12
  125.9 10.3 %owned_sums.1 = (bf16[1024,128]{1,0:T(8,128)(2,1)}, bf16[1024,128]{1,0:T(8,128)(2,1)}, f32[8,128]{1,0:T(8,128)}) custom-call(s32[1]{0:T(128)} %bitcast.9.core_ref, bf16[32,528,128]{2,1,0:T(8,128)(2,1)} %all-to-all-done.recv_hbm), custom_call_target="tpu_custom_call" | custom-call | flops 1 | bytes 1 | tf_op jit(solution)/shard_map/owned_sums/pallas_call | solution.py:247
  136.2 0.0 copy-start.4
  136.2 0.1 collective-permute-start.15
  136.4 0.1 convert_add_fusion.1
  136.5 0.1 convert_add_fusion
  136.7 2.9 %collective-permute-start.14 = (bf16[512,256]{1,0:T(8,128)(2,1)S(1)}, bf16[512,256]{1,0:T(8,128)(2,1)S(1)}, u32[]{:S(2)}, u32[]{:S(2)}) collective-permute-start(bf16[512,256]{1,0:T(8,128)(2,1)S(1)} %get-tuple-element.132), channel_id=1, source_target_pairs={{0,32},{4,36},{8,40},{12,44},{16,48},{20,52},{24,56},{28,60},{32,0... | collective-permute-start | bytes 786440 | tf_op jit(solution)/shard_map/ppermute | solution.py:616
  139.6 4.6 %collective-permute-start.13 = (bf16[512,256]{1,0:T(8,128)(2,1)S(1)}, bf16[512,256]{1,0:T(8,128)(2,1)S(1)}, u32[]{:S(2)}, u32[]{:S(2)}) collective-permute-start(bf16[512,256]{1,0:T(8,128)(2,1)S(1)} %get-tuple-element.133), channel_id=1, source_target_pairs={{0,8},{4,12},{8,0},{12,4},{16,24},{20,28},{24,16},{28,20},{32,40},... | collective-permute-start | bytes 786440 | tf_op jit(solution)/shard_map/ppermute | solution.py:616
  144.2 0.1 add_convert_fusion.2
  144.3 2.8 %collective-permute-start.16 = (bf16[1024,128]{1,0:T(8,128)(2,1)S(1)}, bf16[1024,128]{1,0:T(8,128)(2,1)S(1)}, u32[]{:S(2)}, u32[]{:S(2)}) collective-permute-start(bf16[1024,128]{1,0:T(8,128)(2,1)S(1)} %add_convert_fusion.2), channel_id=1, source_target_pairs={{0,2},{1,3},{2,0},{3,1},{4,6},{5,7},{6,4},{7,5},{8,10},{9,11},{10,... | collective-permute-start | bytes 786440 | tf_op jit(solution)/shard_map/ppermute | solution.py:621
  147.1 0.1 add_convert_fusion.3
  147.2 3.7 %collective-permute-done.13 = bf16[512,256]{1,0:T(8,128)(2,1)S(1)} collective-permute-done((bf16[512,256]{1,0:T(8,128)(2,1)S(1)}, bf16[512,256]{1,0:T(8,128)(2,1)S(1)}, u32[]{:S(2)}, u32[]{:S(2)}) %collective-permute-start.13) | collective-permute-done | bytes 262176 | tf_op jit(solution)/shard_map/ppermute | solution.py:616
  150.8 0.1 add_convert_fusion.4
  151.0 4.1 %collective-permute-start.18 = (bf16[1040,128]{1,0:T(8,128)(2,1)S(1)}, bf16[1040,128]{1,0:T(8,128)(2,1)S(1)}, u32[]{:S(2)}, u32[]{:S(2)}) collective-permute-start(bf16[1040,128]{1,0:T(8,128)(2,1)S(1)} %pad.4), channel_id=1, source_target_pairs={{0,4},{4,0},{8,12},{12,8},{16,20},{20,16},{24,28},{28,24},{32,36},... | collective-permute-start | bytes 798728 | tf_op jit(solution)/shard_map/ppermute | solution.py:622
  155.1 0.1 add_convert_fusion.1
  155.1 0.1 collective-permute-start.17
  155.3 5.7 %collective-permute-done.18 = bf16[1040,128]{1,0:T(8,128)(2,1)S(1)} collective-permute-done((bf16[1040,128]{1,0:T(8,128)(2,1)S(1)}, bf16[1040,128]{1,0:T(8,128)(2,1)S(1)}, u32[]{:S(2)}, u32[]{:S(2)}) %collective-permute-start.18) | collective-permute-done | bytes 266272 | tf_op jit(solution)/shard_map/ppermute | solution.py:622
  161.0 0.1 multiply_bitcast_fusion
  161.1 1.0 copy.13
  162.2 0.3 fusion.2
  162.5 0.6 fusion.5
  163.1 1.3 fusion.1
  (30 shorter events, 0.2 us)
Async XLA Ops:
  0.7 20.6 %copy-start.5 = (s32[1,512,16,1]{1,3,2,0:T(1,128)S(1)}, s32[1,512,16,1]{1,3,2,0:T(1,128)}, u32[]{:S(2)}) copy-start(s32[1,512,16,1]{1,3,2,0:T(1,128)} %param.14) | copy-start | bytes 98308
  9.2 6.3 %collective-permute-start = (bf16[512,1024]{1,0:T(8,128)(2,1)}, bf16[512,1024]{1,0:T(8,128)(2,1)S(1)}, u32[]{:S(2)}, u32[]{:S(2)}) collective-permute-start(bf16[512,1024]{1,0:T(8,128)(2,1)} %get-tuple-element.65), channel_id=1, source_target_pairs={{0,1},{1,0},{2,3},{3,2},{4,5},{5,4},{6,7},{7,6},{8,9},{9,8},{10,11... | collective-permute-start | bytes 3145736 | tf_op jit(solution)/shard_map/ppermute | solution.py:586
  9.3 28.2 %collective-permute-start.1 = (bf16[512,1024]{1,0:T(8,128)(2,1)}, bf16[512,1024]{1,0:T(8,128)(2,1)}, u32[]{:S(2)}, u32[]{:S(2)}) collective-permute-start(bf16[512,1024]{1,0:T(8,128)(2,1)} %get-tuple-element.73), channel_id=1, source_target_pairs={{0,32},{4,36},{8,40},{12,44},{16,48},{20,52},{24,56},{28,60},{32,6... | collective-permute-start | bytes 3145736 | tf_op jit(solution)/shard_map/ppermute | solution.py:588
  11.3 26.2 %collective-permute-start.2 = (bf16[512,1024]{1,0:T(8,128)(2,1)}, bf16[512,1024]{1,0:T(8,128)(2,1)}, u32[]{:S(2)}, u32[]{:S(2)}) collective-permute-start(bf16[512,1024]{1,0:T(8,128)(2,1)} %get-tuple-element.74), channel_id=1, source_target_pairs={{0,96},{4,100},{8,104},{12,108},{16,112},{20,116},{24,120},{28,124... | collective-permute-start | bytes 3145736 | tf_op jit(solution)/shard_map/ppermute | solution.py:588
  13.5 25.4 %collective-permute-start.3 = (bf16[512,1024]{1,0:T(8,128)(2,1)}, bf16[512,1024]{1,0:T(8,128)(2,1)}, u32[]{:S(2)}, u32[]{:S(2)}) collective-permute-start(bf16[512,1024]{1,0:T(8,128)(2,1)} %get-tuple-element.75), channel_id=1, source_target_pairs={{0,8},{4,12},{8,16},{12,20},{16,24},{20,28},{24,0},{28,4},{32,40},... | collective-permute-start | bytes 3145736 | tf_op jit(solution)/shard_map/ppermute | solution.py:588
  13.7 26.4 %collective-permute-start.4 = (bf16[512,1024]{1,0:T(8,128)(2,1)}, bf16[512,1024]{1,0:T(8,128)(2,1)}, u32[]{:S(2)}, u32[]{:S(2)}) collective-permute-start(bf16[512,1024]{1,0:T(8,128)(2,1)} %get-tuple-element.76), channel_id=1, source_target_pairs={{0,24},{4,28},{8,0},{12,4},{16,8},{20,12},{24,16},{28,20},{32,56},... | collective-permute-start | bytes 3145736 | tf_op jit(solution)/shard_map/ppermute | solution.py:588
  18.2 26.4 %collective-permute-start.5 = (bf16[512,1024]{1,0:T(8,128)(2,1)}, bf16[512,1024]{1,0:T(8,128)(2,1)}, u32[]{:S(2)}, u32[]{:S(2)}) collective-permute-start(bf16[512,1024]{1,0:T(8,128)(2,1)} %add_convert_fusion), channel_id=1, source_target_pairs={{0,2},{1,3},{2,0},{3,1},{4,6},{5,7},{6,4},{7,5},{8,10},{9,11},{10,... | collective-permute-start | bytes 3145736 | tf_op jit(solution)/shard_map/ppermute | solution.py:591
  40.1 11.0 %collective-permute-start.6 = (bf16[512,1024]{1,0:T(8,128)(2,1)}, bf16[512,1024]{1,0:T(8,128)(2,1)}, u32[]{:S(2)}, u32[]{:S(2)}) collective-permute-start(bf16[512,1024]{1,0:T(8,128)(2,1)} %get-tuple-element.93), channel_id=1, source_target_pairs={{0,1},{1,0},{2,3},{3,2},{4,5},{5,4},{6,7},{7,6},{8,9},{9,8},{10,11... | collective-permute-start | bytes 3145736 | tf_op jit(solution)/shard_map/ppermute | solution.py:598
  44.6 19.0 %collective-permute-start.10 = (bf16[256,1024]{1,0:T(8,128)(2,1)}, bf16[256,1024]{1,0:T(8,128)(2,1)S(1)}, u32[]{:S(2)}, u32[]{:S(2)}) collective-permute-start(bf16[256,1024]{1,0:T(8,128)(2,1)} %get-tuple-element.100), channel_id=1, source_target_pairs={{0,24},{4,28},{8,0},{12,4},{16,8},{20,12},{24,16},{28,20},{32,56},... | collective-permute-start | bytes 1572872 | tf_op jit(solution)/shard_map/ppermute | solution.py:601
  45.4 18.2 %collective-permute-start.7 = (bf16[256,1024]{1,0:T(8,128)(2,1)}, bf16[256,1024]{1,0:T(8,128)(2,1)}, u32[]{:S(2)}, u32[]{:S(2)}) collective-permute-start(bf16[256,1024]{1,0:T(8,128)(2,1)} %get-tuple-element.97), channel_id=1, source_target_pairs={{0,32},{4,36},{8,40},{12,44},{16,48},{20,52},{24,56},{28,60},{32,6... | collective-permute-start | bytes 1572872 | tf_op jit(solution)/shard_map/ppermute | solution.py:601
  45.4 18.3 %collective-permute-start.8 = (bf16[256,1024]{1,0:T(8,128)(2,1)}, bf16[256,1024]{1,0:T(8,128)(2,1)}, u32[]{:S(2)}, u32[]{:S(2)}) collective-permute-start(bf16[256,1024]{1,0:T(8,128)(2,1)} %get-tuple-element.98), channel_id=1, source_target_pairs={{0,96},{4,100},{8,104},{12,108},{16,112},{20,116},{24,120},{28,124... | collective-permute-start | bytes 1572872 | tf_op jit(solution)/shard_map/ppermute | solution.py:601
  48.6 15.0 %collective-permute-start.9 = (bf16[256,1024]{1,0:T(8,128)(2,1)}, bf16[256,1024]{1,0:T(8,128)(2,1)}, u32[]{:S(2)}, u32[]{:S(2)}) collective-permute-start(bf16[256,1024]{1,0:T(8,128)(2,1)} %get-tuple-element.99), channel_id=1, source_target_pairs={{0,8},{4,12},{8,16},{12,20},{16,24},{20,28},{24,0},{28,4},{32,40},... | collective-permute-start | bytes 1572872 | tf_op jit(solution)/shard_map/ppermute | solution.py:601
  63.6 0.8 copy-start.3
  64.4 55.0 %all-to-all-start = ((bf16[32,528,128]{2,1,0:T(8,128)(2,1)}), bf16[32,528,128]{2,1,0:T(8,128)(2,1)}, u32[]{:S(2)}, u32[]{:S(2)}) async-start(bf16[32,528,128]{2,1,0:T(8,128)(2,1)} %place_entries.1), calls=%async_computation | async-start | bytes 8650752 | tf_op jit(solution)/shard_map/all_to_all | solution.py:605
  76.4 60.0 %copy-start.2 = (bf16[512,512]{1,0:T(8,128)(2,1)S(1)}, bf16[512,512]{1,0:T(8,128)(2,1)}, u32[]{:S(2)}) copy-start(bf16[512,512]{1,0:T(8,128)(2,1)} %get-tuple-element.105) | copy-start | bytes 1572868
  76.4 60.1 %copy-start.1 = (bf16[512,512]{1,0:T(8,128)(2,1)S(1)}, bf16[512,512]{1,0:T(8,128)(2,1)}, u32[]{:S(2)}) copy-start(bf16[512,512]{1,0:T(8,128)(2,1)} %get-tuple-element.114) | copy-start | bytes 1572868
  119.4 16.9 %collective-permute-start.11 = (bf16[512,512]{1,0:T(8,128)(2,1)}, bf16[512,512]{1,0:T(8,128)(2,1)S(1)}, u32[]{:S(2)}, u32[]{:S(2)}) collective-permute-start(bf16[512,512]{1,0:T(8,128)(2,1)} %get-tuple-element.111), channel_id=1, source_target_pairs={{0,16},{4,20},{8,24},{12,28},{16,0},{20,4},{24,8},{28,12},{32,48},... | collective-permute-start | bytes 1572872 | tf_op jit(solution)/shard_map/ppermute | solution.py:609
  125.0 11.4 %collective-permute-start.12 = (bf16[512,512]{1,0:T(8,128)(2,1)}, bf16[512,512]{1,0:T(8,128)(2,1)S(1)}, u32[]{:S(2)}, u32[]{:S(2)}) collective-permute-start(bf16[512,512]{1,0:T(8,128)(2,1)} %get-tuple-element.112), channel_id=1, source_target_pairs={{0,64},{4,68},{8,72},{12,76},{16,80},{20,84},{24,88},{28,92},{32,9... | collective-permute-start | bytes 1572872 | tf_op jit(solution)/shard_map/ppermute | solution.py:609
  136.2 8.0 %copy-start.4 = (bf16[1024,128]{1,0:T(8,128)(2,1)S(1)}, bf16[1024,128]{1,0:T(8,128)(2,1)}, u32[]{:S(2)}) copy-start(bf16[1024,128]{1,0:T(8,128)(2,1)} %get-tuple-element.118) | copy-start | bytes 786436
  136.2 7.9 %collective-permute-start.15 = (bf16[1024,128]{1,0:T(8,128)(2,1)}, bf16[1024,128]{1,0:T(8,128)(2,1)S(1)}, u32[]{:S(2)}, u32[]{:S(2)}) collective-permute-start(bf16[1024,128]{1,0:T(8,128)(2,1)} %get-tuple-element.117), channel_id=1, source_target_pairs={{0,1},{1,0},{2,3},{3,2},{4,5},{5,4},{6,7},{7,6},{8,9},{9,8},{10,11... | collective-permute-start | bytes 786440 | tf_op jit(solution)/shard_map/ppermute | solution.py:611
  136.7 10.4 %collective-permute-start.14 = (bf16[512,256]{1,0:T(8,128)(2,1)S(1)}, bf16[512,256]{1,0:T(8,128)(2,1)S(1)}, u32[]{:S(2)}, u32[]{:S(2)}) collective-permute-start(bf16[512,256]{1,0:T(8,128)(2,1)S(1)} %get-tuple-element.132), channel_id=1, source_target_pairs={{0,32},{4,36},{8,40},{12,44},{16,48},{20,52},{24,56},{28,60},{32,0... | collective-permute-start | bytes 786440 | tf_op jit(solution)/shard_map/ppermute | solution.py:616
  139.6 11.3 %collective-permute-start.13 = (bf16[512,256]{1,0:T(8,128)(2,1)S(1)}, bf16[512,256]{1,0:T(8,128)(2,1)S(1)}, u32[]{:S(2)}, u32[]{:S(2)}) collective-permute-start(bf16[512,256]{1,0:T(8,128)(2,1)S(1)} %get-tuple-element.133), channel_id=1, source_target_pairs={{0,8},{4,12},{8,0},{12,4},{16,24},{20,28},{24,16},{28,20},{32,40},... | collective-permute-start | bytes 786440 | tf_op jit(solution)/shard_map/ppermute | solution.py:616
  144.3 18.2 %copy-start.6 = (f32[2048]{0:T(1024)S(1)}, f32[2048]{0:T(1024)}, u32[]{:S(2)}) copy-start(f32[2048]{0:T(1024)} %param.17) | copy-start | bytes 24580
  144.3 18.8 %copy-start = (f32[2048,128]{1,0:T(8,128)S(1)}, f32[2048,128]{1,0:T(8,128)}, u32[]{:S(2)}) copy-start(f32[2048,128]{1,0:T(8,128)} %param.16) | copy-start | bytes 3145732
  144.3 10.8 %collective-permute-start.16 = (bf16[1024,128]{1,0:T(8,128)(2,1)S(1)}, bf16[1024,128]{1,0:T(8,128)(2,1)S(1)}, u32[]{:S(2)}, u32[]{:S(2)}) collective-permute-start(bf16[1024,128]{1,0:T(8,128)(2,1)S(1)} %add_convert_fusion.2), channel_id=1, source_target_pairs={{0,2},{1,3},{2,0},{3,1},{4,6},{5,7},{6,4},{7,5},{8,10},{9,11},{10,... | collective-permute-start | bytes 786440 | tf_op jit(solution)/shard_map/ppermute | solution.py:621
  151.0 10.0 %collective-permute-start.18 = (bf16[1040,128]{1,0:T(8,128)(2,1)S(1)}, bf16[1040,128]{1,0:T(8,128)(2,1)S(1)}, u32[]{:S(2)}, u32[]{:S(2)}) collective-permute-start(bf16[1040,128]{1,0:T(8,128)(2,1)S(1)} %pad.4), channel_id=1, source_target_pairs={{0,4},{4,0},{8,12},{12,8},{16,20},{20,16},{24,28},{28,24},{32,36},... | collective-permute-start | bytes 798728 | tf_op jit(solution)/shard_map/ppermute | solution.py:622
  155.1 5.9 %collective-permute-start.17 = (bf16[1024,128]{1,0:T(8,128)(2,1)S(1)}, bf16[1024,128]{1,0:T(8,128)(2,1)S(1)}, u32[]{:S(2)}, u32[]{:S(2)}) collective-permute-start(bf16[1024,128]{1,0:T(8,128)(2,1)S(1)} %add_convert_fusion.1), channel_id=1, source_target_pairs={{0,1},{1,0},{2,3},{3,2},{4,5},{5,4},{6,7},{7,6},{8,9},{9,8},{10,11... | collective-permute-start | bytes 786440 | tf_op jit(solution)/shard_map/ppermute | solution.py:626

commit v8 on v7

--- a/solution.py
+++ b/solution.py
@@ -529,9 +529,10 @@
             ],
             axis=0,
         ).astype(BF16)
+        total = jnp.transpose(total, (1, 0))
         high = place >= 2
-        results[2 * route][...] = jnp.where(high, total[:, 512:], total[:, :512])
-        results[2 * route + 1][...] = jnp.where(high, total[:, :512], total[:, 512:])
+        results[2 * route][...] = jnp.where(high, total[512:, :], total[:512, :])
+        results[2 * route + 1][...] = jnp.where(high, total[:512, :], total[512:, :])
 
 
 def own_terms(z, y, embedded, turned, first, second):
@@ -612,19 +613,19 @@
     keep, *got = lax.optimization_barrier((keep, *got))
     quarters = []
     for half, other, place in ((keep_y, got[0], y), (keep_z, got[1], z)):
-        quarters.append([part.astype(BF16) for part in halves_of(summed(half, [other]), place % 2, 1)])
+        quarters.append([part.astype(BF16) for part in halves_of(summed(half, [other]), place % 2, 0)])
     got = [lax.ppermute(quarters[0][1], "wide", y_flip(1)), lax.ppermute(quarters[1][1], "wide", z_flip(1))]
     keep, from_core, *_ = lax.optimization_barrier((keep, from_core, quarters[0][1], quarters[1][1]))
     chip = summed(keep, [from_core]).astype(BF16)
-    pair = jnp.concatenate([summed(quarters[0][0], got[:1]), summed(quarters[1][0], got[1:])], axis=0).astype(BF16)
-    x_keep, x_send = halves_of(pair, x_lo, 1)
+    pair = jnp.concatenate([summed(quarters[0][0], got[:1]), summed(quarters[1][0], got[1:])], axis=1).astype(BF16)
+    x_keep, x_send = halves_of(pair, x_lo, 0)
     other_chip, _ = lax.optimization_barrier((lax.ppermute(chip, "narrow", X_HI), x_send))
-    x_got = lax.ppermute(jnp.pad(x_send, ((0, 16), (0, 0))), "wide", X_LO)[:1024]
+    x_got = lax.ppermute(jnp.pad(x_send, ((0, 8), (0, 0))), "wide", X_LO)[:E]
 
     bias_grad = bias_sums.reshape(-1)
     mine = summed(chip, [other_chip]).astype(BF16)
     mate, x_got = lax.optimization_barrier((lax.ppermute(mine, "narrow", CORE), x_got))
-    weight_grad = summed(x_keep, [x_got]).T * norm_factor
+    weight_grad = summed(x_keep, [x_got]) * norm_factor
     row_grad = jnp.concatenate([jnp.where(core == 0, mine, mate), jnp.where(core == 0, mate, mine)], axis=0).astype(F32)
     new_state = adagrad_state + jnp.mean(row_grad * row_grad, axis=1)
     new_table = emb_table - LEARN_RATE * row_grad / jnp.sqrt(new_state)[:, None]

time: 166 us -> 164 us (0.988)
  starting transfers between devices: 42.5 us -> 31.2 us
  Pallas kernels: 56 us -> 62.2 us
  waiting for transfers between devices: 56.9 us -> 61.1 us
    pallas_call x1, Pallas kernels: 10.3 us -> 16.5 us  [owned_sums(): pl.pallas_call(functools.partial(sums_kernel, norm_factor), out_shape=[ja...]
    ppermute x1, waiting for transfers between devices: 0.01 us -> 4.55 us  [body(): lax.ppermute(quarters[1][1], 'wide', z_flip(1))]
    ppermute x1, starting transfers between devices: 4.59 us -> 0.09 us  [body(): lax.ppermute(quarters[0][1], 'wide', y_flip(1))]
    ppermute x1, starting transfers between devices: 4.08 us -> 0.09 us  [body(): x_got = lax.ppermute(jnp.pad(x_send, ((0, 8), (0, 0))), 'wide', X_LO)[:E]]
    ppermute x1, waiting for transfers between devices: 3.68 us -> 0.05 us  [body(): lax.ppermute(quarters[0][1], 'wide', y_flip(1))]
    ppermute x1, starting transfers between devices: 2.87 us -> 0.09 us  [body(): lax.ppermute(quarters[1][1], 'wide', z_flip(1))]
    ppermute x1, waiting for transfers between devices: 0.01 us -> 2.21 us  [body(): lax.ppermute(chip, 'narrow', X_HI)]
  transfers between devices with their start and end apart: 20 -> 20, of which waited for: 7 -> 9; matrix products, arithmetic and copies ran while one was open for 2% -> 2% of each run, Pallas kernels for 29% -> 33%
where the time goes in v8:
time: 164 us
  Pallas kernels  62.2 us (38%)
  waiting for transfers between devices  61.1 us (37%)
  starting transfers between devices  31.2 us (19%)
  other arithmetic  6.48 us (4%)
    all_to_all x1, waiting for transfers between devices, body(): lax.all_to_all(payload, 'wide', split_axis=0, concat_axis=0, tiled=True)  43 us
    pallas_call x1, Pallas kernels, owned_sums(): pl.pallas_call(functools.partial(sums_kernel, norm_factor), out_shape=[ja...  16.5 us
    pallas_call x1, Pallas kernels, kept_terms(): pl.pallas_call(kept_kernel, out_shape=[shape((samples, width), F32), shap...  15.2 us
    pallas_call x1, Pallas kernels, place_entries(): pl.pallas_call(place_kernel, out_shape=jax.ShapeDtypeStruct((N_WIDE, BLOC...  12.5 us
    pallas_call x1, Pallas kernels, sent_terms(): pl.pallas_call(sent_kernel, out_shape=[full] * 2 + [shape((512, 1024), BF...  8.51 us
    ppermute x4, starting transfers between devices, body(): second = [lax.ppermute(second[q], 'wide', ways[q]) for q in range(4)]  6.47 us
    pallas_call x1, Pallas kernels, own_terms(): pl.pallas_call(own_kernel, out_shape=[jax.ShapeDtypeStruct((512, 512), BF...  6.35 us
    ppermute x4, starting transfers between devices, body(): first = [lax.ppermute(first[q], 'wide', ways[q]) for q in range(4)]  6.21 us
  transfers between devices with their start and end apart: 20, of which 9 were waited for; matrix products, arithmetic and copies ran while one was open for 2% of the time, Pallas kernels for 33%

profile of v8, /device:TPU:24, one launch (start us, length us, event | category | flops | bytes accessed | tf_op | source)
XLA Modules:
  0.0 163.6 jit_solution(15050402469360082734)
XLA Ops:
  0.7 8.5 %sent_terms.1 = (bf16[512,1024]{1,0:T(8,128)(2,1)}, bf16[512,1024]{1,0:T(8,128)(2,1)}, bf16[512,1024]{1,0:T(8,128)(2,1)}, bf16[512,1024]{1,0:T(8,128)(2,1)}, bf1...) custom-call(s32[1]{0:T(128)} %bitcast.2.n_ref, ...), custom_call_target="tpu_custom_call" | custom-call | flops 1 | bytes 1 | tf_op jit(solution)/shard_map/sent_terms/pallas_call | solution.py:351
  9.2 0.1 collective-permute-start
  9.3 2.0 %collective-permute-start.1 = (bf16[512,1024]{1,0:T(8,128)(2,1)}, bf16[512,1024]{1,0:T(8,128)(2,1)}, u32[]{:S(2)}, u32[]{:S(2)}) collective-permute-start(bf16[512,1024]{1,0:T(8,128)(2,1)} %get-tuple-element.73), channel_id=1, source_target_pairs={{0,32},{4,36},{8,40},{12,44},{16,48},{20,52},{24,56},{28,60},{32,6... | collective-permute-start | bytes 3145736 | tf_op jit(solution)/shard_map/ppermute | solution.py:589
  11.3 2.2 %collective-permute-start.2 = (bf16[512,1024]{1,0:T(8,128)(2,1)}, bf16[512,1024]{1,0:T(8,128)(2,1)}, u32[]{:S(2)}, u32[]{:S(2)}) collective-permute-start(bf16[512,1024]{1,0:T(8,128)(2,1)} %get-tuple-element.74), channel_id=1, source_target_pairs={{0,96},{4,100},{8,104},{12,108},{16,112},{20,116},{24,120},{28,124... | collective-permute-start | bytes 3145736 | tf_op jit(solution)/shard_map/ppermute | solution.py:589
  13.5 0.2 collective-permute-start.3
  13.7 1.8 %collective-permute-start.4 = (bf16[512,1024]{1,0:T(8,128)(2,1)}, bf16[512,1024]{1,0:T(8,128)(2,1)}, u32[]{:S(2)}, u32[]{:S(2)}) collective-permute-start(bf16[512,1024]{1,0:T(8,128)(2,1)} %get-tuple-element.76), channel_id=1, source_target_pairs={{0,24},{4,28},{8,0},{12,4},{16,8},{20,12},{24,16},{28,20},{32,56},... | collective-permute-start | bytes 3145736 | tf_op jit(solution)/shard_map/ppermute | solution.py:589
  15.5 2.7 %add_convert_fusion = bf16[512,1024]{1,0:T(8,128)(2,1)} fusion(bf16[512,1024]{1,0:T(8,128)(2,1)S(1)} %collective-permute-done, bf16[512,1024]{1,0:T(8,128)(2,1)} %get-tuple-element.64), kind=kLoop, calls=%fused_computation | loop fusion | flops 2097152 | bytes 3145728 | tf_op jit(solution)/shard_map/convert_element_type | solution.py:590
  18.2 3.0 %collective-permute-start.5 = (bf16[512,1024]{1,0:T(8,128)(2,1)}, bf16[512,1024]{1,0:T(8,128)(2,1)}, u32[]{:S(2)}, u32[]{:S(2)}) collective-permute-start(bf16[512,1024]{1,0:T(8,128)(2,1)} %add_convert_fusion), channel_id=1, source_target_pairs={{0,2},{1,3},{2,0},{3,1},{4,6},{5,7},{6,4},{7,5},{8,10},{9,11},{10,... | collective-permute-start | bytes 3145736 | tf_op jit(solution)/shard_map/ppermute | solution.py:592
  21.2 0.6 copy.15
  21.9 15.2 %kept_terms.1 = (f32[512,1024]{1,0:T(8,128)}, s32[64,128]{1,0:T(8,128)}, f32[64,512]{1,0:T(8,128)}, f32[8,128]{1,0:T(8,128)}, bf16[512,1024]{1,0:T(8,128)(2,1)},...) custom-call(s32[1]{0:T(128)} %bitcast.2.n_ref, ...), custom_call_target="tpu_custom_call" | custom-call | flops 1 | bytes 1 | tf_op jit(solution)/shard_map/kept_terms/pallas_call | solution.py:479
  37.1 0.4 collective-permute-done.1.refs_0_
  37.5 1.5 collective-permute-done.3.refs_2_
  38.9 1.2 collective-permute-done.4.refs_3_
  40.1 3.2 %passed_on.1 = (bf16[256,1024]{1,0:T(8,128)(2,1)}, bf16[256,1024]{1,0:T(8,128)(2,1)}, bf16[256,1024]{1,0:T(8,128)(2,1)}, bf16[256,1024]{1,0:T(8,128)(2,1)}) custom-call(bf16[512,1024]{1,0:T(8,128)(2,1)} %collective-permute-done.1.refs_0_, bf16[512,1024]{1,0:T(8,128)(2,1)} %collective-permute-done.2.refs_1_, ...), custom_call_target="tpu_custom_call" | custom-call | flops 1 | bytes 1 | tf_op jit(solution)/shard_map/passed_on/pallas_call | solution.py:394
  43.3 1.3 collective-permute-done.5.far_hbm
  44.6 0.8 collective-permute-start.10
  45.4 3.2 %collective-permute-start.8 = (bf16[256,1024]{1,0:T(8,128)(2,1)}, bf16[256,1024]{1,0:T(8,128)(2,1)}, u32[]{:S(2)}, u32[]{:S(2)}) collective-permute-start(bf16[256,1024]{1,0:T(8,128)(2,1)} %get-tuple-element.98), channel_id=1, source_target_pairs={{0,96},{4,100},{8,104},{12,108},{16,112},{20,116},{24,120},{28,124... | collective-permute-start | bytes 1572872 | tf_op jit(solution)/shard_map/ppermute | solution.py:602
  48.6 2.5 %collective-permute-start.9 = (bf16[256,1024]{1,0:T(8,128)(2,1)}, bf16[256,1024]{1,0:T(8,128)(2,1)}, u32[]{:S(2)}, u32[]{:S(2)}) collective-permute-start(bf16[256,1024]{1,0:T(8,128)(2,1)} %get-tuple-element.99), channel_id=1, source_target_pairs={{0,8},{4,12},{8,16},{12,20},{16,24},{20,28},{24,0},{28,4},{32,40},... | collective-permute-start | bytes 1572872 | tf_op jit(solution)/shard_map/ppermute | solution.py:602
  51.1 12.5 %place_entries.1 = bf16[32,528,128]{2,1,0:T(8,128)(2,1)} custom-call(s32[8192]{0:T(1024)} %bitcast.19, f32[512,1024]{1,0:T(8,128)} %get-tuple-element.92.base_hbm, bf16[512,1024]{1,0:T(8,128)(2,1)} %collective-permute-done.6.mate_hbm, bf16[512,1024]{1,0:T(8,128)(2,1)} %collective-permute-done.5.far_hbm, f32[64,512]{1,0:T(8,128)} %get-tuple-element.95.ids_ref, ...), custom_call_target="tpu_custom_call" | custom-call | flops 1 | bytes 1 | tf_op jit(solution)/shard_map/place_entries/pallas_call | solution.py:165
  63.6 0.0 copy-start.3
  63.6 0.8 copy-done.3
  64.4 5.7 %all-to-all-start = ((bf16[32,528,128]{2,1,0:T(8,128)(2,1)}), bf16[32,528,128]{2,1,0:T(8,128)(2,1)}, u32[]{:S(2)}, u32[]{:S(2)}) async-start(bf16[32,528,128]{2,1,0:T(8,128)(2,1)} %place_entries.1), calls=%async_computation | async-start | bytes 8650752 | tf_op jit(solution)/shard_map/all_to_all | solution.py:606
  70.1 6.4 %own_terms.1 = (bf16[512,512]{1,0:T(8,128)(2,1)}, bf16[512,512]{1,0:T(8,128)(2,1)}, bf16[512,512]{1,0:T(8,128)(2,1)}, bf16[512,512]{1,0:T(8,128)(2,1)}) custom-call(s32[1]{0:T(128)} %bitcast.z_ref, s32[1]{0:T(128)} %bitcast.1.y_ref, bf16[512,4096]{1,0:T(8,128)(2,1)} %embedded_hbm.5, bf16[1024,512]{1,0:T(8,128)(2,1)} %get-tuple-element.68.turned_hbm, ...), custom_call_target="tpu_custom_call" | custom-call | flops 1 | bytes 1 | tf_op jit(solution)/shard_map/own_terms/pallas_call | solution.py:541
  76.5 43.0 %all-to-all-done.recv_hbm = bf16[32,528,128]{2,1,0:T(8,128)(2,1)} async-done(((bf16[32,528,128]{2,1,0:T(8,128)(2,1)}), bf16[32,528,128]{2,1,0:T(8,128)(2,1)}, u32[]{:S(2)}, u32[]{:S(2)}) %all-to-all-start) | async-done | bytes 4325408 | tf_op jit(solution)/shard_map/all_to_all | solution.py:606
  119.4 5.5 %collective-permute-start.11 = (bf16[512,512]{1,0:T(8,128)(2,1)}, bf16[512,512]{1,0:T(8,128)(2,1)S(1)}, u32[]{:S(2)}, u32[]{:S(2)}) collective-permute-start(bf16[512,512]{1,0:T(8,128)(2,1)} %get-tuple-element.111), channel_id=1, source_target_pairs={{0,16},{4,20},{8,24},{12,28},{16,0},{20,4},{24,8},{28,12},{32,48},... | collective-permute-start | bytes 1572872 | tf_op jit(solution)/shard_map/ppermute | solution.py:610
  125.0 1.0 collective-permute-start.12
  125.9 16.5 %owned_sums.1 = (bf16[1024,128]{1,0:T(8,128)(2,1)}, bf16[1024,128]{1,0:T(8,128)(2,1)}, f32[8,128]{1,0:T(8,128)}) custom-call(s32[1]{0:T(128)} %bitcast.9.core_ref, bf16[32,528,128]{2,1,0:T(8,128)(2,1)} %all-to-all-done.recv_hbm), custom_call_target="tpu_custom_call" | custom-call | flops 1 | bytes 1 | tf_op jit(solution)/shard_map/owned_sums/pallas_call | solution.py:247
  142.4 0.1 collective-permute-start.15
  142.6 0.1 convert_add_fusion.1
  142.7 0.1 convert_add_fusion
  142.9 0.1 collective-permute-start.14
  143.1 0.1 collective-permute-start.13
  143.2 1.1 collective-permute-done.15
  144.3 0.1 add_convert_fusion.2
  144.3 2.8 %collective-permute-start.16 = (bf16[1024,128]{1,0:T(8,128)(2,1)S(1)}, bf16[1024,128]{1,0:T(8,128)(2,1)S(1)}, u32[]{:S(2)}, u32[]{:S(2)}) collective-permute-start(bf16[1024,128]{1,0:T(8,128)(2,1)S(1)} %add_convert_fusion.2), channel_id=1, source_target_pairs={{0,2},{1,3},{2,0},{3,1},{4,6},{5,7},{6,4},{7,5},{8,10},{9,11},{10,... | collective-permute-start | bytes 786440 | tf_op jit(solution)/shard_map/ppermute | solution.py:622
  147.2 4.6 %collective-permute-done.14 = bf16[256,512]{1,0:T(8,128)(2,1)S(1)} collective-permute-done((bf16[256,512]{1,0:T(8,128)(2,1)S(1)}, bf16[256,512]{1,0:T(8,128)(2,1)S(1)}, u32[]{:S(2)}, u32[]{:S(2)}) %collective-permute-start.14) | collective-permute-done | bytes 262176 | tf_op jit(solution)/shard_map/ppermute | solution.py:617
  151.7 0.1 add_convert_fusion.3
  151.8 0.0 collective-permute-done.13
  151.8 0.1 add_convert_fusion.4
  152.0 0.1 collective-permute-start.18
  152.1 2.2 %collective-permute-done.16 = bf16[1024,128]{1,0:T(8,128)(2,1)S(1)} collective-permute-done((bf16[1024,128]{1,0:T(8,128)(2,1)S(1)}, bf16[1024,128]{1,0:T(8,128)(2,1)S(1)}, u32[]{:S(2)}, u32[]{:S(2)}) %collective-permute-start.16) | collective-permute-done | bytes 262176 | tf_op jit(solution)/shard_map/ppermute | solution.py:622
  154.3 0.1 add_convert_fusion.1
  154.4 0.1 collective-permute-start.17
  154.5 5.8 %collective-permute-done.18 = bf16[136,1024]{1,0:T(8,128)(2,1)S(1)} collective-permute-done((bf16[136,1024]{1,0:T(8,128)(2,1)S(1)}, bf16[136,1024]{1,0:T(8,128)(2,1)S(1)}, u32[]{:S(2)}, u32[]{:S(2)}) %collective-permute-start.18) | collective-permute-done | bytes 278560 | tf_op jit(solution)/shard_map/ppermute | solution.py:623
  160.4 0.3 fusion.2
  160.8 0.6 fusion.5
  161.4 1.3 fusion.1
  162.7 0.9 add_multiply_fusion
  (29 shorter events, 0.2 us)
Async XLA Ops:
  0.7 20.6 %copy-start.5 = (s32[1,512,16,1]{1,3,2,0:T(1,128)S(1)}, s32[1,512,16,1]{1,3,2,0:T(1,128)}, u32[]{:S(2)}) copy-start(s32[1,512,16,1]{1,3,2,0:T(1,128)} %param.14) | copy-start | bytes 98308
  9.2 6.3 %collective-permute-start = (bf16[512,1024]{1,0:T(8,128)(2,1)}, bf16[512,1024]{1,0:T(8,128)(2,1)S(1)}, u32[]{:S(2)}, u32[]{:S(2)}) collective-permute-start(bf16[512,1024]{1,0:T(8,128)(2,1)} %get-tuple-element.65), channel_id=1, source_target_pairs={{0,1},{1,0},{2,3},{3,2},{4,5},{5,4},{6,7},{7,6},{8,9},{9,8},{10,11... | collective-permute-start | bytes 3145736 | tf_op jit(solution)/shard_map/ppermute | solution.py:587
  9.3 28.2 %collective-permute-start.1 = (bf16[512,1024]{1,0:T(8,128)(2,1)}, bf16[512,1024]{1,0:T(8,128)(2,1)}, u32[]{:S(2)}, u32[]{:S(2)}) collective-permute-start(bf16[512,1024]{1,0:T(8,128)(2,1)} %get-tuple-element.73), channel_id=1, source_target_pairs={{0,32},{4,36},{8,40},{12,44},{16,48},{20,52},{24,56},{28,60},{32,6... | collective-permute-start | bytes 3145736 | tf_op jit(solution)/shard_map/ppermute | solution.py:589
  11.3 26.2 %collective-permute-start.2 = (bf16[512,1024]{1,0:T(8,128)(2,1)}, bf16[512,1024]{1,0:T(8,128)(2,1)}, u32[]{:S(2)}, u32[]{:S(2)}) collective-permute-start(bf16[512,1024]{1,0:T(8,128)(2,1)} %get-tuple-element.74), channel_id=1, source_target_pairs={{0,96},{4,100},{8,104},{12,108},{16,112},{20,116},{24,120},{28,124... | collective-permute-start | bytes 3145736 | tf_op jit(solution)/shard_map/ppermute | solution.py:589
  13.5 25.4 %collective-permute-start.3 = (bf16[512,1024]{1,0:T(8,128)(2,1)}, bf16[512,1024]{1,0:T(8,128)(2,1)}, u32[]{:S(2)}, u32[]{:S(2)}) collective-permute-start(bf16[512,1024]{1,0:T(8,128)(2,1)} %get-tuple-element.75), channel_id=1, source_target_pairs={{0,8},{4,12},{8,16},{12,20},{16,24},{20,28},{24,0},{28,4},{32,40},... | collective-permute-start | bytes 3145736 | tf_op jit(solution)/shard_map/ppermute | solution.py:589
  13.7 26.4 %collective-permute-start.4 = (bf16[512,1024]{1,0:T(8,128)(2,1)}, bf16[512,1024]{1,0:T(8,128)(2,1)}, u32[]{:S(2)}, u32[]{:S(2)}) collective-permute-start(bf16[512,1024]{1,0:T(8,128)(2,1)} %get-tuple-element.76), channel_id=1, source_target_pairs={{0,24},{4,28},{8,0},{12,4},{16,8},{20,12},{24,16},{28,20},{32,56},... | collective-permute-start | bytes 3145736 | tf_op jit(solution)/shard_map/ppermute | solution.py:589
  18.2 26.4 %collective-permute-start.5 = (bf16[512,1024]{1,0:T(8,128)(2,1)}, bf16[512,1024]{1,0:T(8,128)(2,1)}, u32[]{:S(2)}, u32[]{:S(2)}) collective-permute-start(bf16[512,1024]{1,0:T(8,128)(2,1)} %add_convert_fusion), channel_id=1, source_target_pairs={{0,2},{1,3},{2,0},{3,1},{4,6},{5,7},{6,4},{7,5},{8,10},{9,11},{10,... | collective-permute-start | bytes 3145736 | tf_op jit(solution)/shard_map/ppermute | solution.py:592
  40.1 11.0 %collective-permute-start.6 = (bf16[512,1024]{1,0:T(8,128)(2,1)}, bf16[512,1024]{1,0:T(8,128)(2,1)}, u32[]{:S(2)}, u32[]{:S(2)}) collective-permute-start(bf16[512,1024]{1,0:T(8,128)(2,1)} %get-tuple-element.93), channel_id=1, source_target_pairs={{0,1},{1,0},{2,3},{3,2},{4,5},{5,4},{6,7},{7,6},{8,9},{9,8},{10,11... | collective-permute-start | bytes 3145736 | tf_op jit(solution)/shard_map/ppermute | solution.py:599
  44.6 19.0 %collective-permute-start.10 = (bf16[256,1024]{1,0:T(8,128)(2,1)}, bf16[256,1024]{1,0:T(8,128)(2,1)S(1)}, u32[]{:S(2)}, u32[]{:S(2)}) collective-permute-start(bf16[256,1024]{1,0:T(8,128)(2,1)} %get-tuple-element.100), channel_id=1, source_target_pairs={{0,24},{4,28},{8,0},{12,4},{16,8},{20,12},{24,16},{28,20},{32,56},... | collective-permute-start | bytes 1572872 | tf_op jit(solution)/shard_map/ppermute | solution.py:602
  45.4 18.2 %collective-permute-start.7 = (bf16[256,1024]{1,0:T(8,128)(2,1)}, bf16[256,1024]{1,0:T(8,128)(2,1)}, u32[]{:S(2)}, u32[]{:S(2)}) collective-permute-start(bf16[256,1024]{1,0:T(8,128)(2,1)} %get-tuple-element.97), channel_id=1, source_target_pairs={{0,32},{4,36},{8,40},{12,44},{16,48},{20,52},{24,56},{28,60},{32,6... | collective-permute-start | bytes 1572872 | tf_op jit(solution)/shard_map/ppermute | solution.py:602
  45.4 18.3 %collective-permute-start.8 = (bf16[256,1024]{1,0:T(8,128)(2,1)}, bf16[256,1024]{1,0:T(8,128)(2,1)}, u32[]{:S(2)}, u32[]{:S(2)}) collective-permute-start(bf16[256,1024]{1,0:T(8,128)(2,1)} %get-tuple-element.98), channel_id=1, source_target_pairs={{0,96},{4,100},{8,104},{12,108},{16,112},{20,116},{24,120},{28,124... | collective-permute-start | bytes 1572872 | tf_op jit(solution)/shard_map/ppermute | solution.py:602
  48.6 15.0 %collective-permute-start.9 = (bf16[256,1024]{1,0:T(8,128)(2,1)}, bf16[256,1024]{1,0:T(8,128)(2,1)}, u32[]{:S(2)}, u32[]{:S(2)}) collective-permute-start(bf16[256,1024]{1,0:T(8,128)(2,1)} %get-tuple-element.99), channel_id=1, source_target_pairs={{0,8},{4,12},{8,16},{12,20},{16,24},{20,28},{24,0},{28,4},{32,40},... | collective-permute-start | bytes 1572872 | tf_op jit(solution)/shard_map/ppermute | solution.py:602
  63.6 0.8 copy-start.3
  64.4 55.0 %all-to-all-start = ((bf16[32,528,128]{2,1,0:T(8,128)(2,1)}), bf16[32,528,128]{2,1,0:T(8,128)(2,1)}, u32[]{:S(2)}, u32[]{:S(2)}) async-start(bf16[32,528,128]{2,1,0:T(8,128)(2,1)} %place_entries.1), calls=%async_computation | async-start | bytes 8650752 | tf_op jit(solution)/shard_map/all_to_all | solution.py:606
  76.4 66.1 %copy-start.2 = (bf16[512,512]{1,0:T(8,128)(2,1)S(1)}, bf16[512,512]{1,0:T(8,128)(2,1)}, u32[]{:S(2)}) copy-start(bf16[512,512]{1,0:T(8,128)(2,1)} %get-tuple-element.105) | copy-start | bytes 1572868
  76.4 66.3 %copy-start.1 = (bf16[512,512]{1,0:T(8,128)(2,1)S(1)}, bf16[512,512]{1,0:T(8,128)(2,1)}, u32[]{:S(2)}) copy-start(bf16[512,512]{1,0:T(8,128)(2,1)} %get-tuple-element.114) | copy-start | bytes 1572868
  119.4 23.1 %collective-permute-start.11 = (bf16[512,512]{1,0:T(8,128)(2,1)}, bf16[512,512]{1,0:T(8,128)(2,1)S(1)}, u32[]{:S(2)}, u32[]{:S(2)}) collective-permute-start(bf16[512,512]{1,0:T(8,128)(2,1)} %get-tuple-element.111), channel_id=1, source_target_pairs={{0,16},{4,20},{8,24},{12,28},{16,0},{20,4},{24,8},{28,12},{32,48},... | collective-permute-start | bytes 1572872 | tf_op jit(solution)/shard_map/ppermute | solution.py:610
  125.0 17.6 %collective-permute-start.12 = (bf16[512,512]{1,0:T(8,128)(2,1)}, bf16[512,512]{1,0:T(8,128)(2,1)S(1)}, u32[]{:S(2)}, u32[]{:S(2)}) collective-permute-start(bf16[512,512]{1,0:T(8,128)(2,1)} %get-tuple-element.112), channel_id=1, source_target_pairs={{0,64},{4,68},{8,72},{12,76},{16,80},{20,84},{24,88},{28,92},{32,9... | collective-permute-start | bytes 1572872 | tf_op jit(solution)/shard_map/ppermute | solution.py:610
  142.4 1.8 %copy-start.4 = (bf16[1024,128]{1,0:T(8,128)(2,1)S(1)}, bf16[1024,128]{1,0:T(8,128)(2,1)}, u32[]{:S(2)}) copy-start(bf16[1024,128]{1,0:T(8,128)(2,1)} %get-tuple-element.118) | copy-start | bytes 786436
  142.4 1.8 %collective-permute-start.15 = (bf16[1024,128]{1,0:T(8,128)(2,1)}, bf16[1024,128]{1,0:T(8,128)(2,1)S(1)}, u32[]{:S(2)}, u32[]{:S(2)}) collective-permute-start(bf16[1024,128]{1,0:T(8,128)(2,1)} %get-tuple-element.117), channel_id=1, source_target_pairs={{0,1},{1,0},{2,3},{3,2},{4,5},{5,4},{6,7},{7,6},{8,9},{9,8},{10,11... | collective-permute-start | bytes 786440 | tf_op jit(solution)/shard_map/ppermute | solution.py:612
  142.9 17.9 %copy-start.6 = (f32[2048]{0:T(1024)S(1)}, f32[2048]{0:T(1024)}, u32[]{:S(2)}) copy-start(f32[2048]{0:T(1024)} %param.17) | copy-start | bytes 24580
  142.9 18.5 %copy-start = (f32[2048,128]{1,0:T(8,128)S(1)}, f32[2048,128]{1,0:T(8,128)}, u32[]{:S(2)}) copy-start(f32[2048,128]{1,0:T(8,128)} %param.16) | copy-start | bytes 3145732
  142.9 8.8 %collective-permute-start.14 = (bf16[256,512]{1,0:T(8,128)(2,1)S(1)}, bf16[256,512]{1,0:T(8,128)(2,1)S(1)}, u32[]{:S(2)}, u32[]{:S(2)}) collective-permute-start(bf16[256,512]{1,0:T(8,128)(2,1)S(1)} %get-tuple-element.128), channel_id=1, source_target_pairs={{0,32},{4,36},{8,40},{12,44},{16,48},{20,52},{24,56},{28,60},{32,0... | collective-permute-start | bytes 786440 | tf_op jit(solution)/shard_map/ppermute | solution.py:617
  143.1 8.8 %collective-permute-start.13 = (bf16[256,512]{1,0:T(8,128)(2,1)S(1)}, bf16[256,512]{1,0:T(8,128)(2,1)S(1)}, u32[]{:S(2)}, u32[]{:S(2)}) collective-permute-start(bf16[256,512]{1,0:T(8,128)(2,1)S(1)} %get-tuple-element.129), channel_id=1, source_target_pairs={{0,8},{4,12},{8,0},{12,4},{16,24},{20,28},{24,16},{28,20},{32,40},... | collective-permute-start | bytes 786440 | tf_op jit(solution)/shard_map/ppermute | solution.py:617
  144.3 9.9 %collective-permute-start.16 = (bf16[1024,128]{1,0:T(8,128)(2,1)S(1)}, bf16[1024,128]{1,0:T(8,128)(2,1)S(1)}, u32[]{:S(2)}, u32[]{:S(2)}) collective-permute-start(bf16[1024,128]{1,0:T(8,128)(2,1)S(1)} %add_convert_fusion.2), channel_id=1, source_target_pairs={{0,2},{1,3},{2,0},{3,1},{4,6},{5,7},{6,4},{7,5},{8,10},{9,11},{10,... | collective-permute-start | bytes 786440 | tf_op jit(solution)/shard_map/ppermute | solution.py:622
  152.0 8.3 %collective-permute-start.18 = (bf16[136,1024]{1,0:T(8,128)(2,1)S(1)}, bf16[136,1024]{1,0:T(8,128)(2,1)S(1)}, u32[]{:S(2)}, u32[]{:S(2)}) collective-permute-start(bf16[136,1024]{1,0:T(8,128)(2,1)S(1)} %pad.4), channel_id=1, source_target_pairs={{0,4},{4,0},{8,12},{12,8},{16,20},{20,16},{24,28},{28,24},{32,36},... | collective-permute-start | bytes 835592 | tf_op jit(solution)/shard_map/ppermute | solution.py:623
  154.4 6.0 %collective-permute-start.17 = (bf16[1024,128]{1,0:T(8,128)(2,1)S(1)}, bf16[1024,128]{1,0:T(8,128)(2,1)S(1)}, u32[]{:S(2)}, u32[]{:S(2)}) collective-permute-start(bf16[1024,128]{1,0:T(8,128)(2,1)S(1)} %add_convert_fusion.1), channel_id=1, source_target_pairs={{0,1},{1,0},{2,3},{3,2},{4,5},{5,4},{6,7},{7,6},{8,9},{9,8},{10,11... | collective-permute-start | bytes 786440 | tf_op jit(solution)/shard_map/ppermute | solution.py:627

commit v9 on v8

--- a/solution.py
+++ b/solution.py
@@ -21,7 +21,7 @@
 BF16 = jnp.bfloat16
 LIGHT = pl.CostEstimate(flops=1, bytes_accessed=1, transcendentals=0)
 VMEM_BYTES = 56 << 20
-VMEM_MOST = 63 << 20
+VMEM_MOST = 127 << 19
 NT = (((1,), (1,)), ((), ()))
 
 

time: 164 us -> 163 us (level)
  waiting for transfers between devices: 61.1 us -> 64.5 us
  starting transfers between devices: 31.2 us -> 27.9 us
    ppermute x1, waiting for transfers between devices: 4.55 us -> 6.46 us  [body(): lax.ppermute(quarters[1][1], 'wide', z_flip(1))]
    ppermute x1, starting transfers between devices: 2.8 us -> 0.9 us  [body(): lax.ppermute(chip, 'narrow', X_HI)]
    ppermute x1, starting transfers between devices: 5.53 us -> 3.8 us  [body(): lax.ppermute(send_y, 'wide', y_flip(2))]
where the time goes in v9:
time: 163 us
  waiting for transfers between devices  64.5 us (40%)
  Pallas kernels  62.3 us (38%)
  starting transfers between devices  27.9 us (17%)
  other arithmetic  6.47 us (4%)
    all_to_all x1, waiting for transfers between devices, body(): lax.all_to_all(payload, 'wide', split_axis=0, concat_axis=0, tiled=True)  44.5 us
    pallas_call x1, Pallas kernels, owned_sums(): pl.pallas_call(functools.partial(sums_kernel, norm_factor), out_shape=[ja...  16.5 us
    pallas_call x1, Pallas kernels, kept_terms(): pl.pallas_call(kept_kernel, out_shape=[shape((samples, width), F32), shap...  15.2 us
    pallas_call x1, Pallas kernels, place_entries(): pl.pallas_call(place_kernel, out_shape=jax.ShapeDtypeStruct((N_WIDE, BLOC...  12.5 us
    pallas_call x1, Pallas kernels, sent_terms(): pl.pallas_call(sent_kernel, out_shape=[full] * 2 + [shape((512, 1024), BF...  8.52 us
    ppermute x4, starting transfers between devices, body(): second = [lax.ppermute(second[q], 'wide', ways[q]) for q in range(4)]  6.47 us
    ppermute x1, waiting for transfers between devices, body(): lax.ppermute(quarters[1][1], 'wide', z_flip(1))  6.46 us
    pallas_call x1, Pallas kernels, own_terms(): pl.pallas_call(own_kernel, out_shape=[jax.ShapeDtypeStruct((512, 512), BF...  6.36 us
  transfers between devices with their start and end apart: 20, of which 9 were waited for; matrix products, arithmetic and copies ran while one was open for 2% of the time, Pallas kernels for 33%

profile of v9, /device:TPU:24, one launch (start us, length us, event | category | flops | bytes accessed | tf_op | source)
XLA Modules:
  0.0 162.9 jit_solution(15451906830612230660)
XLA Ops:
  0.7 8.5 %sent_terms.1 = (bf16[512,1024]{1,0:T(8,128)(2,1)}, bf16[512,1024]{1,0:T(8,128)(2,1)}, bf16[512,1024]{1,0:T(8,128)(2,1)}, bf16[512,1024]{1,0:T(8,128)(2,1)}, bf1...) custom-call(s32[1]{0:T(128)} %bitcast.2.n_ref, ...), custom_call_target="tpu_custom_call" | custom-call | flops 1 | bytes 1 | tf_op jit(solution)/shard_map/sent_terms/pallas_call | solution.py:351
  9.2 0.1 collective-permute-start
  9.3 2.0 %collective-permute-start.1 = (bf16[512,1024]{1,0:T(8,128)(2,1)}, bf16[512,1024]{1,0:T(8,128)(2,1)}, u32[]{:S(2)}, u32[]{:S(2)}) collective-permute-start(bf16[512,1024]{1,0:T(8,128)(2,1)} %get-tuple-element.73), channel_id=1, source_target_pairs={{0,32},{4,36},{8,40},{12,44},{16,48},{20,52},{24,56},{28,60},{32,6... | collective-permute-start | bytes 3145736 | tf_op jit(solution)/shard_map/ppermute | solution.py:589
  11.3 2.2 %collective-permute-start.2 = (bf16[512,1024]{1,0:T(8,128)(2,1)}, bf16[512,1024]{1,0:T(8,128)(2,1)}, u32[]{:S(2)}, u32[]{:S(2)}) collective-permute-start(bf16[512,1024]{1,0:T(8,128)(2,1)} %get-tuple-element.74), channel_id=1, source_target_pairs={{0,96},{4,100},{8,104},{12,108},{16,112},{20,116},{24,120},{28,124... | collective-permute-start | bytes 3145736 | tf_op jit(solution)/shard_map/ppermute | solution.py:589
  13.5 0.2 collective-permute-start.3
  13.7 1.8 %collective-permute-start.4 = (bf16[512,1024]{1,0:T(8,128)(2,1)}, bf16[512,1024]{1,0:T(8,128)(2,1)}, u32[]{:S(2)}, u32[]{:S(2)}) collective-permute-start(bf16[512,1024]{1,0:T(8,128)(2,1)} %get-tuple-element.76), channel_id=1, source_target_pairs={{0,24},{4,28},{8,0},{12,4},{16,8},{20,12},{24,16},{28,20},{32,56},... | collective-permute-start | bytes 3145736 | tf_op jit(solution)/shard_map/ppermute | solution.py:589
  15.5 2.7 %add_convert_fusion = bf16[512,1024]{1,0:T(8,128)(2,1)} fusion(bf16[512,1024]{1,0:T(8,128)(2,1)S(1)} %collective-permute-done, bf16[512,1024]{1,0:T(8,128)(2,1)} %get-tuple-element.64), kind=kLoop, calls=%fused_computation | loop fusion | flops 2097152 | bytes 3145728 | tf_op jit(solution)/shard_map/convert_element_type | solution.py:590
  18.2 3.0 %collective-permute-start.5 = (bf16[512,1024]{1,0:T(8,128)(2,1)}, bf16[512,1024]{1,0:T(8,128)(2,1)}, u32[]{:S(2)}, u32[]{:S(2)}) collective-permute-start(bf16[512,1024]{1,0:T(8,128)(2,1)} %add_convert_fusion), channel_id=1, source_target_pairs={{0,2},{1,3},{2,0},{3,1},{4,6},{5,7},{6,4},{7,5},{8,10},{9,11},{10,... | collective-permute-start | bytes 3145736 | tf_op jit(solution)/shard_map/ppermute | solution.py:592
  21.2 0.6 copy.15
  21.9 15.2 %kept_terms.1 = (f32[512,1024]{1,0:T(8,128)}, s32[64,128]{1,0:T(8,128)}, f32[64,512]{1,0:T(8,128)}, f32[8,128]{1,0:T(8,128)}, bf16[512,1024]{1,0:T(8,128)(2,1)},...) custom-call(s32[1]{0:T(128)} %bitcast.2.n_ref, ...), custom_call_target="tpu_custom_call" | custom-call | flops 1 | bytes 1 | tf_op jit(solution)/shard_map/kept_terms/pallas_call | solution.py:479
  37.1 0.4 collective-permute-done.1.refs_0_
  37.5 1.5 collective-permute-done.3.refs_2_
  38.9 1.2 collective-permute-done.4.refs_3_
  40.2 3.2 %passed_on.1 = (bf16[256,1024]{1,0:T(8,128)(2,1)}, bf16[256,1024]{1,0:T(8,128)(2,1)}, bf16[256,1024]{1,0:T(8,128)(2,1)}, bf16[256,1024]{1,0:T(8,128)(2,1)}) custom-call(bf16[512,1024]{1,0:T(8,128)(2,1)} %collective-permute-done.1.refs_0_, bf16[512,1024]{1,0:T(8,128)(2,1)} %collective-permute-done.2.refs_1_, ...), custom_call_target="tpu_custom_call" | custom-call | flops 1 | bytes 1 | tf_op jit(solution)/shard_map/passed_on/pallas_call | solution.py:394
  43.3 1.3 collective-permute-done.5.far_hbm
  44.6 0.8 collective-permute-start.10
  45.4 3.2 %collective-permute-start.8 = (bf16[256,1024]{1,0:T(8,128)(2,1)}, bf16[256,1024]{1,0:T(8,128)(2,1)}, u32[]{:S(2)}, u32[]{:S(2)}) collective-permute-start(bf16[256,1024]{1,0:T(8,128)(2,1)} %get-tuple-element.98), channel_id=1, source_target_pairs={{0,96},{4,100},{8,104},{12,108},{16,112},{20,116},{24,120},{28,124... | collective-permute-start | bytes 1572872 | tf_op jit(solution)/shard_map/ppermute | solution.py:602
  48.6 2.5 %collective-permute-start.9 = (bf16[256,1024]{1,0:T(8,128)(2,1)}, bf16[256,1024]{1,0:T(8,128)(2,1)}, u32[]{:S(2)}, u32[]{:S(2)}) collective-permute-start(bf16[256,1024]{1,0:T(8,128)(2,1)} %get-tuple-element.99), channel_id=1, source_target_pairs={{0,8},{4,12},{8,16},{12,20},{16,24},{20,28},{24,0},{28,4},{32,40},... | collective-permute-start | bytes 1572872 | tf_op jit(solution)/shard_map/ppermute | solution.py:602
  51.1 12.5 %place_entries.1 = bf16[32,528,128]{2,1,0:T(8,128)(2,1)} custom-call(s32[8192]{0:T(1024)} %bitcast.19, f32[512,1024]{1,0:T(8,128)} %get-tuple-element.92.base_hbm, bf16[512,1024]{1,0:T(8,128)(2,1)} %collective-permute-done.6.mate_hbm, bf16[512,1024]{1,0:T(8,128)(2,1)} %collective-permute-done.5.far_hbm, f32[64,512]{1,0:T(8,128)} %get-tuple-element.95.ids_ref, ...), custom_call_target="tpu_custom_call" | custom-call | flops 1 | bytes 1 | tf_op jit(solution)/shard_map/place_entries/pallas_call | solution.py:165
  63.6 5.8 %all-to-all-start = ((bf16[32,528,128]{2,1,0:T(8,128)(2,1)}), bf16[32,528,128]{2,1,0:T(8,128)(2,1)}, u32[]{:S(2)}, u32[]{:S(2)}) async-start(bf16[32,528,128]{2,1,0:T(8,128)(2,1)} %place_entries.1), calls=%async_computation | async-start | bytes 8650752 | tf_op jit(solution)/shard_map/all_to_all | solution.py:606
  69.4 6.4 %own_terms.1 = (bf16[512,512]{1,0:T(8,128)(2,1)}, bf16[512,512]{1,0:T(8,128)(2,1)}, bf16[512,512]{1,0:T(8,128)(2,1)}, bf16[512,512]{1,0:T(8,128)(2,1)}) custom-call(s32[1]{0:T(128)} %bitcast.z_ref, s32[1]{0:T(128)} %bitcast.1.y_ref, bf16[512,4096]{1,0:T(8,128)(2,1)} %embedded_hbm.5, bf16[1024,512]{1,0:T(8,128)(2,1)} %get-tuple-element.68.turned_hbm, ...), custom_call_target="tpu_custom_call" | custom-call | flops 1 | bytes 1 | tf_op jit(solution)/shard_map/own_terms/pallas_call | solution.py:541
  75.8 0.0 copy-start.2
  75.8 44.5 %all-to-all-done.recv_hbm = bf16[32,528,128]{2,1,0:T(8,128)(2,1)} async-done(((bf16[32,528,128]{2,1,0:T(8,128)(2,1)}), bf16[32,528,128]{2,1,0:T(8,128)(2,1)}, u32[]{:S(2)}, u32[]{:S(2)}) %all-to-all-start) | async-done | bytes 4325408 | tf_op jit(solution)/shard_map/all_to_all | solution.py:606
  120.3 3.8 %collective-permute-start.11 = (bf16[512,512]{1,0:T(8,128)(2,1)}, bf16[512,512]{1,0:T(8,128)(2,1)S(1)}, u32[]{:S(2)}, u32[]{:S(2)}) collective-permute-start(bf16[512,512]{1,0:T(8,128)(2,1)} %get-tuple-element.111), channel_id=1, source_target_pairs={{0,16},{4,20},{8,24},{12,28},{16,0},{20,4},{24,8},{28,12},{32,48},... | collective-permute-start | bytes 1572872 | tf_op jit(solution)/shard_map/ppermute | solution.py:610
  124.1 1.2 collective-permute-start.12
  125.3 16.5 %owned_sums.1 = (bf16[1024,128]{1,0:T(8,128)(2,1)}, bf16[1024,128]{1,0:T(8,128)(2,1)}, f32[8,128]{1,0:T(8,128)}) custom-call(s32[1]{0:T(128)} %bitcast.9.core_ref, bf16[32,528,128]{2,1,0:T(8,128)(2,1)} %all-to-all-done.recv_hbm), custom_call_target="tpu_custom_call" | custom-call | flops 1 | bytes 1 | tf_op jit(solution)/shard_map/owned_sums/pallas_call | solution.py:247
  141.8 0.1 collective-permute-start.15
  141.9 0.1 convert_add_fusion.1
  142.0 0.1 convert_add_fusion
  142.2 0.0 copy-start.5
  142.3 0.1 collective-permute-start.14
  142.4 0.1 collective-permute-start.13
  142.5 1.1 collective-permute-done.15
  143.6 0.1 add_convert_fusion.2
  143.7 0.9 collective-permute-start.16
  144.6 6.5 %collective-permute-done.14 = bf16[256,512]{1,0:T(8,128)(2,1)S(1)} collective-permute-done((bf16[256,512]{1,0:T(8,128)(2,1)S(1)}, bf16[256,512]{1,0:T(8,128)(2,1)S(1)}, u32[]{:S(2)}, u32[]{:S(2)}) %collective-permute-start.14) | collective-permute-done | bytes 262176 | tf_op jit(solution)/shard_map/ppermute | solution.py:617
  151.0 0.1 add_convert_fusion.3
  151.1 0.0 collective-permute-done.13
  151.2 0.1 add_convert_fusion.4
  151.3 0.1 collective-permute-start.18
  151.4 3.0 %collective-permute-done.16 = bf16[1024,128]{1,0:T(8,128)(2,1)S(1)} collective-permute-done((bf16[1024,128]{1,0:T(8,128)(2,1)S(1)}, bf16[1024,128]{1,0:T(8,128)(2,1)S(1)}, u32[]{:S(2)}, u32[]{:S(2)}) %collective-permute-start.16) | collective-permute-done | bytes 262176 | tf_op jit(solution)/shard_map/ppermute | solution.py:622
  154.4 0.1 add_convert_fusion.1
  154.5 0.1 collective-permute-start.17
  154.6 5.0 %collective-permute-done.18 = bf16[136,1024]{1,0:T(8,128)(2,1)S(1)} collective-permute-done((bf16[136,1024]{1,0:T(8,128)(2,1)S(1)}, bf16[136,1024]{1,0:T(8,128)(2,1)S(1)}, u32[]{:S(2)}, u32[]{:S(2)}) %collective-permute-start.18) | collective-permute-done | bytes 278560 | tf_op jit(solution)/shard_map/ppermute | solution.py:623
  159.7 0.3 fusion.2
  160.1 0.6 fusion.5
  160.7 1.3 fusion.1
  162.0 0.9 add_multiply_fusion
  (27 shorter events, 0.2 us)
Async XLA Ops:
  0.7 20.6 %copy-start.4 = (s32[1,512,16,1]{1,3,2,0:T(1,128)S(1)}, s32[1,512,16,1]{1,3,2,0:T(1,128)}, u32[]{:S(2)}) copy-start(s32[1,512,16,1]{1,3,2,0:T(1,128)} %param.14) | copy-start | bytes 98308
  9.2 6.3 %collective-permute-start = (bf16[512,1024]{1,0:T(8,128)(2,1)}, bf16[512,1024]{1,0:T(8,128)(2,1)S(1)}, u32[]{:S(2)}, u32[]{:S(2)}) collective-permute-start(bf16[512,1024]{1,0:T(8,128)(2,1)} %get-tuple-element.65), channel_id=1, source_target_pairs={{0,1},{1,0},{2,3},{3,2},{4,5},{5,4},{6,7},{7,6},{8,9},{9,8},{10,11... | collective-permute-start | bytes 3145736 | tf_op jit(solution)/shard_map/ppermute | solution.py:587
  9.3 28.2 %collective-permute-start.1 = (bf16[512,1024]{1,0:T(8,128)(2,1)}, bf16[512,1024]{1,0:T(8,128)(2,1)}, u32[]{:S(2)}, u32[]{:S(2)}) collective-permute-start(bf16[512,1024]{1,0:T(8,128)(2,1)} %get-tuple-element.73), channel_id=1, source_target_pairs={{0,32},{4,36},{8,40},{12,44},{16,48},{20,52},{24,56},{28,60},{32,6... | collective-permute-start | bytes 3145736 | tf_op jit(solution)/shard_map/ppermute | solution.py:589
  11.3 26.2 %collective-permute-start.2 = (bf16[512,1024]{1,0:T(8,128)(2,1)}, bf16[512,1024]{1,0:T(8,128)(2,1)}, u32[]{:S(2)}, u32[]{:S(2)}) collective-permute-start(bf16[512,1024]{1,0:T(8,128)(2,1)} %get-tuple-element.74), channel_id=1, source_target_pairs={{0,96},{4,100},{8,104},{12,108},{16,112},{20,116},{24,120},{28,124... | collective-permute-start | bytes 3145736 | tf_op jit(solution)/shard_map/ppermute | solution.py:589
  13.5 25.4 %collective-permute-start.3 = (bf16[512,1024]{1,0:T(8,128)(2,1)}, bf16[512,1024]{1,0:T(8,128)(2,1)}, u32[]{:S(2)}, u32[]{:S(2)}) collective-permute-start(bf16[512,1024]{1,0:T(8,128)(2,1)} %get-tuple-element.75), channel_id=1, source_target_pairs={{0,8},{4,12},{8,16},{12,20},{16,24},{20,28},{24,0},{28,4},{32,40},... | collective-permute-start | bytes 3145736 | tf_op jit(solution)/shard_map/ppermute | solution.py:589
  13.7 26.4 %collective-permute-start.4 = (bf16[512,1024]{1,0:T(8,128)(2,1)}, bf16[512,1024]{1,0:T(8,128)(2,1)}, u32[]{:S(2)}, u32[]{:S(2)}) collective-permute-start(bf16[512,1024]{1,0:T(8,128)(2,1)} %get-tuple-element.76), channel_id=1, source_target_pairs={{0,24},{4,28},{8,0},{12,4},{16,8},{20,12},{24,16},{28,20},{32,56},... | collective-permute-start | bytes 3145736 | tf_op jit(solution)/shard_map/ppermute | solution.py:589
  18.2 26.4 %collective-permute-start.5 = (bf16[512,1024]{1,0:T(8,128)(2,1)}, bf16[512,1024]{1,0:T(8,128)(2,1)}, u32[]{:S(2)}, u32[]{:S(2)}) collective-permute-start(bf16[512,1024]{1,0:T(8,128)(2,1)} %add_convert_fusion), channel_id=1, source_target_pairs={{0,2},{1,3},{2,0},{3,1},{4,6},{5,7},{6,4},{7,5},{8,10},{9,11},{10,... | collective-permute-start | bytes 3145736 | tf_op jit(solution)/shard_map/ppermute | solution.py:592
  40.1 10.9 %collective-permute-start.6 = (bf16[512,1024]{1,0:T(8,128)(2,1)}, bf16[512,1024]{1,0:T(8,128)(2,1)}, u32[]{:S(2)}, u32[]{:S(2)}) collective-permute-start(bf16[512,1024]{1,0:T(8,128)(2,1)} %get-tuple-element.93), channel_id=1, source_target_pairs={{0,1},{1,0},{2,3},{3,2},{4,5},{5,4},{6,7},{7,6},{8,9},{9,8},{10,11... | collective-permute-start | bytes 3145736 | tf_op jit(solution)/shard_map/ppermute | solution.py:599
  44.6 19.0 %collective-permute-start.10 = (bf16[256,1024]{1,0:T(8,128)(2,1)}, bf16[256,1024]{1,0:T(8,128)(2,1)}, u32[]{:S(2)}, u32[]{:S(2)}) collective-permute-start(bf16[256,1024]{1,0:T(8,128)(2,1)} %get-tuple-element.100), channel_id=1, source_target_pairs={{0,24},{4,28},{8,0},{12,4},{16,8},{20,12},{24,16},{28,20},{32,56},... | collective-permute-start | bytes 1572872 | tf_op jit(solution)/shard_map/ppermute | solution.py:602
  45.4 18.2 %collective-permute-start.7 = (bf16[256,1024]{1,0:T(8,128)(2,1)}, bf16[256,1024]{1,0:T(8,128)(2,1)}, u32[]{:S(2)}, u32[]{:S(2)}) collective-permute-start(bf16[256,1024]{1,0:T(8,128)(2,1)} %get-tuple-element.97), channel_id=1, source_target_pairs={{0,32},{4,36},{8,40},{12,44},{16,48},{20,52},{24,56},{28,60},{32,6... | collective-permute-start | bytes 1572872 | tf_op jit(solution)/shard_map/ppermute | solution.py:602
  45.4 18.2 %collective-permute-start.8 = (bf16[256,1024]{1,0:T(8,128)(2,1)}, bf16[256,1024]{1,0:T(8,128)(2,1)}, u32[]{:S(2)}, u32[]{:S(2)}) collective-permute-start(bf16[256,1024]{1,0:T(8,128)(2,1)} %get-tuple-element.98), channel_id=1, source_target_pairs={{0,96},{4,100},{8,104},{12,108},{16,112},{20,116},{24,120},{28,124... | collective-permute-start | bytes 1572872 | tf_op jit(solution)/shard_map/ppermute | solution.py:602
  48.6 15.0 %collective-permute-start.9 = (bf16[256,1024]{1,0:T(8,128)(2,1)}, bf16[256,1024]{1,0:T(8,128)(2,1)}, u32[]{:S(2)}, u32[]{:S(2)}) collective-permute-start(bf16[256,1024]{1,0:T(8,128)(2,1)} %get-tuple-element.99), channel_id=1, source_target_pairs={{0,8},{4,12},{8,16},{12,20},{16,24},{20,28},{24,0},{28,4},{32,40},... | collective-permute-start | bytes 1572872 | tf_op jit(solution)/shard_map/ppermute | solution.py:602
  63.6 56.7 %all-to-all-start = ((bf16[32,528,128]{2,1,0:T(8,128)(2,1)}), bf16[32,528,128]{2,1,0:T(8,128)(2,1)}, u32[]{:S(2)}, u32[]{:S(2)}) async-start(bf16[32,528,128]{2,1,0:T(8,128)(2,1)} %place_entries.1), calls=%async_computation | async-start | bytes 8650752 | tf_op jit(solution)/shard_map/all_to_all | solution.py:606
  75.8 66.1 %copy-start.2 = (bf16[512,512]{1,0:T(8,128)(2,1)S(1)}, bf16[512,512]{1,0:T(8,128)(2,1)}, u32[]{:S(2)}) copy-start(bf16[512,512]{1,0:T(8,128)(2,1)} %get-tuple-element.105) | copy-start | bytes 1572868
  75.8 66.2 %copy-start.1 = (bf16[512,512]{1,0:T(8,128)(2,1)S(1)}, bf16[512,512]{1,0:T(8,128)(2,1)}, u32[]{:S(2)}) copy-start(bf16[512,512]{1,0:T(8,128)(2,1)} %get-tuple-element.114) | copy-start | bytes 1572868
  120.3 21.6 %collective-permute-start.11 = (bf16[512,512]{1,0:T(8,128)(2,1)}, bf16[512,512]{1,0:T(8,128)(2,1)S(1)}, u32[]{:S(2)}, u32[]{:S(2)}) collective-permute-start(bf16[512,512]{1,0:T(8,128)(2,1)} %get-tuple-element.111), channel_id=1, source_target_pairs={{0,16},{4,20},{8,24},{12,28},{16,0},{20,4},{24,8},{28,12},{32,48},... | collective-permute-start | bytes 1572872 | tf_op jit(solution)/shard_map/ppermute | solution.py:610
  124.1 17.8 %collective-permute-start.12 = (bf16[512,512]{1,0:T(8,128)(2,1)}, bf16[512,512]{1,0:T(8,128)(2,1)S(1)}, u32[]{:S(2)}, u32[]{:S(2)}) collective-permute-start(bf16[512,512]{1,0:T(8,128)(2,1)} %get-tuple-element.112), channel_id=1, source_target_pairs={{0,64},{4,68},{8,72},{12,76},{16,80},{20,84},{24,88},{28,92},{32,9... | collective-permute-start | bytes 1572872 | tf_op jit(solution)/shard_map/ppermute | solution.py:610
  141.8 1.8 %copy-start.3 = (bf16[1024,128]{1,0:T(8,128)(2,1)S(1)}, bf16[1024,128]{1,0:T(8,128)(2,1)}, u32[]{:S(2)}) copy-start(bf16[1024,128]{1,0:T(8,128)(2,1)} %get-tuple-element.118) | copy-start | bytes 786436
  141.8 1.8 %collective-permute-start.15 = (bf16[1024,128]{1,0:T(8,128)(2,1)}, bf16[1024,128]{1,0:T(8,128)(2,1)S(1)}, u32[]{:S(2)}, u32[]{:S(2)}) collective-permute-start(bf16[1024,128]{1,0:T(8,128)(2,1)} %get-tuple-element.117), channel_id=1, source_target_pairs={{0,1},{1,0},{2,3},{3,2},{4,5},{5,4},{6,7},{7,6},{8,9},{9,8},{10,11... | collective-permute-start | bytes 786440 | tf_op jit(solution)/shard_map/ppermute | solution.py:612
  142.2 17.9 %copy-start.5 = (f32[2048]{0:T(1024)S(1)}, f32[2048]{0:T(1024)}, u32[]{:S(2)}) copy-start(f32[2048]{0:T(1024)} %param.17) | copy-start | bytes 24580
  142.2 18.5 %copy-start = (f32[2048,128]{1,0:T(8,128)S(1)}, f32[2048,128]{1,0:T(8,128)}, u32[]{:S(2)}) copy-start(f32[2048,128]{1,0:T(8,128)} %param.16) | copy-start | bytes 3145732
  142.3 8.8 %collective-permute-start.14 = (bf16[256,512]{1,0:T(8,128)(2,1)S(1)}, bf16[256,512]{1,0:T(8,128)(2,1)S(1)}, u32[]{:S(2)}, u32[]{:S(2)}) collective-permute-start(bf16[256,512]{1,0:T(8,128)(2,1)S(1)} %get-tuple-element.128), channel_id=1, source_target_pairs={{0,32},{4,36},{8,40},{12,44},{16,48},{20,52},{24,56},{28,60},{32,0... | collective-permute-start | bytes 786440 | tf_op jit(solution)/shard_map/ppermute | solution.py:617
  142.4 8.8 %collective-permute-start.13 = (bf16[256,512]{1,0:T(8,128)(2,1)S(1)}, bf16[256,512]{1,0:T(8,128)(2,1)S(1)}, u32[]{:S(2)}, u32[]{:S(2)}) collective-permute-start(bf16[256,512]{1,0:T(8,128)(2,1)S(1)} %get-tuple-element.129), channel_id=1, source_target_pairs={{0,8},{4,12},{8,0},{12,4},{16,24},{20,28},{24,16},{28,20},{32,40},... | collective-permute-start | bytes 786440 | tf_op jit(solution)/shard_map/ppermute | solution.py:617
  143.7 10.7 %collective-permute-start.16 = (bf16[1024,128]{1,0:T(8,128)(2,1)S(1)}, bf16[1024,128]{1,0:T(8,128)(2,1)S(1)}, u32[]{:S(2)}, u32[]{:S(2)}) collective-permute-start(bf16[1024,128]{1,0:T(8,128)(2,1)S(1)} %add_convert_fusion.2), channel_id=1, source_target_pairs={{0,2},{1,3},{2,0},{3,1},{4,6},{5,7},{6,4},{7,5},{8,10},{9,11},{10,... | collective-permute-start | bytes 786440 | tf_op jit(solution)/shard_map/ppermute | solution.py:622
  151.3 8.3 %collective-permute-start.18 = (bf16[136,1024]{1,0:T(8,128)(2,1)S(1)}, bf16[136,1024]{1,0:T(8,128)(2,1)S(1)}, u32[]{:S(2)}, u32[]{:S(2)}) collective-permute-start(bf16[136,1024]{1,0:T(8,128)(2,1)S(1)} %pad.4), channel_id=1, source_target_pairs={{0,4},{4,0},{8,12},{12,8},{16,20},{20,16},{24,28},{28,24},{32,36},... | collective-permute-start | bytes 835592 | tf_op jit(solution)/shard_map/ppermute | solution.py:623
  154.5 5.2 %collective-permute-start.17 = (bf16[1024,128]{1,0:T(8,128)(2,1)S(1)}, bf16[1024,128]{1,0:T(8,128)(2,1)S(1)}, u32[]{:S(2)}, u32[]{:S(2)}) collective-permute-start(bf16[1024,128]{1,0:T(8,128)(2,1)S(1)} %add_convert_fusion.1), channel_id=1, source_target_pairs={{0,1},{1,0},{2,3},{3,2},{4,5},{5,4},{6,7},{7,6},{8,9},{9,8},{10,11... | collective-permute-start | bytes 786440 | tf_op jit(solution)/shard_map/ppermute | solution.py:627
